TPU v7x, 32 devices: a whole 2x2x4 slice. The times are simulated.
32 devices in a mesh: dp: 8 (over z, x), tensor: 4 (over y, core).
Axes of the slice: x: 2, y: 2, z: 4, core: 2. Of those that a mesh axis runs over, the one named last changes fastest.
Arguments:
- patches: bfloat16 [64, 197, 768], P('dp'), may hold values from -6 to 6
- attn_gain: bfloat16 [768], replicated, may hold values from 0.25 to 1.75
- attn_shift: bfloat16 [768], replicated, may hold values from -3 to 3
- qkv_weight: bfloat16 [3, 768, 768], P(None, 'dp', 'tensor'), may hold values from -0.21875 to 0.21875
- qv_bias: bfloat16 [2, 768], P(None, 'tensor'), may hold values from -3 to 3
- out_weight: bfloat16 [768, 768], P('tensor', 'dp'), may hold values from -0.875 to 0.875
- out_bias: bfloat16 [768], replicated, may hold values from -3 to 3
- mlp_gain: bfloat16 [768], replicated, may hold values from 0.25 to 1.75
- mlp_shift: bfloat16 [768], replicated, may hold values from -3 to 3
- fc1_weight: bfloat16 [768, 3072], P('dp', 'tensor'), may hold values from -0.21875 to 0.21875
- fc1_bias: bfloat16 [3072], P('tensor'), may hold values from -3 to 3
- fc2_weight: bfloat16 [3072, 768], P('tensor', 'dp'), may hold values from -0.109375 to 0.109375
- fc2_bias: bfloat16 [768], replicated, may hold values from -3 to 3
- cotangent: bfloat16 [64, 197, 768], P('dp'), may hold values from -6 to 6
Outputs:
- encoded: bfloat16 [64, 197, 768], P('dp')
- patch_grad: bfloat16 [64, 197, 768], P('dp')
- attn_gain_grad: float32 [768], replicated
- attn_shift_grad: float32 [768], replicated
- qkv_weight_grad: float32 [3, 768, 768], P(None, 'dp', 'tensor')
- qv_bias_grad: float32 [2, 768], P(None, 'tensor')
- out_weight_grad: float32 [768, 768], P('tensor', 'dp')
- out_bias_grad: float32 [768], replicated
- mlp_gain_grad: float32 [768], replicated
- mlp_shift_grad: float32 [768], replicated
- fc1_weight_grad: float32 [768, 3072], P('dp', 'tensor')
- fc1_bias_grad: float32 [3072], P('tensor')
- fc2_weight_grad: float32 [3072, 768], P('tensor', 'dp')
- fc2_bias_grad: float32 [768], replicated
All inputs are finite; a program needn't handle non-finite values.
Results may differ from a plain program's by a relative error of at most 0.02.
Values may be sent and summed in bfloat16 or wider, within the bound.
No kernel may reach another device: no remote copies, remote signals or barrier semaphores. Data moves between devices by JAX's collectives and lax.ppermute only.
A program may use at most 128 MiB of HBM per device.

v0:
```python
from functools import partial

import jax
import jax.numpy as jnp
from jax import lax
from jax.sharding import PartitionSpec as P

HEAD_DIM = 64


EPS = 1e-06


def layer_norm(values, gain, shift):
    centre = values - jnp.mean(values, -1, keepdims=True)
    inverse = lax.rsqrt(jnp.mean(centre * centre, -1, keepdims=True) + EPS)
    normed = centre * inverse
    return (normed * gain + shift, normed, inverse)


def row_total(values):
    return jnp.sum(values.reshape(-1, values.shape[-1]), 0)


def norm_back(upstream, normed, inverse, gain):
    scaled = upstream * gain
    inner = (
        scaled
        - jnp.mean(scaled, -1, keepdims=True)
        - normed * jnp.mean(scaled * normed, -1, keepdims=True)
    )
    return (inverse * inner, row_total(upstream * normed), row_total(upstream))


def split_heads(values):
    return values.reshape(values.shape[0], values.shape[1], values.shape[2] // HEAD_DIM, HEAD_DIM)


def on_device(
    patches,
    attn_gain,
    attn_shift,
    qkv_weight,
    qv_bias,
    out_weight,
    out_bias,
    mlp_gain,
    mlp_shift,
    fc1_weight,
    fc1_bias,
    fc2_weight,
    fc2_bias,
    cotangent,
):
    low_type = jnp.bfloat16
    wide = jnp.float32
    factor = HEAD_DIM ** (-0.5)
    w_qkv, w_out, w_fc1, w_fc2 = (
        lax.all_gather(qkv_weight, "dp", axis=1, tiled=True),
        lax.all_gather(out_weight, "dp", axis=1, tiled=True),
        lax.all_gather(fc1_weight, "dp", axis=0, tiled=True),
        lax.all_gather(fc2_weight, "dp", axis=1, tiled=True),
    )
    count, length = (patches.shape[0], patches.shape[1])
    inputs = patches.astype(wide)
    gain_one = attn_gain.astype(wide)
    gain_two = mlp_gain.astype(wide)
    norm_one, normed_one, inverse_one = layer_norm(inputs, gain_one, attn_shift.astype(wide))
    norm_one_low = norm_one.astype(low_type)
    projected = jnp.einsum("bsd,kde->kbse", norm_one_low, w_qkv, preferred_element_type=wide)
    bias_pair = qv_bias.astype(wide)
    qkv_low = jnp.stack(
        (projected[0] + bias_pair[0], projected[1], projected[2] + bias_pair[1])
    ).astype(low_type)
    query_low = split_heads(qkv_low[0])
    key_low = split_heads(qkv_low[1])
    value_low = split_heads(qkv_low[2])
    scores = jnp.einsum("bqhe,bkhe->bhqk", query_low, key_low, preferred_element_type=wide) * factor
    lse = jax.nn.logsumexp(scores, -1, keepdims=True)
    probs = jnp.exp(scores - lse)
    mixed = jnp.einsum(
        "bhqk,bkhe->bqhe", probs.astype(low_type), value_low, preferred_element_type=wide
    )
    attended = mixed.reshape(count, length, -1).astype(low_type)
    attn_part = jnp.einsum("bse,ed->bsd", attended, w_out, preferred_element_type=wide)
    attn_full = lax.psum(attn_part.astype(jnp.bfloat16), "tensor").astype(jnp.float32)
    hidden_state = inputs + attn_full + out_bias.astype(wide)
    norm_two, normed_two, inverse_two = layer_norm(hidden_state, gain_two, mlp_shift.astype(wide))
    norm_two_low = norm_two.astype(low_type)
    pre_act = jnp.einsum(
        "bsd,df->bsf", norm_two_low, w_fc1, preferred_element_type=wide
    ) + fc1_bias.astype(wide)
    activated, gelu_pull = jax.vjp(partial(jax.nn.gelu, approximate=False), pre_act)
    act_low = activated.astype(low_type)
    mlp_part = jnp.einsum("bsf,fd->bsd", act_low, w_fc2, preferred_element_type=wide)
    mlp_full = lax.psum(mlp_part.astype(jnp.bfloat16), "tensor").astype(jnp.float32)
    encoded = (hidden_state + mlp_full + fc2_bias.astype(wide)).astype(low_type)
    w_qkv, w_out, w_fc1, w_fc2 = (
        lax.all_gather(qkv_weight, "dp", axis=1, tiled=True),
        lax.all_gather(out_weight, "dp", axis=1, tiled=True),
        lax.all_gather(fc1_weight, "dp", axis=0, tiled=True),
        lax.all_gather(fc2_weight, "dp", axis=1, tiled=True),
    )
    upstream = cotangent.astype(wide)
    fc2_bias_part = jnp.sum(upstream, (0, 1))
    fc2_grad_part = jnp.einsum("bsf,bsd->fd", act_low, cotangent, preferred_element_type=wide)
    dact = jnp.einsum("bsd,fd->bsf", cotangent, w_fc2, preferred_element_type=wide)
    dpre_low = gelu_pull(dact)[0].astype(low_type)
    fc1_bias_part = jnp.sum(dpre_low.astype(wide), (0, 1))
    fc1_grad_part = jnp.einsum("bsd,bsf->df", norm_two_low, dpre_low, preferred_element_type=wide)
    dnorm_two_part = jnp.einsum("bsf,df->bsd", dpre_low, w_fc1, preferred_element_type=wide)
    dnorm_two = lax.psum(dnorm_two_part.astype(jnp.bfloat16), "tensor").astype(jnp.float32)
    dhidden_norm, gain_two_part, shift_two_part = norm_back(
        dnorm_two, normed_two, inverse_two, gain_two
    )
    dhidden = upstream + dhidden_norm
    out_bias_part = row_total(dhidden)
    dhidden_low = dhidden.astype(low_type)
    out_grad_part = jnp.einsum("bse,bsd->ed", attended, dhidden_low, preferred_element_type=wide)
    dattended = split_heads(
        jnp.einsum("bsd,ed->bse", dhidden_low, w_out, preferred_element_type=wide).astype(low_type)
    )
    again_scores = (
        jnp.einsum("bqhe,bkhe->bhqk", query_low, key_low, preferred_element_type=wide) * factor
    )
    again_probs = jnp.exp(again_scores - lse)
    dvalue = jnp.einsum(
        "bhqk,bqhe->bkhe", again_probs.astype(low_type), dattended, preferred_element_type=wide
    )
    dprobs = jnp.einsum("bqhe,bkhe->bhqk", dattended, value_low, preferred_element_type=wide)
    dscores = (again_probs * (dprobs - jnp.sum(dprobs * again_probs, -1, keepdims=True))).astype(
        low_type
    )
    dquery = jnp.einsum("bhqk,bkhe->bqhe", dscores, key_low, preferred_element_type=wide) * factor
    dkey = jnp.einsum("bhqk,bqhe->bkhe", dscores, query_low, preferred_element_type=wide) * factor
    dqkv_low = jnp.stack(
        (
            dquery.reshape(count, length, -1),
            dkey.reshape(count, length, -1),
            dvalue.reshape(count, length, -1),
        )
    ).astype(low_type)
    qkv_grad_part = jnp.einsum("bsd,kbse->kde", norm_one_low, dqkv_low, preferred_element_type=wide)
    bias_sums = jnp.sum(dqkv_low.astype(wide), (1, 2))
    qv_bias_part = jnp.stack((bias_sums[0], bias_sums[2]))
    dnorm_one_part = jnp.einsum("kbse,kde->bsd", dqkv_low, w_qkv, preferred_element_type=wide)
    dnorm_one = lax.psum(dnorm_one_part.astype(jnp.bfloat16), "tensor").astype(jnp.float32)
    dinput_norm, gain_one_part, shift_one_part = norm_back(
        dnorm_one, normed_one, inverse_one, gain_one
    )
    patch_grad = (dhidden + dinput_norm).astype(low_type)
    qkv_grad, out_grad, fc1_grad, fc2_grad = (
        lax.psum_scatter(qkv_grad_part, "dp", scatter_dimension=1, tiled=True),
        lax.psum_scatter(out_grad_part, "dp", scatter_dimension=1, tiled=True),
        lax.psum_scatter(fc1_grad_part, "dp", scatter_dimension=0, tiled=True),
        lax.psum_scatter(fc2_grad_part, "dp", scatter_dimension=1, tiled=True),
    )
    small = lax.psum(
        (
            gain_one_part,
            shift_one_part,
            qv_bias_part,
            out_bias_part,
            gain_two_part,
            shift_two_part,
            fc1_bias_part,
            fc2_bias_part,
        ),
        "dp",
    )
    return (
        encoded,
        patch_grad,
        small[0],
        small[1],
        qkv_grad,
        small[2],
        out_grad,
        small[3],
        small[4],
        small[5],
        fc1_grad,
        small[6],
        fc2_grad,
        small[7],
    )


def solution(mesh):
    return jax.shard_map(
        on_device,
        mesh=mesh,
        in_specs=(
            P("dp", None, None),
            P(),
            P(),
            P(None, "dp", "tensor"),
            P(None, "tensor"),
            P("tensor", "dp"),
            P(),
            P(),
            P(),
            P("dp", "tensor"),
            P("tensor"),
            P("tensor", "dp"),
            P(),
            P("dp", None, None),
        ),
        out_specs=(
            P("dp", None, None),
            P("dp", None, None),
            P(),
            P(),
            P(None, "dp", "tensor"),
            P(None, "tensor"),
            P("tensor", "dp"),
            P(),
            P(),
            P(),
            P("dp", "tensor"),
            P("tensor"),
            P("tensor", "dp"),
            P(),
        ),
        check_vma=False,
    )
```

profile of v0, /device:TPU:0, one launch (start us, length us, event | category | flops | bytes accessed | tf_op | source)
XLA Modules:
  0.0 565.5 jit_solution(15152475741183422523)
XLA Ops:
  14.2 40.5 %all_gather.16 = bf16[3,768,192]{2,0,1:T(4,128)(2,1)} all-gather(bf16[3,96,192]{2,0,1:T(4,128)(2,1)S(1)} %copy.46), channel_id=1, replica_groups=mesh['dp'=8,'tensor'=4] {'dp'}, dimensions={1}, use_global_device_ids=true | all-gather | bytes 995328 | tf_op jit(solution)/shard_map/all_gather | solution.py:59
  64.2 31.3 %all_gather.17 = bf16[192,768]{0,1:T(8,128)(2,1)S(1)} all-gather(bf16[192,96]{0,1:T(8,128)(2,1)S(1)} %copy.49), channel_id=1, replica_groups=mesh['dp'=8,'tensor'=4] {'dp'}, dimensions={1}, use_global_device_ids=true | all-gather | bytes 331776 | tf_op jit(solution)/shard_map/all_gather | solution.py:60
  103.8 55.0 %all-reduce.6.cloned.1.call-done = bf16[8,197,768]{2,1,0:T(8,128)(2,1)} async-done(((bf16[8,197,768]{2,1,0:T(8,128)(2,1)}), bf16[8,197,768]{2,1,0:T(8,128)(2,1)}) %all-reduce.6.cloned.1.call-update) | async-done | bytes 2420752 | tf_op jit(solution)/shard_map/psum | solution.py:86
  163.7 6.8 %fusion.40 = (u8[197,768]{1,0:T(8,128)(4,1)S(1)}, u8[197,768]{1,0:T(8,128)(4,1)S(1)}, f32[8,197,768]{2,1,0:T(8,128)S(1)}) fusion(f32[768]{0:T(1024)S(1)} %convert_element_type.117, bf16[768,768]{1,0:T(8,128)(2,1)} %all-gather.3.cloned.1.call-done, f32[768]{0:T(1024)S(1)} %convert_element_type.115, f32[768]{0:T(1024)S(1)} %convert_element_type.114, ...), kind=kOutput, calls=%fused_computation.95 | convolution fusion | flops 1886661120 | bytes 11190080 | tf_op jit(solution)/shard_map/bsd,df->bsf/dot_general | solution.py:90
  172.8 12.2 %multiply_convert_fusion.1 = (bf16[8,197,768]{2,1,0:T(8,128)(2,1)}, f32[8,197,768]{2,1,0:T(8,128)}) fusion(f32[8,197,768]{2,1,0:T(8,128)S(1)} %get-tuple-element.77, f32[768]{0:T(1024)S(1)} %convert_element_type.117, u8[197,768]{1,0:T(8,128)(4,1)S(1)} %get-tuple-element.45, u8[197,768]{1,0:T(8,128)(4,1)S(1)} %get-tuple-element.44), kind=kLoop, calls=%fused_computation.48 | loop fusion | flops 85936128 | bytes 12409344 | tf_op jit(solution)/shard_map/convert_element_type | solution.py:94
  187.4 9.0 %convert_reduce_fusion.4 = (f32[768]{0:T(1024)S(1)}, bf16[8,197,768]{2,1,0:T(8,128)(2,1)S(1)}) fusion(f32[8,197,768]{2,1,0:T(8,128)} %get-tuple-element.65, bf16[768,768]{0,1:T(8,128)(2,1)} %all-gather.5.cloned.1.call-done, bf16[8,197,768]{2,0,1:T(8,128)(2,1)} %param.27, f32[8,197,768]{2,1,0:T(8,128)} %copy-done.17, f32[768]{0:T(1024)S(1)} %convert_element_type.117), kind=kOutput, calls=%fused_computation.43 | convolution fusion | flops 1879700736 | bytes 15710208 | tf_op jit(solution)/shard_map/bsd,fd->bsf/dot_general | solution.py:107
  201.8 5.6 convolution_convert_fusion.1
  207.4 50.1 %all-reduce.8.cloned.1.call-done = bf16[8,197,768]{2,1,0:T(8,128)(2,1)} async-done(((bf16[8,197,768]{2,1,0:T(8,128)(2,1)}), bf16[8,197,768]{2,1,0:T(8,128)(2,1)}) %all-reduce.8.cloned.1.call-update) | async-done | bytes 2420752 | tf_op jit(solution)/shard_map/psum | solution.py:112
  257.5 5.6 fusion.23
  271.1 4.5 multiply_reduce_fusion
  283.1 3.7 convolution_convert_fusion.3
  287.7 4.0 bitcast_convert_fusion
  292.8 5.3 convolution_bitcast_fusion.3
  298.1 4.3 copy.77
  302.4 4.7 reshape.117
  307.1 7.2 %convolution_bitcast_fusion.2 = f32[768,768]{1,0:T(8,128)} fusion(bf16[8,197,768]{2,1,0:T(8,128)(2,1)} %copy-done.35, f32[768]{0:T(1024)S(1)} %convert_element_type.115, f32[768]{0:T(1024)S(1)} %convert_element_type.114, f32[8,197]{1,0:T(8,128)S(1)} %add_rsqrt_fusion, f32[8,197]{1,0:T(8,128)S(1)} %broadcast_multiply_fusion.4, ...), kind=kOutput, calls=%fused_computation.76 | convolution fusion | flops 1870018560 | bytes 9643328 | tf_op jit(solution)/shard_map/bsd,bsf->df/dot_general | solution.py:110
  314.7 6.4 %convolution_bitcast_fusion.1 = f32[768,768]{0,1:T(8,128)} fusion(bf16[8,197,768]{2,1,0:T(8,128)(2,1)} %get-tuple-element.64, bf16[8,197,768]{2,0,1:T(8,128)(2,1)} %param.27), kind=kOutput, calls=%fused_computation.75 | convolution fusion | flops 1859125248 | bytes 7200768 | tf_op jit(solution)/shard_map/bsf,bsd->fd/dot_general | solution.py:106
  323.1 19.6 %reduce-scatter.15.cloned.1.call-done = f32[96,192]{1,0:T(8,128)} async-done(((f32[768,192]{1,0:T(8,128)}), f32[96,192]{1,0:T(8,128)}) %reduce-scatter.15.cloned.1.call-update) | async-done | bytes 73744
  344.3 45.1 %all-reduce.10.cloned.1.call-done = (bf16[8,197,768]{2,1,0:T(8,128)(2,1)}, bf16[8,197,768]{2,1,0:T(8,128)(2,1)}) async-done(((bf16[8,197,768]{2,1,0:T(8,128)(2,1)}, bf16[8,197,768]{2,1,0:T(8,128)(2,1)}), (bf16[8,197,768]{2,1,0:T(8,128)(2,1)}, bf16[8,197,768]{2,1,0:T(8,128)(2,1)})) %all-reduce.10.cloned.1.call-update) | async-done | bytes 4841488 | tf_op jit(solution)/shard_map/psum | solution.py:96
  389.4 4.5 fusion.24
  394.0 5.2 fusion.15
  402.9 37.8 %all-reduce = (f32[768]{0:T(1024)}, f32[768]{0:T(1024)}, f32[2,192]{1,0:T(2,128)}, f32[768]{0:T(1024)}, f32[768]{0:T(1024)}, /*index=5*/f32[768]{0:T(1024)}, f32[768]{0:T(1024)}, f32[768]{0:T(1024)}) all-reduce(f32[768]{0:T(1024)S(1)} %get-tuple-element.46, ...), channel_id=1, replica_groups=mesh['dp'=8,'tensor'=4] {'dp'}, use_global_device_ids=true, to_apply=%region_16.0 | all-reduce | flops 5760 | bytes 46080 | tf_op jit(solution)/shard_map/psum | solution.py:158
  442.6 42.7 %reduce-scatter.9.cloned.1.call-done = f32[96,768]{1,0:T(8,128)} async-done(((f32[768,768]{1,0:T(8,128)}), f32[96,768]{1,0:T(8,128)}) %reduce-scatter.9.cloned.1.call-update) | async-done | bytes 294928 | tf_op jit(solution)/shard_map/reduce_scatter | solution.py:155
  485.3 72.7 %reduce-scatter.11.cloned.1.call-done = f32[768,96]{0,1:T(8,128)} async-done(((f32[768,768]{0,1:T(8,128)}), f32[768,96]{0,1:T(8,128)}) %reduce-scatter.11.cloned.1.call-update) | async-done | bytes 294928 | tf_op jit(solution)/shard_map/reduce_scatter | solution.py:156
  (144 shorter events, 65.7 us)
Async XLA Ops:
  8.0 49.3 %copy-start.1 = (bf16[8,197,768]{2,0,1:T(8,128)(2,1)S(1)}, bf16[8,197,768]{2,0,1:T(8,128)(2,1)}, u32[]{:S(2)}) copy-start(bf16[8,197,768]{2,0,1:T(8,128)(2,1)} %param.14) | copy-start | bytes 7262212
  8.0 6.0 %copy-start.25 = (bf16[3,96,192]{2,1,0:T(8,128)(2,1)S(1)}, bf16[3,96,192]{2,1,0:T(8,128)(2,1)}, u32[]{:S(2)}) copy-start(bf16[3,96,192]{2,1,0:T(8,128)(2,1)} %param.17) | copy-start | bytes 331780
  8.0 49.2 %copy-start.28 = (bf16[768]{0:T(1024)(128)(2,1)S(1)}, bf16[768]{0:T(1024)(128)(2,1)}, u32[]{:S(2)}) copy-start(bf16[768]{0:T(1024)(128)(2,1)} %param.16) | copy-start | bytes 4612
  8.0 49.2 %copy-start.27 = (bf16[2,192]{1,0:T(2,128)(2,1)S(1)}, bf16[2,192]{1,0:T(2,128)(2,1)}, u32[]{:S(2)}) copy-start(bf16[2,192]{1,0:T(2,128)(2,1)} %param.18) | copy-start | bytes 2308
  8.1 150.8 %all-reduce.6.cloned.1.call-start = ((), (), s32[]{:S(2)}) async-start(), calls=%async_computation.4 | async-start | bytes 4915200 | tf_op jit(solution)/shard_map/psum | solution.py:86
  60.0 35.5 %copy-start.12 = (bf16[1,8,197,192]{2,3,0,1:T(8,128)(2,1)}, bf16[1,8,197,192]{2,3,0,1:T(8,128)(2,1)S(1)}, u32[]{:S(2)}) copy-start(bf16[1,8,197,192]{2,3,0,1:T(8,128)(2,1)S(1)} %get-tuple-element.67) | copy-start | bytes 1815556
  95.5 8.3 %copy-start.29 = (bf16[768]{0:T(1024)(128)(2,1)S(1)}, bf16[768]{0:T(1024)(128)(2,1)}, u32[]{:S(2)}) copy-start(bf16[768]{0:T(1024)(128)(2,1)} %param.20) | copy-start | bytes 4612
  95.5 8.3 %copy-start.30 = (bf16[768]{0:T(1024)(128)(2,1)S(1)}, bf16[768]{0:T(1024)(128)(2,1)}, u32[]{:S(2)}) copy-start(bf16[768]{0:T(1024)(128)(2,1)} %param.21) | copy-start | bytes 4612
  95.5 8.3 %copy-start.31 = (bf16[768]{0:T(1024)(128)(2,1)S(1)}, bf16[768]{0:T(1024)(128)(2,1)}, u32[]{:S(2)}) copy-start(bf16[768]{0:T(1024)(128)(2,1)} %param.24) | copy-start | bytes 4612
  95.5 8.3 %copy-start.32 = (bf16[768]{0:T(1024)(128)(2,1)S(1)}, bf16[768]{0:T(1024)(128)(2,1)}, u32[]{:S(2)}) copy-start(bf16[768]{0:T(1024)(128)(2,1)} %param.22) | copy-start | bytes 4612
  102.5 61.2 %all-gather.3.cloned.1.call-start = ((), (), s32[]{:S(2)}) async-start(), calls=%async_computation.5 | async-start | bytes 1327104 | tf_op jit(solution)/shard_map/all_gather | solution.py:61
  103.1 84.3 %all-gather.5.cloned.1.call-start = ((), (), s32[]{:S(2)}) async-start(), calls=%async_computation.6 | async-start | bytes 1327104 | tf_op jit(solution)/shard_map/all_gather | solution.py:62
  103.7 153.7 %all-reduce.8.cloned.1.call-start = ((), (), s32[]{:S(2)}) async-start(), calls=%async_computation.7 | async-start | bytes 4915200 | tf_op jit(solution)/shard_map/psum | solution.py:112
  187.4 10.5 %copy-start.34 = (bf16[768,768]{1,0:T(8,128)(2,1)S(1)}, bf16[768,768]{1,0:T(8,128)(2,1)}, u32[]{:S(2)}) copy-start(bf16[768,768]{1,0:T(8,128)(2,1)} %all-gather.3.cloned.1.call-done) | copy-start | bytes 3538948
  201.6 141.1 %reduce-scatter.15.cloned.1.call-start = ((), (), s32[]{:S(2)}) async-start(), calls=%async_computation.11 | async-start | bytes 884736
  257.5 5.6 copy-start.24
  268.9 6.7 %slice-start = ((s8[4915200]{0:T(1024)(128)(4,1)}), s8[720896]{0:T(1024)(128)(4,1)S(1)}, s32[]{:S(2)}) async-start(s8[4915200]{0:T(1024)(128)(4,1)} %bitcast.94), calls=%async_computation.13 | async-start | bytes 1441792
  279.9 109.5 %all-reduce.10.cloned.1.call-start = ((), (), s32[]{:S(2)}) async-start(), calls=%async_computation.12 | async-start | bytes 9830400 | tf_op jit(solution)/shard_map/psum | solution.py:96
  280.1 7.6 %copy-start.16 = (bf16[3,768,192]{2,0,1:T(4,128)(2,1)S(1)}, bf16[3,768,192]{2,0,1:T(4,128)(2,1)}, u32[]{:S(2)}) copy-start(bf16[3,768,192]{2,0,1:T(4,128)(2,1)} %all_gather.16) | copy-start | bytes 2654212
  280.1 7.6 %copy-start.22 = (bf16[8,3,64,197]{3,2,1,0:T(8,128)(2,1)S(1)}, bf16[8,3,64,197]{3,2,1,0:T(8,128)(2,1)}, u32[]{:S(2)}) copy-start(bf16[8,3,64,197]{3,2,1,0:T(8,128)(2,1)} %multiply_convert_fusion.3) | copy-start | bytes 1815556
  291.7 149.0 %reduce-scatter.13.cloned.1.call-start = ((), (), s32[]{:S(2)}) async-start(), calls=%async_computation.10 | async-start | bytes 2211840
  307.1 178.2 %reduce-scatter.9.cloned.1.call-start = ((), (), s32[]{:S(2)}) async-start(), calls=%async_computation.8 | async-start | bytes 2654208 | tf_op jit(solution)/shard_map/reduce_scatter | solution.py:155
  314.4 6.8 %copy-start.33 = (bf16[768]{0:T(1024)(128)(2,1)S(1)}, bf16[768]{0:T(1024)(128)(2,1)}, u32[]{:S(2)}) copy-start(bf16[768]{0:T(1024)(128)(2,1)} %param.26) | copy-start | bytes 4612
  314.4 243.6 %reduce-scatter.11.cloned.1.call-start = ((), (), s32[]{:S(2)}) async-start(), calls=%async_computation.9 | async-start | bytes 2654208 | tf_op jit(solution)/shard_map/reduce_scatter | solution.py:156
  (23 other events, 67.3 us)
Sparse Core Ops, SparseCore 0:
  102.7 56.0 all-reduce.5
  201.7 55.7 all-reduce.7
  291.8 97.5 all-reduce.9
Sparse Core Ops, SparseCore 1:
  105.2 40.2 all-gather.2
  147.6 39.8 all-gather.4
  279.9 62.7 reduce-scatter.14
  346.2 65.8 reduce-scatter.12
  416.6 68.7 reduce-scatter.8
  489.8 68.1 reduce-scatter.10
where the time goes:
time: 573 us; the launch traced here: 566 us
  waiting for transfers between devices  289 us (50%)
  blocking collectives  110 us (19%)
  matrix products  74.3 us (13%)
  other arithmetic  46 us (8%)
  local copies, waits for them, and re-layouts  29.6 us (5%)
  between operations  16.4 us (3%)
    reduce_scatter x1, waiting for transfers between devices, on_device(): lax.psum_scatter(fc2_grad_part, 'dp', scatter_dimension=1, tiled=True)  72.7 us
    psum x1, waiting for transfers between devices, on_device(): lax.psum(attn_part.astype(jnp.bfloat16), 'tensor').astype(jnp.float32)  55 us
    psum x1, waiting for transfers between devices, on_device(): lax.psum(dnorm_two_part.astype(jnp.bfloat16), 'tensor').astype(jnp.float32)  50.1 us
    psum x1, waiting for transfers between devices, on_device(): lax.psum(mlp_part.astype(jnp.bfloat16), 'tensor').astype(jnp.float32)  45.1 us
    reduce_scatter x1, waiting for transfers between devices, on_device(): lax.psum_scatter(fc1_grad_part, 'dp', scatter_dimension=0, tiled=True)  42.7 us
    all_gather x1, blocking collectives, on_device(): lax.all_gather(qkv_weight, 'dp', axis=1, tiled=True)  40.5 us
    psum x1, blocking collectives, on_device(): lax.psum((gain_one_part, shift_one_part, qv_bias_part, out_bias_part, gai...  37.8 us
    all_gather x1, blocking collectives, on_device(): lax.all_gather(out_weight, 'dp', axis=1, tiled=True)  31.3 us
  transfers between devices with their start and end apart: 9, of which 7 were waited for; matrix products, arithmetic and copies ran while one was open for 15% of the time, Pallas kernels for 0%

commit v1 on v0

v1 whole, which is shorter than its diff:
```python
from functools import partial

import jax
import jax.numpy as jnp
from jax import lax
from jax.sharding import PartitionSpec as P

HEAD_DIM = 64
EPS = 1e-06
AXES = ("dp", "tensor")
bf16 = jnp.bfloat16
f32 = jnp.float32


def layer_norm(values, gain, shift):
    centre = values - jnp.mean(values, -1, keepdims=True)
    inverse = lax.rsqrt(jnp.mean(centre * centre, -1, keepdims=True) + EPS)
    normed = centre * inverse
    return (normed * gain + shift, normed, inverse)


def row_total(values):
    return jnp.sum(values.reshape(-1, values.shape[-1]), 0)


def norm_back(upstream, normed, inverse, gain):
    scaled = upstream * gain
    inner = (
        scaled
        - jnp.mean(scaled, -1, keepdims=True)
        - normed * jnp.mean(scaled * normed, -1, keepdims=True)
    )
    return (inverse * inner, row_total(upstream * normed), row_total(upstream))


def dot(spec, left, right):
    return jnp.einsum(spec, left, right, preferred_element_type=f32)


def gather_weight(piece, n_dp, n_t):
    whole = lax.all_gather(piece, AXES, axis=0, tiled=False)
    whole = whole.reshape(n_dp, n_t, piece.shape[0], piece.shape[1]).transpose(1, 0, 2, 3)
    return whole.reshape(n_t, n_dp * piece.shape[0], piece.shape[1])


def scatter_grad(part, n_dp, n_t):
    rows = part.shape[1] // n_dp
    part = part.astype(bf16).reshape(n_t, n_dp, rows, part.shape[2]).transpose(1, 0, 2, 3)
    part = part.reshape(n_dp * n_t * rows, part.shape[3])
    return lax.psum_scatter(part, AXES, scatter_dimension=0, tiled=True).astype(f32)


def on_device(
    n_dp,
    n_t,
    patches,
    attn_gain,
    attn_shift,
    qkv_weight,
    qv_bias,
    out_weight,
    out_bias,
    mlp_gain,
    mlp_shift,
    fc1_weight,
    fc1_bias,
    fc2_weight,
    fc2_bias,
    cotangent,
):
    factor = HEAD_DIM ** (-0.5)
    t_me = lax.axis_index("tensor")
    width = qkv_weight.shape[2]
    heads = width // HEAD_DIM
    rows = qkv_weight.shape[1]
    attn_piece = jnp.concatenate(
        (qkv_weight[0], qkv_weight[1], qkv_weight[2], out_weight.T), axis=1
    )
    w_attn = gather_weight(attn_piece, n_dp, n_t)
    w_fc1 = gather_weight(fc1_weight, n_dp, n_t)
    w_fc2 = gather_weight(fc2_weight.T, n_dp, n_t)
    biases = lax.all_gather(
        jnp.concatenate((qv_bias.reshape(-1), fc1_bias)), "tensor", axis=0, tiled=False
    ).astype(f32)
    q_bias = biases[:, :width]
    v_bias = biases[:, width : 2 * width]
    f_bias = biases[:, 2 * width :]

    count = patches.shape[0] // n_t
    length = patches.shape[1]
    mine = lax.dynamic_slice_in_dim(patches, t_me * count, count, 0)
    cot = lax.dynamic_slice_in_dim(cotangent, t_me * count, count, 0)
    inputs = mine.astype(f32)
    gain_one = attn_gain.astype(f32)
    gain_two = mlp_gain.astype(f32)
    norm_one, normed_one, inverse_one = layer_norm(inputs, gain_one, attn_shift.astype(f32))
    norm_one_low = norm_one.astype(bf16)
    projected = dot("bsd,tde->tbse", norm_one_low, w_attn[:, :, : 3 * width])

    def heads_of(values):
        return values.reshape(n_t, count, length, heads, HEAD_DIM)

    query = heads_of((projected[..., :width] + q_bias[:, None, None, :]).astype(bf16))
    key = heads_of(projected[..., width : 2 * width].astype(bf16))
    value = heads_of((projected[..., 2 * width :] + v_bias[:, None, None, :]).astype(bf16))
    scores = dot("tbqhe,tbkhe->tbhqk", query, key) * factor
    lse = jax.nn.logsumexp(scores, -1, keepdims=True)
    probs = jnp.exp(scores - lse)
    mixed = dot("tbhqk,tbkhe->tbqhe", probs.astype(bf16), value)
    attended = mixed.reshape(n_t, count, length, width).astype(bf16)
    attn_full = dot("tbse,tde->bsd", attended, w_attn[:, :, 3 * width :])
    hidden_state = inputs + attn_full + out_bias.astype(f32)
    norm_two, normed_two, inverse_two = layer_norm(hidden_state, gain_two, mlp_shift.astype(f32))
    norm_two_low = norm_two.astype(bf16)
    pre_act = dot("bsd,tdf->tbsf", norm_two_low, w_fc1) + f_bias[:, None, None, :]
    activated, gelu_pull = jax.vjp(partial(jax.nn.gelu, approximate=False), pre_act)
    act_low = activated.astype(bf16)
    upstream = cot.astype(f32)
    fc2_grad = scatter_grad(dot("bsd,tbsf->tdf", cot, act_low), n_dp, n_t)
    dact = dot("bsd,tdf->tbsf", cot, w_fc2)
    dpre_low = gelu_pull(dact)[0].astype(bf16)
    fc1_grad = scatter_grad(dot("bsd,tbsf->tdf", norm_two_low, dpre_low), n_dp, n_t)
    dnorm_two = dot("tbsf,tdf->bsd", dpre_low, w_fc1)
    mlp_full = dot("tbsf,tdf->bsd", act_low, w_fc2)
    encoded_mine = (hidden_state + mlp_full + fc2_bias.astype(f32)).astype(bf16)
    encoded = lax.all_gather(encoded_mine, "tensor", axis=0, tiled=True)
    dhidden_norm, gain_two_part, shift_two_part = norm_back(
        dnorm_two, normed_two, inverse_two, gain_two
    )
    dhidden = upstream + dhidden_norm
    dhidden_low = dhidden.astype(bf16)
    out_grad_part = dot("bsd,tbse->tde", dhidden_low, attended)
    dattended = heads_of(dot("bsd,tde->tbse", dhidden_low, w_attn[:, :, 3 * width :]).astype(bf16))
    dvalue = dot("tbhqk,tbqhe->tbkhe", probs.astype(bf16), dattended)
    dprobs = dot("tbqhe,tbkhe->tbhqk", dattended, value)
    dscores = (probs * (dprobs - jnp.sum(dprobs * probs, -1, keepdims=True))).astype(bf16)
    dquery = dot("tbhqk,tbkhe->tbqhe", dscores, key) * factor
    dkey = dot("tbhqk,tbqhe->tbkhe", dscores, query) * factor
    shape = (n_t, count, length, width)
    dqkv = jnp.concatenate(
        (dquery.reshape(shape), dkey.reshape(shape), dvalue.reshape(shape)), -1
    ).astype(bf16)
    qkv_grad_part = dot("bsd,tbse->tde", norm_one_low, dqkv)
    attn_grad = scatter_grad(jnp.concatenate((qkv_grad_part, out_grad_part), -1), n_dp, n_t)
    dnorm_one = dot("tbse,tde->bsd", dqkv, w_attn[:, :, : 3 * width])
    dinput_norm, gain_one_part, shift_one_part = norm_back(
        dnorm_one, normed_one, inverse_one, gain_one
    )
    patch_mine = (dhidden + dinput_norm).astype(bf16)
    patch_grad = lax.all_gather(patch_mine, "tensor", axis=0, tiled=True)
    d_sums = jnp.sum(dqkv.astype(f32), (1, 2))
    small = jnp.concatenate(
        (
            gain_one_part,
            shift_one_part,
            row_total(dhidden),
            gain_two_part,
            shift_two_part,
            row_total(upstream),
            d_sums[:, :width].reshape(-1),
            d_sums[:, 2 * width :].reshape(-1),
            jnp.sum(dpre_low.astype(f32), (1, 2)).reshape(-1),
        )
    )
    small = lax.psum(small, AXES)
    d = gain_one.shape[0]
    cuts = [small[i * d : (i + 1) * d] for i in range(6)]
    at = 6 * d
    q_sum = lax.dynamic_slice_in_dim(small[at : at + n_t * width], t_me * width, width, 0)
    at += n_t * width
    v_sum = lax.dynamic_slice_in_dim(small[at : at + n_t * width], t_me * width, width, 0)
    at += n_t * width
    f_width = fc1_weight.shape[1]
    f_sum = lax.dynamic_slice_in_dim(small[at:], t_me * f_width, f_width, 0)
    return (
        encoded,
        patch_grad,
        cuts[0],
        cuts[1],
        jnp.stack([attn_grad[:, i * width : (i + 1) * width] for i in range(3)]),
        jnp.stack((q_sum, v_sum)),
        attn_grad[:, 3 * width :].T,
        cuts[2],
        cuts[3],
        cuts[4],
        fc1_grad,
        f_sum,
        fc2_grad.T,
        cuts[5],
    )


def solution(mesh):
    return jax.shard_map(
        partial(on_device, mesh.shape["dp"], mesh.shape["tensor"]),
        mesh=mesh,
        in_specs=(
            P("dp", None, None),
            P(),
            P(),
            P(None, "dp", "tensor"),
            P(None, "tensor"),
            P("tensor", "dp"),
            P(),
            P(),
            P(),
            P("dp", "tensor"),
            P("tensor"),
            P("tensor", "dp"),
            P(),
            P("dp", None, None),
        ),
        out_specs=(
            P("dp", None, None),
            P("dp", None, None),
            P(),
            P(),
            P(None, "dp", "tensor"),
            P(None, "tensor"),
            P("tensor", "dp"),
            P(),
            P(),
            P(),
            P("dp", "tensor"),
            P("tensor"),
            P("tensor", "dp"),
            P(),
        ),
        check_vma=False,
    )
```

time: 573 us -> 658 us (1.15)
  waiting for transfers between devices: 289 us -> 436 us
  blocking collectives: 110 us -> 46.2 us
  local copies, waits for them, and re-layouts: 29.6 us -> 59.2 us
  other arithmetic: 46 us -> 24.7 us
    all_gather x2 -> x5, waiting for transfers between devices: 2.42 us -> 171 us  [the longest x3 171 us: gather_weight(): whole = lax.all_gather(piece, AXES, axis=0, tiled=False)]
    psum x3 -> x0, waiting for transfers between devices: 150 us -> none  [the longest x1 55 us: on_device(): lax.psum(attn_part.astype(jnp.bfloat16), 'tensor').astype(jnp.float32)]
    reduce_scatter x2 -> x3, waiting for transfers between devices: 115 us -> 264 us  [scatter_grad(): lax.psum_scatter(part, AXES, scatter_dimension=0, tiled=True).astype(f32)]
    all_gather x2 -> x1, blocking collectives: 71.8 us -> 6.21 us  [on_device(): lax.all_gather(jnp.concatenate((qv_bias.reshape(-1), fc1_bias)), 'tensor'...]
    unnamed x11 -> x8, waiting for transfers between devices: 20.7 us -> 1.47 us
    transpose x0 -> x6, local copies, waits for them, and re-layouts: none -> 16.4 us  [the longest x3 7.59 us: scatter_grad(): part.astype(bf16).reshape(n_t, n_dp, rows, part.shape[2])]
    reshape x0 -> x9, local copies, waits for them, and re-layouts: none -> 15.9 us  [the longest x2 9.75 us: gather_weight(): whole.reshape(n_dp, n_t, piece.shape[0], piece.shape[1])]
    unnamed x85 -> x68, local copies, waits for them, and re-layouts: 27 us -> 14.9 us
  transfers between devices with their start and end apart: 9 -> 8, of which waited for: 7 -> 6; matrix products, arithmetic and copies ran while one was open for 15% -> 16% of each run, Pallas kernels for 0% -> 0%
where the time goes in v1:
time: 658 us; the launch traced here: 652 us
  waiting for transfers between devices  436 us (66%)
  matrix products  69.7 us (11%)
  local copies, waits for them, and re-layouts  59.2 us (9%)
  blocking collectives  46.2 us (7%)
  other arithmetic  24.7 us (4%)
  between operations  15.2 us (2%)
    reduce_scatter x3, waiting for transfers between devices, scatter_grad(): lax.psum_scatter(part, AXES, scatter_dimension=0, tiled=True).astype(f32)  264 us
    all_gather x3, waiting for transfers between devices, gather_weight(): whole = lax.all_gather(piece, AXES, axis=0, tiled=False)  171 us
    dot_general x18, matrix products, dot(): return jnp.einsum(spec, left, right, preferred_element_type=f32)  69.7 us
    psum x1, blocking collectives, on_device(): small = lax.psum(small, AXES)  40 us
    unnamed x68, local copies, waits for them, and re-layouts  14.9 us
  transfers between devices with their start and end apart: 8, of which 6 were waited for; matrix products, arithmetic and copies ran while one was open for 16% of the time, Pallas kernels for 0%

profile of v1, /device:TPU:0, one launch (start us, length us, event | category | flops | bytes accessed | tf_op | source)
XLA Modules:
  0.0 651.9 jit_solution(5248795071901612956)
XLA Ops:
  16.9 6.2 all-gather.4
  23.1 4.5 constant_dynamic-slice_fusion
  28.2 49.0 %all-gather.17.cloned.1.call-done = bf16[3072,768]{1,0:T(8,128)(2,1)} async-done(((bf16[96,768]{1,0:T(8,128)(2,1)}), bf16[3072,768]{1,0:T(8,128)(2,1)}) %all-gather.17.cloned.1.call-update) | async-done | bytes 4718608 | tf_op jit(solution)/shard_map/all_gather | solution.py:41
  77.2 4.9 copy.98
  82.2 60.4 %all-gather.19.cloned.1.call-done = bf16[3072,768]{1,0:T(8,128)(2,1)} async-done(((bf16[96,768]{1,0:T(8,128)(2,1)}), bf16[3072,768]{1,0:T(8,128)(2,1)}) %all-gather.19.cloned.1.call-update) | async-done | bytes 4718608 | tf_op jit(solution)/shard_map/all_gather | solution.py:41
  142.6 4.8 copy.99
  147.4 61.1 %all-gather.15.cloned.1.call-done = bf16[3072,768]{1,0:T(8,128)(2,1)} async-done(((bf16[96,768]{1,0:T(8,128)(2,1)}), bf16[3072,768]{1,0:T(8,128)(2,1)}) %all-gather.15.cloned.1.call-update) | async-done | bytes 4718608 | tf_op jit(solution)/shard_map/all_gather | solution.py:41
  216.1 3.4 fusion.33
  225.6 4.0 fusion.85
  230.0 12.0 %fusion.9 = (bf16[4,2,197,768]{3,2,0,1:T(8,128)(2,1)S(1)}, f32[4,2,197,768]{3,2,0,1:T(8,128)S(1)}, f32[2,197,4,768]{3,1,2,0:T(8,128)S(1)}) fusion(f32[4,768]{1,0:T(4,128)S(1)} %slice.114, bf16[4,768,768,1]{2,1,0,3:T(8,128)(2,1)S(1)} %bitcast.290, f32[2,197,768]{2,1,0:T(8,128)S(1)} %get-tuple-element.93, f32[768]{0:T(1024)S(1)} %convert_element_type.118, ...), kind=kOutput, calls=%fused_computation.20 | convolution fusion | flops 1940522496 | bytes 18054224 | tf_op jit(solution)/shard_map/bsd,tdf->tbsf/dot_general | solution.py:37
  242.0 3.8 convert_reduce_fusion
  257.6 4.0 convolution_convert_fusion
  263.1 3.9 multiply_reduce_fusion
  276.4 5.1 fusion.56
  287.6 6.4 fusion.26
  294.0 6.0 copy.107
  307.0 4.8 bitcast_convert_fusion.1
  315.4 4.6 bitcast_convert_fusion
  325.2 40.0 %psum.7 = f32[9216]{0:T(1024)S(1)} all-reduce(f32[9216]{0:T(1024)S(1)} %constant_dynamic-update-slice_fusion), channel_id=1, replica_groups=mesh['dp'=8,'tensor'=4] {'dp','tensor'}, use_global_device_ids=true, to_apply=%region_19.0 | all-reduce | flops 9216 | bytes 73728 | tf_op jit(solution)/shard_map/psum | solution.py:165
  367.1 3.6 copy.112
  370.7 3.6 copy.113
  374.3 44.5 %reduce-scatter.4.cloned.1.call-done = bf16[96,768]{1,0:T(8,128)(2,1)} async-done(((bf16[3072,768]{1,0:T(8,128)(2,1)}), bf16[96,768]{1,0:T(8,128)(2,1)}) %reduce-scatter.4.cloned.1.call-update) | async-done | bytes 147472 | tf_op jit(solution)/shard_map/reduce_scatter | solution.py:50
  420.7 110.7 %reduce-scatter.6.cloned.1.call-done = bf16[96,768]{1,0:T(8,128)(2,1)} async-done(((bf16[3072,768]{1,0:T(8,128)(2,1)}), bf16[96,768]{1,0:T(8,128)(2,1)}) %reduce-scatter.6.cloned.1.call-update) | async-done | bytes 147472 | tf_op jit(solution)/shard_map/reduce_scatter | solution.py:50
  533.8 109.2 %reduce-scatter.8.cloned.1.call-done = bf16[96,768]{1,0:T(8,128)(2,1)} async-done(((bf16[3072,768]{1,0:T(8,128)(2,1)}), bf16[96,768]{1,0:T(8,128)(2,1)}) %reduce-scatter.8.cloned.1.call-update) | async-done | bytes 147472 | tf_op jit(solution)/shard_map/reduce_scatter | solution.py:50
  (156 shorter events, 76.2 us)
Async XLA Ops:
  7.2 70.1 %all-gather.17.cloned.1.call-start = ((), (), s32[]{:S(2)}) async-start(), calls=%async_computation.9 | async-start | bytes 4866048 | tf_op jit(solution)/shard_map/all_gather | solution.py:41
  7.9 134.7 %all-gather.19.cloned.1.call-start = ((), (), s32[]{:S(2)}) async-start(), calls=%async_computation.10 | async-start | bytes 4866048 | tf_op jit(solution)/shard_map/all_gather | solution.py:41
  8.7 199.8 %all-gather.15.cloned.1.call-start = ((), (), s32[]{:S(2)}) async-start(), calls=%async_computation.8 | async-start | bytes 4866048 | tf_op jit(solution)/shard_map/all_gather | solution.py:41
  11.3 355.9 %all-gather.11.cloned.1.call-start = ((), (), s32[]{:S(2)}) async-start(), calls=%async_computation.3 | async-start | bytes 3072000 | tf_op jit(solution)/shard_map/all_gather | solution.py:126
  27.6 198.0 %copy-start.1 = (bf16[2,197,768]{2,0,1:T(2,128)(2,1)}, bf16[2,197,768]{2,0,1:T(2,128)(2,1)S(1)}, u32[]{:S(2)}) copy-start(bf16[2,197,768]{2,0,1:T(2,128)(2,1)S(1)} %get-tuple-element.102) | copy-start | bytes 1815556
  216.1 9.2 %copy-start.3 = (bf16[4,2,197,192]{2,3,1,0:T(8,128)(2,1)}, bf16[4,2,197,192]{2,3,1,0:T(8,128)(2,1)S(1)}, u32[]{:S(2)}) copy-start(bf16[4,2,197,192]{2,3,1,0:T(8,128)(2,1)S(1)} %copy.95) | copy-start | bytes 1815556
  223.1 6.8 %slice-start.2 = ((s8[4718592]{0:T(1024)(128)(4,1)}), s8[4194304]{0:T(1024)(128)(4,1)S(1)}, s32[]{:S(2)}) async-start(s8[4718592]{0:T(1024)(128)(4,1)} %bitcast.288), calls=%async_computation.13 | async-start | bytes 8388608
  224.2 5.8 slice-start.3
  225.6 4.3 copy-start.18
  225.6 16.4 %slice-start.4 = ((s8[4718592]{0:T(1024)(128)(4,1)}), s8[4194304]{0:T(1024)(128)(4,1)S(1)}, s32[]{:S(2)}) async-start(s8[4718592]{0:T(1024)(128)(4,1)} %bitcast.292), calls=%async_computation.15 | async-start | bytes 8388608
  229.6 22.6 %copy-start.6 = (f32[2,197,768]{2,1,0:T(8,128)}, f32[2,197,768]{2,1,0:T(8,128)S(1)}, u32[]{:S(2)}) copy-start(f32[2,197,768]{2,1,0:T(8,128)S(1)} %get-tuple-element.93) | copy-start | bytes 3631108
  230.0 12.0 %slice-start.5 = ((s8[4718592]{0:T(1024)(128)(4,1)}), s8[524288]{0:T(1024)(128)(4,1)S(1)}, s32[]{:S(2)}) async-start(s8[4718592]{0:T(1024)(128)(4,1)} %bitcast.292), calls=%async_computation.16 | async-start | bytes 1048576
  230.0 12.0 %copy-start.16 = (bf16[2,197,768]{2,0,1:T(2,128)(2,1)S(1)}, bf16[2,197,768]{2,0,1:T(2,128)(2,1)}, u32[]{:S(2)}) copy-start(bf16[2,197,768]{2,0,1:T(2,128)(2,1)} %get-tuple-element.101) | copy-start | bytes 1815556
  242.0 7.2 %copy-start.20 = (bf16[4,2,197,768]{3,2,0,1:T(8,128)(2,1)}, bf16[4,2,197,768]{3,2,0,1:T(8,128)(2,1)S(1)}, u32[]{:S(2)}) copy-start(bf16[4,2,197,768]{3,2,0,1:T(8,128)(2,1)S(1)} %get-tuple-element.66) | copy-start | bytes 7262212
  252.2 118.5 %all-gather.13.cloned.1.call-start = ((), (), s32[]{:S(2)}) async-start(), calls=%async_computation.4 | async-start | bytes 3072000 | tf_op jit(solution)/shard_map/all_gather | solution.py:150
  257.6 9.4 %slice-start = ((s8[4915200]{0:T(1024)(128)(4,1)}), s8[720896]{0:T(1024)(128)(4,1)S(1)}, s32[]{:S(2)}) async-start(s8[4915200]{0:T(1024)(128)(4,1)} %bitcast.268), calls=%async_computation.11 | async-start | bytes 1441792
  263.1 4.0 slice-start.1
  270.0 6.4 copy-start.2
  276.4 5.1 copy-start.14
  276.4 5.1 copy-start.9
  282.8 4.7 copy-start.12
  282.9 136.0 %reduce-scatter.4.cloned.1.call-start = ((), (), s32[]{:S(2)}) async-start(), calls=%async_computation.5 | async-start | bytes 4866048 | tf_op jit(solution)/shard_map/reduce_scatter | solution.py:50
  305.8 225.6 %reduce-scatter.6.cloned.1.call-start = ((), (), s32[]{:S(2)}) async-start(), calls=%async_computation.6 | async-start | bytes 4866048 | tf_op jit(solution)/shard_map/reduce_scatter | solution.py:50
  314.4 328.6 %reduce-scatter.8.cloned.1.call-start = ((), (), s32[]{:S(2)}) async-start(), calls=%async_computation.7 | async-start | bytes 4866048 | tf_op jit(solution)/shard_map/reduce_scatter | solution.py:50
  (11 other events, 22.6 us)
Sparse Core Ops, SparseCore 0:
  10.9 66.2 all-gather.16
  80.1 62.3 all-gather.18
  146.1 62.3 all-gather.14
  252.3 23.4 all-gather.10
  283.0 23.3 all-gather.12
  311.7 107.1 reduce-scatter.3
  425.3 106.0 reduce-scatter.5
  536.9 106.0 reduce-scatter.7

commit v2 on v1

--- a/solution.py
+++ b/solution.py
@@ -3,6 +3,8 @@
 import jax
 import jax.numpy as jnp
 from jax import lax
+from jax.experimental import pallas as pl
+from jax.experimental.pallas import tpu as pltpu
 from jax.sharding import PartitionSpec as P
 
 HEAD_DIM = 64
@@ -37,17 +39,158 @@
     return jnp.einsum(spec, left, right, preferred_element_type=f32)
 
 
-def gather_weight(piece, n_dp, n_t):
-    whole = lax.all_gather(piece, AXES, axis=0, tiled=False)
-    whole = whole.reshape(n_dp, n_t, piece.shape[0], piece.shape[1]).transpose(1, 0, 2, 3)
-    return whole.reshape(n_t, n_dp * piece.shape[0], piece.shape[1])
-
-
-def scatter_grad(part, n_dp, n_t):
-    rows = part.shape[1] // n_dp
-    part = part.astype(bf16).reshape(n_t, n_dp, rows, part.shape[2]).transpose(1, 0, 2, 3)
-    part = part.reshape(n_dp * n_t * rows, part.shape[3])
-    return lax.psum_scatter(part, AXES, scatter_dimension=0, tiled=True).astype(f32)
+PARTS = 3
+TILE = 16
+
+
+class Cube:
+    def __init__(self, n_dp, n_t, rows):
+        self.n_dp, self.n_t, self.rows = n_dp, n_t, rows
+        self.n = n_dp * n_t
+        bits = [1 << i for i in range(self.n.bit_length() - 1)]
+        self.fast = (1 << len(bits)) == self.n and len(bits) >= 4 and rows % (PARTS * TILE) == 0
+        spin = bits[1:4]
+        self.far = bits[4:]
+        self.orders = [spin[p:] + spin[:p] for p in range(PARTS)]
+        self.step = rows // PARTS
+
+    def swap(self, value, mask):
+        return lax.ppermute(value, AXES, [(i, i ^ mask) for i in range(self.n)])
+
+    def place(self, part, index):
+        masks = [1 << i for i in range(1, self.n.bit_length() - 1) if (1 << i) >= 16]
+        masks = masks + self.orders[part][::-1]
+        out = index * 0
+        for k, mask in enumerate(masks):
+            out = out | (((index // mask) % 2) << k)
+        return out
+
+
+def copy_call(body, inputs, out_shapes, n_copies, index):
+    def kernel(index_ref, *refs):
+        sems = refs[-1]
+        copies = []
+        for src, dst in body(index_ref, refs[: len(inputs)], refs[len(inputs) : -1]):
+            copies.append(pltpu.make_async_copy(src, dst, sems.at[len(copies)]))
+        for copy in copies:
+            copy.start()
+        for copy in copies:
+            copy.wait()
+
+    moved = sum(x.size * x.dtype.itemsize for x in inputs)
+    return pl.pallas_call(
+        kernel,
+        out_shape=out_shapes,
+        in_specs=[pl.BlockSpec(memory_space=pltpu.SMEM)]
+        + [pl.BlockSpec(memory_space=pl.ANY)] * len(inputs),
+        out_specs=jax.tree.map(lambda _: pl.BlockSpec(memory_space=pl.ANY), out_shapes),
+        scratch_shapes=[pltpu.SemaphoreType.DMA((n_copies,))],
+        cost_estimate=pl.CostEstimate(flops=0, bytes_accessed=2 * moved, transcendentals=0),
+    )(index, *inputs)
+
+
+def gather_weight(cube, piece):
+    rows, cols = piece.shape
+    n_dp, n_t = cube.n_dp, cube.n_t
+    if not cube.fast:
+        whole = lax.all_gather(piece, AXES, axis=0, tiled=False)
+        whole = whole.reshape(n_dp, n_t, rows, cols).transpose(1, 0, 2, 3)
+        whole = whole.reshape(n_t, n_dp * rows, cols)
+        return jnp.take(whole, lax.axis_index("tensor") ^ jnp.arange(n_t), axis=0)
+    have = piece[None]
+    for mask in cube.far:
+        have = jnp.concatenate((have, cube.swap(have, mask)))
+    step = cube.step
+    held = [have[:, p * step : (p + 1) * step] for p in range(PARTS)]
+    for k in range(3):
+        came = [cube.swap(held[p], cube.orders[p][::-1][k]) for p in range(PARTS)]
+        held = [jnp.concatenate((held[p], came[p])) for p in range(PARTS)]
+    other = [cube.swap(held[p], 1) for p in range(PARTS)]
+    dp = lax.axis_index("dp")
+    offsets = jnp.stack([cube.place(p, dp * n_t) for p in range(PARTS)]).astype(jnp.int32)
+
+    def body(index_ref, ins, outs):
+        for t in range(n_t):
+            for d in range(n_dp):
+                for p in range(PARTS):
+                    at = index_ref[p] ^ cube.place(p, d * n_t + t)
+                    src = ins[p + PARTS * (t % 2)].at[at]
+                    yield src, outs[0].at[t, pl.ds(d * rows + p * step, step)]
+
+    out = jax.ShapeDtypeStruct((n_t, n_dp * rows, cols), piece.dtype)
+    return copy_call(body, held + other, [out], n_dp * n_t * PARTS, offsets)[0]
+
+
+def scatter_grad(cube, part):
+    n_dp, n_t, rows = cube.n_dp, cube.n_t, cube.rows
+    cols = part.shape[2]
+    part = part.astype(bf16)
+    if not cube.fast:
+        part = jnp.take(part, lax.axis_index("tensor") ^ jnp.arange(n_t), axis=0)
+        part = part.reshape(n_t, n_dp, rows, cols).transpose(1, 0, 2, 3)
+        part = part.reshape(n_dp * n_t * rows, cols)
+        return lax.psum_scatter(part, AXES, scatter_dimension=0, tiled=True).astype(f32)
+    step = cube.step
+    dp = lax.axis_index("dp")
+    offsets = jnp.stack([cube.place(p, dp * n_t) for p in range(PARTS)]).astype(jnp.int32)
+
+    def body(index_ref, ins, outs):
+        for t in range(n_t):
+            for d in range(n_dp):
+                for p in range(PARTS):
+                    at = index_ref[p] ^ cube.place(p, d * n_t + t)
+                    dst = outs[p + PARTS * (t % 2)].at[at]
+                    yield ins[0].at[t, pl.ds(d * rows + p * step, step)], dst
+
+    half = n_dp * n_t // 2
+    out = jax.ShapeDtypeStruct((half, step, cols), bf16)
+    blocks = copy_call(body, [part], [out] * (2 * PARTS), n_dp * n_t * PARTS, offsets)
+    terms = [[blocks[p], cube.swap(blocks[p + PARTS], 1)] for p in range(PARTS)]
+
+    def total(values):
+        value = values[0].astype(f32)
+        for more in values[1:]:
+            value = value + more.astype(f32)
+        return value
+
+    size = half
+    for k in range(3):
+        size //= 2
+        came = [
+            cube.swap(total([v[size : 2 * size] for v in terms[p]]).astype(bf16), cube.orders[p][k])
+            for p in range(PARTS)
+        ]
+        terms = [[v[:size] for v in terms[p]] + [came[p]] for p in range(PARTS)]
+    joined = [jnp.concatenate(vs, axis=1) for vs in zip(*terms)]
+    for mask in cube.far[::-1]:
+        size //= 2
+        came = cube.swap(total([v[size : 2 * size] for v in joined]).astype(bf16), mask)
+        joined = [v[:size] for v in joined] + [came]
+    return total(joined)[0]
+
+
+def sum_all(cube, value):
+    if not cube.fast:
+        return lax.psum(value, AXES)
+    for mask in [1] + cube.orders[0] + cube.far:
+        value = value + cube.swap(value, mask)
+    return value
+
+
+def gather_images(cube, mine):
+    if not cube.fast or cube.n_t != 4:
+        return lax.all_gather(mine, "tensor", axis=0, tiled=True)
+    count = mine.shape[0]
+    there = cube.swap(mine, 2)
+    pieces = [mine, cube.swap(mine, 1), there, cube.swap(there, 1)]
+    index = lax.axis_index("tensor").astype(jnp.int32).reshape(1)
+
+    def body(index_ref, ins, outs):
+        for r in range(4):
+            yield ins[r], outs[0].at[pl.ds((index_ref[0] ^ r) * count, count)]
+
+    out = jax.ShapeDtypeStruct((4 * count,) + mine.shape[1:], mine.dtype)
+    return copy_call(body, pieces, [out], 4, index)[0]
 
 
 def on_device(
@@ -70,18 +213,24 @@
 ):
     factor = HEAD_DIM ** (-0.5)
     t_me = lax.axis_index("tensor")
+    cube = Cube(n_dp, n_t, qkv_weight.shape[1])
+    order = t_me ^ jnp.arange(n_t)
     width = qkv_weight.shape[2]
     heads = width // HEAD_DIM
-    rows = qkv_weight.shape[1]
     attn_piece = jnp.concatenate(
         (qkv_weight[0], qkv_weight[1], qkv_weight[2], out_weight.T), axis=1
     )
-    w_attn = gather_weight(attn_piece, n_dp, n_t)
-    w_fc1 = gather_weight(fc1_weight, n_dp, n_t)
-    w_fc2 = gather_weight(fc2_weight.T, n_dp, n_t)
-    biases = lax.all_gather(
-        jnp.concatenate((qv_bias.reshape(-1), fc1_bias)), "tensor", axis=0, tiled=False
-    ).astype(f32)
+    w_attn = gather_weight(cube, attn_piece)
+    f_width = fc1_weight.shape[1]
+    w_mlp = gather_weight(cube, jnp.concatenate((fc1_weight, fc2_weight.T), axis=1))
+    w_fc1, w_fc2 = (w_mlp[..., :f_width], w_mlp[..., f_width:])
+    biases = jnp.concatenate((qv_bias.reshape(-1), fc1_bias))[None]
+    if cube.fast and n_t == 4:
+        biases = jnp.concatenate((biases, cube.swap(biases, 1)))
+        biases = jnp.concatenate((biases, cube.swap(biases, 2)))
+    else:
+        biases = jnp.take(lax.all_gather(biases[0], "tensor", axis=0, tiled=False), order, axis=0)
+    biases = biases.astype(f32)
     q_bias = biases[:, :width]
     v_bias = biases[:, width : 2 * width]
     f_bias = biases[:, 2 * width :]
@@ -116,14 +265,17 @@
     activated, gelu_pull = jax.vjp(partial(jax.nn.gelu, approximate=False), pre_act)
     act_low = activated.astype(bf16)
     upstream = cot.astype(f32)
-    fc2_grad = scatter_grad(dot("bsd,tbsf->tdf", cot, act_low), n_dp, n_t)
+    fc2_grad_part = dot("bsd,tbsf->tdf", cot, act_low)
     dact = dot("bsd,tdf->tbsf", cot, w_fc2)
     dpre_low = gelu_pull(dact)[0].astype(bf16)
-    fc1_grad = scatter_grad(dot("bsd,tbsf->tdf", norm_two_low, dpre_low), n_dp, n_t)
+    fc1_grad_part = dot("bsd,tbsf->tdf", norm_two_low, dpre_low)
+    mlp_grad = scatter_grad(
+        cube, jnp.concatenate((fc1_grad_part.astype(bf16), fc2_grad_part.astype(bf16)), -1)
+    )
     dnorm_two = dot("tbsf,tdf->bsd", dpre_low, w_fc1)
     mlp_full = dot("tbsf,tdf->bsd", act_low, w_fc2)
     encoded_mine = (hidden_state + mlp_full + fc2_bias.astype(f32)).astype(bf16)
-    encoded = lax.all_gather(encoded_mine, "tensor", axis=0, tiled=True)
+    encoded = gather_images(cube, encoded_mine)
     dhidden_norm, gain_two_part, shift_two_part = norm_back(
         dnorm_two, normed_two, inverse_two, gain_two
     )
@@ -141,14 +293,16 @@
         (dquery.reshape(shape), dkey.reshape(shape), dvalue.reshape(shape)), -1
     ).astype(bf16)
     qkv_grad_part = dot("bsd,tbse->tde", norm_one_low, dqkv)
-    attn_grad = scatter_grad(jnp.concatenate((qkv_grad_part, out_grad_part), -1), n_dp, n_t)
+    attn_grad = scatter_grad(cube, jnp.concatenate((qkv_grad_part, out_grad_part), -1))
     dnorm_one = dot("tbse,tde->bsd", dqkv, w_attn[:, :, : 3 * width])
     dinput_norm, gain_one_part, shift_one_part = norm_back(
         dnorm_one, normed_one, inverse_one, gain_one
     )
     patch_mine = (dhidden + dinput_norm).astype(bf16)
-    patch_grad = lax.all_gather(patch_mine, "tensor", axis=0, tiled=True)
+    patch_grad = gather_images(cube, patch_mine)
     d_sums = jnp.sum(dqkv.astype(f32), (1, 2))
+    d_sums = jnp.take(d_sums, order, axis=0)
+    f_sums = jnp.take(jnp.sum(dpre_low.astype(f32), (1, 2)), order, axis=0)
     small = jnp.concatenate(
         (
             gain_one_part,
@@ -159,10 +313,10 @@
             row_total(upstream),
             d_sums[:, :width].reshape(-1),
             d_sums[:, 2 * width :].reshape(-1),
-            jnp.sum(dpre_low.astype(f32), (1, 2)).reshape(-1),
+            f_sums.reshape(-1),
         )
     )
-    small = lax.psum(small, AXES)
+    small = sum_all(cube, small)
     d = gain_one.shape[0]
     cuts = [small[i * d : (i + 1) * d] for i in range(6)]
     at = 6 * d
@@ -170,7 +324,6 @@
     at += n_t * width
     v_sum = lax.dynamic_slice_in_dim(small[at : at + n_t * width], t_me * width, width, 0)
     at += n_t * width
-    f_width = fc1_weight.shape[1]
     f_sum = lax.dynamic_slice_in_dim(small[at:], t_me * f_width, f_width, 0)
     return (
         encoded,
@@ -183,9 +336,9 @@
         cuts[2],
         cuts[3],
         cuts[4],
-        fc1_grad,
+        mlp_grad[:, :f_width],
         f_sum,
-        fc2_grad.T,
+        mlp_grad[:, f_width:].T,
         cuts[5],
     )
 

time: 658 us -> 1370 us (2.08)
  Pallas kernels: 0 us -> 1020 us
  waiting for transfers between devices: 436 us -> 78.4 us
  starting transfers between devices: 0.58 us -> 57.7 us
  blocking collectives: 46.2 us -> 0 us
  other arithmetic: 24.7 us -> 65.6 us
    pallas_call x0 -> x6, Pallas kernels: none -> 1020 us  [copy_call(): pl.pallas_call(kernel, out_shape=out_shapes, in_specs=[pl.BlockSpec(memor...]
    reduce_scatter x3 -> x0, waiting for transfers between devices: 264 us -> none  [scatter_grad(): lax.psum_scatter(part, AXES, scatter_dimension=0, tiled=True).astype(f32)]
    all_gather x5 -> x0, waiting for transfers between devices: 171 us -> none  [the longest x3 171 us: gather_weight(): whole = lax.all_gather(piece, AXES, axis=0, tiled=False)]
    ppermute x0 -> x65, waiting for transfers between devices: none -> 78.4 us  [swap(): return lax.ppermute(value, AXES, [(i, i ^ mask) for i in range(self.n)])]
    ppermute x0 -> x65, starting transfers between devices: none -> 57.7 us  [swap(): return lax.ppermute(value, AXES, [(i, i ^ mask) for i in range(self.n)])]
    psum x1 -> x0, blocking collectives: 40 us -> none  [on_device(): small = lax.psum(small, AXES)]
    concatenate x2 -> x32, other arithmetic: 1.46 us -> 29.7 us  [the longest x18 12.3 us: gather_weight(): held = [jnp.concatenate((held[p], came[p])) for p in range(PARTS)]]
    convert_element_type x2 -> x21, other arithmetic: 2.57 us -> 18.9 us  [the longest x18 17.9 us: scatter_grad(): total([v[size:2 * size] for v in terms[p]]).astype(bf16)]
  transfers between devices with their start and end apart: 8 -> 65, of which waited for: 6 -> 26; matrix products, arithmetic and copies ran while one was open for 16% -> 13% of each run, Pallas kernels for 0% -> 54%
where the time goes in v2:
time: 1370 us; the launch traced here: 1360 us
  Pallas kernels  1020 us (74%)
  waiting for transfers between devices  78.4 us (6%)
  matrix products  72.7 us (5%)
  other arithmetic  65.6 us (5%)
  local copies, waits for them, and re-layouts  64.1 us (5%)
  starting transfers between devices  57.7 us (4%)
    pallas_call x6, Pallas kernels, copy_call(): pl.pallas_call(kernel, out_shape=out_shapes, in_specs=[pl.BlockSpec(memor...  1020 us
    ppermute x65, waiting for transfers between devices, swap(): return lax.ppermute(value, AXES, [(i, i ^ mask) for i in range(self.n)])  78.4 us
    dot_general x18, matrix products, dot(): return jnp.einsum(spec, left, right, preferred_element_type=f32)  72.7 us
    ppermute x65, starting transfers between devices, swap(): return lax.ppermute(value, AXES, [(i, i ^ mask) for i in range(self.n)])  57.7 us
  transfers between devices with their start and end apart: 65, of which 26 were waited for; matrix products, arithmetic and copies ran while one was open for 13% of the time, Pallas kernels for 54%

profile of v2, /device:TPU:0, one launch (start us, length us, event | category | flops | bytes accessed | tf_op | source)
XLA Modules:
  0.0 1360.5 jit_solution(3003575774897102627)
XLA Ops:
  46.1 5.8 collective-permute-done.6
  54.7 4.1 collective-permute-done.23
  62.8 8.0 collective-permute-done.20
  75.9 145.6 %shard_map.245 = bf16[4,768,768]{2,1,0:T(8,128)(2,1)} custom-call(s32[3]{0:T(128)} %pad_add_fusion.index_ref, bf16[16,32,768]{2,1,0:T(8,128)(2,1)} %copy-done.13, bf16[16,32,768]{2,1,0:T(8,128)(2,1)} %copy-done.12, bf16[16,32,768]{2,1,0:T(8,128)(2,1)} %copy-done.14, bf16[16,32,768]{2,1,0:T(8,128)(2,1)} %copy-done.42, bf16[16,32,768]{2,1,0:T(8,128)(2,1)} %copy-done.41, ...), custom_call_target="tpu_custom_call" | custom-call | bytes 9437184 | tf_op jit(solution)/shard_map/pallas_call | solution.py:81
  221.5 3.9 fusion.35
  234.5 4.0 pad_maximum_fusion.4.refs_1_
  254.4 288.5 %shard_map.246 = bf16[4,768,1536]{2,1,0:T(8,128)(2,1)} custom-call(s32[3]{0:T(128)} %pad_add_fusion.index_ref, bf16[16,32,1536]{2,1,0:T(8,128)(2,1)} %pad_maximum_fusion.3.refs_0_, bf16[16,32,1536]{2,1,0:T(8,128)(2,1)} %pad_maximum_fusion.4.refs_1_, bf16[16,32,1536]{2,1,0:T(8,128)(2,1)} %pad_maximum_fusion.5.refs_2_, ...), custom_call_target="tpu_custom_call" | custom-call | bytes 18874368 | tf_op jit(solution)/shard_map/pallas_call | solution.py:81
  543.0 16.9 %fusion.9 = (bf16[4,2,197,768]{3,2,1,0:T(8,128)(2,1)S(1)}, f32[4,2,197,768]{3,2,1,0:T(8,128)S(1)}, f32[4,768,2,197]{1,3,2,0:T(8,128)}) fusion(f32[4,768]{1,0:T(4,128)S(1)} %fusion.85, f32[2,197,768]{2,1,0:T(8,128)} %copy-done.7, f32[768]{0:T(1024)S(1)} %convert_element_type.398, f32[768]{0:T(1024)S(1)} %convert_element_type.397, ...), kind=kOutput, calls=%fused_computation.23 | convolution fusion | flops 1940522496 | bytes 18072656 | tf_op jit(solution)/shard_map/bsd,tdf->tbsf/dot_general | solution.py:39
  565.0 6.1 convert_reduce_fusion
  573.6 4.6 fusion.22
  578.2 4.3 fusion.23
  599.1 5.4 fusion.62
  605.4 6.1 bitcast_convert_fusion.2
  623.7 6.0 copy.148
  630.5 5.1 pad_maximum_fusion.1.refs_0_
  635.6 145.6 %shard_map.249 = (bf16[16,32,768]{2,1,0:T(8,128)(2,1)}, bf16[16,32,768]{2,1,0:T(8,128)(2,1)}, bf16[16,32,768]{2,1,0:T(8,128)(2,1)}, bf16[16,32,768]{2,1,0:T(8,12...) custom-call(s32[3]{0:T(128)} %pad_add_fusion.index_ref, bf16[4,768,768]{2,1,0:T(8,128)(2,1)} %pad_maximum_fusion.1.refs_0_), custom_call_target="tpu_custom_call" | custom-call | bytes 9437184 | tf_op jit(solution)/shard_map/pallas_call | solution.py:81
  789.3 9.2 pad_maximum_fusion.refs_0_
  799.7 288.5 %shard_map.250 = (bf16[16,32,1536]{2,1,0:T(8,128)(2,1)}, bf16[16,32,1536]{2,1,0:T(8,128)(2,1)}, bf16[16,32,1536]{2,1,0:T(8,128)(2,1)}, bf16[16,32,1536]{2,1,0:T(...) custom-call(s32[3]{0:T(128)} %pad_add_fusion.index_ref, ...), custom_call_target="tpu_custom_call" | custom-call | bytes 18874368 | tf_op jit(solution)/shard_map/pallas_call | solution.py:81
  1106.8 8.3 collective-permute-done.42
  1118.0 7.5 collective-permute-done.44
  1128.0 75.6 %shard_map.247 = bf16[8,197,768]{2,1,0:T(8,128)(2,1)} custom-call(s32[1]{0:T(128)} %bitcast.index_ref, bf16[2,197,768]{2,1,0:T(8,128)(2,1)} %copy-done.18, bf16[2,197,768]{2,1,0:T(8,128)(2,1)} %copy.131.refs_1_, bf16[2,197,768]{2,1,0:T(8,128)(2,1)} %copy.132.refs_2_, bf16[2,197,768]{2,1,0:T(8,128)(2,1)} %copy.133.refs_3_), custom_call_target="tpu_custom_call" | custom-call | bytes 4841472 | tf_op jit(solution)/shard_map/pallas_call | solution.py:81
  1209.6 75.6 %shard_map.248 = bf16[8,197,768]{2,1,0:T(8,128)(2,1)} custom-call(s32[1]{0:T(128)} %bitcast.index_ref, bf16[2,197,768]{2,1,0:T(8,128)(2,1)} %copy-done.4, bf16[2,197,768]{2,1,0:T(8,128)(2,1)} %copy.145.refs_1_, bf16[2,197,768]{2,1,0:T(8,128)(2,1)} %copy.146.refs_2_, bf16[2,197,768]{2,1,0:T(8,128)(2,1)} %copy.147.refs_3_), custom_call_target="tpu_custom_call" | custom-call | bytes 4841472 | tf_op jit(solution)/shard_map/pallas_call | solution.py:81
  1314.1 8.0 collective-permute-done.55
  1350.2 7.5 collective-permute-done.64
  (423 shorter events, 217.7 us)
Async XLA Ops:
  4.7 18.0 %collective-permute-start = (bf16[1,96,768]{2,1,0:T(8,128)(2,1)S(1)}, bf16[1,96,768]{2,1,0:T(8,128)(2,1)}, u32[]{:S(2)}, u32[]{:S(2)}) collective-permute-start(bf16[1,96,768]{2,1,0:T(8,128)(2,1)S(1)} %maximum_bitcast_fusion.1), channel_id=1, source_target_pairs={{0,16},{1,17},{2,18},{3,19},{4,20},{5,21},{6,22},{7,23},{8,24},{9,... | collective-permute-start | bytes 442376 | tf_op jit(solution)/shard_map/ppermute | solution.py:58
  9.4 23.8 %collective-permute-start.15 = (bf16[1,96,1536]{2,1,0:T(8,128)(2,1)S(1)}, bf16[1,96,1536]{2,1,0:T(8,128)(2,1)}, u32[]{:S(2)}, u32[]{:S(2)}) collective-permute-start(bf16[1,96,1536]{2,1,0:T(8,128)(2,1)S(1)} %maximum_bitcast_fusion), channel_id=1, source_target_pairs={{0,16},{1,17},{2,18},{3,19},{4,20},{5,21},{6,22},{7,23},{8,24},{9,... | collective-permute-start | bytes 884744 | tf_op jit(solution)/shard_map/ppermute | solution.py:58
  36.3 18.3 %collective-permute-start.19 = (bf16[2,32,1536]{2,1,0:T(8,128)(2,1)S(1)}, bf16[2,32,1536]{2,1,0:T(8,128)(2,1)S(1)}, u32[]{:S(2)}, u32[]{:S(2)}) collective-permute-start(bf16[2,32,1536]{2,1,0:T(8,128)(2,1)S(1)} %get-tuple-element.113), channel_id=1, source_target_pairs={{0,2},{1,3},{2,0},{3,1},{4,6},{5,7},{6,4},{7,5},{8,10},{9,11},{10,... | collective-permute-start | bytes 589832 | tf_op jit(solution)/shard_map/ppermute | solution.py:58
  53.7 19.7 %collective-permute-start.11 = (bf16[16,32,768]{2,1,0:T(8,128)(2,1)S(1)}, bf16[16,32,768]{2,1,0:T(8,128)(2,1)S(1)}, u32[]{:S(2)}, u32[]{:S(2)}) collective-permute-start(bf16[16,32,768]{2,1,0:T(8,128)(2,1)S(1)} %pad_maximum_fusion.7.refs_1_), channel_id=1, source_target_pairs={{0,1},{1,0},{2,3},{3,2},{4,5},{5,4},{6,7},{7,6},{8,9},{9,8},{10,11... | collective-permute-start | bytes 2359304 | tf_op jit(solution)/shard_map/ppermute | solution.py:58
  53.9 21.1 %collective-permute-start.10 = (bf16[16,32,768]{2,1,0:T(8,128)(2,1)S(1)}, bf16[16,32,768]{2,1,0:T(8,128)(2,1)S(1)}, u32[]{:S(2)}, u32[]{:S(2)}) collective-permute-start(bf16[16,32,768]{2,1,0:T(8,128)(2,1)S(1)} %pad_maximum_fusion.6.refs_0_), channel_id=1, source_target_pairs={{0,1},{1,0},{2,3},{3,2},{4,5},{5,4},{6,7},{7,6},{8,9},{9,8},{10,11... | collective-permute-start | bytes 2359304 | tf_op jit(solution)/shard_map/ppermute | solution.py:58
  54.6 21.3 %collective-permute-start.12 = (bf16[16,32,768]{2,1,0:T(8,128)(2,1)S(1)}, bf16[16,32,768]{2,1,0:T(8,128)(2,1)}, u32[]{:S(2)}, u32[]{:S(2)}) collective-permute-start(bf16[16,32,768]{2,1,0:T(8,128)(2,1)S(1)} %pad_maximum_fusion.8.refs_2_), channel_id=1, source_target_pairs={{0,1},{1,0},{2,3},{3,2},{4,5},{5,4},{6,7},{7,6},{8,9},{9,8},{10,11... | collective-permute-start | bytes 2359304 | tf_op jit(solution)/shard_map/ppermute | solution.py:58
  61.2 180.3 %collective-permute-start.24 = (bf16[8,32,1536]{2,1,0:T(8,128)(2,1)}, bf16[8,32,1536]{2,1,0:T(8,128)(2,1)}, u32[]{:S(2)}, u32[]{:S(2)}) collective-permute-start(bf16[8,32,1536]{2,1,0:T(8,128)(2,1)} %pad_maximum_fusion.11), channel_id=1, source_target_pairs={{0,8},{1,9},{2,10},{3,11},{4,12},{5,13},{6,14},{7,15},{8,0},{9,1},... | collective-permute-start | bytes 2359304 | tf_op jit(solution)/shard_map/ppermute | solution.py:58
  70.8 167.6 %collective-permute-start.18 = (bf16[8,32,1536]{2,1,0:T(8,128)(2,1)}, bf16[8,32,1536]{2,1,0:T(8,128)(2,1)}, u32[]{:S(2)}, u32[]{:S(2)}) collective-permute-start(bf16[8,32,1536]{2,1,0:T(8,128)(2,1)} %pad_maximum_fusion.9), channel_id=1, source_target_pairs={{0,2},{1,3},{2,0},{3,1},{4,6},{5,7},{6,4},{7,5},{8,10},{9,11},{10,... | collective-permute-start | bytes 2359304 | tf_op jit(solution)/shard_map/ppermute | solution.py:58
  73.4 160.9 %collective-permute-start.21 = (bf16[8,32,1536]{2,1,0:T(8,128)(2,1)}, bf16[8,32,1536]{2,1,0:T(8,128)(2,1)}, u32[]{:S(2)}, u32[]{:S(2)}) collective-permute-start(bf16[8,32,1536]{2,1,0:T(8,128)(2,1)} %pad_maximum_fusion.10), channel_id=1, source_target_pairs={{0,4},{1,5},{2,6},{3,7},{4,0},{5,1},{6,2},{7,3},{8,12},{9,13},{10,... | collective-permute-start | bytes 2359304 | tf_op jit(solution)/shard_map/ppermute | solution.py:58
  564.2 526.9 %collective-permute-start.29 = (bf16[2,197,768]{2,0,1:T(2,128)(2,1)}, bf16[2,197,768]{2,0,1:T(2,128)(2,1)}, u32[]{:S(2)}, u32[]{:S(2)}) collective-permute-start(bf16[2,197,768]{2,0,1:T(2,128)(2,1)} %copy.129), channel_id=1, source_target_pairs={{0,2},{1,3},{2,0},{3,1},{4,6},{5,7},{6,4},{7,5},{8,10},{9,11},{10,... | collective-permute-start | bytes 1815560 | tf_op jit(solution)/shard_map/ppermute | solution.py:58
  564.7 526.8 %collective-permute-start.28 = (bf16[2,197,768]{2,0,1:T(2,128)(2,1)}, bf16[2,197,768]{2,0,1:T(2,128)(2,1)}, u32[]{:S(2)}, u32[]{:S(2)}) collective-permute-start(bf16[2,197,768]{2,0,1:T(2,128)(2,1)} %copy.129), channel_id=1, source_target_pairs={{0,1},{1,0},{2,3},{3,2},{4,5},{5,4},{6,7},{7,6},{8,9},{9,8},{10,11... | collective-permute-start | bytes 1815560 | tf_op jit(solution)/shard_map/ppermute | solution.py:58
  629.7 156.1 %collective-permute-start.37 = (f32[9216]{0:T(1024)S(1)}, f32[9216]{0:T(1024)S(1)}, u32[]{:S(2)}, u32[]{:S(2)}) collective-permute-start(f32[9216]{0:T(1024)S(1)} %add.389), channel_id=1, source_target_pairs={{0,8},{1,9},{2,10},{3,11},{4,12},{5,13},{6,14},{7,15},{8,0},{9,1},... | collective-permute-start | bytes 110600 | tf_op jit(solution)/shard_map/ppermute | solution.py:58
  784.3 315.8 %collective-permute-start.32 = (bf16[2,197,768]{2,0,1:T(2,128)(2,1)}, bf16[2,197,768]{2,0,1:T(2,128)(2,1)}, u32[]{:S(2)}, u32[]{:S(2)}) collective-permute-start(bf16[2,197,768]{2,0,1:T(2,128)(2,1)} %copy.143), channel_id=1, source_target_pairs={{0,2},{1,3},{2,0},{3,1},{4,6},{5,7},{6,4},{7,5},{8,10},{9,11},{10,... | collective-permute-start | bytes 1815560 | tf_op jit(solution)/shard_map/ppermute | solution.py:58
  785.8 316.5 %collective-permute-start.39 = (bf16[16,32,768]{2,1,0:T(8,128)(2,1)}, bf16[16,32,768]{2,1,0:T(8,128)(2,1)}, u32[]{:S(2)}, u32[]{:S(2)}) collective-permute-start(bf16[16,32,768]{2,1,0:T(8,128)(2,1)} %get-tuple-element.29), channel_id=1, source_target_pairs={{0,1},{1,0},{2,3},{3,2},{4,5},{5,4},{6,7},{7,6},{8,9},{9,8},{10,11... | collective-permute-start | bytes 2359304 | tf_op jit(solution)/shard_map/ppermute | solution.py:58
  799.4 298.5 %collective-permute-start.31 = (bf16[2,197,768]{2,0,1:T(2,128)(2,1)}, bf16[2,197,768]{2,0,1:T(2,128)(2,1)}, u32[]{:S(2)}, u32[]{:S(2)}) collective-permute-start(bf16[2,197,768]{2,0,1:T(2,128)(2,1)} %copy.143), channel_id=1, source_target_pairs={{0,1},{1,0},{2,3},{3,2},{4,5},{5,4},{6,7},{7,6},{8,9},{9,8},{10,11... | collective-permute-start | bytes 1815560 | tf_op jit(solution)/shard_map/ppermute | solution.py:58
  1097.9 205.2 %collective-permute-start.52 = (bf16[16,32,1536]{2,1,0:T(8,128)(2,1)}, bf16[16,32,1536]{2,1,0:T(8,128)(2,1)}, u32[]{:S(2)}, u32[]{:S(2)}) collective-permute-start(bf16[16,32,1536]{2,1,0:T(8,128)(2,1)} %get-tuple-element.35), channel_id=1, source_target_pairs={{0,1},{1,0},{2,3},{3,2},{4,5},{5,4},{6,7},{7,6},{8,9},{9,8},{10,11... | collective-permute-start | bytes 4718600 | tf_op jit(solution)/shard_map/ppermute | solution.py:58
  1100.1 205.7 %collective-permute-start.53 = (bf16[16,32,1536]{2,1,0:T(8,128)(2,1)}, bf16[16,32,1536]{2,1,0:T(8,128)(2,1)}, u32[]{:S(2)}, u32[]{:S(2)}) collective-permute-start(bf16[16,32,1536]{2,1,0:T(8,128)(2,1)} %get-tuple-element.36), channel_id=1, source_target_pairs={{0,1},{1,0},{2,3},{3,2},{4,5},{5,4},{6,7},{7,6},{8,9},{9,8},{10,11... | collective-permute-start | bytes 4718600 | tf_op jit(solution)/shard_map/ppermute | solution.py:58
  1102.4 24.6 %collective-permute-start.30 = (bf16[2,197,768]{2,0,1:T(2,128)(2,1)}, bf16[2,197,768]{2,0,1:T(2,128)(2,1)S(1)}, u32[]{:S(2)}, u32[]{:S(2)}) collective-permute-start(bf16[2,197,768]{2,0,1:T(2,128)(2,1)} %collective-permute-done.29), channel_id=1, source_target_pairs={{0,1},{1,0},{2,3},{3,2},{4,5},{5,4},{6,7},{7,6},{8,9},{9,8},{10,11... | collective-permute-start | bytes 1815560 | tf_op jit(solution)/shard_map/ppermute | solution.py:58
  1117.2 90.0 %collective-permute-start.33 = (bf16[2,197,768]{2,0,1:T(2,128)(2,1)}, bf16[2,197,768]{2,0,1:T(2,128)(2,1)}, u32[]{:S(2)}, u32[]{:S(2)}) collective-permute-start(bf16[2,197,768]{2,0,1:T(2,128)(2,1)} %collective-permute-done.32), channel_id=1, source_target_pairs={{0,1},{1,0},{2,3},{3,2},{4,5},{5,4},{6,7},{7,6},{8,9},{9,8},{10,11... | collective-permute-start | bytes 1815560 | tf_op jit(solution)/shard_map/ppermute | solution.py:58
  1125.6 163.2 %collective-permute-start.45 = (bf16[4,32,768]{2,1,0:T(8,128)(2,1)}, bf16[4,32,768]{2,1,0:T(8,128)(2,1)}, u32[]{:S(2)}, u32[]{:S(2)}) collective-permute-start(bf16[4,32,768]{2,1,0:T(8,128)(2,1)} %add_convert_fusion.16), channel_id=1, source_target_pairs={{0,4},{1,5},{2,6},{3,7},{4,0},{5,1},{6,2},{7,3},{8,12},{9,13},{10,... | collective-permute-start | bytes 589832 | tf_op jit(solution)/shard_map/ppermute | solution.py:58
  1127.0 181.0 %collective-permute-start.54 = (bf16[16,32,1536]{2,1,0:T(8,128)(2,1)}, bf16[16,32,1536]{2,1,0:T(8,128)(2,1)}, u32[]{:S(2)}, u32[]{:S(2)}) collective-permute-start(bf16[16,32,1536]{2,1,0:T(8,128)(2,1)} %get-tuple-element.37), channel_id=1, source_target_pairs={{0,1},{1,0},{2,3},{3,2},{4,5},{5,4},{6,7},{7,6},{8,9},{9,8},{10,11... | collective-permute-start | bytes 4718600 | tf_op jit(solution)/shard_map/ppermute | solution.py:58
  1207.2 83.1 %collective-permute-start.46 = (bf16[4,32,768]{2,1,0:T(8,128)(2,1)S(1)}, bf16[4,32,768]{2,1,0:T(8,128)(2,1)}, u32[]{:S(2)}, u32[]{:S(2)}) collective-permute-start(bf16[4,32,768]{2,1,0:T(8,128)(2,1)S(1)} %copy-done.51), channel_id=1, source_target_pairs={{0,8},{1,9},{2,10},{3,11},{4,12},{5,13},{6,14},{7,15},{8,0},{9,1},... | collective-permute-start | bytes 589832 | tf_op jit(solution)/shard_map/ppermute | solution.py:58
  1307.2 18.2 %collective-permute-start.56 = (bf16[8,32,1536]{2,1,0:T(8,128)(2,1)S(1)}, bf16[8,32,1536]{2,1,0:T(8,128)(2,1)S(1)}, u32[]{:S(2)}, u32[]{:S(2)}) collective-permute-start(bf16[8,32,1536]{2,1,0:T(8,128)(2,1)S(1)} %add_convert_fusion.1), channel_id=1, source_target_pairs={{0,4},{1,5},{2,6},{3,7},{4,0},{5,1},{6,2},{7,3},{8,12},{9,13},{10,... | collective-permute-start | bytes 2359304 | tf_op jit(solution)/shard_map/ppermute | solution.py:58
  1309.4 20.1 %collective-permute-start.57 = (bf16[8,32,1536]{2,1,0:T(8,128)(2,1)S(1)}, bf16[8,32,1536]{2,1,0:T(8,128)(2,1)S(1)}, u32[]{:S(2)}, u32[]{:S(2)}) collective-permute-start(bf16[8,32,1536]{2,1,0:T(8,128)(2,1)S(1)} %add_convert_fusion), channel_id=1, source_target_pairs={{0,8},{1,9},{2,10},{3,11},{4,12},{5,13},{6,14},{7,15},{8,0},{9,1},... | collective-permute-start | bytes 2359304 | tf_op jit(solution)/shard_map/ppermute | solution.py:58
  (100 other events, 1115.3 us)

commit v3 on v1

v3 whole, which is shorter than its diff:
```python
from functools import partial

import jax
import jax.numpy as jnp
from jax import lax
from jax.experimental import pallas as pl
from jax.experimental.pallas import tpu as pltpu
from jax.sharding import PartitionSpec as P

HEAD_DIM = 64
EPS = 1e-06
AXES = ("dp", "tensor")
PARTS = 3
TILE = 16
FACTOR = HEAD_DIM ** (-0.5)
bf16 = jnp.bfloat16
f32 = jnp.float32


class Cube:
    def __init__(self, n_dp, n_t, rows):
        self.n_dp, self.n_t, self.rows = n_dp, n_t, rows
        self.n = n_dp * n_t
        n_bits = self.n.bit_length() - 1
        bits = list(range(n_bits))
        self.fast = (1 << n_bits) == self.n and n_t == 4 and n_bits >= 4
        self.fast = self.fast and rows % (PARTS * TILE) == 0
        spin = bits[1:4]
        self.far = bits[4:]
        self.orders = [spin[p:] + spin[:p] for p in range(PARTS)]
        self.step = rows // PARTS

    def swap(self, value, bit):
        return lax.ppermute(value, AXES, [(i, i ^ (1 << bit)) for i in range(self.n)])

    def place(self, part, index):
        out = index * 0
        for k, bit in enumerate(self.far + self.orders[part][::-1]):
            out = out | (((index >> bit) & 1) << k)
        return out

    def offsets(self):
        own = lax.axis_index("dp") * self.n_t
        return jnp.stack([self.place(p, own) for p in range(PARTS)]).astype(jnp.int32)

    def load(self, offset_ref, refs, t, out_ref):
        if not self.fast:
            out_ref[...] = refs[0][t]
            return
        for core in range(2):

            @pl.when((t & 1) == core)
            def _():
                for p in range(PARTS):
                    base = offset_ref[p] ^ self.place(p, t)
                    for d in range(self.n_dp):
                        at = base ^ self.place(p, d * self.n_t)
                        rows = pl.ds(d * self.rows + p * self.step, self.step)
                        out_ref[rows, :] = refs[core * PARTS + p][at]

    def store(self, offset_ref, refs, t, from_ref):
        if not self.fast:
            refs[0][t] = from_ref[...]
            return
        for core in range(2):

            @pl.when((t & 1) == core)
            def _():
                for p in range(PARTS):
                    base = offset_ref[p] ^ self.place(p, t)
                    for d in range(self.n_dp):
                        at = base ^ self.place(p, d * self.n_t)
                        rows = pl.ds(d * self.rows + p * self.step, self.step)
                        refs[core * PARTS + p][at] = from_ref[rows, :]

    def grad_shapes(self, cols):
        if not self.fast:
            return [jax.ShapeDtypeStruct((self.n_t, self.n_dp * self.rows, cols), bf16)]
        return [jax.ShapeDtypeStruct((self.n // 2, self.step, cols), bf16)] * (2 * PARTS)


def tie(*values):
    return lax.optimization_barrier(values)


def total(values):
    value = values[0].astype(f32)
    for more in values[1:]:
        value = value + more.astype(f32)
    return value


def gather_far(cube, piece):
    have = piece[None]
    for bit in cube.far:
        have = jnp.concatenate((have, cube.swap(have, bit)))
    return tuple(have[:, p * cube.step : (p + 1) * cube.step] for p in range(PARTS))


def gather_step(cube, held, k):
    came = [cube.swap(held[p], cube.orders[p][::-1][k]) for p in range(PARTS)]
    return tuple(jnp.concatenate((held[p], came[p])) for p in range(PARTS))


def gather_core(cube, held):
    return list(held) + [cube.swap(h, 0) for h in held]


def gather_plain(cube, piece):
    rows, cols = piece.shape
    whole = lax.all_gather(piece, AXES, axis=0, tiled=False)
    whole = whole.reshape(cube.n_dp, cube.n_t, rows, cols).transpose(1, 0, 2, 3)
    whole = whole.reshape(cube.n_t, cube.n_dp * rows, cols)
    return [jnp.take(whole, lax.axis_index("tensor") ^ jnp.arange(cube.n_t), axis=0)]


def scatter_plain(cube, part):
    n_t, n_dp, rows, cols = cube.n_t, cube.n_dp, cube.rows, part.shape[2]
    part = jnp.take(part, lax.axis_index("tensor") ^ jnp.arange(n_t), axis=0)
    part = part.reshape(n_t, n_dp, rows, cols).transpose(1, 0, 2, 3)
    part = part.reshape(n_dp * n_t * rows, cols)
    return lax.psum_scatter(part, AXES, scatter_dimension=0, tiled=True).astype(f32)


def scatter_core(cube, blocks):
    return [[blocks[p], cube.swap(blocks[p + PARTS], 0)] for p in range(PARTS)]


def scatter_sends(cube, terms):
    size = terms[0][0].shape[0] // 2
    return tuple(total([v[size : 2 * size] for v in ts]).astype(bf16) for ts in terms)


def scatter_step(cube, terms, sends, k):
    came = [cube.swap(sends[p], cube.orders[p][k]) for p in range(PARTS)]
    return [
        [v[: v.shape[0] // 2] for v in (ts if k == 0 else ts)] + [c] for ts, c in zip(terms, came)
    ]


def scatter_far(cube, terms):
    joined = [jnp.concatenate(vs, axis=1) for vs in zip(*terms)]
    for bit in cube.far[::-1]:
        size = joined[0].shape[0] // 2
        came = cube.swap(total([v[size:] for v in joined]).astype(bf16), bit)
        joined = [v[:size] for v in joined] + [came]
    return total(joined)[0]


def sum_all(cube, value):
    if not cube.fast:
        return lax.psum(value, AXES)
    for bit in [0] + cube.orders[0] + cube.far:
        value = value + cube.swap(value, bit)
    return value


def gather_images(cube, mine, length):
    if not cube.fast:
        return lax.all_gather(mine[:, :length], "tensor", axis=0, tiled=True)
    count = mine.shape[0]
    there = cube.swap(mine, 1)
    pieces = [mine, cube.swap(mine, 0), there, cube.swap(there, 0)]
    index = lax.axis_index("tensor").astype(jnp.int32).reshape(1)

    def kernel(index_ref, *refs):
        for r in range(4):
            for i in range(count):
                refs[4][(index_ref[0] ^ r) * count + i] = refs[r][i, :length, :]

    return call(
        kernel,
        jax.ShapeDtypeStruct((4 * count, length, mine.shape[2]), mine.dtype),
        index,
        pieces,
        [],
        0,
    )


def call(kernel, out_shapes, index, inputs, scratch, flops):
    moved = sum(x.size * x.dtype.itemsize for x in inputs)
    moved += sum(x.size * x.dtype.itemsize for x in jax.tree.leaves(out_shapes))
    return pl.pallas_call(
        kernel,
        out_shape=out_shapes,
        in_specs=[pl.BlockSpec(memory_space=pltpu.SMEM)]
        + [pl.BlockSpec(memory_space=pltpu.VMEM)] * len(inputs),
        out_specs=jax.tree.map(lambda _: pl.BlockSpec(memory_space=pltpu.VMEM), out_shapes),
        scratch_shapes=scratch,
        compiler_params=pltpu.CompilerParams(vmem_limit_bytes=56 * 1024 * 1024),
        cost_estimate=pl.CostEstimate(flops=flops, bytes_accessed=moved, transcendentals=0),
    )(index, *inputs)


def nn(left, right):
    return lax.dot_general(left, right, (((1,), (0,)), ((), ())), preferred_element_type=f32)


def nt(left, right):
    return lax.dot_general(left, right, (((1,), (1,)), ((), ())), preferred_element_type=f32)


def tn(left, right):
    return lax.dot_general(left, right, (((0,), (0,)), ((), ())), preferred_element_type=f32)


def normed_of(values):
    centre = values - jnp.mean(values, -1, keepdims=True)
    inverse = lax.rsqrt(jnp.mean(centre * centre, -1, keepdims=True) + EPS)
    return (centre * inverse, inverse)


def norm_back(upstream, normed, inverse, gain):
    scaled = upstream * gain
    inner = (
        scaled
        - jnp.mean(scaled, -1, keepdims=True)
        - normed * jnp.mean(scaled * normed, -1, keepdims=True)
    )
    return inverse * inner


def column_sum(values):
    return jnp.sum(values, 0, keepdims=True)


def attend_kernel(cube, count, length, width, n_w, index_ref, *refs):
    x_ref, vec_ref, bias_ref = refs[:3]
    w_refs = refs[3 : 3 + n_w]
    n1_ref, qkv_ref, att_ref, hidden_ref, n2_ref, w_ref, sum_ref = refs[3 + n_w :]
    x = x_ref[...].astype(f32)
    normed, _ = normed_of(x)
    n1_ref[...] = (normed * vec_ref[0:1] + vec_ref[1:2]).astype(bf16)
    sum_ref[...] = x + vec_ref[2:3]
    tokens = x.shape[0] // count
    heads = width // HEAD_DIM
    keep = lax.broadcasted_iota(jnp.int32, (tokens, tokens), 1) < length

    def step(t, carry):
        cube.load(index_ref, w_refs, t, w_ref)
        qkv = nn(n1_ref[...], w_ref[:, : 3 * width]) + bias_ref[t]
        qkv_ref[t] = qkv.astype(bf16)
        for b in range(count):
            rows = slice(b * tokens, (b + 1) * tokens)
            found = []
            for h in range(heads):
                q = qkv_ref[t, rows, h * HEAD_DIM : (h + 1) * HEAD_DIM]
                k = qkv_ref[t, rows, width + h * HEAD_DIM : width + (h + 1) * HEAD_DIM]
                v = qkv_ref[t, rows, 2 * width + h * HEAD_DIM : 2 * width + (h + 1) * HEAD_DIM]
                scores = jnp.where(keep, nt(q, k) * FACTOR, -1e30)
                weights = jnp.exp(scores - jnp.max(scores, -1, keepdims=True))
                probs = weights * (1.0 / jnp.sum(weights, -1, keepdims=True))
                found.append(nn(probs.astype(bf16), v).astype(bf16))
            att_ref[t, rows, :] = jnp.concatenate(found, axis=1)
        sum_ref[...] += nt(att_ref[t], w_ref[:, 3 * width :])
        return carry

    lax.fori_loop(0, cube.n_t, step, 0)
    hidden = sum_ref[...]
    hidden_ref[...] = hidden
    normed, _ = normed_of(hidden)
    n2_ref[...] = (normed * vec_ref[3:4] + vec_ref[4:5]).astype(bf16)


def mlp_kernel(cube, width, n_w, index_ref, *refs):
    n2_ref, cot_ref, hidden_ref, vec_ref, bias_ref = refs[:5]
    w_refs = refs[5 : 5 + n_w]
    enc_ref, dhidden_ref, small_ref = refs[5 + n_w : 8 + n_w]
    g_refs = refs[8 + n_w : 8 + 2 * n_w]
    w_ref, grad_ref, mlp_ref, dnorm_ref = refs[8 + 2 * n_w :]
    mlp_ref[...] = hidden_ref[...] + vec_ref[5:6]
    dnorm_ref[...] = jnp.zeros_like(dnorm_ref)

    def step(t, carry):
        cube.load(index_ref, w_refs, t, w_ref)
        pre = nn(n2_ref[...], w_ref[:, :width]) + bias_ref[t]
        cdf = 0.5 * (1.0 + lax.erf(pre * (0.5**0.5)))
        slope = cdf + pre * (jnp.exp(-0.5 * pre * pre) * 0.3989422804014327)
        act = (pre * cdf).astype(bf16)
        mlp_ref[...] += nt(act, w_ref[:, width:])
        dpre = (slope * nn(cot_ref[...], w_ref[:, width:])).astype(bf16)
        small_ref[pl.ds(t, 1)] = column_sum(dpre.astype(f32))[None]
        dnorm_ref[...] += nt(dpre, w_ref[:, :width])
        grad_ref[:, :width] = tn(n2_ref[...], dpre).astype(bf16)
        grad_ref[:, width:] = tn(cot_ref[...], act).astype(bf16)
        cube.store(index_ref, g_refs, t, grad_ref)
        return carry

    lax.fori_loop(0, cube.n_t, step, 0)
    enc_ref[...] = mlp_ref[...].astype(bf16)
    normed, inverse = normed_of(hidden_ref[...])
    dnorm = dnorm_ref[...]
    cot = cot_ref[...].astype(f32)
    dhidden = cot + norm_back(dnorm, normed, inverse, vec_ref[3:4])
    dhidden_ref[...] = dhidden
    small_ref[cube.n_t] = column_sum(dnorm * normed)
    small_ref[cube.n_t + 1] = column_sum(dnorm)
    small_ref[cube.n_t + 2] = column_sum(cot)
    small_ref[cube.n_t + 3] = column_sum(dhidden)


def attend_back_kernel(cube, count, length, width, n_w, index_ref, *refs):
    x_ref, n1_ref, qkv_ref, att_ref, dhidden_ref, vec_ref = refs[:6]
    w_refs = refs[6 : 6 + n_w]
    patch_ref, small_ref, dbias_ref = refs[6 + n_w : 9 + n_w]
    g_refs = refs[9 + n_w : 9 + 2 * n_w]
    w_ref, grad_ref, dnorm_ref, low_ref, dqkv_ref = refs[9 + 2 * n_w :]
    low_ref[...] = dhidden_ref[...].astype(bf16)
    dnorm_ref[...] = jnp.zeros_like(dnorm_ref)
    tokens = x_ref.shape[0] // count
    heads = width // HEAD_DIM
    keep = lax.broadcasted_iota(jnp.int32, (tokens, tokens), 0) < length

    def step(t, carry):
        cube.load(index_ref, w_refs, t, w_ref)
        datt = nn(low_ref[...], w_ref[:, 3 * width :]).astype(bf16)
        grad_ref[:, 3 * width :] = tn(low_ref[...], att_ref[t]).astype(bf16)
        for b in range(count):
            rows = slice(b * tokens, (b + 1) * tokens)
            dqs, dks, dvs = [], [], []
            for h in range(heads):
                q = qkv_ref[t, rows, h * HEAD_DIM : (h + 1) * HEAD_DIM]
                k = qkv_ref[t, rows, width + h * HEAD_DIM : width + (h + 1) * HEAD_DIM]
                v = qkv_ref[t, rows, 2 * width + h * HEAD_DIM : 2 * width + (h + 1) * HEAD_DIM]
                do = datt[rows, h * HEAD_DIM : (h + 1) * HEAD_DIM]
                scores = jnp.where(keep, nt(k, q) * FACTOR, -1e30)
                weights = jnp.exp(scores - jnp.max(scores, 0, keepdims=True))
                probs = weights * (1.0 / jnp.sum(weights, 0, keepdims=True))
                dvs.append(nn(probs.astype(bf16), do))
                dprobs = nt(v, do)
                inner = jnp.sum(dprobs * probs, 0, keepdims=True)
                dscores = (probs * (dprobs - inner)).astype(bf16)
                dks.append(nn(dscores, q) * FACTOR)
                dqs.append(tn(dscores, k) * FACTOR)
            dqkv_ref[rows, :] = jnp.concatenate(dqs + dks + dvs, axis=1).astype(bf16)
        dqkv = dqkv_ref[...]
        dbias_ref[pl.ds(t, 1)] = column_sum(dqkv.astype(f32))[None]
        dnorm_ref[...] += nt(dqkv, w_ref[:, : 3 * width])
        grad_ref[:, : 3 * width] = tn(n1_ref[...], dqkv).astype(bf16)
        cube.store(index_ref, g_refs, t, grad_ref)
        return carry

    lax.fori_loop(0, cube.n_t, step, 0)
    normed, inverse = normed_of(x_ref[...].astype(f32))
    dnorm = dnorm_ref[...]
    patch = dhidden_ref[...] + norm_back(dnorm, normed, inverse, vec_ref[0:1])
    patch_ref[...] = patch.astype(bf16)
    small_ref[0] = column_sum(dnorm * normed)
    small_ref[1] = column_sum(dnorm)


def on_device(
    n_dp,
    n_t,
    patches,
    attn_gain,
    attn_shift,
    qkv_weight,
    qv_bias,
    out_weight,
    out_bias,
    mlp_gain,
    mlp_shift,
    fc1_weight,
    fc1_bias,
    fc2_weight,
    fc2_bias,
    cotangent,
):
    t_me = lax.axis_index("tensor")
    cube = Cube(n_dp, n_t, qkv_weight.shape[1])
    order = t_me ^ jnp.arange(n_t)
    width = qkv_weight.shape[2]
    f_width = fc1_weight.shape[1]
    d = patches.shape[2]
    attn_piece = jnp.concatenate(
        (qkv_weight[0], qkv_weight[1], qkv_weight[2], out_weight.T), axis=1
    )
    mlp_piece = jnp.concatenate((fc1_weight, fc2_weight.T), axis=1)
    index = cube.offsets()
    biases = jnp.concatenate((qv_bias.reshape(-1), fc1_bias))[None]
    if cube.fast:
        held = gather_far(cube, attn_piece)
        held_mlp = gather_far(cube, mlp_piece)
        biases = jnp.concatenate((biases, cube.swap(biases, 0)))
        biases = jnp.concatenate((biases, cube.swap(biases, 1)))
        held = gather_step(cube, held, 0)
        held, held_mlp = tie(held, held_mlp)
        held = gather_step(cube, held, 1)
        held_mlp = gather_step(cube, held_mlp, 0)
        held, held_mlp = tie(held, held_mlp)
        held = gather_step(cube, held, 2)
        held_mlp = gather_step(cube, held_mlp, 1)
        w_attn = gather_core(cube, held)
        w_attn, held_mlp = tie(tuple(w_attn), held_mlp)
        held_mlp = gather_step(cube, held_mlp, 2)
        w_mlp = gather_core(cube, held_mlp)
    else:
        w_attn = gather_plain(cube, attn_piece)
        w_mlp = gather_plain(cube, mlp_piece)
        biases = jnp.take(lax.all_gather(biases[0], "tensor", axis=0, tiled=False), order, axis=0)
    n_w = len(w_attn)
    biases = biases.astype(f32)
    qkv_bias = jnp.concatenate(
        (biases[:, :width], jnp.zeros((n_t, width), f32), biases[:, width : 2 * width]), axis=1
    )[:, None]
    f_bias = biases[:, None, 2 * width :]
    vecs = jnp.stack((attn_gain, attn_shift, out_bias, mlp_gain, mlp_shift, fc2_bias)).astype(f32)

    count = patches.shape[0] // n_t
    length = patches.shape[1]
    padded = -(-length // TILE) * TILE
    tokens = count * padded

    def own_images(values):
        mine = lax.dynamic_slice_in_dim(values, t_me * count, count, 0)
        return jnp.pad(mine, ((0, 0), (0, padded - length), (0, 0))).reshape(tokens, d)

    x = own_images(patches)
    cot = own_images(cotangent)
    spots = 2 * tokens * d * n_t
    attn_macs = spots * 4 * width // 2 + 4 * count * n_t * padded * padded * width

    def shape(*dims, dtype=bf16):
        return jax.ShapeDtypeStruct(dims, dtype)

    n1, qkv, att, hidden, n2 = call(
        partial(attend_kernel, cube, count, length, width, n_w),
        [
            shape(tokens, d),
            shape(n_t, tokens, 3 * width),
            shape(n_t, tokens, width),
            shape(tokens, d, dtype=f32),
            shape(tokens, d),
        ],
        index,
        [x, vecs, qkv_bias, *w_attn],
        [pltpu.VMEM((d, 4 * width), bf16), pltpu.VMEM((tokens, d), f32)],
        2 * attn_macs,
    )
    enc, dhidden, mlp_small, *mlp_grads = call(
        partial(mlp_kernel, cube, f_width, n_w),
        [
            shape(tokens, d),
            shape(tokens, d, dtype=f32),
            shape(n_t + 4, 1, d, dtype=f32),
            *cube.grad_shapes(2 * f_width),
        ],
        index,
        [n2, cot, hidden, vecs, f_bias, *w_mlp],
        [pltpu.VMEM((d, 2 * f_width), bf16)] * 2 + [pltpu.VMEM((tokens, d), f32)] * 2,
        6 * spots * f_width,
    )
    if cube.fast:
        mlp_terms = scatter_core(cube, mlp_grads)
        sends = scatter_sends(cube, mlp_terms)
        sends, dhidden, att = tie(sends, dhidden, att)
        mlp_terms = scatter_step(cube, mlp_terms, sends, 0)
    patch, attn_small, dbias, *attn_grads = call(
        partial(attend_back_kernel, cube, count, length, width, n_w),
        [
            shape(tokens, d),
            shape(2, 1, d, dtype=f32),
            shape(n_t, 1, 3 * width, dtype=f32),
            *cube.grad_shapes(4 * width),
        ],
        index,
        [x, n1, qkv, att, dhidden, vecs, *w_attn],
        [
            pltpu.VMEM((d, 4 * width), bf16),
            pltpu.VMEM((d, 4 * width), bf16),
            pltpu.VMEM((tokens, d), f32),
            pltpu.VMEM((tokens, d), bf16),
            pltpu.VMEM((tokens, 3 * width), bf16),
        ],
        4 * attn_macs,
    )
    encoded = gather_images(cube, enc.reshape(count, padded, d), length)
    patch_grad = gather_images(cube, patch.reshape(count, padded, d), length)
    if cube.fast:
        attn_terms = scatter_core(cube, attn_grads)
        for k in range(3):
            sends = scatter_sends(cube, attn_terms)
            attn_terms = scatter_step(cube, attn_terms, sends, k)
            if k > 0:
                sends = scatter_sends(cube, mlp_terms)
                mlp_terms = scatter_step(cube, mlp_terms, sends, k)
        mlp_grad = scatter_far(cube, mlp_terms)
        attn_grad = scatter_far(cube, attn_terms)
    else:
        mlp_grad = scatter_plain(cube, mlp_grads[0])
        attn_grad = scatter_plain(cube, attn_grads[0])
    dbias = jnp.take(dbias[:, 0], order, axis=0)
    f_sums = jnp.take(mlp_small[:n_t, 0], order, axis=0)
    small = jnp.concatenate(
        (
            attn_small.reshape(-1),
            mlp_small[n_t:].reshape(-1),
            dbias[:, :width].reshape(-1),
            dbias[:, 2 * width :].reshape(-1),
            f_sums.reshape(-1),
        )
    )
    small = sum_all(cube, small)
    cuts = [small[i * d : (i + 1) * d] for i in range(6)]
    at = 6 * d
    q_sum = lax.dynamic_slice_in_dim(small[at : at + n_t * width], t_me * width, width, 0)
    at += n_t * width
    v_sum = lax.dynamic_slice_in_dim(small[at : at + n_t * width], t_me * width, width, 0)
    at += n_t * width
    f_sum = lax.dynamic_slice_in_dim(small[at:], t_me * f_width, f_width, 0)
    return (
        encoded,
        patch_grad,
        cuts[0],
        cuts[1],
        jnp.stack([attn_grad[:, i * width : (i + 1) * width] for i in range(3)]),
        jnp.stack((q_sum, v_sum)),
        attn_grad[:, 3 * width :].T,
        cuts[5],
        cuts[2],
        cuts[3],
        mlp_grad[:, :f_width],
        f_sum,
        mlp_grad[:, f_width:].T,
        cuts[4],
    )


def solution(mesh):
    return jax.shard_map(
        partial(on_device, mesh.shape["dp"], mesh.shape["tensor"]),
        mesh=mesh,
        in_specs=(
            P("dp", None, None),
            P(),
            P(),
            P(None, "dp", "tensor"),
            P(None, "tensor"),
            P("tensor", "dp"),
            P(),
            P(),
            P(),
            P("dp", "tensor"),
            P("tensor"),
            P("tensor", "dp"),
            P(),
            P("dp", None, None),
        ),
        out_specs=(
            P("dp", None, None),
            P("dp", None, None),
            P(),
            P(),
            P(None, "dp", "tensor"),
            P(None, "tensor"),
            P("tensor", "dp"),
            P(),
            P(),
            P(),
            P("dp", "tensor"),
            P("tensor"),
            P("tensor", "dp"),
            P(),
        ),
        check_vma=False,
    )
```

time: 658 us -> 310 us (0.47)
  waiting for transfers between devices: 436 us -> 114 us
  matrix products: 69.7 us -> 0 us
  Pallas kernels: 0 us -> 68.9 us
  starting transfers between devices: 0.58 us -> 62.4 us
  blocking collectives: 46.2 us -> 0 us
  local copies, waits for them, and re-layouts: 59.2 us -> 34.3 us
  between operations: 15.2 us -> 1.87 us
    reduce_scatter x3 -> x0, waiting for transfers between devices: 264 us -> none  [scatter_grad(): lax.psum_scatter(part, AXES, scatter_dimension=0, tiled=True).astype(f32)]
    all_gather x5 -> x0, waiting for transfers between devices: 171 us -> none  [the longest x3 171 us: gather_weight(): whole = lax.all_gather(piece, AXES, axis=0, tiled=False)]
    ppermute x0 -> x65, waiting for transfers between devices: none -> 114 us  [swap(): return lax.ppermute(value, AXES, [(i, i ^ 1 << bit) for i in range(self.n)])]
    dot_general x18 -> x0, matrix products: 69.7 us -> none  [dot(): return jnp.einsum(spec, left, right, preferred_element_type=f32)]
    pallas_call x0 -> x5, Pallas kernels: none -> 68.9 us  [call(): pl.pallas_call(kernel, out_shape=out_shapes, in_specs=[pl.BlockSpec(memor...]
    ppermute x0 -> x65, starting transfers between devices: none -> 62.4 us  [swap(): return lax.ppermute(value, AXES, [(i, i ^ 1 << bit) for i in range(self.n)])]
    psum x1 -> x0, blocking collectives: 40 us -> none  [on_device(): small = lax.psum(small, AXES)]
    reshape x9 -> x4, local copies, waits for them, and re-layouts: 15.9 us -> 0.26 us  [the longest x1 0.09 us: on_device(): biases = jnp.concatenate((qv_bias.reshape(-1), fc1_bias))[None]]
  transfers between devices with their start and end apart: 8 -> 65, of which waited for: 6 -> 26; matrix products, arithmetic and copies ran while one was open for 16% -> 18% of each run, Pallas kernels for 0% -> 14%
where the time goes in v3:
time: 310 us; the launch traced here: 309 us
  waiting for transfers between devices  114 us (37%)
  Pallas kernels  68.9 us (22%)
  starting transfers between devices  62.4 us (20%)
  local copies, waits for them, and re-layouts  34.3 us (11%)
  other arithmetic  27.6 us (9%)
    ppermute x65, waiting for transfers between devices, swap(): return lax.ppermute(value, AXES, [(i, i ^ 1 << bit) for i in range(self.n)])  114 us
    pallas_call x5, Pallas kernels, call(): pl.pallas_call(kernel, out_shape=out_shapes, in_specs=[pl.BlockSpec(memor...  68.9 us
    ppermute x65, starting transfers between devices, swap(): return lax.ppermute(value, AXES, [(i, i ^ 1 << bit) for i in range(self.n)])  62.4 us
    convert_element_type x18, other arithmetic, scatter_sends(): total([v[size:2 * size] for v in ts]).astype(bf16)  19.9 us
    unnamed x104, local copies, waits for them, and re-layouts  14.2 us
  transfers between devices with their start and end apart: 65, of which 26 were waited for; matrix products, arithmetic and copies ran while one was open for 18% of the time, Pallas kernels for 14%

profile of v3, /device:TPU:0, one launch (start us, length us, event | category | flops | bytes accessed | tf_op | source)
XLA Modules:
  0.0 308.7 jit_solution(14489099094818773239)
XLA Ops:
  2.5 4.1 %collective-permute-start.2 = (bf16[1,96,768]{2,1,0:T(8,128)(2,1)S(1)}, bf16[1,96,768]{2,1,0:T(8,128)(2,1)S(1)}, u32[]{:S(2)}, u32[]{:S(2)}) collective-permute-start(bf16[1,96,768]{2,1,0:T(8,128)(2,1)S(1)} %maximum_bitcast_fusion.1), channel_id=1, source_target_pairs={{0,16},{1,17},{2,18},{3,19},{4,20},{5,21},{6,22},{7,23},{8,24},{9,... | collective-permute-start | bytes 442376 | tf_op jit(solution)/shard_map/ppermute | solution.py:34
  6.6 7.0 %collective-permute-done.2 = bf16[1,96,768]{2,1,0:T(8,128)(2,1)S(1)} collective-permute-done((bf16[1,96,768]{2,1,0:T(8,128)(2,1)S(1)}, bf16[1,96,768]{2,1,0:T(8,128)(2,1)S(1)}, u32[]{:S(2)}, u32[]{:S(2)}) %collective-permute-start.2) | collective-permute-done | bytes 147488 | tf_op jit(solution)/shard_map/ppermute | solution.py:34
  17.9 4.0 %collective-permute-start.3 = (bf16[2,32,768]{2,1,0:T(8,128)(2,1)S(1)}, bf16[2,32,768]{2,1,0:T(8,128)(2,1)S(1)}, u32[]{:S(2)}, u32[]{:S(2)}) collective-permute-start(bf16[2,32,768]{2,1,0:T(8,128)(2,1)S(1)} %get-tuple-element.136), channel_id=1, source_target_pairs={{0,8},{1,9},{2,10},{3,11},{4,12},{5,13},{6,14},{7,15},{8,0},{9,1},... | collective-permute-start | bytes 294920 | tf_op jit(solution)/shard_map/ppermute | solution.py:34
  24.5 6.7 %collective-permute-done.6 = bf16[1,96,1536]{2,1,0:T(8,128)(2,1)S(1)} collective-permute-done((bf16[1,96,1536]{2,1,0:T(8,128)(2,1)S(1)}, bf16[1,96,1536]{2,1,0:T(8,128)(2,1)S(1)}, u32[]{:S(2)}, u32[]{:S(2)}) %collective-permute-start.6) | collective-permute-done | bytes 294944 | tf_op jit(solution)/shard_map/ppermute | solution.py:34
  41.1 2.8 collective-permute-done.7
  49.8 6.3 %collective-permute-done.15 = bf16[8,32,768]{2,1,0:T(8,128)(2,1)S(1)} collective-permute-done((bf16[8,32,768]{2,1,0:T(8,128)(2,1)S(1)}, bf16[8,32,768]{2,1,0:T(8,128)(2,1)S(1)}, u32[]{:S(2)}, u32[]{:S(2)}) %collective-permute-start.15) | collective-permute-done | bytes 393248 | tf_op jit(solution)/shard_map/ppermute | solution.py:34
  62.9 6.5 %collective-permute-done.19 = bf16[4,32,1536]{2,1,0:T(8,128)(2,1)S(1)} collective-permute-done((bf16[4,32,1536]{2,1,0:T(8,128)(2,1)S(1)}, bf16[4,32,1536]{2,1,0:T(8,128)(2,1)S(1)}, u32[]{:S(2)}, u32[]{:S(2)}) %collective-permute-start.19) | collective-permute-done | bytes 393248 | tf_op jit(solution)/shard_map/ppermute | solution.py:34
  74.5 11.7 %collective-permute-done.24 = bf16[8,32,1536]{2,1,0:T(8,128)(2,1)S(1)} collective-permute-done((bf16[8,32,1536]{2,1,0:T(8,128)(2,1)S(1)}, bf16[8,32,1536]{2,1,0:T(8,128)(2,1)S(1)}, u32[]{:S(2)}, u32[]{:S(2)}) %collective-permute-start.24) | collective-permute-done | bytes 786464 | tf_op jit(solution)/shard_map/ppermute | solution.py:34
  89.5 3.7 %constant_dynamic-slice_fusion = (bf16[2,197,768]{2,0,1:T(2,128)(2,1)S(1)}, bf16[2,197,768]{2,0,1:T(2,128)(2,1)S(1)}) fusion(bf16[8,197,768]{2,0,1:T(8,128)(2,1)} %param.27, s32[]{:T(128)S(6)} %select_n.41, bf16[8,197,768]{2,0,1:T(8,128)(2,1)} %param.14), kind=kLoop, calls=%fused_computation.111 | loop fusion | bytes 2420740 | tf_op jit(solution)/shard_map/dynamic_slice | solution.py:417
  100.8 14.6 %shard_map.245 = (bf16[416,768]{1,0:T(8,128)(2,1)}, bf16[4,416,576]{2,1,0:T(8,128)(2,1)}, bf16[4,416,192]{2,1,0:T(8,128)(2,1)}, f32[416,768]{1,0:T(8,128)}, bf16[416,768]{1,0:T(8,128)(2,1)}) custom-call(s32[3]{0:T(128)} %pad_add_fusion.index_ref, bf16[416,768]{1,0:T(8,128)(2,1)} %bitcast.49, f32[6,768]{1,0:T(8,128)} %convert_element_type.297.refs_1_.refs_3_.refs_5_, ...), custom_call_target="tpu_custom_call" | custom-call | flops 2494562304 | bytes 10497024 | tf_op jit(solution)/shard_map/pallas_call | solution.py:184
  115.4 24.2 %shard_map.246 = (bf16[416,768]{1,0:T(8,128)(2,1)}, f32[416,768]{1,0:T(8,128)}, f32[8,1,768]{2,1,0:T(1,128)}, bf16[16,32,1536]{2,1,0:T(8,128)(2,1)}, bf16[16,32,...) custom-call(s32[3]{0:T(128)} %pad_add_fusion.index_ref, ...), custom_call_target="tpu_custom_call" | custom-call | flops 11777605632 | bytes 23402496 | tf_op jit(solution)/shard_map/pallas_call | solution.py:184
  142.9 13.9 %collective-permute-done.29.refs_2_ = bf16[2,208,768]{2,1,0:T(8,128)(2,1)S(1)} collective-permute-done((bf16[2,208,768]{2,1,0:T(8,128)(2,1)}, bf16[2,208,768]{2,1,0:T(8,128)(2,1)S(1)}, u32[]{:S(2)}, u32[]{:S(2)}) %collective-permute-start.29) | collective-permute-done | bytes 639008 | tf_op jit(solution)/shard_map/ppermute | solution.py:34
  164.8 23.5 %shard_map.248 = (bf16[416,768]{1,0:T(8,128)(2,1)}, f32[2,1,768]{2,1,0:T(1,128)}, f32[4,1,576]{2,1,0:T(1,128)}, bf16[16,32,768]{2,1,0:T(8,128)(2,1)}, bf16[16,32...) custom-call(s32[3]{0:T(128)} %pad_add_fusion.index_ref, ...), custom_call_target="tpu_custom_call" | custom-call | flops 4989124608 | bytes 15221760 | tf_op jit(solution)/shard_map/pallas_call | solution.py:184
  196.5 3.3 %shard_map.247 = bf16[8,197,768]{2,1,0:T(8,128)(2,1)} custom-call(s32[1]{0:T(128)} %bitcast.index_ref, bf16[2,208,768]{2,1,0:T(8,128)(2,1)} %bitcast.57, bf16[2,208,768]{2,1,0:T(8,128)(2,1)} %collective-permute-done.28.refs_1_, bf16[2,208,768]{2,1,0:T(8,128)(2,1)} %copy-done.17, bf16[2,208,768]{2,1,0:T(8,128)(2,1)} %collective-permute-done.30.refs_3_), custom_call_target="tpu_custom_call" | custom-call | bytes 4976640 | tf_op jit(solution)/shard_map/pallas_call | solution.py:184
  199.8 3.7 %copy.32 = bf16[8,197,768]{2,0,1:T(8,128)(2,1)} copy(bf16[8,197,768]{2,1,0:T(8,128)(2,1)} %shard_map.247) | data formatting | bytes 4841472
  209.5 5.7 %collective-permute-done.40 = f32[9216]{0:T(1024)S(1)} collective-permute-done((f32[9216]{0:T(1024)S(1)}, f32[9216]{0:T(1024)S(1)}, u32[]{:S(2)}, u32[]{:S(2)}) %collective-permute-start.40) | collective-permute-done | bytes 36896 | tf_op jit(solution)/shard_map/ppermute | solution.py:34
  215.2 2.9 collective-permute-start.41
  231.1 10.0 %collective-permute-done.35.refs_2_ = bf16[2,208,768]{2,1,0:T(8,128)(2,1)S(1)} collective-permute-done((bf16[2,208,768]{2,1,0:T(8,128)(2,1)S(1)}, bf16[2,208,768]{2,1,0:T(8,128)(2,1)S(1)}, u32[]{:S(2)}, u32[]{:S(2)}) %collective-permute-start.35) | collective-permute-done | bytes 639008 | tf_op jit(solution)/shard_map/ppermute | solution.py:34
  241.8 7.1 %collective-permute-done.60 = bf16[4,32,1536]{2,1,0:T(8,128)(2,1)S(1)} collective-permute-done((bf16[4,32,1536]{2,1,0:T(8,128)(2,1)S(1)}, bf16[4,32,1536]{2,1,0:T(8,128)(2,1)S(1)}, u32[]{:S(2)}, u32[]{:S(2)}) %collective-permute-start.60) | collective-permute-done | bytes 393248 | tf_op jit(solution)/shard_map/ppermute | solution.py:34
  252.8 6.5 %collective-permute-done.47 = bf16[8,32,768]{2,1,0:T(8,128)(2,1)S(1)} collective-permute-done((bf16[8,32,768]{2,1,0:T(8,128)(2,1)S(1)}, bf16[8,32,768]{2,1,0:T(8,128)(2,1)S(1)}, u32[]{:S(2)}, u32[]{:S(2)}) %collective-permute-start.47) | collective-permute-done | bytes 393248 | tf_op jit(solution)/shard_map/ppermute | solution.py:34
  268.2 3.2 %shard_map.249 = bf16[8,197,768]{2,1,0:T(8,128)(2,1)} custom-call(s32[1]{0:T(128)} %bitcast.index_ref, bf16[2,208,768]{2,1,0:T(8,128)(2,1)} %bitcast.52, bf16[2,208,768]{2,1,0:T(8,128)(2,1)} %copy-done.19, bf16[2,208,768]{2,1,0:T(8,128)(2,1)} %copy-done.18, bf16[2,208,768]{2,1,0:T(8,128)(2,1)} %copy-done.20), custom_call_target="tpu_custom_call" | custom-call | bytes 4976640 | tf_op jit(solution)/shard_map/pallas_call | solution.py:184
  271.5 3.6 %copy.33 = bf16[8,197,768]{2,0,1:T(8,128)(2,1)} copy(bf16[8,197,768]{2,1,0:T(8,128)(2,1)} %shard_map.249) | data formatting | bytes 4841472
  286.4 3.3 %collective-permute-done.51 = bf16[2,32,768]{2,1,0:T(8,128)(2,1)S(1)} collective-permute-done((bf16[2,32,768]{2,1,0:T(8,128)(2,1)S(1)}, bf16[2,32,768]{2,1,0:T(8,128)(2,1)S(1)}, u32[]{:S(2)}, u32[]{:S(2)}) %collective-permute-start.51) | collective-permute-done | bytes 98336 | tf_op jit(solution)/shard_map/ppermute | solution.py:34
  293.7 8.6 %collective-permute-done.54 = bf16[1,96,768]{2,1,0:T(8,128)(2,1)S(1)} collective-permute-done((bf16[1,96,768]{2,1,0:T(8,128)(2,1)S(1)}, bf16[1,96,768]{2,1,0:T(8,128)(2,1)S(1)}, u32[]{:S(2)}, u32[]{:S(2)}) %collective-permute-start.54) | collective-permute-done | bytes 147488 | tf_op jit(solution)/shard_map/ppermute | solution.py:34
  (350 shorter events, 119.9 us)
Async XLA Ops:
  69.6 16.6 %collective-permute-start.24 = (bf16[8,32,1536]{2,1,0:T(8,128)(2,1)S(1)}, bf16[8,32,1536]{2,1,0:T(8,128)(2,1)S(1)}, u32[]{:S(2)}, u32[]{:S(2)}) collective-permute-start(bf16[8,32,1536]{2,1,0:T(8,128)(2,1)S(1)} %pad_maximum_fusion.2), channel_id=1, source_target_pairs={{0,8},{1,9},{2,10},{3,11},{4,12},{5,13},{6,14},{7,15},{8,0},{9,1},... | collective-permute-start | bytes 2359304 | tf_op jit(solution)/shard_map/ppermute | solution.py:34
  70.9 16.2 %collective-permute-start.23 = (bf16[8,32,1536]{2,1,0:T(8,128)(2,1)S(1)}, bf16[8,32,1536]{2,1,0:T(8,128)(2,1)S(1)}, u32[]{:S(2)}, u32[]{:S(2)}) collective-permute-start(bf16[8,32,1536]{2,1,0:T(8,128)(2,1)S(1)} %pad_maximum_fusion.1), channel_id=1, source_target_pairs={{0,4},{1,5},{2,6},{3,7},{4,0},{5,1},{6,2},{7,3},{8,12},{9,13},{10,... | collective-permute-start | bytes 2359304 | tf_op jit(solution)/shard_map/ppermute | solution.py:34
  87.2 28.3 %collective-permute-start.27 = (bf16[16,32,1536]{2,1,0:T(8,128)(2,1)}, bf16[16,32,1536]{2,1,0:T(8,128)(2,1)}, u32[]{:S(2)}, u32[]{:S(2)}) collective-permute-start(bf16[16,32,1536]{2,1,0:T(8,128)(2,1)} %constant_dynamic-update-slice_fusion.10.refs_7_), channel_id=1, source_target_pairs={{0,1},{1,0},{2,3},{3,2},{4,5},{5,4},{6,7},{7,6},{8,9},{9,8},{10,11... | collective-permute-start | bytes 4718600 | tf_op jit(solution)/shard_map/ppermute | solution.py:34
  88.1 27.3 %collective-permute-start.26 = (bf16[16,32,1536]{2,1,0:T(8,128)(2,1)}, bf16[16,32,1536]{2,1,0:T(8,128)(2,1)}, u32[]{:S(2)}, u32[]{:S(2)}) collective-permute-start(bf16[16,32,1536]{2,1,0:T(8,128)(2,1)} %constant_dynamic-update-slice_fusion.8.refs_6_), channel_id=1, source_target_pairs={{0,1},{1,0},{2,3},{3,2},{4,5},{5,4},{6,7},{7,6},{8,9},{9,8},{10,11... | collective-permute-start | bytes 4718600 | tf_op jit(solution)/shard_map/ppermute | solution.py:34
  88.7 26.7 %collective-permute-start.25 = (bf16[16,32,1536]{2,1,0:T(8,128)(2,1)S(1)}, bf16[16,32,1536]{2,1,0:T(8,128)(2,1)}, u32[]{:S(2)}, u32[]{:S(2)}) collective-permute-start(bf16[16,32,1536]{2,1,0:T(8,128)(2,1)S(1)} %constant_dynamic-update-slice_fusion.6.refs_5_), channel_id=1, source_target_pairs={{0,1},{1,0},{2,3},{3,2},{4,5},{5,4},{6,7},{7,6},{8,9},{9,8},{10,11... | collective-permute-start | bytes 4718600 | tf_op jit(solution)/shard_map/ppermute | solution.py:34
  139.7 17.2 %collective-permute-start.33 = (bf16[16,32,1536]{2,1,0:T(8,128)(2,1)}, bf16[16,32,1536]{2,1,0:T(8,128)(2,1)S(1)}, u32[]{:S(2)}, u32[]{:S(2)}) collective-permute-start(bf16[16,32,1536]{2,1,0:T(8,128)(2,1)} %get-tuple-element.94), channel_id=1, source_target_pairs={{0,1},{1,0},{2,3},{3,2},{4,5},{5,4},{6,7},{7,6},{8,9},{9,8},{10,11... | collective-permute-start | bytes 4718600 | tf_op jit(solution)/shard_map/ppermute | solution.py:34
  139.8 20.4 %collective-permute-start.32 = (bf16[16,32,1536]{2,1,0:T(8,128)(2,1)}, bf16[16,32,1536]{2,1,0:T(8,128)(2,1)}, u32[]{:S(2)}, u32[]{:S(2)}) collective-permute-start(bf16[16,32,1536]{2,1,0:T(8,128)(2,1)} %get-tuple-element.92), channel_id=1, source_target_pairs={{0,1},{1,0},{2,3},{3,2},{4,5},{5,4},{6,7},{7,6},{8,9},{9,8},{10,11... | collective-permute-start | bytes 4718600 | tf_op jit(solution)/shard_map/ppermute | solution.py:34
  140.2 16.6 %collective-permute-start.29 = (bf16[2,208,768]{2,1,0:T(8,128)(2,1)}, bf16[2,208,768]{2,1,0:T(8,128)(2,1)S(1)}, u32[]{:S(2)}, u32[]{:S(2)}) collective-permute-start(bf16[2,208,768]{2,1,0:T(8,128)(2,1)} %bitcast.55), channel_id=1, source_target_pairs={{0,2},{1,3},{2,0},{3,1},{4,6},{5,7},{6,4},{7,5},{8,10},{9,11},{10,... | collective-permute-start | bytes 1916936 | tf_op jit(solution)/shard_map/ppermute | solution.py:34
  141.0 21.6 %collective-permute-start.31 = (bf16[16,32,1536]{2,1,0:T(8,128)(2,1)}, bf16[16,32,1536]{2,1,0:T(8,128)(2,1)}, u32[]{:S(2)}, u32[]{:S(2)}) collective-permute-start(bf16[16,32,1536]{2,1,0:T(8,128)(2,1)} %get-tuple-element.90), channel_id=1, source_target_pairs={{0,1},{1,0},{2,3},{3,2},{4,5},{5,4},{6,7},{7,6},{8,9},{9,8},{10,11... | collective-permute-start | bytes 4718600 | tf_op jit(solution)/shard_map/ppermute | solution.py:34
  141.0 55.5 %collective-permute-start.28 = (bf16[2,208,768]{2,1,0:T(8,128)(2,1)}, bf16[2,208,768]{2,1,0:T(8,128)(2,1)}, u32[]{:S(2)}, u32[]{:S(2)}) collective-permute-start(bf16[2,208,768]{2,1,0:T(8,128)(2,1)} %bitcast.56), channel_id=1, source_target_pairs={{0,1},{1,0},{2,3},{3,2},{4,5},{5,4},{6,7},{7,6},{8,9},{9,8},{10,11... | collective-permute-start | bytes 1916936 | tf_op jit(solution)/shard_map/ppermute | solution.py:34
  156.8 39.6 %collective-permute-start.30 = (bf16[2,208,768]{2,1,0:T(8,128)(2,1)S(1)}, bf16[2,208,768]{2,1,0:T(8,128)(2,1)}, u32[]{:S(2)}, u32[]{:S(2)}) collective-permute-start(bf16[2,208,768]{2,1,0:T(8,128)(2,1)S(1)} %collective-permute-done.29.refs_2_), channel_id=1, source_target_pairs={{0,1},{1,0},{2,3},{3,2},{4,5},{5,4},{6,7},{7,6},{8,9},{9,8},{10,11... | collective-permute-start | bytes 1916936 | tf_op jit(solution)/shard_map/ppermute | solution.py:34
  194.6 27.5 %collective-permute-start.57 = (bf16[8,32,1536]{2,1,0:T(8,128)(2,1)}, bf16[8,32,1536]{2,1,0:T(8,128)(2,1)S(1)}, u32[]{:S(2)}, u32[]{:S(2)}) collective-permute-start(bf16[8,32,1536]{2,1,0:T(8,128)(2,1)} %add_convert_fusion), channel_id=1, source_target_pairs={{0,8},{1,9},{2,10},{3,11},{4,12},{5,13},{6,14},{7,15},{8,0},{9,1},... | collective-permute-start | bytes 2359304 | tf_op jit(solution)/shard_map/ppermute | solution.py:34
  203.6 23.3 %collective-permute-start.55 = (bf16[8,32,1536]{2,1,0:T(8,128)(2,1)S(1)}, bf16[8,32,1536]{2,1,0:T(8,128)(2,1)S(1)}, u32[]{:S(2)}, u32[]{:S(2)}) collective-permute-start(bf16[8,32,1536]{2,1,0:T(8,128)(2,1)S(1)} %copy-done.13), channel_id=1, source_target_pairs={{0,2},{1,3},{2,0},{3,1},{4,6},{5,7},{6,4},{7,5},{8,10},{9,11},{10,... | collective-permute-start | bytes 2359304 | tf_op jit(solution)/shard_map/ppermute | solution.py:34
  204.0 19.8 %collective-permute-start.56 = (bf16[8,32,1536]{2,1,0:T(8,128)(2,1)S(1)}, bf16[8,32,1536]{2,1,0:T(8,128)(2,1)S(1)}, u32[]{:S(2)}, u32[]{:S(2)}) collective-permute-start(bf16[8,32,1536]{2,1,0:T(8,128)(2,1)S(1)} %copy-done.14), channel_id=1, source_target_pairs={{0,4},{1,5},{2,6},{3,7},{4,0},{5,1},{6,2},{7,3},{8,12},{9,13},{10,... | collective-permute-start | bytes 2359304 | tf_op jit(solution)/shard_map/ppermute | solution.py:34
  206.0 35.2 %collective-permute-start.42 = (bf16[16,32,768]{2,1,0:T(8,128)(2,1)S(1)}, bf16[16,32,768]{2,1,0:T(8,128)(2,1)S(1)}, u32[]{:S(2)}, u32[]{:S(2)}) collective-permute-start(bf16[16,32,768]{2,1,0:T(8,128)(2,1)S(1)} %copy-done.38), channel_id=1, source_target_pairs={{0,1},{1,0},{2,3},{3,2},{4,5},{5,4},{6,7},{7,6},{8,9},{9,8},{10,11... | collective-permute-start | bytes 2359304 | tf_op jit(solution)/shard_map/ppermute | solution.py:34
  223.8 17.3 %collective-permute-start.35 = (bf16[2,208,768]{2,1,0:T(8,128)(2,1)S(1)}, bf16[2,208,768]{2,1,0:T(8,128)(2,1)S(1)}, u32[]{:S(2)}, u32[]{:S(2)}) collective-permute-start(bf16[2,208,768]{2,1,0:T(8,128)(2,1)S(1)} %bitcast.53), channel_id=1, source_target_pairs={{0,2},{1,3},{2,0},{3,1},{4,6},{5,7},{6,4},{7,5},{8,10},{9,11},{10,... | collective-permute-start | bytes 1916936 | tf_op jit(solution)/shard_map/ppermute | solution.py:34
  226.9 22.0 %collective-permute-start.60 = (bf16[4,32,1536]{2,1,0:T(8,128)(2,1)S(1)}, bf16[4,32,1536]{2,1,0:T(8,128)(2,1)S(1)}, u32[]{:S(2)}, u32[]{:S(2)}) collective-permute-start(bf16[4,32,1536]{2,1,0:T(8,128)(2,1)S(1)} %add_convert_fusion.3), channel_id=1, source_target_pairs={{0,2},{1,3},{2,0},{3,1},{4,6},{5,7},{6,4},{7,5},{8,10},{9,11},{10,... | collective-permute-start | bytes 1179656 | tf_op jit(solution)/shard_map/ppermute | solution.py:34
  228.5 21.3 %collective-permute-start.59 = (bf16[4,32,1536]{2,1,0:T(8,128)(2,1)S(1)}, bf16[4,32,1536]{2,1,0:T(8,128)(2,1)S(1)}, u32[]{:S(2)}, u32[]{:S(2)}) collective-permute-start(bf16[4,32,1536]{2,1,0:T(8,128)(2,1)S(1)} %add_convert_fusion.4), channel_id=1, source_target_pairs={{0,8},{1,9},{2,10},{3,11},{4,12},{5,13},{6,14},{7,15},{8,0},{9,1},... | collective-permute-start | bytes 1179656 | tf_op jit(solution)/shard_map/ppermute | solution.py:34
  229.6 21.0 %collective-permute-start.58 = (bf16[4,32,1536]{2,1,0:T(8,128)(2,1)S(1)}, bf16[4,32,1536]{2,1,0:T(8,128)(2,1)S(1)}, u32[]{:S(2)}, u32[]{:S(2)}) collective-permute-start(bf16[4,32,1536]{2,1,0:T(8,128)(2,1)S(1)} %add_convert_fusion.5), channel_id=1, source_target_pairs={{0,4},{1,5},{2,6},{3,7},{4,0},{5,1},{6,2},{7,3},{8,12},{9,13},{10,... | collective-permute-start | bytes 1179656 | tf_op jit(solution)/shard_map/ppermute | solution.py:34
  241.1 25.0 %collective-permute-start.34 = (bf16[2,208,768]{2,1,0:T(8,128)(2,1)S(1)}, bf16[2,208,768]{2,1,0:T(8,128)(2,1)S(1)}, u32[]{:S(2)}, u32[]{:S(2)}) collective-permute-start(bf16[2,208,768]{2,1,0:T(8,128)(2,1)S(1)} %bitcast.54), channel_id=1, source_target_pairs={{0,1},{1,0},{2,3},{3,2},{4,5},{5,4},{6,7},{7,6},{8,9},{9,8},{10,11... | collective-permute-start | bytes 1916936 | tf_op jit(solution)/shard_map/ppermute | solution.py:34
  241.1 26.0 %collective-permute-start.36 = (bf16[2,208,768]{2,1,0:T(8,128)(2,1)S(1)}, bf16[2,208,768]{2,1,0:T(8,128)(2,1)S(1)}, u32[]{:S(2)}, u32[]{:S(2)}) collective-permute-start(bf16[2,208,768]{2,1,0:T(8,128)(2,1)S(1)} %collective-permute-done.35.refs_2_), channel_id=1, source_target_pairs={{0,1},{1,0},{2,3},{3,2},{4,5},{5,4},{6,7},{7,6},{8,9},{9,8},{10,11... | collective-permute-start | bytes 1916936 | tf_op jit(solution)/shard_map/ppermute | solution.py:34
  259.3 27.0 %collective-permute-start.63 = (bf16[2,32,1536]{2,1,0:T(8,128)(2,1)}, bf16[2,32,1536]{2,1,0:T(8,128)(2,1)S(1)}, u32[]{:S(2)}, u32[]{:S(2)}) collective-permute-start(bf16[2,32,1536]{2,1,0:T(8,128)(2,1)} %add_convert_fusion.10), channel_id=1, source_target_pairs={{0,4},{1,5},{2,6},{3,7},{4,0},{5,1},{6,2},{7,3},{8,12},{9,13},{10,... | collective-permute-start | bytes 589832 | tf_op jit(solution)/shard_map/ppermute | solution.py:34
  261.3 24.1 %collective-permute-start.62 = (bf16[2,32,1536]{2,1,0:T(8,128)(2,1)}, bf16[2,32,1536]{2,1,0:T(8,128)(2,1)}, u32[]{:S(2)}, u32[]{:S(2)}) collective-permute-start(bf16[2,32,1536]{2,1,0:T(8,128)(2,1)} %add_convert_fusion.11), channel_id=1, source_target_pairs={{0,2},{1,3},{2,0},{3,1},{4,6},{5,7},{6,4},{7,5},{8,10},{9,11},{10,... | collective-permute-start | bytes 589832 | tf_op jit(solution)/shard_map/ppermute | solution.py:34
  266.1 18.1 %collective-permute-start.61 = (bf16[2,32,1536]{2,1,0:T(8,128)(2,1)}, bf16[2,32,1536]{2,1,0:T(8,128)(2,1)S(1)}, u32[]{:S(2)}, u32[]{:S(2)}) collective-permute-start(bf16[2,32,1536]{2,1,0:T(8,128)(2,1)} %add_convert_fusion.12), channel_id=1, source_target_pairs={{0,8},{1,9},{2,10},{3,11},{4,12},{5,13},{6,14},{7,15},{8,0},{9,1},... | collective-permute-start | bytes 589832 | tf_op jit(solution)/shard_map/ppermute | solution.py:34
  (85 other events, 809.6 us)

commit v4 on v1

v4 whole, which is shorter than its diff:
```python
from functools import partial

import jax
import jax.numpy as jnp
from jax import lax
from jax.experimental import pallas as pl
from jax.experimental.pallas import tpu as pltpu
from jax.sharding import PartitionSpec as P

HEAD_DIM = 64
EPS = 1e-06
AXES = ("dp", "tensor")
TILE = 16
FACTOR = HEAD_DIM ** (-0.5)
bf16 = jnp.bfloat16
f32 = jnp.float32


class Cube:
    def __init__(self, n_dp, n_t, rows):
        self.n_dp, self.n_t, self.rows = n_dp, n_t, rows
        self.n = n_dp * n_t
        n_bits = self.n.bit_length() - 1
        self.fast = (1 << n_bits) == self.n and n_bits >= 4 and rows % TILE == 0
        far = list(range(n_bits - 1, 3, -1))
        self.orders = ([2, 1, 3] + far, [1, 3, 2] + far)
        self.steps = len(self.orders[0])
        self.half = self.n // 2

    def swap(self, value, k):
        return lax.ppermute(
            value, AXES, [(i, i ^ (1 << self.orders[i & 1][k])) for i in range(self.n)]
        )

    def flip(self, value, bit):
        return lax.ppermute(value, AXES, [(i, i ^ (1 << bit)) for i in range(self.n)])

    def table(self):
        if not self.fast:
            return jnp.zeros((1,), jnp.int32)
        rows = lax.axis_index("dp") ^ jnp.arange(self.n_dp)
        core = lax.axis_index("tensor") & 1
        relative = (rows[None, :] << 2) | (jnp.arange(2)[:, None] << 1)
        found = []
        for order in self.orders:
            place = relative * 0
            for k, bit in enumerate(order[::-1]):
                place = place | (((relative >> bit) & 1) << k)
            found.append(place)
        both = jnp.where(core == 0, jnp.stack(found), jnp.stack(found[::-1]))
        return both.reshape(-1).astype(jnp.int32)

    def at(self, table_ref, core, y, block):
        return table_ref[(core * 2 + y) * self.n_dp + block]

    def buffers(self, cols):
        blocks = (self.half, self.rows, cols) if self.fast else (1, 8, 128)
        shard = pltpu.VMEM((self.n_dp * self.rows, cols), bf16)
        return [pltpu.VMEM(blocks, bf16), shard, pltpu.SemaphoreType.DMA((2,))]

    def fetch(self, refs, scratch):
        if not self.fast:
            return lambda: None
        held, _, sems = scratch
        part = self.half // 2
        copies = [
            pltpu.make_async_copy(refs[i], held.at[pl.ds(i * part, part)], sems.at[i])
            for i in range(2)
        ]
        for copy in copies:
            copy.start()

        def wait():
            for copy in copies:
                copy.wait()

        return wait

    def load(self, table_ref, refs, scratch, core, y):
        held, shard, sems = scratch
        if not self.fast:
            copy = pltpu.make_async_copy(refs[0].at[2 * y + core], shard, sems.at[0])
            copy.start()
            copy.wait()
            return
        for d in range(self.n_dp):
            shard[d * self.rows : (d + 1) * self.rows, :] = held[self.at(table_ref, core, y, d)]

    def store(self, table_ref, ref, core, y, value):
        if not self.fast:
            ref[y] = value
            return
        for d in range(self.n_dp):
            rows = value[d * self.rows : (d + 1) * self.rows]
            ref[self.at(table_ref, core, y, d)] = rows

    def grad_shape(self, cols):
        if not self.fast:
            return jax.ShapeDtypeStruct((2, self.n_dp * self.rows, cols), bf16)
        return jax.ShapeDtypeStruct((self.half, self.rows, cols), bf16)

    def of_core(self, buffers, core):
        return buffers[2 * core : 2 * core + 2] if self.fast else buffers


def gather_plain(cube, piece):
    rows, cols = piece.shape
    whole = lax.all_gather(piece, AXES, axis=0, tiled=False)
    whole = whole.reshape(cube.n_dp, cube.n_t, rows, cols).transpose(1, 0, 2, 3)
    whole = whole.reshape(cube.n_t, cube.n_dp * rows, cols)
    return [jnp.take(whole, lax.axis_index("tensor") ^ jnp.arange(cube.n_t), axis=0)]


def scatter_plain(cube, own, other):
    n_t, n_dp, rows, cols = cube.n_t, cube.n_dp, cube.rows, own.shape[2]
    part = jnp.stack((own, other), axis=1).reshape(n_t, n_dp * rows, cols)
    part = jnp.take(part, lax.axis_index("tensor") ^ jnp.arange(n_t), axis=0)
    part = part.reshape(n_t, n_dp, rows, cols).transpose(1, 0, 2, 3)
    part = part.reshape(n_dp * n_t * rows, cols)
    return lax.psum_scatter(part, AXES, scatter_dimension=0, tiled=True).astype(f32)


def join(pairs, after=()):
    def kernel(*refs):
        outs = refs[2 * len(pairs) + len(after) :]
        for i, out in enumerate(outs):
            size = pairs[i][0].shape[0]
            out[:size] = refs[2 * i][...]
            out[size:] = refs[2 * i + 1][...]

    shapes = [
        jax.ShapeDtypeStruct((2 * p[0].shape[0],) + p[0].shape[1:], p[0].dtype) for p in pairs
    ]
    return plain_call(kernel, shapes, [x for p in pairs for x in p], None, after)


def sends(groups, after=()):
    sizes = [min(v.shape[0] for v in g) // 2 for g in groups]
    specs, shapes = [], []
    for g, size in zip(groups, sizes):
        block = (size,) + g[0].shape[1:]
        specs += [pl.BlockSpec(block, lambda i: (1, 0, 0)) for _ in g]
        shapes.append(jax.ShapeDtypeStruct(block, bf16))

    def kernel(*refs):
        outs = refs[-len(groups) :]
        start = 0
        for g, out in zip(groups, outs):
            value = refs[start][...].astype(f32)
            for ref in refs[start + 1 : start + len(g)]:
                value = value + ref[...].astype(f32)
            out[...] = value.astype(bf16)
            start += len(g)

    return plain_call(kernel, shapes, [v for g in groups for v in g], specs, after)


def finish(group, after=()):
    block = (1,) + group[0].shape[1:]

    def kernel(*refs):
        value = refs[0][0].astype(f32)
        for ref in refs[1 : len(group)]:
            value = value + ref[0].astype(f32)
        refs[-1][...] = value

    specs = [pl.BlockSpec(block, lambda i: (0, 0, 0)) for _ in group]
    return plain_call(kernel, [jax.ShapeDtypeStruct(block[1:], f32)], group, specs, after)[0]


def plain_call(kernel, shapes, inputs, specs, after):
    moved = 2 * sum(x.size * x.dtype.itemsize for x in shapes)
    if specs is None:
        specs = [pl.BlockSpec(x.shape, lambda i: (0, 0, 0)) for x in inputs]
    return pl.pallas_call(
        kernel,
        grid=(1,),
        out_shape=shapes,
        in_specs=specs + [pl.BlockSpec(memory_space=pl.ANY)] * len(after),
        out_specs=[pl.BlockSpec(x.shape, lambda i, n=len(x.shape): (0,) * n) for x in shapes],
        compiler_params=pltpu.CompilerParams(vmem_limit_bytes=48 * 1024 * 1024),
        cost_estimate=pl.CostEstimate(flops=0, bytes_accessed=2 * moved, transcendentals=0),
    )(*inputs, *after)


def sum_all(cube, value):
    if not cube.fast:
        return lax.psum(value, AXES)
    value = value + cube.flip(value, 0)
    for k in range(cube.steps):
        value = value + cube.flip(value, cube.orders[0][k])
    return value


def place_images(cube, pieces, length, after=()):
    if not cube.fast:
        return lax.all_gather(pieces[0][:, :length], "tensor", axis=0, tiled=True)
    count = pieces[0].shape[0]
    index = lax.axis_index("tensor").astype(jnp.int32).reshape(1)

    def kernel(index_ref, *refs):
        for r in range(4):
            for i in range(count):
                refs[-1][(index_ref[0] ^ r) * count + i] = refs[r][i, :length, :]

    shape = (4 * count, length, pieces[0].shape[2])
    return call(kernel, [jax.ShapeDtypeStruct(shape, bf16)], index, pieces, [], [], 0, after)[0]


def call(kernel, out_shapes, index, inputs, weights, scratch, flops, after=()):
    inputs_all = [*inputs, *weights]
    moved = sum(x.size * x.dtype.itemsize for x in inputs_all)
    moved += sum(x.size * x.dtype.itemsize for x in out_shapes)
    n_in, n_w, n_out = len(inputs), len(weights), len(out_shapes)

    def body(index_ref, *refs):
        rest = refs[n_in + n_w + len(after) :]
        kernel(index_ref, *refs[: n_in + n_w], *rest)

    return pl.pallas_call(
        body,
        out_shape=out_shapes,
        in_specs=[pl.BlockSpec(memory_space=pltpu.SMEM)]
        + [pl.BlockSpec(memory_space=pltpu.VMEM)] * n_in
        + [pl.BlockSpec(memory_space=pl.ANY)] * (n_w + len(after)),
        out_specs=[pl.BlockSpec(memory_space=pltpu.VMEM)] * n_out,
        scratch_shapes=scratch,
        compiler_params=pltpu.CompilerParams(vmem_limit_bytes=56 * 1024 * 1024),
        cost_estimate=pl.CostEstimate(flops=flops, bytes_accessed=moved, transcendentals=0),
    )(index, *inputs, *weights, *after)


def nn(left, right):
    return lax.dot_general(left, right, (((1,), (0,)), ((), ())), preferred_element_type=f32)


def nt(left, right):
    return lax.dot_general(left, right, (((1,), (1,)), ((), ())), preferred_element_type=f32)


def tn(left, right):
    return lax.dot_general(left, right, (((0,), (0,)), ((), ())), preferred_element_type=f32)


def normed_of(values):
    centre = values - jnp.mean(values, -1, keepdims=True)
    inverse = lax.rsqrt(jnp.mean(centre * centre, -1, keepdims=True) + EPS)
    return (centre * inverse, inverse)


def norm_back(upstream, normed, inverse, gain):
    scaled = upstream * gain
    inner = (
        scaled
        - jnp.mean(scaled, -1, keepdims=True)
        - normed * jnp.mean(scaled * normed, -1, keepdims=True)
    )
    return inverse * inner


def column_sum(values):
    return jnp.sum(values, 0, keepdims=True)


def attend_kernel(cube, count, length, width, n_w, table_ref, *refs):
    x_ref, vec_ref, bias_ref = refs[:3]
    w_refs = refs[3 : 3 + n_w]
    n1_ref, qkv_ref, att_ref, hidden_ref, n2_ref = refs[3 + n_w : 8 + n_w]
    scratch, sum_ref = (refs[8 + n_w : 11 + n_w], refs[11 + n_w : 14 + n_w]), refs[14 + n_w]
    waits = [cube.fetch(cube.of_core(w_refs, core), scratch[core]) for core in range(2)]
    x = x_ref[...].astype(f32)
    normed, _ = normed_of(x)
    n1_ref[...] = (normed * vec_ref[0:1] + vec_ref[1:2]).astype(bf16)
    sum_ref[...] = x + vec_ref[2:3]
    tokens = x.shape[0] // count
    heads = width // HEAD_DIM
    keep = lax.broadcasted_iota(jnp.int32, (tokens, tokens), 1) < length

    for core in range(2):
        waits[core]()
        w_ref = scratch[core][1]

        def step(y, carry):
            t = 2 * y + core
            cube.load(table_ref, cube.of_core(w_refs, core), scratch[core], core, y)
            qkv = nn(n1_ref[...], w_ref[:, : 3 * width]) + bias_ref[t]
            qkv_ref[t] = qkv.astype(bf16)
            for b in range(count):
                rows = slice(b * tokens, (b + 1) * tokens)
                found = []
                for h in range(heads):
                    q = qkv_ref[t, rows, h * HEAD_DIM : (h + 1) * HEAD_DIM]
                    k = qkv_ref[t, rows, width + h * HEAD_DIM : width + (h + 1) * HEAD_DIM]
                    v = qkv_ref[t, rows, 2 * width + h * HEAD_DIM : 2 * width + (h + 1) * HEAD_DIM]
                    scores = jnp.where(keep, nt(q, k) * FACTOR, -1e30)
                    weights = jnp.exp(scores - jnp.max(scores, -1, keepdims=True))
                    probs = weights * (1.0 / jnp.sum(weights, -1, keepdims=True))
                    found.append(nn(probs.astype(bf16), v).astype(bf16))
                att_ref[t, rows, :] = jnp.concatenate(found, axis=1)
            sum_ref[...] += nt(att_ref[t], w_ref[:, 3 * width :])
            return carry

        lax.fori_loop(0, cube.n_t // 2, step, 0)
    hidden = sum_ref[...]
    hidden_ref[...] = hidden
    normed, _ = normed_of(hidden)
    n2_ref[...] = (normed * vec_ref[3:4] + vec_ref[4:5]).astype(bf16)


def gelu_kernel(cube, core, n_w, table_ref, *refs):
    n2_ref, cot_ref, bias_ref = refs[:3]
    w_refs = refs[3 : 3 + n_w]
    act_ref, slope_ref, grad_ref = refs[3 + n_w : 6 + n_w]
    scratch = refs[6 + n_w :]
    cube.fetch(w_refs, scratch)()

    def step(y, carry):
        cube.load(table_ref, w_refs, scratch, core, y)
        pre = nn(n2_ref[...], scratch[1][...]) + bias_ref[2 * y + core]
        cdf = 0.5 * (1.0 + lax.erf(pre * (0.5**0.5)))
        slope = cdf + pre * (jnp.exp(-0.5 * pre * pre) * 0.3989422804014327)
        act_ref[y] = (pre * cdf).astype(bf16)
        slope_ref[y] = slope.astype(bf16)
        cube.store(table_ref, grad_ref, core, y, tn(cot_ref[...], act_ref[y]).astype(bf16))
        return carry

    lax.fori_loop(0, cube.n_t // 2, step, 0)


def mlp_kernel(cube, core, first, n_w, table_ref, *refs):
    n2_ref, cot_ref, act_ref, slope_ref, mlp_in, dnorm_in, hidden_ref, vec_ref = refs[:8]
    one_refs, two_refs = refs[8 : 8 + n_w], refs[8 + n_w : 8 + 2 * n_w]
    outs = refs[8 + 2 * n_w :]
    grad_ref, sums_ref = outs[:2]
    if first:
        mlp_ref, dnorm_ref = outs[2:4]
        rest = outs[4:]
    else:
        enc_ref, dhidden_ref, small_ref = outs[2:5]
        rest = outs[5:]
    one, two = rest[:3], rest[3:6]
    if not first:
        mlp_ref, dnorm_ref = rest[6:8]
    waits = [cube.fetch(one_refs, one), cube.fetch(two_refs, two)]
    for wait in waits:
        wait()

    def step(y, carry):
        cube.load(table_ref, one_refs, one, core, y)
        cube.load(table_ref, two_refs, two, core, y)
        dact = nn(cot_ref[...], two[1][...])
        dpre = (slope_ref[y].astype(f32) * dact).astype(bf16)
        sums_ref[pl.ds(y, 1)] = column_sum(dpre.astype(f32))[None]
        cube.store(table_ref, grad_ref, core, y, tn(n2_ref[...], dpre).astype(bf16))
        dnorm_ref[...] += nt(dpre, one[1][...])
        mlp_ref[...] += nt(act_ref[y], two[1][...])
        return carry

    if first:
        mlp_ref[...] = mlp_in[...] + vec_ref[5:6]
        dnorm_ref[...] = jnp.zeros_like(dnorm_ref)
        lax.fori_loop(0, cube.n_t // 2, step, 0)
        return
    mlp_ref[...] = mlp_in[...]
    dnorm_ref[...] = dnorm_in[...]
    lax.fori_loop(0, cube.n_t // 2, step, 0)
    enc_ref[...] = mlp_ref[...].astype(bf16)
    normed, inverse = normed_of(hidden_ref[...])
    dnorm = dnorm_ref[...]
    cot = cot_ref[...].astype(f32)
    dhidden = cot + norm_back(dnorm, normed, inverse, vec_ref[3:4])
    dhidden_ref[...] = dhidden
    small_ref[0] = column_sum(dnorm * normed)
    small_ref[1] = column_sum(dnorm)
    small_ref[2] = column_sum(cot)
    small_ref[3] = column_sum(dhidden)


def attend_back_kernel(cube, core, first, count, length, width, n_w, table_ref, *refs):
    x_ref, n1_ref, qkv_ref, att_ref, dhidden_ref, dnorm_in, vec_ref = refs[:7]
    w_refs = refs[7 : 7 + n_w]
    outs = refs[7 + n_w :]
    grad_ref, dbias_ref = outs[:2]
    if first:
        dnorm_ref = outs[2]
        rest = outs[3:]
    else:
        patch_ref, small_ref = outs[2:4]
        rest = outs[4:]
    scratch = rest[:3]
    low_ref, dqkv_ref = rest[3:5]
    if not first:
        dnorm_ref = rest[5]
    wait = cube.fetch(w_refs, scratch)
    low_ref[...] = dhidden_ref[...].astype(bf16)
    dnorm_ref[...] = jnp.zeros_like(dnorm_ref) if first else dnorm_in[...]
    tokens = x_ref.shape[0] // count
    heads = width // HEAD_DIM
    keep = lax.broadcasted_iota(jnp.int32, (tokens, tokens), 0) < length
    wait()
    w_ref = scratch[1]

    def step(y, carry):
        t = 2 * y + core
        cube.load(table_ref, w_refs, scratch, core, y)
        datt = nn(low_ref[...], w_ref[:, 3 * width :]).astype(bf16)
        for b in range(count):
            rows = slice(b * tokens, (b + 1) * tokens)
            dqs, dks, dvs = [], [], []
            for h in range(heads):
                q = qkv_ref[t, rows, h * HEAD_DIM : (h + 1) * HEAD_DIM]
                k = qkv_ref[t, rows, width + h * HEAD_DIM : width + (h + 1) * HEAD_DIM]
                v = qkv_ref[t, rows, 2 * width + h * HEAD_DIM : 2 * width + (h + 1) * HEAD_DIM]
                do = datt[rows, h * HEAD_DIM : (h + 1) * HEAD_DIM]
                scores = jnp.where(keep, nt(k, q) * FACTOR, -1e30)
                weights = jnp.exp(scores - jnp.max(scores, 0, keepdims=True))
                probs = weights * (1.0 / jnp.sum(weights, 0, keepdims=True))
                dvs.append(nn(probs.astype(bf16), do))
                dprobs = nt(v, do)
                inner = jnp.sum(dprobs * probs, 0, keepdims=True)
                dscores = (probs * (dprobs - inner)).astype(bf16)
                dks.append(nn(dscores, q) * FACTOR)
                dqs.append(tn(dscores, k) * FACTOR)
            dqkv_ref[rows, :] = jnp.concatenate(dqs + dks + dvs, axis=1).astype(bf16)
        dqkv = dqkv_ref[...]
        dbias_ref[pl.ds(y, 1)] = column_sum(dqkv.astype(f32))[None]
        dnorm_ref[...] += nt(dqkv, w_ref[:, : 3 * width])
        grad = jnp.concatenate((tn(n1_ref[...], dqkv), tn(low_ref[...], att_ref[t])), axis=1)
        cube.store(table_ref, grad_ref, core, y, grad.astype(bf16))
        return carry

    lax.fori_loop(0, cube.n_t // 2, step, 0)
    if first:
        return
    normed, inverse = normed_of(x_ref[...].astype(f32))
    dnorm = dnorm_ref[...]
    patch = dhidden_ref[...] + norm_back(dnorm, normed, inverse, vec_ref[0:1])
    patch_ref[...] = patch.astype(bf16)
    small_ref[0] = column_sum(dnorm * normed)
    small_ref[1] = column_sum(dnorm)


def on_device(
    n_dp,
    n_t,
    patches,
    attn_gain,
    attn_shift,
    qkv_weight,
    qv_bias,
    out_weight,
    out_bias,
    mlp_gain,
    mlp_shift,
    fc1_weight,
    fc1_bias,
    fc2_weight,
    fc2_bias,
    cotangent,
):
    t_me = lax.axis_index("tensor")
    cube = Cube(n_dp, n_t, qkv_weight.shape[1])
    order = t_me ^ jnp.arange(n_t)
    width = qkv_weight.shape[2]
    f_width = fc1_weight.shape[1]
    d = patches.shape[2]
    table = cube.table()
    count = patches.shape[0] // n_t
    length = patches.shape[1]
    padded = -(-length // TILE) * TILE
    tokens = count * padded

    def own_images(values):
        mine = lax.dynamic_slice_in_dim(values, t_me * count, count, 0)
        return jnp.pad(mine, ((0, 0), (0, padded - length), (0, 0))).reshape(tokens, d)

    def shape(*dims, dtype=bf16):
        return jax.ShapeDtypeStruct(dims, dtype)

    attn_piece = jnp.concatenate(
        (qkv_weight[0], qkv_weight[1], qkv_weight[2], out_weight.T), axis=1
    )
    two_piece = fc2_weight.T
    biases = jnp.concatenate((qv_bias.reshape(-1), fc1_bias))[None]
    x = own_images(patches)
    cot = own_images(cotangent)
    vecs = jnp.stack((attn_gain, attn_shift, out_bias, mlp_gain, mlp_shift, fc2_bias)).astype(f32)

    def bias_parts(biases):
        biases = biases.astype(f32)
        zeros = jnp.zeros((n_t, width), f32)
        qkv = (biases[:, :width], zeros, biases[:, width : 2 * width])
        return (jnp.concatenate(qkv, axis=1)[:, None], biases[:, None, 2 * width :])

    last = cube.steps - 1
    if cube.fast:
        held = attn_piece[None]
        one = fc1_weight[None]
        two = two_piece[None]
        biases = jnp.concatenate((biases, cube.flip(biases, 0)))
        biases = jnp.concatenate((biases, cube.flip(biases, 1)))
        qkv_bias, f_bias = bias_parts(biases)
        for k in range(last, 0, -1):
            pairs = [(held, cube.swap(held, k))]
            if k < last:
                pairs.append((one, cube.swap(one, k + 1)))
            if k < last - 1:
                pairs.append((two, cube.swap(two, k + 2)))
            found = join(pairs, (x, cot) if k == last else ())
            if k == last:
                one, two = lax.optimization_barrier((one, two))
            held = found[0]
            one = found[1] if k < last else one
            two = found[2] if k < last - 1 else two
        came = cube.swap(held, 0)
        pairs = [(one, cube.swap(one, 1)), (two, cube.swap(two, 2))]
        w_attn = [held, came, cube.flip(held, 0), cube.flip(came, 0)]
        one, two = join(pairs, (came,))
        slot = (one, two)
    else:
        w_attn = gather_plain(cube, attn_piece)
        w_one = gather_plain(cube, fc1_weight)
        w_two = gather_plain(cube, two_piece)
        biases = jnp.take(lax.all_gather(biases[0], "tensor", axis=0, tiled=False), order, axis=0)
        qkv_bias, f_bias = bias_parts(biases)
        slot = ()
    n_w = len(w_attn)
    n_c = len(cube.of_core(w_attn, 0))
    spots = 2 * tokens * d * n_t
    attn_macs = spots * 2 * width + 4 * count * n_t * padded * padded * width
    buffers = cube.buffers(d)

    n1, qkv, att, hidden, n2 = call(
        partial(attend_kernel, cube, count, length, width, n_w),
        [
            shape(tokens, d),
            shape(n_t, tokens, 3 * width),
            shape(n_t, tokens, width),
            shape(tokens, d, dtype=f32),
            shape(tokens, d),
        ],
        table,
        [x, vecs, qkv_bias],
        w_attn,
        buffers * 2 + [pltpu.VMEM((tokens, d), f32)],
        2 * attn_macs,
        slot,
    )
    if cube.fast:
        came = cube.swap(one, 0)
        w_one = [one, came, cube.flip(one, 0), cube.flip(came, 0)]
        two = join([(two, cube.swap(two, 1))], (n2,))[0]
        slot = (two,)

    def gelu(core, after):
        return call(
            partial(gelu_kernel, cube, core, n_c),
            [shape(n_t // 2, tokens, f_width)] * 2 + [cube.grad_shape(f_width)],
            table,
            [n2, cot, f_bias],
            cube.of_core(w_one, core),
            buffers,
            spots * f_width,
            after,
        )

    act_other, slope_other, two_other = gelu(1, slot)
    act_own, slope_own, two_own = gelu(0, (two_other,))
    if cube.fast:
        came = cube.swap(two, 0)
        w_two = [two, came, cube.flip(two, 0), cube.flip(came, 0)]
        two_terms = [two_own, cube.flip(two_other, 0)]
        (s_two,) = sends([two_terms], ())
        slot = (s_two,)
    else:
        slot = ()

    def mlp(core, first, act, slope, mlp_in, dnorm_in, after):
        if first:
            outs = [shape(tokens, d, dtype=f32)] * 2
            scratch = []
        else:
            outs = [shape(tokens, d), shape(tokens, d, dtype=f32), shape(4, 1, d, dtype=f32)]
            scratch = [pltpu.VMEM((tokens, d), f32)] * 2
        return call(
            partial(mlp_kernel, cube, core, first, n_c),
            [cube.grad_shape(f_width), shape(n_t // 2, 1, f_width, dtype=f32)] + outs,
            table,
            [n2, cot, act, slope, mlp_in, dnorm_in, hidden, vecs],
            [*cube.of_core(w_one, core), *cube.of_core(w_two, core)],
            buffers * 2 + scratch,
            2 * spots * f_width,
            after,
        )

    one_other, f_other, mlp_sum, dnorm = mlp(1, True, act_other, slope_other, hidden, vecs, slot)
    one_own, f_own, enc, dhidden, mlp_small = mlp(
        0, False, act_own, slope_own, mlp_sum, dnorm, (one_other,)
    )
    images = enc.reshape(count, padded, d)
    if cube.fast:
        two_terms.append(cube.swap(s_two, 0))
        one_terms = [one_own, cube.flip(one_other, 0)]
        s_two, s_one = sends([two_terms, one_terms], (dhidden,))
        slot = (s_two, s_one)
        there = cube.flip(images, 1)
        enc_pieces = [images, cube.flip(images, 0), there, cube.flip(there, 0)]
    else:
        enc_pieces = [images]

    def attend_back(core, first, dnorm_in, after):
        if first:
            outs = [shape(tokens, d, dtype=f32)]
            scratch = []
        else:
            outs = [shape(tokens, d), shape(2, 1, d, dtype=f32)]
            scratch = [pltpu.VMEM((tokens, d), f32)]
        return call(
            partial(attend_back_kernel, cube, core, first, count, length, width, n_c),
            [cube.grad_shape(4 * width), shape(n_t // 2, 1, 3 * width, dtype=f32)] + outs,
            table,
            [x, n1, qkv, att, dhidden, dnorm_in, vecs],
            cube.of_core(w_attn, core),
            buffers
            + [pltpu.VMEM((tokens, d), bf16), pltpu.VMEM((tokens, 3 * width), bf16)]
            + scratch,
            2 * attn_macs,
            after,
        )

    attn_other, dbias_other, dnorm = attend_back(1, True, vecs, slot)
    if cube.fast:
        two_terms.append(cube.swap(s_two, 1))
        (s_two,) = sends([two_terms], (dnorm,))
        slot = (s_two,)
    attn_own, dbias_own, patch, attn_small = attend_back(0, False, dnorm, slot)
    images = patch.reshape(count, padded, d)
    if cube.fast:
        there = cube.flip(images, 1)
        patch_pieces = [images, cube.flip(images, 0), there, cube.flip(there, 0)]
        two_terms.append(cube.swap(s_two, 2))
        one_terms.append(cube.swap(s_one, 0))
        attn_terms = [attn_own, cube.flip(attn_other, 0)]
        s_attn, s_one, s_two = sends([attn_terms, one_terms, two_terms])
        k_attn, k_one, k_two = 0, 1, 3
        while True:
            attn_terms.append(cube.swap(s_attn, k_attn))
            if k_one <= last:
                one_terms.append(cube.swap(s_one, k_one))
            if k_two <= last:
                two_terms.append(cube.swap(s_two, k_two))
            k_attn, k_one, k_two = (k_attn + 1, k_one + 1, k_two + 1)
            if k_attn > last:
                break
            groups = [attn_terms]
            groups += [one_terms] if k_one <= last else []
            groups += [two_terms] if k_two <= last else []
            found = sends(groups)
            s_attn = found[0]
            s_one = found[1] if k_one <= last else None
            s_two = found[2] if k_two <= last else None
        two_grad = finish(two_terms)
        one_grad = finish(one_terms)
        attn_grad = finish(attn_terms)
    else:
        patch_pieces = [images]
        two_grad = scatter_plain(cube, two_own, two_other)
        one_grad = scatter_plain(cube, one_own, one_other)
        attn_grad = scatter_plain(cube, attn_own, attn_other)
    encoded = place_images(cube, enc_pieces, length)
    patch_grad = place_images(cube, patch_pieces, length)

    def in_order(own, other):
        both = jnp.stack((own[:, 0], other[:, 0]), axis=1)
        return jnp.take(both.reshape((n_t,) + own.shape[2:]), order, axis=0)

    dbias = in_order(dbias_own, dbias_other)
    f_sums = in_order(f_own, f_other)
    small = jnp.concatenate(
        (
            attn_small.reshape(-1),
            mlp_small.reshape(-1),
            dbias[:, :width].reshape(-1),
            dbias[:, 2 * width :].reshape(-1),
            f_sums.reshape(-1),
        )
    )
    small = sum_all(cube, small)
    cuts = [small[i * d : (i + 1) * d] for i in range(6)]
    at = 6 * d
    q_sum = lax.dynamic_slice_in_dim(small[at : at + n_t * width], t_me * width, width, 0)
    at += n_t * width
    v_sum = lax.dynamic_slice_in_dim(small[at : at + n_t * width], t_me * width, width, 0)
    at += n_t * width
    f_sum = lax.dynamic_slice_in_dim(small[at:], t_me * f_width, f_width, 0)
    return (
        encoded,
        patch_grad,
        cuts[0],
        cuts[1],
        jnp.stack([attn_grad[:, i * width : (i + 1) * width] for i in range(3)]),
        jnp.stack((q_sum, v_sum)),
        attn_grad[:, 3 * width :].T,
        cuts[5],
        cuts[2],
        cuts[3],
        one_grad,
        f_sum,
        two_grad.T,
        cuts[4],
    )


def solution(mesh):
    return jax.shard_map(
        partial(on_device, mesh.shape["dp"], mesh.shape["tensor"]),
        mesh=mesh,
        in_specs=(
            P("dp", None, None),
            P(),
            P(),
            P(None, "dp", "tensor"),
            P(None, "tensor"),
            P("tensor", "dp"),
            P(),
            P(),
            P(),
            P("dp", "tensor"),
            P("tensor"),
            P("tensor", "dp"),
            P(),
            P("dp", None, None),
        ),
        out_specs=(
            P("dp", None, None),
            P("dp", None, None),
            P(),
            P(),
            P(None, "dp", "tensor"),
            P(None, "tensor"),
            P("tensor", "dp"),
            P(),
            P(),
            P(),
            P("dp", "tensor"),
            P("tensor"),
            P("tensor", "dp"),
            P(),
        ),
        check_vma=False,
    )
```

time: 658 us -> 331 us (0.50)
  waiting for transfers between devices: 436 us -> 102 us
  Pallas kernels: 0 us -> 111 us
  matrix products: 69.7 us -> 0 us
  starting transfers between devices: 0.58 us -> 50.2 us
  blocking collectives: 46.2 us -> 0 us
  between operations: 15.2 us -> 1.22 us
  other arithmetic: 24.7 us -> 11.6 us
    reduce_scatter x3 -> x0, waiting for transfers between devices: 264 us -> none  [scatter_grad(): lax.psum_scatter(part, AXES, scatter_dimension=0, tiled=True).astype(f32)]
    all_gather x5 -> x0, waiting for transfers between devices: 171 us -> none  [the longest x3 171 us: gather_weight(): whole = lax.all_gather(piece, AXES, axis=0, tiled=False)]
    pallas_call x0 -> x24, Pallas kernels: none -> 111 us  [the longest x9 92.3 us: call(): pl.pallas_call(body, out_shape=out_shapes, in_specs=[pl.BlockSpec(memory_...]
    ppermute x0 -> x46, waiting for transfers between devices: none -> 102 us  [the longest x24 95.6 us: swap(): lax.ppermute(value, AXES, [(i, i ^ 1 << self.orders[i & 1][k]) for i in r...]
    dot_general x18 -> x0, matrix products: 69.7 us -> none  [dot(): return jnp.einsum(spec, left, right, preferred_element_type=f32)]
    ppermute x0 -> x46, starting transfers between devices: none -> 50.2 us  [the longest x24 32.9 us: swap(): lax.ppermute(value, AXES, [(i, i ^ 1 << self.orders[i & 1][k]) for i in r...]
    psum x1 -> x0, blocking collectives: 40 us -> none  [on_device(): small = lax.psum(small, AXES)]
    transpose x5 -> x0, local copies, waits for them, and re-layouts: 16.3 us -> none  [the longest x3 7.59 us: scatter_grad(): part.astype(bf16).reshape(n_t, n_dp, rows, part.shape[2])]
  transfers between devices with their start and end apart: 8 -> 46, of which waited for: 6 -> 20; matrix products, arithmetic and copies ran while one was open for 16% -> 14% of each run, Pallas kernels for 0% -> 22%
where the time goes in v4:
time: 331 us; the launch traced here: 329 us
  Pallas kernels  111 us (34%)
  waiting for transfers between devices  102 us (31%)
  local copies, waits for them, and re-layouts  53.3 us (16%)
  starting transfers between devices  50.2 us (15%)
  other arithmetic  11.6 us (4%)
    ppermute x24, waiting for transfers between devices, swap(): lax.ppermute(value, AXES, [(i, i ^ 1 << self.orders[i & 1][k]) for i in r...  95.6 us
    pallas_call x9, Pallas kernels, call(): pl.pallas_call(body, out_shape=out_shapes, in_specs=[pl.BlockSpec(memory_...  92.3 us
    ppermute x24, starting transfers between devices, swap(): lax.ppermute(value, AXES, [(i, i ^ 1 << self.orders[i & 1][k]) for i in r...  32.9 us
    unnamed x98, local copies, waits for them, and re-layouts  29.1 us
    pallas_call x15, Pallas kernels, plain_call(): pl.pallas_call(kernel, grid=(1,), out_shape=shapes, in_specs=specs + [pl....  18.4 us
    ppermute x22, starting transfers between devices, flip(): return lax.ppermute(value, AXES, [(i, i ^ 1 << bit) for i in range(self.n)])  17.3 us
    another operation x7, local copies, waits for them, and re-layouts, on_device(): jnp.stack((attn_gain, attn_shift, out_bias, mlp_gain, mlp_shift, fc2_bias))  8.97 us
  transfers between devices with their start and end apart: 46, of which 20 were waited for; matrix products, arithmetic and copies ran while one was open for 14% of the time, Pallas kernels for 22%

profile of v4, /device:TPU:0, one launch (start us, length us, event | category | flops | bytes accessed | tf_op | source)
XLA Modules:
  0.0 329.2 jit_solution(7249010943200272933)
XLA Ops:
  2.5 4.1 %collective-permute-start.2 = (bf16[1,96,768]{2,1,0:T(8,128)(2,1)S(1)}, bf16[1,96,768]{2,1,0:T(8,128)(2,1)S(1)}, u32[]{:S(2)}, u32[]{:S(2)}) collective-permute-start(bf16[1,96,768]{2,1,0:T(8,128)(2,1)S(1)} %maximum_bitcast_fusion.refs_0_), channel_id=1, source_target_pairs={{0,16},{1,17},{2,18},{3,19},{4,20},{5,21},{6,22},{7,23},{8,24},{9,... | collective-permute-start | bytes 442376 | tf_op jit(solution)/shard_map/ppermute | solution.py:31
  6.6 3.7 %constant_dynamic-slice_fusion = (bf16[2,197,768]{2,0,1:T(2,128)(2,1)S(1)}, bf16[2,197,768]{2,0,1:T(2,128)(2,1)S(1)}) fusion(bf16[8,197,768]{2,0,1:T(8,128)(2,1)} %param.27, s32[]{:T(128)S(6)} %select_n.56, bf16[8,197,768]{2,0,1:T(8,128)(2,1)} %param.14), kind=kLoop, calls=%fused_computation.48 | loop fusion | bytes 2420740 | tf_op jit(solution)/shard_map/dynamic_slice | solution.py:474
  14.4 3.4 %collective-permute-start.4 = (bf16[1,96,768]{2,1,0:T(8,128)(2,1)S(1)}, bf16[1,96,768]{2,1,0:T(8,128)(2,1)S(1)}, u32[]{:S(2)}, u32[]{:S(2)}) collective-permute-start(bf16[1,96,768]{2,1,0:T(8,128)(2,1)S(1)} %bitcast.45), channel_id=1, source_target_pairs={{0,16},{1,17},{2,18},{3,19},{4,20},{5,21},{6,22},{7,23},{8,24},{9,... | collective-permute-start | bytes 442376 | tf_op jit(solution)/shard_map/ppermute | solution.py:31
  17.8 4.7 %collective-permute-done.4.refs_3_ = bf16[1,96,768]{2,1,0:T(8,128)(2,1)S(1)} collective-permute-done((bf16[1,96,768]{2,1,0:T(8,128)(2,1)S(1)}, bf16[1,96,768]{2,1,0:T(8,128)(2,1)S(1)}, u32[]{:S(2)}, u32[]{:S(2)}) %collective-permute-start.4) | collective-permute-done | bytes 147488 | tf_op jit(solution)/shard_map/ppermute | solution.py:31
  29.4 7.5 %collective-permute-done.7.refs_5_ = bf16[1,96,768]{2,1,0:T(8,128)(2,1)S(1)} collective-permute-done((bf16[1,96,768]{2,1,0:T(8,128)(2,1)S(1)}, bf16[1,96,768]{2,1,0:T(8,128)(2,1)S(1)}, u32[]{:S(2)}, u32[]{:S(2)}) %collective-permute-start.7) | collective-permute-done | bytes 147488 | tf_op jit(solution)/shard_map/ppermute | solution.py:31
  39.2 3.4 %collective-permute-start.12 = (bf16[2,96,768]{2,1,0:T(8,128)(2,1)S(1)}, bf16[2,96,768]{2,1,0:T(8,128)(2,1)S(1)}, u32[]{:S(2)}, u32[]{:S(2)}) collective-permute-start(bf16[2,96,768]{2,1,0:T(8,128)(2,1)S(1)} %get-tuple-element.65.refs_2_), channel_id=1, source_target_pairs={{0,8},{1,5},{2,10},{3,7},{4,12},{5,1},{6,14},{7,3},{8,0},{9,13},{1... | collective-permute-start | bytes 884744 | tf_op jit(solution)/shard_map/ppermute | solution.py:31
  42.6 7.9 %collective-permute-done.12.refs_3_ = bf16[2,96,768]{2,1,0:T(8,128)(2,1)S(1)} collective-permute-done((bf16[2,96,768]{2,1,0:T(8,128)(2,1)S(1)}, bf16[2,96,768]{2,1,0:T(8,128)(2,1)S(1)}, u32[]{:S(2)}, u32[]{:S(2)}) %collective-permute-start.12) | collective-permute-done | bytes 294944 | tf_op jit(solution)/shard_map/ppermute | solution.py:31
  50.5 3.5 %collective-permute-done.11.refs_1_ = bf16[4,96,768]{2,1,0:T(8,128)(2,1)S(1)} collective-permute-done((bf16[4,96,768]{2,1,0:T(8,128)(2,1)S(1)}, bf16[4,96,768]{2,1,0:T(8,128)(2,1)S(1)}, u32[]{:S(2)}, u32[]{:S(2)}) %collective-permute-start.11) | collective-permute-done | bytes 589856 | tf_op jit(solution)/shard_map/ppermute | solution.py:31
  62.2 12.2 %collective-permute-done.13.refs_4_.refs_9_ = bf16[8,96,768]{2,1,0:T(8,128)(2,1)} collective-permute-done((bf16[8,96,768]{2,1,0:T(8,128)(2,1)S(1)}, bf16[8,96,768]{2,1,0:T(8,128)(2,1)}, u32[]{:S(2)}, u32[]{:S(2)}) %collective-permute-start.13) | collective-permute-done | bytes 1179680 | tf_op jit(solution)/shard_map/ppermute | solution.py:31
  94.5 14.2 %shard_map.249 = (bf16[416,768]{1,0:T(8,128)(2,1)}, bf16[4,416,576]{2,1,0:T(8,128)(2,1)}, bf16[4,416,192]{2,1,0:T(8,128)(2,1)}, f32[416,768]{1,0:T(8,128)}, bf16[416,768]{1,0:T(8,128)(2,1)}) custom-call(s32[32]{0:T(128)} %select_n.55.index_ref, bf16[416,768]{1,0:T(8,128)(2,1)} %bitcast.35, f32[6,768]{1,0:T(8,128)} %convert_element_type.9.refs_1_.refs_5_.refs_7_.refs_6_, ...), custom_call_target="tpu_custom_call" | custom-call | flops 2494562304 | bytes 10497024 | tf_op jit(solution)/shard_map/pallas_call | solution.py:220
  111.0 8.1 %shard_map.251 = (bf16[2,416,768]{2,1,0:T(8,128)(2,1)}, bf16[2,416,768]{2,1,0:T(8,128)(2,1)}, bf16[16,96,768]{2,1,0:T(8,128)(2,1)}) custom-call(s32[32]{0:T(128)} %select_n.55.index_ref, bf16[416,768]{1,0:T(8,128)(2,1)} %get-tuple-element.68.refs_2_.refs_0_, bf16[416,768]{1,0:T(8,128)(2,1)} %bitcast.39, f32[4,1,768]{2,1,0:T(1,128)} %broadcast_in_dim.49.refs_2_, ...), custom_call_target="tpu_custom_call" | custom-call | flops 1962934272 | bytes 8564736 | tf_op jit(solution)/shard_map/pallas_call | solution.py:220
  121.5 15.9 %collective-permute-done.18.refs_11_ = bf16[8,96,768]{2,1,0:T(8,128)(2,1)S(1)} collective-permute-done((bf16[8,96,768]{2,1,0:T(8,128)(2,1)S(1)}, bf16[8,96,768]{2,1,0:T(8,128)(2,1)S(1)}, u32[]{:S(2)}, u32[]{:S(2)}) %collective-permute-start.18) | collective-permute-done | bytes 1179680 | tf_op jit(solution)/shard_map/ppermute | solution.py:31
  137.4 8.4 %shard_map.252 = (bf16[2,416,768]{2,1,0:T(8,128)(2,1)}, bf16[2,416,768]{2,1,0:T(8,128)(2,1)}, bf16[16,96,768]{2,1,0:T(8,128)(2,1)}) custom-call(s32[32]{0:T(128)} %select_n.55.index_ref, bf16[416,768]{1,0:T(8,128)(2,1)} %get-tuple-element.68.refs_2_.refs_0_, bf16[416,768]{1,0:T(8,128)(2,1)} %bitcast.40, f32[4,1,768]{2,1,0:T(1,128)} %broadcast_in_dim.49.refs_2_, ...), custom_call_target="tpu_custom_call" | custom-call | flops 1962934272 | bytes 8564736 | tf_op jit(solution)/shard_map/pallas_call | solution.py:220
  151.1 12.1 %shard_map.254 = (bf16[16,96,768]{2,1,0:T(8,128)(2,1)}, f32[2,1,768]{2,1,0:T(1,128)}, f32[416,768]{1,0:T(8,128)}, f32[416,768]{1,0:T(8,128)}) custom-call(s32[32]{0:T(128)} %select_n.55.index_ref, bf16[416,768]{1,0:T(8,128)(2,1)} %get-tuple-element.68.refs_2_.refs_0_, bf16[416,768]{1,0:T(8,128)(2,1)} %bitcast.41, ...), custom_call_target="tpu_custom_call" | custom-call | flops 3925868544 | bytes 16066560 | tf_op jit(solution)/shard_map/pallas_call | solution.py:220
  163.7 13.0 %shard_map.255 = (bf16[16,96,768]{2,1,0:T(8,128)(2,1)}, f32[2,1,768]{2,1,0:T(1,128)}, bf16[416,768]{1,0:T(8,128)(2,1)}, f32[416,768]{1,0:T(8,128)}, f32[4,1,768]{2,1,0:T(1,128)}) custom-call(s32[32]{0:T(128)} %select_n.55.index_ref, bf16[416,768]{1,0:T(8,128)(2,1)} %get-tuple-element.68.refs_2_.refs_0_, bf16[416,768]{1,0:T(8,128)(2,1)} %bitcast.42, ...), custom_call_target="tpu_custom_call" | custom-call | flops 3925868544 | bytes 16699392 | tf_op jit(solution)/shard_map/pallas_call | solution.py:220
  182.4 3.6 %shard_map.257 = (bf16[4,96,768]{2,1,0:T(8,128)(2,1)}, bf16[8,96,768]{2,1,0:T(8,128)(2,1)}) custom-call(bf16[16,96,768]{2,1,0:T(8,128)(2,1)} %get-tuple-element.75.refs_0_.refs_5_, bf16[16,96,768]{2,1,0:T(8,128)(2,1)} %copy-done.3, bf16[8,96,768]{2,1,0:T(8,128)(2,1)S(1)} %collective-permute-done.24.refs_2_.refs_7_, ...), custom_call_target="tpu_custom_call" | custom-call | bytes 7077888 | tf_op jit(solution)/shard_map/pallas_call | solution.py:175
  186.0 14.8 %shard_map.258 = (bf16[16,96,768]{2,1,0:T(8,128)(2,1)}, f32[2,1,576]{2,1,0:T(1,128)}, f32[416,768]{1,0:T(8,128)}) custom-call(s32[32]{0:T(128)} %select_n.55.index_ref, bf16[416,768]{1,0:T(8,128)(2,1)} %bitcast.36, bf16[416,768]{1,0:T(8,128)(2,1)} %get-tuple-element.80.refs_1_, bf16[4,416,576]{2,1,0:T(8,128)(2,1)} %get-tuple-element.81.refs_2_, ...), custom_call_target="tpu_custom_call" | custom-call | flops 2494562304 | bytes 11149824 | tf_op jit(solution)/shard_map/pallas_call | solution.py:220
  201.6 16.2 %collective-permute-done.26.refs_3_.refs_8_ = bf16[4,96,768]{2,1,0:T(8,128)(2,1)} collective-permute-done((bf16[4,96,768]{2,1,0:T(8,128)(2,1)}, bf16[4,96,768]{2,1,0:T(8,128)(2,1)}, u32[]{:S(2)}, u32[]{:S(2)}) %collective-permute-start.26) | collective-permute-done | bytes 589856 | tf_op jit(solution)/shard_map/ppermute | solution.py:31
  224.8 15.1 %shard_map.260 = (bf16[16,96,768]{2,1,0:T(8,128)(2,1)}, f32[2,1,576]{2,1,0:T(1,128)}, bf16[416,768]{1,0:T(8,128)(2,1)}, f32[2,1,768]{2,1,0:T(1,128)}) custom-call(s32[32]{0:T(128)} %select_n.55.index_ref, bf16[416,768]{1,0:T(8,128)(2,1)} %bitcast.37, bf16[416,768]{1,0:T(8,128)(2,1)} %get-tuple-element.80.refs_1_, ...), custom_call_target="tpu_custom_call" | custom-call | flops 2494562304 | bytes 11776512 | tf_op jit(solution)/shard_map/pallas_call | solution.py:220
  240.0 3.7 %shard_map.262 = (bf16[8,96,768]{2,1,0:T(8,128)(2,1)}, bf16[4,96,768]{2,1,0:T(8,128)(2,1)S(1)}, bf16[1,96,768]{2,1,0:T(8,128)(2,1)S(1)}) custom-call(bf16[16,96,768]{2,1,0:T(8,128)(2,1)} %get-tuple-element.95.refs_0_, bf16[16,96,768]{2,1,0:T(8,128)(2,1)} %collective-permute-done.35.refs_1_, ...), custom_call_target="tpu_custom_call" | custom-call | bytes 7667712 | tf_op jit(solution)/shard_map/pallas_call | solution.py:175
  263.7 8.9 %collective-permute-done.39.refs_6_.refs_7_.refs_3_ = bf16[4,96,768]{2,1,0:T(8,128)(2,1)} collective-permute-done((bf16[4,96,768]{2,1,0:T(8,128)(2,1)}, bf16[4,96,768]{2,1,0:T(8,128)(2,1)}, u32[]{:S(2)}, u32[]{:S(2)}) %collective-permute-start.39) | collective-permute-done | bytes 589856 | tf_op jit(solution)/shard_map/ppermute | solution.py:31
  287.3 4.6 %collective-permute-done.41.refs_8_.refs_4_ = bf16[2,96,768]{2,1,0:T(8,128)(2,1)S(1)} collective-permute-done((bf16[2,96,768]{2,1,0:T(8,128)(2,1)S(1)}, bf16[2,96,768]{2,1,0:T(8,128)(2,1)S(1)}, u32[]{:S(2)}, u32[]{:S(2)}) %collective-permute-start.41) | collective-permute-done | bytes 294944 | tf_op jit(solution)/shard_map/ppermute | solution.py:31
  300.3 3.7 %copy.32 = bf16[8,197,768]{2,0,1:T(8,128)(2,1)} copy(bf16[8,197,768]{2,1,0:T(8,128)(2,1)} %shard_map.256) | data formatting | bytes 4841472
  315.5 3.7 %copy.33 = bf16[8,197,768]{2,0,1:T(8,128)(2,1)} copy(bf16[8,197,768]{2,1,0:T(8,128)(2,1)} %shard_map.261) | data formatting | bytes 4841472
  (251 shorter events, 131.5 us)
Async XLA Ops:
  37.7 19.4 %collective-permute-start.8 = (bf16[8,96,768]{2,1,0:T(8,128)(2,1)S(1)}, bf16[8,96,768]{2,1,0:T(8,128)(2,1)S(1)}, u32[]{:S(2)}, u32[]{:S(2)}) collective-permute-start(bf16[8,96,768]{2,1,0:T(8,128)(2,1)S(1)} %get-tuple-element.63.refs_3_.refs_7_), channel_id=1, source_target_pairs={{0,4},{1,3},{2,6},{3,1},{4,0},{5,7},{6,2},{7,5},{8,12},{9,11},{10,... | collective-permute-start | bytes 3538952 | tf_op jit(solution)/shard_map/ppermute | solution.py:31
  58.3 17.8 %collective-permute-start = (bf16[1,1152]{1,0:T(2,128)(2,1)S(1)}, bf16[1,1152]{1,0:T(2,128)(2,1)S(1)}, u32[]{:S(2)}, u32[]{:S(2)}) collective-permute-start(bf16[1,1152]{1,0:T(2,128)(2,1)S(1)} %broadcast_in_dim.43), channel_id=1, source_target_pairs={{0,1},{1,0},{2,3},{3,2},{4,5},{5,4},{6,7},{7,6},{8,9},{9,8},{10,11... | collective-permute-start | bytes 6920 | tf_op jit(solution)/shard_map/ppermute | solution.py:36
  61.6 32.9 %collective-permute-start.9 = (bf16[8,96,768]{2,1,0:T(8,128)(2,1)S(1)}, bf16[8,96,768]{2,1,0:T(8,128)(2,1)}, u32[]{:S(2)}, u32[]{:S(2)}) collective-permute-start(bf16[8,96,768]{2,1,0:T(8,128)(2,1)S(1)} %get-tuple-element.63.refs_3_.refs_7_), channel_id=1, source_target_pairs={{0,1},{1,0},{2,3},{3,2},{4,5},{5,4},{6,7},{7,6},{8,9},{9,8},{10,11... | collective-permute-start | bytes 3538952 | tf_op jit(solution)/shard_map/ppermute | solution.py:36
  61.7 32.8 %collective-permute-start.10 = (bf16[8,96,768]{2,1,0:T(8,128)(2,1)S(1)}, bf16[8,96,768]{2,1,0:T(8,128)(2,1)}, u32[]{:S(2)}, u32[]{:S(2)}) collective-permute-start(bf16[8,96,768]{2,1,0:T(8,128)(2,1)S(1)} %collective-permute-done.8.refs_4_.refs_8_), channel_id=1, source_target_pairs={{0,1},{1,0},{2,3},{3,2},{4,5},{5,4},{6,7},{7,6},{8,9},{9,8},{10,11... | collective-permute-start | bytes 3538952 | tf_op jit(solution)/shard_map/ppermute | solution.py:36
  62.1 48.9 %collective-permute-start.14 = (bf16[8,96,768]{2,1,0:T(8,128)(2,1)S(1)}, bf16[8,96,768]{2,1,0:T(8,128)(2,1)}, u32[]{:S(2)}, u32[]{:S(2)}) collective-permute-start(bf16[8,96,768]{2,1,0:T(8,128)(2,1)S(1)} %get-tuple-element.66.refs_7_.refs_3_.refs_8_), channel_id=1, source_target_pairs={{0,1},{1,0},{2,3},{3,2},{4,5},{5,4},{6,7},{7,6},{8,9},{9,8},{10,11... | collective-permute-start | bytes 3538952 | tf_op jit(solution)/shard_map/ppermute | solution.py:36
  74.5 36.6 %collective-permute-start.15 = (bf16[8,96,768]{2,1,0:T(8,128)(2,1)}, bf16[8,96,768]{2,1,0:T(8,128)(2,1)}, u32[]{:S(2)}, u32[]{:S(2)}) collective-permute-start(bf16[8,96,768]{2,1,0:T(8,128)(2,1)} %collective-permute-done.13.refs_4_.refs_9_), channel_id=1, source_target_pairs={{0,1},{1,0},{2,3},{3,2},{4,5},{5,4},{6,7},{7,6},{8,9},{9,8},{10,11... | collective-permute-start | bytes 3538952 | tf_op jit(solution)/shard_map/ppermute | solution.py:36
  91.1 17.6 %collective-permute-start.16 = (bf16[4,96,768]{2,1,0:T(8,128)(2,1)}, bf16[4,96,768]{2,1,0:T(8,128)(2,1)S(1)}, u32[]{:S(2)}, u32[]{:S(2)}) collective-permute-start(bf16[4,96,768]{2,1,0:T(8,128)(2,1)} %copy-done.26), channel_id=1, source_target_pairs={{0,2},{1,9},{2,0},{3,11},{4,6},{5,13},{6,4},{7,15},{8,10},{9,1},{1... | collective-permute-start | bytes 1769480 | tf_op jit(solution)/shard_map/ppermute | solution.py:31
  119.2 26.7 %collective-permute-start.20 = (bf16[16,96,768]{2,1,0:T(8,128)(2,1)}, bf16[16,96,768]{2,1,0:T(8,128)(2,1)S(1)}, u32[]{:S(2)}, u32[]{:S(2)}) collective-permute-start(bf16[16,96,768]{2,1,0:T(8,128)(2,1)} %get-tuple-element.69.refs_5_), channel_id=1, source_target_pairs={{0,1},{1,0},{2,3},{3,2},{4,5},{5,4},{6,7},{7,6},{8,9},{9,8},{10,11... | collective-permute-start | bytes 7077896 | tf_op jit(solution)/shard_map/ppermute | solution.py:36
  121.5 28.3 %collective-permute-start.17 = (bf16[8,96,768]{2,1,0:T(8,128)(2,1)S(1)}, bf16[8,96,768]{2,1,0:T(8,128)(2,1)S(1)}, u32[]{:S(2)}, u32[]{:S(2)}) collective-permute-start(bf16[8,96,768]{2,1,0:T(8,128)(2,1)S(1)} %copy-done.16), channel_id=1, source_target_pairs={{0,1},{1,0},{2,3},{3,2},{4,5},{5,4},{6,7},{7,6},{8,9},{9,8},{10,11... | collective-permute-start | bytes 3538952 | tf_op jit(solution)/shard_map/ppermute | solution.py:36
  200.8 39.2 %collective-permute-start.35 = (bf16[16,96,768]{2,1,0:T(8,128)(2,1)}, bf16[16,96,768]{2,1,0:T(8,128)(2,1)}, u32[]{:S(2)}, u32[]{:S(2)}) collective-permute-start(bf16[16,96,768]{2,1,0:T(8,128)(2,1)} %get-tuple-element.96), channel_id=1, source_target_pairs={{0,1},{1,0},{2,3},{3,2},{4,5},{5,4},{6,7},{7,6},{8,9},{9,8},{10,11... | collective-permute-start | bytes 7077896 | tf_op jit(solution)/shard_map/ppermute | solution.py:36
  200.9 39.1 %collective-permute-start.36 = (bf16[8,96,768]{2,1,0:T(8,128)(2,1)}, bf16[8,96,768]{2,1,0:T(8,128)(2,1)S(1)}, u32[]{:S(2)}, u32[]{:S(2)}) collective-permute-start(bf16[8,96,768]{2,1,0:T(8,128)(2,1)} %get-tuple-element.86.refs_10_), channel_id=1, source_target_pairs={{0,4},{1,3},{2,6},{3,1},{4,0},{5,7},{6,2},{7,5},{8,12},{9,11},{10,... | collective-permute-start | bytes 3538952 | tf_op jit(solution)/shard_map/ppermute | solution.py:31
  221.5 18.4 %collective-permute-start.37 = (bf16[2,96,768]{2,1,0:T(8,128)(2,1)S(1)}, bf16[2,96,768]{2,1,0:T(8,128)(2,1)S(1)}, u32[]{:S(2)}, u32[]{:S(2)}) collective-permute-start(bf16[2,96,768]{2,1,0:T(8,128)(2,1)S(1)} %shard_map.259.refs_9_), channel_id=1, source_target_pairs={{0,8},{1,5},{2,10},{3,7},{4,12},{5,1},{6,14},{7,3},{8,0},{9,13},{1... | collective-permute-start | bytes 884744 | tf_op jit(solution)/shard_map/ppermute | solution.py:31
  223.0 55.4 %collective-permute-start.22 = (bf16[2,208,768]{2,1,0:T(8,128)(2,1)}, bf16[2,208,768]{2,1,0:T(8,128)(2,1)}, u32[]{:S(2)}, u32[]{:S(2)}) collective-permute-start(bf16[2,208,768]{2,1,0:T(8,128)(2,1)} %bitcast.12.refs_0_), channel_id=1, source_target_pairs={{0,2},{1,3},{2,0},{3,1},{4,6},{5,7},{6,4},{7,5},{8,10},{9,11},{10,... | collective-permute-start | bytes 1916936 | tf_op jit(solution)/shard_map/ppermute | solution.py:36
  245.2 27.4 %collective-permute-start.38 = (bf16[8,96,768]{2,1,0:T(8,128)(2,1)}, bf16[8,96,768]{2,1,0:T(8,128)(2,1)}, u32[]{:S(2)}, u32[]{:S(2)}) collective-permute-start(bf16[8,96,768]{2,1,0:T(8,128)(2,1)} %get-tuple-element.97), channel_id=1, source_target_pairs={{0,4},{1,3},{2,6},{3,1},{4,0},{5,7},{6,2},{7,5},{8,12},{9,11},{10,... | collective-permute-start | bytes 3538952 | tf_op jit(solution)/shard_map/ppermute | solution.py:31
  250.9 35.5 %collective-permute-start.28 = (bf16[2,208,768]{2,1,0:T(8,128)(2,1)}, bf16[2,208,768]{2,1,0:T(8,128)(2,1)}, u32[]{:S(2)}, u32[]{:S(2)}) collective-permute-start(bf16[2,208,768]{2,1,0:T(8,128)(2,1)} %bitcast.13.refs_0_), channel_id=1, source_target_pairs={{0,2},{1,3},{2,0},{3,1},{4,6},{5,7},{6,4},{7,5},{8,10},{9,11},{10,... | collective-permute-start | bytes 1916936 | tf_op jit(solution)/shard_map/ppermute | solution.py:36
  254.6 18.0 %collective-permute-start.39 = (bf16[4,96,768]{2,1,0:T(8,128)(2,1)}, bf16[4,96,768]{2,1,0:T(8,128)(2,1)}, u32[]{:S(2)}, u32[]{:S(2)}) collective-permute-start(bf16[4,96,768]{2,1,0:T(8,128)(2,1)} %copy-done.30), channel_id=1, source_target_pairs={{0,2},{1,9},{2,0},{3,11},{4,6},{5,13},{6,4},{7,15},{8,10},{9,1},{1... | collective-permute-start | bytes 1769480 | tf_op jit(solution)/shard_map/ppermute | solution.py:31
  274.4 17.5 %collective-permute-start.40 = (bf16[4,96,768]{2,1,0:T(8,128)(2,1)S(1)}, bf16[4,96,768]{2,1,0:T(8,128)(2,1)S(1)}, u32[]{:S(2)}, u32[]{:S(2)}) collective-permute-start(bf16[4,96,768]{2,1,0:T(8,128)(2,1)S(1)} %get-tuple-element.99), channel_id=1, source_target_pairs={{0,2},{1,9},{2,0},{3,11},{4,6},{5,13},{6,4},{7,15},{8,10},{9,1},{1... | collective-permute-start | bytes 1769480 | tf_op jit(solution)/shard_map/ppermute | solution.py:31
  275.6 19.7 %collective-permute-start.21 = (bf16[2,208,768]{2,1,0:T(8,128)(2,1)}, bf16[2,208,768]{2,1,0:T(8,128)(2,1)}, u32[]{:S(2)}, u32[]{:S(2)}) collective-permute-start(bf16[2,208,768]{2,1,0:T(8,128)(2,1)} %bitcast.12.refs_0_), channel_id=1, source_target_pairs={{0,1},{1,0},{2,3},{3,2},{4,5},{5,4},{6,7},{7,6},{8,9},{9,8},{10,11... | collective-permute-start | bytes 1916936 | tf_op jit(solution)/shard_map/ppermute | solution.py:36
  278.5 18.6 %collective-permute-start.23 = (bf16[2,208,768]{2,1,0:T(8,128)(2,1)}, bf16[2,208,768]{2,1,0:T(8,128)(2,1)}, u32[]{:S(2)}, u32[]{:S(2)}) collective-permute-start(bf16[2,208,768]{2,1,0:T(8,128)(2,1)} %collective-permute-done.22.refs_2_), channel_id=1, source_target_pairs={{0,1},{1,0},{2,3},{3,2},{4,5},{5,4},{6,7},{7,6},{8,9},{9,8},{10,11... | collective-permute-start | bytes 1916936 | tf_op jit(solution)/shard_map/ppermute | solution.py:36
  291.9 19.5 %collective-permute-start.27 = (bf16[2,208,768]{2,1,0:T(8,128)(2,1)}, bf16[2,208,768]{2,1,0:T(8,128)(2,1)S(1)}, u32[]{:S(2)}, u32[]{:S(2)}) collective-permute-start(bf16[2,208,768]{2,1,0:T(8,128)(2,1)} %bitcast.13.refs_0_), channel_id=1, source_target_pairs={{0,1},{1,0},{2,3},{3,2},{4,5},{5,4},{6,7},{7,6},{8,9},{9,8},{10,11... | collective-permute-start | bytes 1916936 | tf_op jit(solution)/shard_map/ppermute | solution.py:36
  291.9 19.5 %collective-permute-start.29 = (bf16[2,208,768]{2,1,0:T(8,128)(2,1)}, bf16[2,208,768]{2,1,0:T(8,128)(2,1)}, u32[]{:S(2)}, u32[]{:S(2)}) collective-permute-start(bf16[2,208,768]{2,1,0:T(8,128)(2,1)} %collective-permute-done.28.refs_2_), channel_id=1, source_target_pairs={{0,1},{1,0},{2,3},{3,2},{4,5},{5,4},{6,7},{7,6},{8,9},{9,8},{10,11... | collective-permute-start | bytes 1916936 | tf_op jit(solution)/shard_map/ppermute | solution.py:36
  304.1 16.9 %collective-permute-start.45 = (bf16[1,96,768]{2,1,0:T(8,128)(2,1)S(1)}, bf16[1,96,768]{2,1,0:T(8,128)(2,1)S(1)}, u32[]{:S(2)}, u32[]{:S(2)}) collective-permute-start(bf16[1,96,768]{2,1,0:T(8,128)(2,1)S(1)} %copy-done.32), channel_id=1, source_target_pairs={{0,16},{1,17},{2,18},{3,19},{4,20},{5,21},{6,22},{7,23},{8,24},{9,... | collective-permute-start | bytes 442376 | tf_op jit(solution)/shard_map/ppermute | solution.py:31
  305.3 18.8 %collective-permute-start.44 = (bf16[1,96,768]{2,1,0:T(8,128)(2,1)S(1)}, bf16[1,96,768]{2,1,0:T(8,128)(2,1)S(1)}, u32[]{:S(2)}, u32[]{:S(2)}) collective-permute-start(bf16[1,96,768]{2,1,0:T(8,128)(2,1)S(1)} %get-tuple-element.102), channel_id=1, source_target_pairs={{0,16},{1,17},{2,18},{3,19},{4,20},{5,21},{6,22},{7,23},{8,24},{9,... | collective-permute-start | bytes 442376 | tf_op jit(solution)/shard_map/ppermute | solution.py:31
  308.1 18.4 %collective-permute-start.43 = (bf16[1,96,768]{2,1,0:T(8,128)(2,1)S(1)}, bf16[1,96,768]{2,1,0:T(8,128)(2,1)S(1)}, u32[]{:S(2)}, u32[]{:S(2)}) collective-permute-start(bf16[1,96,768]{2,1,0:T(8,128)(2,1)S(1)} %shard_map.265), channel_id=1, source_target_pairs={{0,16},{1,17},{2,18},{3,19},{4,20},{5,21},{6,22},{7,23},{8,24},{9,... | collective-permute-start | bytes 442376 | tf_op jit(solution)/shard_map/ppermute | solution.py:31
  (66 other events, 610.4 us)

commit v5 on v4

--- a/solution.py
+++ b/solution.py
@@ -11,6 +11,7 @@
 EPS = 1e-06
 AXES = ("dp", "tensor")
 TILE = 16
+ROWS = 32
 FACTOR = HEAD_DIM ** (-0.5)
 bf16 = jnp.bfloat16
 f32 = jnp.float32
@@ -35,23 +36,15 @@
     def flip(self, value, bit):
         return lax.ppermute(value, AXES, [(i, i ^ (1 << bit)) for i in range(self.n)])
 
-    def table(self):
-        if not self.fast:
-            return jnp.zeros((1,), jnp.int32)
-        rows = lax.axis_index("dp") ^ jnp.arange(self.n_dp)
-        core = lax.axis_index("tensor") & 1
-        relative = (rows[None, :] << 2) | (jnp.arange(2)[:, None] << 1)
+    def at(self, ids_ref, core, y, block):
+        relative = ((ids_ref[0] ^ block) << 2) | (y << 1)
         found = []
         for order in self.orders:
-            place = relative * 0
+            place = 0
             for k, bit in enumerate(order[::-1]):
                 place = place | (((relative >> bit) & 1) << k)
             found.append(place)
-        both = jnp.where(core == 0, jnp.stack(found), jnp.stack(found[::-1]))
-        return both.reshape(-1).astype(jnp.int32)
-
-    def at(self, table_ref, core, y, block):
-        return table_ref[(core * 2 + y) * self.n_dp + block]
+        return jnp.where((ids_ref[1] & 1) == core, found[0], found[1])
 
     def buffers(self, cols):
         blocks = (self.half, self.rows, cols) if self.fast else (1, 8, 128)
@@ -76,7 +69,7 @@
 
         return wait
 
-    def load(self, table_ref, refs, scratch, core, y):
+    def load(self, ids_ref, refs, scratch, core, y):
         held, shard, sems = scratch
         if not self.fast:
             copy = pltpu.make_async_copy(refs[0].at[2 * y + core], shard, sems.at[0])
@@ -84,15 +77,15 @@
             copy.wait()
             return
         for d in range(self.n_dp):
-            shard[d * self.rows : (d + 1) * self.rows, :] = held[self.at(table_ref, core, y, d)]
-
-    def store(self, table_ref, ref, core, y, value):
+            shard[d * self.rows : (d + 1) * self.rows, :] = held[self.at(ids_ref, core, y, d)]
+
+    def store(self, ids_ref, ref, core, y, value):
         if not self.fast:
             ref[y] = value
             return
         for d in range(self.n_dp):
             rows = value[d * self.rows : (d + 1) * self.rows]
-            ref[self.at(table_ref, core, y, d)] = rows
+            ref[self.at(ids_ref, core, y, d)] = rows
 
     def grad_shape(self, cols):
         if not self.fast:
@@ -168,28 +161,122 @@
     return plain_call(kernel, [jax.ShapeDtypeStruct(block[1:], f32)], group, specs, after)[0]
 
 
-def plain_call(kernel, shapes, inputs, specs, after):
-    moved = 2 * sum(x.size * x.dtype.itemsize for x in shapes)
+def plain_call(kernel, shapes, inputs, specs, after, ids=None, scratch=()):
     if specs is None:
         specs = [pl.BlockSpec(x.shape, lambda i: (0, 0, 0)) for x in inputs]
+    if ids is not None:
+        specs = [pl.BlockSpec(memory_space=pltpu.SMEM)] + specs
+        inputs = [ids, *inputs]
     return pl.pallas_call(
         kernel,
         grid=(1,),
         out_shape=shapes,
         in_specs=specs + [pl.BlockSpec(memory_space=pl.ANY)] * len(after),
         out_specs=[pl.BlockSpec(x.shape, lambda i, n=len(x.shape): (0,) * n) for x in shapes],
+        scratch_shapes=list(scratch),
         compiler_params=pltpu.CompilerParams(vmem_limit_bytes=48 * 1024 * 1024),
-        cost_estimate=pl.CostEstimate(flops=0, bytes_accessed=2 * moved, transcendentals=0),
+        cost_estimate=pl.CostEstimate(flops=0, bytes_accessed=1024, transcendentals=0),
     )(*inputs, *after)
 
 
-def sum_all(cube, value):
-    if not cube.fast:
-        return lax.psum(value, AXES)
-    value = value + cube.flip(value, 0)
-    for k in range(cube.steps):
-        value = value + cube.flip(value, cube.orders[0][k])
-    return value
+def sends_with_small(cube, group, groups, small, ids, after=()):
+    rows = cube.rows
+    kept = [v.shape[0] // rows * rows for v in group]
+    size = min(kept) // 2
+    d = group[0].shape[1]
+    first = len(small) > 1
+    specs, inputs = [], list(group)
+    for v in group:
+        if v.shape[0] % size == 0:
+            specs.append(pl.BlockSpec((size, d), lambda i: (1, 0)))
+        else:
+            specs.append(pl.BlockSpec(v.shape, lambda i: (0, 0)))
+    exact = [v.shape[0] % size == 0 for v in group]
+    for v in small:
+        specs.append(pl.BlockSpec(v.shape, lambda i, n=len(v.shape): (0,) * n))
+        inputs.append(v)
+    sizes = [min(v.shape[0] for v in g) // 2 for g in groups]
+    shapes = [
+        jax.ShapeDtypeStruct((size + ROWS, d), bf16),
+        jax.ShapeDtypeStruct((ROWS, d), bf16),
+    ]
+    for g, half in zip(groups, sizes):
+        block = (half,) + g[0].shape[1:]
+        specs += [pl.BlockSpec(block, lambda i: (1, 0, 0)) for _ in g]
+        shapes.append(jax.ShapeDtypeStruct(block, bf16))
+        inputs += g
+    n_out = len(shapes)
+
+    def kernel(ids_ref, *refs):
+        outs = refs[len(inputs) + len(after) :]
+        total_ref = outs[n_out]
+        terms = refs[: len(group)]
+        value = None
+        for ref, whole in zip(terms, exact):
+            part = (ref[...] if whole else ref[size : 2 * size, :]).astype(f32)
+            value = part if value is None else value + part
+        outs[0][:size, :] = value.astype(bf16)
+        extra = refs[len(group) : len(group) + len(small)]
+        if first:
+            gather_small(cube, ids_ref, extra, total_ref)
+        else:
+            last = terms[-1]
+            total_ref[...] = extra[0][...].astype(f32) + last[kept[-1] :, :].astype(f32)
+        low = total_ref[...].astype(bf16)
+        outs[0][size:, :] = low
+        outs[1][...] = low
+        start = len(group) + len(small)
+        for g, out in zip(groups, outs[2:n_out]):
+            value = refs[start][...].astype(f32)
+            for ref in refs[start + 1 : start + len(g)]:
+                value = value + ref[...].astype(f32)
+            out[...] = value.astype(bf16)
+            start += len(g)
+
+    return plain_call(kernel, shapes, inputs, specs, after, ids, [pltpu.VMEM((ROWS, d), f32)])
+
+
+def gather_small(cube, ids_ref, refs, out_ref):
+    attn_ref, mlp_ref = refs[:2]
+    out_ref[...] = jnp.zeros_like(out_ref)
+    for i in range(2):
+        out_ref[i : i + 1, :] = attn_ref[i]
+    for i in range(4):
+        out_ref[2 + i : 3 + i, :] = mlp_ref[i]
+    n_t = cube.n_t
+    for core in range(2):
+        for y in range(n_t // 2):
+            t = (2 * y + core) ^ ids_ref[1]
+            dbias = refs[2 + core][y]
+            width = dbias.shape[1] // 3
+            out_ref[pl.ds(6 + t, 1), :] = refs[4 + core][y]
+            out_ref[pl.ds(6 + n_t + t, 1), :width] = dbias[:, :width]
+            out_ref[pl.ds(6 + 2 * n_t + t, 1), :width] = dbias[:, 2 * width :]
+
+
+def finish_with_small(cube, group, small):
+    rows = cube.rows
+    d = group[0].shape[1]
+    tail = group[-1].shape[0] - rows
+    specs = [
+        pl.BlockSpec((rows, d), lambda i: (0, 0))
+        if v.shape[0] % rows == 0
+        else pl.BlockSpec(v.shape, lambda i: (0, 0))
+        for v in group
+    ]
+    specs.append(pl.BlockSpec(small.shape, lambda i: (0, 0)))
+
+    def kernel(*refs):
+        value = None
+        for ref in refs[: len(group)]:
+            part = ref[:rows, :].astype(f32)
+            value = part if value is None else value + part
+        refs[-2][...] = value
+        extra = refs[len(group) - 1][rows : rows + tail, :].astype(f32)
+        refs[-1][...] = (refs[len(group)][...].astype(f32) + extra).astype(bf16)
+
+    shapes = [jax.ShapeDtypeStruct((rows, d), f32), jax.ShapeDtypeStruct(small.shape, bf16)]
+    return plain_call(kernel, shapes, [*group, small], specs, ())
 
 
 def place_images(cube, pieces, length, after=()):
@@ -204,13 +291,10 @@
                 refs[-1][(index_ref[0] ^ r) * count + i] = refs[r][i, :length, :]
 
     shape = (4 * count, length, pieces[0].shape[2])
-    return call(kernel, [jax.ShapeDtypeStruct(shape, bf16)], index, pieces, [], [], 0, after)[0]
-
-
-def call(kernel, out_shapes, index, inputs, weights, scratch, flops, after=()):
-    inputs_all = [*inputs, *weights]
-    moved = sum(x.size * x.dtype.itemsize for x in inputs_all)
-    moved += sum(x.size * x.dtype.itemsize for x in out_shapes)
+    return call(kernel, [jax.ShapeDtypeStruct(shape, bf16)], index, pieces, [], [], after)[0]
+
+
+def call(kernel, out_shapes, index, inputs, weights, scratch, after=()):
     n_in, n_w, n_out = len(inputs), len(weights), len(out_shapes)
 
     def body(index_ref, *refs):
@@ -226,7 +310,7 @@
         out_specs=[pl.BlockSpec(memory_space=pltpu.VMEM)] * n_out,
         scratch_shapes=scratch,
         compiler_params=pltpu.CompilerParams(vmem_limit_bytes=56 * 1024 * 1024),
-        cost_estimate=pl.CostEstimate(flops=flops, bytes_accessed=moved, transcendentals=0),
+        cost_estimate=pl.CostEstimate(flops=0, bytes_accessed=1024, transcendentals=0),
     )(index, *inputs, *weights, *after)
 
 
@@ -262,52 +346,56 @@
     return jnp.sum(values, 0, keepdims=True)
 
 
-def attend_kernel(cube, count, length, width, n_w, table_ref, *refs):
-    x_ref, vec_ref, bias_ref = refs[:3]
-    w_refs = refs[3 : 3 + n_w]
-    n1_ref, qkv_ref, att_ref, hidden_ref, n2_ref = refs[3 + n_w : 8 + n_w]
-    scratch, sum_ref = (refs[8 + n_w : 11 + n_w], refs[11 + n_w : 14 + n_w]), refs[14 + n_w]
-    waits = [cube.fetch(cube.of_core(w_refs, core), scratch[core]) for core in range(2)]
-    x = x_ref[...].astype(f32)
-    normed, _ = normed_of(x)
-    n1_ref[...] = (normed * vec_ref[0:1] + vec_ref[1:2]).astype(bf16)
-    sum_ref[...] = x + vec_ref[2:3]
-    tokens = x.shape[0] // count
+def attend_kernel(cube, core, first, count, length, width, n_w, ids_ref, *refs):
+    x_ref, n1_in, sum_in, vec_ref, bias_ref = refs[:5]
+    w_refs = refs[5 : 5 + n_w]
+    qkv_ref, att_ref = refs[5 + n_w : 7 + n_w]
+    scratch = refs[9 + n_w : 12 + n_w]
+    wait = cube.fetch(w_refs, scratch)
+    if first:
+        n1_ref, sum_ref = refs[7 + n_w : 9 + n_w]
+        x = x_ref[...].astype(f32)
+        normed, _ = normed_of(x)
+        n1_ref[...] = (normed * vec_ref[0:1] + vec_ref[1:2]).astype(bf16)
+        sum_ref[...] = x + vec_ref[2:3]
+    else:
+        hidden_ref, n2_ref = refs[7 + n_w : 9 + n_w]
+        n1_ref, sum_ref = n1_in, hidden_ref
+        sum_ref[...] = sum_in[...]
+    tokens = x_ref.shape[0] // count
     heads = width // HEAD_DIM
     keep = lax.broadcasted_iota(jnp.int32, (tokens, tokens), 1) < length
 
-    for core in range(2):
-        waits[core]()
-        w_ref = scratch[core][1]
-
-        def step(y, carry):
-            t = 2 * y + core
-            cube.load(table_ref, cube.of_core(w_refs, core), scratch[core], core, y)
-            qkv = nn(n1_ref[...], w_ref[:, : 3 * width]) + bias_ref[t]
-            qkv_ref[t] = qkv.astype(bf16)
-            for b in range(count):
-                rows = slice(b * tokens, (b + 1) * tokens)
-                found = []
-                for h in range(heads):
-                    q = qkv_ref[t, rows, h * HEAD_DIM : (h + 1) * HEAD_DIM]
-                    k = qkv_ref[t, rows, width + h * HEAD_DIM : width + (h + 1) * HEAD_DIM]
-                    v = qkv_ref[t, rows, 2 * width + h * HEAD_DIM : 2 * width + (h + 1) * HEAD_DIM]
-                    scores = jnp.where(keep, nt(q, k) * FACTOR, -1e30)
-                    weights = jnp.exp(scores - jnp.max(scores, -1, keepdims=True))
-                    probs = weights * (1.0 / jnp.sum(weights, -1, keepdims=True))
-                    found.append(nn(probs.astype(bf16), v).astype(bf16))
-                att_ref[t, rows, :] = jnp.concatenate(found, axis=1)
-            sum_ref[...] += nt(att_ref[t], w_ref[:, 3 * width :])
-            return carry
-
-        lax.fori_loop(0, cube.n_t // 2, step, 0)
-    hidden = sum_ref[...]
-    hidden_ref[...] = hidden
-    normed, _ = normed_of(hidden)
+    wait()
+    w_ref = scratch[1]
+
+    def step(y, carry):
+        cube.load(ids_ref, w_refs, scratch, core, y)
+        qkv = nn(n1_ref[...], w_ref[:, : 3 * width]) + bias_ref[2 * y + core]
+        qkv_ref[y] = qkv.astype(bf16)
+        for b in range(count):
+            rows = slice(b * tokens, (b + 1) * tokens)
+            found = []
+            for h in range(heads):
+                q = qkv_ref[y, rows, h * HEAD_DIM : (h + 1) * HEAD_DIM]
+                k = qkv_ref[y, rows, width + h * HEAD_DIM : width + (h + 1) * HEAD_DIM]
+                v = qkv_ref[y, rows, 2 * width + h * HEAD_DIM : 2 * width + (h + 1) * HEAD_DIM]
+                scores = jnp.where(keep, nt(q, k) * FACTOR, -1e30)
+                weights = jnp.exp(scores - jnp.max(scores, -1, keepdims=True))
+                probs = weights * (1.0 / jnp.sum(weights, -1, keepdims=True))
+                found.append(nn(probs.astype(bf16), v).astype(bf16))
+            att_ref[y, rows, :] = jnp.concatenate(found, axis=1)
+        sum_ref[...] += nt(att_ref[y], w_ref[:, 3 * width :])
+        return carry
+
+    lax.fori_loop(0, cube.n_t // 2, step, 0)
+    if first:
+        return
+    normed, _ = normed_of(hidden_ref[...])
     n2_ref[...] = (normed * vec_ref[3:4] + vec_ref[4:5]).astype(bf16)
 
 
-def gelu_kernel(cube, core, n_w, table_ref, *refs):
+def gelu_kernel(cube, core, n_w, ids_ref, *refs):
     n2_ref, cot_ref, bias_ref = refs[:3]
     w_refs = refs[3 : 3 + n_w]
     act_ref, slope_ref, grad_ref = refs[3 + n_w : 6 + n_w]
@@ -315,19 +403,19 @@
     cube.fetch(w_refs, scratch)()
 
     def step(y, carry):
-        cube.load(table_ref, w_refs, scratch, core, y)
+        cube.load(ids_ref, w_refs, scratch, core, y)
         pre = nn(n2_ref[...], scratch[1][...]) + bias_ref[2 * y + core]
         cdf = 0.5 * (1.0 + lax.erf(pre * (0.5**0.5)))
         slope = cdf + pre * (jnp.exp(-0.5 * pre * pre) * 0.3989422804014327)
         act_ref[y] = (pre * cdf).astype(bf16)
         slope_ref[y] = slope.astype(bf16)
-        cube.store(table_ref, grad_ref, core, y, tn(cot_ref[...], act_ref[y]).astype(bf16))
+        cube.store(ids_ref, grad_ref, core, y, tn(cot_ref[...], act_ref[y]).astype(bf16))
         return carry
 
     lax.fori_loop(0, cube.n_t // 2, step, 0)
 
 
-def mlp_kernel(cube, core, first, n_w, table_ref, *refs):
+def mlp_kernel(cube, core, first, n_w, ids_ref, *refs):
     n2_ref, cot_ref, act_ref, slope_ref, mlp_in, dnorm_in, hidden_ref, vec_ref = refs[:8]
     one_refs, two_refs = refs[8 : 8 + n_w], refs[8 + n_w : 8 + 2 * n_w]
     outs = refs[8 + 2 * n_w :]
@@ -346,12 +434,12 @@
         wait()
 
     def step(y, carry):
-        cube.load(table_ref, one_refs, one, core, y)
-        cube.load(table_ref, two_refs, two, core, y)
+        cube.load(ids_ref, one_refs, one, core, y)
+        cube.load(ids_ref, two_refs, two, core, y)
         dact = nn(cot_ref[...], two[1][...])
         dpre = (slope_ref[y].astype(f32) * dact).astype(bf16)
         sums_ref[pl.ds(y, 1)] = column_sum(dpre.astype(f32))[None]
-        cube.store(table_ref, grad_ref, core, y, tn(n2_ref[...], dpre).astype(bf16))
+        cube.store(ids_ref, grad_ref, core, y, tn(n2_ref[...], dpre).astype(bf16))
         dnorm_ref[...] += nt(dpre, one[1][...])
         mlp_ref[...] += nt(act_ref[y], two[1][...])
         return carry
@@ -376,7 +464,7 @@
     small_ref[3] = column_sum(dhidden)
 
 
-def attend_back_kernel(cube, core, first, count, length, width, n_w, table_ref, *refs):
+def attend_back_kernel(cube, core, first, count, length, width, n_w, ids_ref, *refs):
     x_ref, n1_ref, qkv_ref, att_ref, dhidden_ref, dnorm_in, vec_ref = refs[:7]
     w_refs = refs[7 : 7 + n_w]
     outs = refs[7 + n_w :]
@@ -385,12 +473,10 @@
         dnorm_ref = outs[2]
         rest = outs[3:]
     else:
-        patch_ref, small_ref = outs[2:4]
+        dnorm_ref, small_ref = outs[2:4]
         rest = outs[4:]
     scratch = rest[:3]
     low_ref, dqkv_ref = rest[3:5]
-    if not first:
-        dnorm_ref = rest[5]
     wait = cube.fetch(w_refs, scratch)
     low_ref[...] = dhidden_ref[...].astype(bf16)
     dnorm_ref[...] = jnp.zeros_like(dnorm_ref) if first else dnorm_in[...]
@@ -401,16 +487,15 @@
     w_ref = scratch[1]
 
     def step(y, carry):
-        t = 2 * y + core
-        cube.load(table_ref, w_refs, scratch, core, y)
+        cube.load(ids_ref, w_refs, scratch, core, y)
         datt = nn(low_ref[...], w_ref[:, 3 * width :]).astype(bf16)
         for b in range(count):
             rows = slice(b * tokens, (b + 1) * tokens)
             dqs, dks, dvs = [], [], []
             for h in range(heads):
-                q = qkv_ref[t, rows, h * HEAD_DIM : (h + 1) * HEAD_DIM]
-                k = qkv_ref[t, rows, width + h * HEAD_DIM : width + (h + 1) * HEAD_DIM]
-                v = qkv_ref[t, rows, 2 * width + h * HEAD_DIM : 2 * width + (h + 1) * HEAD_DIM]
+                q = qkv_ref[y, rows, h * HEAD_DIM : (h + 1) * HEAD_DIM]
+                k = qkv_ref[y, rows, width + h * HEAD_DIM : width + (h + 1) * HEAD_DIM]
+                v = qkv_ref[y, rows, 2 * width + h * HEAD_DIM : 2 * width + (h + 1) * HEAD_DIM]
                 do = datt[rows, h * HEAD_DIM : (h + 1) * HEAD_DIM]
                 scores = jnp.where(keep, nt(k, q) * FACTOR, -1e30)
                 weights = jnp.exp(scores - jnp.max(scores, 0, keepdims=True))
@@ -425,19 +510,23 @@
         dqkv = dqkv_ref[...]
         dbias_ref[pl.ds(y, 1)] = column_sum(dqkv.astype(f32))[None]
         dnorm_ref[...] += nt(dqkv, w_ref[:, : 3 * width])
-        grad = jnp.concatenate((tn(n1_ref[...], dqkv), tn(low_ref[...], att_ref[t])), axis=1)
-        cube.store(table_ref, grad_ref, core, y, grad.astype(bf16))
+        grad = jnp.concatenate((tn(n1_ref[...], dqkv), tn(low_ref[...], att_ref[y])), axis=1)
+        cube.store(ids_ref, grad_ref, core, y, grad.astype(bf16))
         return carry
 
     lax.fori_loop(0, cube.n_t // 2, step, 0)
     if first:
         return
-    normed, inverse = normed_of(x_ref[...].astype(f32))
+    normed, _ = normed_of(x_ref[...].astype(f32))
     dnorm = dnorm_ref[...]
-    patch = dhidden_ref[...] + norm_back(dnorm, normed, inverse, vec_ref[0:1])
-    patch_ref[...] = patch.astype(bf16)
     small_ref[0] = column_sum(dnorm * normed)
     small_ref[1] = column_sum(dnorm)
+
+
+def patch_kernel(ids_ref, x_ref, dhidden_ref, dnorm_ref, vec_ref, patch_ref):
+    normed, inverse = normed_of(x_ref[...].astype(f32))
+    patch = dhidden_ref[...] + norm_back(dnorm_ref[...], normed, inverse, vec_ref[0:1])
+    patch_ref[...] = patch.astype(bf16)
 
 
 def on_device(
@@ -464,7 +553,7 @@
     width = qkv_weight.shape[2]
     f_width = fc1_weight.shape[1]
     d = patches.shape[2]
-    table = cube.table()
+    ids = jnp.stack((lax.axis_index("dp"), t_me)).astype(jnp.int32)
     count = patches.shape[0] // n_t
     length = patches.shape[1]
     padded = -(-length // TILE) * TILE
@@ -504,16 +593,12 @@
             pairs = [(held, cube.swap(held, k))]
             if k < last:
                 pairs.append((one, cube.swap(one, k + 1)))
-            if k < last - 1:
-                pairs.append((two, cube.swap(two, k + 2)))
-            found = join(pairs, (x, cot) if k == last else ())
-            if k == last:
-                one, two = lax.optimization_barrier((one, two))
+            tokens_in = (x, cot) if k == last else (vecs, qkv_bias, f_bias) if k == 1 else ()
+            found = join(pairs, tokens_in)
             held = found[0]
             one = found[1] if k < last else one
-            two = found[2] if k < last - 1 else two
         came = cube.swap(held, 0)
-        pairs = [(one, cube.swap(one, 1)), (two, cube.swap(two, 2))]
+        pairs = [(one, cube.swap(one, 1)), (two, cube.swap(two, last))]
         w_attn = [held, came, cube.flip(held, 0), cube.flip(came, 0)]
         one, two = join(pairs, (came,))
         slot = (one, two)
@@ -524,28 +609,31 @@
         biases = jnp.take(lax.all_gather(biases[0], "tensor", axis=0, tiled=False), order, axis=0)
         qkv_bias, f_bias = bias_parts(biases)
         slot = ()
-    n_w = len(w_attn)
     n_c = len(cube.of_core(w_attn, 0))
-    spots = 2 * tokens * d * n_t
-    attn_macs = spots * 2 * width + 4 * count * n_t * padded * padded * width
     buffers = cube.buffers(d)
 
-    n1, qkv, att, hidden, n2 = call(
-        partial(attend_kernel, cube, count, length, width, n_w),
-        [
-            shape(tokens, d),
-            shape(n_t, tokens, 3 * width),
-            shape(n_t, tokens, width),
-            shape(tokens, d, dtype=f32),
-            shape(tokens, d),
-        ],
-        table,
-        [x, vecs, qkv_bias],
-        w_attn,
-        buffers * 2 + [pltpu.VMEM((tokens, d), f32)],
-        2 * attn_macs,
-        slot,
-    )
+    def attend(core, first, n1, sums, after):
+        if first:
+            outs = [shape(tokens, d), shape(tokens, d, dtype=f32)]
+        else:
+            outs = [shape(tokens, d, dtype=f32), shape(tokens, d)]
+        return call(
+            partial(attend_kernel, cube, core, first, count, length, width, n_c),
+            [shape(n_t // 2, tokens, 3 * width), shape(n_t // 2, tokens, width)] + outs,
+            ids,
+            [x, n1, sums, vecs, qkv_bias],
+            cube.of_core(w_attn, core),
+            buffers,
+            after,
+        )
+
+    qkv_own, att_own, n1, sums = attend(0, True, vecs, vecs, slot)
+    if cube.fast:
+        for k in range(last - 1, 1, -1):
+            two = join([(two, cube.swap(two, k))], (n1,))[0]
+        slot = (two,)
+    qkv_other, att_other, hidden, n2 = attend(1, False, n1, sums, slot)
+    qkvs, atts = (qkv_own, qkv_other), (att_own, att_other)
     if cube.fast:
         came = cube.swap(one, 0)
         w_one = [one, came, cube.flip(one, 0), cube.flip(came, 0)]
@@ -556,24 +644,19 @@
         return call(
             partial(gelu_kernel, cube, core, n_c),
             [shape(n_t // 2, tokens, f_width)] * 2 + [cube.grad_shape(f_width)],
-            table,
+            ids,
             [n2, cot, f_bias],
             cube.of_core(w_one, core),
             buffers,
-            spots * f_width,
             after,
         )
 
-    act_other, slope_other, two_other = gelu(1, slot)
-    act_own, slope_own, two_own = gelu(0, (two_other,))
+    act_own, slope_own, two_own = gelu(0, slot)
+    act_other, slope_other, two_other = gelu(1, (two_own,))
     if cube.fast:
         came = cube.swap(two, 0)
         w_two = [two, came, cube.flip(two, 0), cube.flip(came, 0)]
         two_terms = [two_own, cube.flip(two_other, 0)]
-        (s_two,) = sends([two_terms], ())
-        slot = (s_two,)
-    else:
-        slot = ()
 
     def mlp(core, first, act, slope, mlp_in, dnorm_in, after):
         if first:
@@ -585,24 +668,28 @@
         return call(
             partial(mlp_kernel, cube, core, first, n_c),
             [cube.grad_shape(f_width), shape(n_t // 2, 1, f_width, dtype=f32)] + outs,
-            table,
+            ids,
             [n2, cot, act, slope, mlp_in, dnorm_in, hidden, vecs],
             [*cube.of_core(w_one, core), *cube.of_core(w_two, core)],
             buffers * 2 + scratch,
-            2 * spots * f_width,
             after,
         )
 
-    one_other, f_other, mlp_sum, dnorm = mlp(1, True, act_other, slope_other, hidden, vecs, slot)
-    one_own, f_own, enc, dhidden, mlp_small = mlp(
-        0, False, act_own, slope_own, mlp_sum, dnorm, (one_other,)
+    one_own, f_own, mlp_sum, dnorm = mlp(0, True, act_own, slope_own, hidden, vecs, (two_other,))
+    slot = (one_own,)
+    if cube.fast:
+        (s_two,) = sends([two_terms], (dnorm,))
+        slot = (s_two,)
+    one_other, f_other, enc, dhidden, mlp_small = mlp(
+        1, False, act_other, slope_other, mlp_sum, dnorm, slot
     )
     images = enc.reshape(count, padded, d)
+    slot = ()
     if cube.fast:
         two_terms.append(cube.swap(s_two, 0))
         one_terms = [one_own, cube.flip(one_other, 0)]
-        s_two, s_one = sends([two_terms, one_terms], (dhidden,))
-        slot = (s_two, s_one)
+        (s_two,) = sends([two_terms], (dhidden,))
+        slot = (s_two,)
         there = cube.flip(images, 1)
         enc_pieces = [images, cube.flip(images, 0), there, cube.flip(there, 0)]
     else:
@@ -613,101 +700,100 @@
             outs = [shape(tokens, d, dtype=f32)]
             scratch = []
         else:
-            outs = [shape(tokens, d), shape(2, 1, d, dtype=f32)]
-            scratch = [pltpu.VMEM((tokens, d), f32)]
+            outs = [shape(tokens, d, dtype=f32), shape(2, 1, d, dtype=f32)]
+            scratch = []
         return call(
             partial(attend_back_kernel, cube, core, first, count, length, width, n_c),
             [cube.grad_shape(4 * width), shape(n_t // 2, 1, 3 * width, dtype=f32)] + outs,
-            table,
-            [x, n1, qkv, att, dhidden, dnorm_in, vecs],
+            ids,
+            [x, n1, qkvs[core], atts[core], dhidden, dnorm_in, vecs],
             cube.of_core(w_attn, core),
             buffers
             + [pltpu.VMEM((tokens, d), bf16), pltpu.VMEM((tokens, 3 * width), bf16)]
             + scratch,
-            2 * attn_macs,
             after,
         )
 
     attn_other, dbias_other, dnorm = attend_back(1, True, vecs, slot)
     if cube.fast:
         two_terms.append(cube.swap(s_two, 1))
-        (s_two,) = sends([two_terms], (dnorm,))
-        slot = (s_two,)
-    attn_own, dbias_own, patch, attn_small = attend_back(0, False, dnorm, slot)
-    images = patch.reshape(count, padded, d)
+        s_one, s_two = sends([one_terms, two_terms], (dnorm,))
+        slot = (s_one, s_two)
+    attn_own, dbias_own, dnorm, attn_small = attend_back(0, False, dnorm, slot)
+
+    def patch_of(after):
+        patch = call(
+            patch_kernel, [shape(tokens, d)], ids, [x, dhidden, dnorm, vecs], [], [], after
+        )[0]
+        return patch.reshape(count, padded, d)
+
     if cube.fast:
+        one_terms.append(cube.swap(s_one, 0))
+        two_terms.append(cube.swap(s_two, 2))
+        flat = (cube.half * cube.rows, d)
+        attn_terms = [attn_own.reshape(flat), cube.flip(attn_other.reshape(flat), 0)]
+        small = (attn_small, mlp_small, dbias_own, dbias_other, f_own, f_other)
+        k_one, k_two = 1, 3
+        for k in range(cube.steps):
+            groups = [one_terms] if k_one <= last else []
+            groups += [two_terms] if k_two <= last else []
+            found = sends_with_small(cube, attn_terms, groups, small, ids)
+            small = (found[1],)
+            if k == 1:
+                images = patch_of((found[1],))
+            attn_terms.append(cube.swap(found[0], k))
+            if k_one <= last:
+                one_terms.append(cube.swap(found[2], k_one))
+            if k_two <= last:
+                two_terms.append(cube.swap(found[3], k_two))
+            k_one, k_two = (k_one + 1, k_two + 1)
         there = cube.flip(images, 1)
         patch_pieces = [images, cube.flip(images, 0), there, cube.flip(there, 0)]
-        two_terms.append(cube.swap(s_two, 2))
-        one_terms.append(cube.swap(s_one, 0))
-        attn_terms = [attn_own, cube.flip(attn_other, 0)]
-        s_attn, s_one, s_two = sends([attn_terms, one_terms, two_terms])
-        k_attn, k_one, k_two = 0, 1, 3
-        while True:
-            attn_terms.append(cube.swap(s_attn, k_attn))
-            if k_one <= last:
-                one_terms.append(cube.swap(s_one, k_one))
-            if k_two <= last:
-                two_terms.append(cube.swap(s_two, k_two))
-            k_attn, k_one, k_two = (k_attn + 1, k_one + 1, k_two + 1)
-            if k_attn > last:
-                break
-            groups = [attn_terms]
-            groups += [one_terms] if k_one <= last else []
-            groups += [two_terms] if k_two <= last else []
-            found = sends(groups)
-            s_attn = found[0]
-            s_one = found[1] if k_one <= last else None
-            s_two = found[2] if k_two <= last else None
         two_grad = finish(two_terms)
         one_grad = finish(one_terms)
-        attn_grad = finish(attn_terms)
+        attn_grad, small = finish_with_small(cube, attn_terms, small[0])
+        small = small.astype(f32) + cube.flip(small, 0).astype(f32)
     else:
-        patch_pieces = [images]
+        patch_pieces = [patch_of(())]
         two_grad = scatter_plain(cube, two_own, two_other)
         one_grad = scatter_plain(cube, one_own, one_other)
         attn_grad = scatter_plain(cube, attn_own, attn_other)
     encoded = place_images(cube, enc_pieces, length)
     patch_grad = place_images(cube, patch_pieces, length)
 
-    def in_order(own, other):
-        both = jnp.stack((own[:, 0], other[:, 0]), axis=1)
-        return jnp.take(both.reshape((n_t,) + own.shape[2:]), order, axis=0)
-
-    dbias = in_order(dbias_own, dbias_other)
-    f_sums = in_order(f_own, f_other)
-    small = jnp.concatenate(
-        (
-            attn_small.reshape(-1),
-            mlp_small.reshape(-1),
-            dbias[:, :width].reshape(-1),
-            dbias[:, 2 * width :].reshape(-1),
-            f_sums.reshape(-1),
-        )
-    )
-    small = sum_all(cube, small)
-    cuts = [small[i * d : (i + 1) * d] for i in range(6)]
-    at = 6 * d
-    q_sum = lax.dynamic_slice_in_dim(small[at : at + n_t * width], t_me * width, width, 0)
-    at += n_t * width
-    v_sum = lax.dynamic_slice_in_dim(small[at : at + n_t * width], t_me * width, width, 0)
-    at += n_t * width
-    f_sum = lax.dynamic_slice_in_dim(small[at:], t_me * f_width, f_width, 0)
+    if not cube.fast:
+
+        def collect(ids_ref, *refs):
+            gather_small(cube, ids_ref, refs[:6], refs[6])
+
+        small = call(
+            collect,
+            [shape(ROWS, d, dtype=f32)],
+            ids,
+            [attn_small, mlp_small, dbias_own, dbias_other, f_own, f_other],
+            [],
+            [],
+        )[0]
+        small = lax.psum(small, AXES)
+
+    def shard_row(at):
+        return lax.dynamic_slice_in_dim(small, at + t_me, 1, 0)
+
     return (
         encoded,
         patch_grad,
-        cuts[0],
-        cuts[1],
+        small[0],
+        small[1],
         jnp.stack([attn_grad[:, i * width : (i + 1) * width] for i in range(3)]),
-        jnp.stack((q_sum, v_sum)),
+        jnp.concatenate((shard_row(6 + n_t), shard_row(6 + 2 * n_t)))[:, :width],
         attn_grad[:, 3 * width :].T,
-        cuts[5],
-        cuts[2],
-        cuts[3],
+        small[5],
+        small[2],
+        small[3],
         one_grad,
-        f_sum,
+        shard_row(6)[0],
         two_grad.T,
-        cuts[4],
+        small[4],
     )
 
 

time: 331 us -> 323 us (0.976)
  local copies, waits for them, and re-layouts: 53.3 us -> 34.7 us
  Pallas kernels: 111 us -> 122 us
  waiting for transfers between devices: 102 us -> 112 us
  other arithmetic: 11.6 us -> 2.16 us
    another operation x7, local copies, waits for them, and re-layouts: 8.97 us -> 0.07 us  [on_device(): jnp.stack((attn_gain, attn_shift, out_bias, mlp_gain, mlp_shift, fc2_bias))]
    pallas_call x9 -> x11, Pallas kernels: 92.3 us -> 99.9 us  [call(): pl.pallas_call(body, out_shape=out_shapes, in_specs=[pl.BlockSpec(memory_...]
    ppermute x22 -> x18, waiting for transfers between devices: 6.37 us -> 12.7 us  [flip(): return lax.ppermute(value, AXES, [(i, i ^ 1 << bit) for i in range(self.n)])]
    ppermute x22 -> x18, starting transfers between devices: 17.3 us -> 12.4 us  [flip(): return lax.ppermute(value, AXES, [(i, i ^ 1 << bit) for i in range(self.n)])]
    ppermute x24, starting transfers between devices: 32.9 us -> 37.4 us  [swap(): lax.ppermute(value, AXES, [(i, i ^ 1 << self.orders[i & 1][k]) for i in r...]
    ppermute x24, waiting for transfers between devices: 95.6 us -> 99.6 us  [swap(): lax.ppermute(value, AXES, [(i, i ^ 1 << self.orders[i & 1][k]) for i in r...]
    pallas_call x15 -> x16, Pallas kernels: 18.4 us -> 21.6 us  [plain_call(): pl.pallas_call(kernel, grid=(1,), out_shape=shapes, in_specs=specs + [pl....]
    unnamed x98 -> x148, local copies, waits for them, and re-layouts: 29.1 us -> 29.1 us
  transfers between devices with their start and end apart: 46 -> 42, of which waited for: 20 -> 19; matrix products, arithmetic and copies ran while one was open for 14% -> 4% of each run, Pallas kernels for 22% -> 32%
where the time goes in v5:
time: 323 us; the launch traced here: 322 us
  Pallas kernels  122 us (38%)
  waiting for transfers between devices  112 us (35%)
  starting transfers between devices  49.8 us (15%)
  local copies, waits for them, and re-layouts  34.7 us (11%)
    pallas_call x11, Pallas kernels, call(): pl.pallas_call(body, out_shape=out_shapes, in_specs=[pl.BlockSpec(memory_...  99.9 us
    ppermute x24, waiting for transfers between devices, swap(): lax.ppermute(value, AXES, [(i, i ^ 1 << self.orders[i & 1][k]) for i in r...  99.6 us
    ppermute x24, starting transfers between devices, swap(): lax.ppermute(value, AXES, [(i, i ^ 1 << self.orders[i & 1][k]) for i in r...  37.4 us
    unnamed x148, local copies, waits for them, and re-layouts  29.1 us
    pallas_call x16, Pallas kernels, plain_call(): pl.pallas_call(kernel, grid=(1,), out_shape=shapes, in_specs=specs + [pl....  21.6 us
    ppermute x18, waiting for transfers between devices, flip(): return lax.ppermute(value, AXES, [(i, i ^ 1 << bit) for i in range(self.n)])  12.7 us
    ppermute x18, starting transfers between devices, flip(): return lax.ppermute(value, AXES, [(i, i ^ 1 << bit) for i in range(self.n)])  12.4 us
  transfers between devices with their start and end apart: 42, of which 19 were waited for; matrix products, arithmetic and copies ran while one was open for 4% of the time, Pallas kernels for 32%

profile of v5, /device:TPU:0, one launch (start us, length us, event | category | flops | bytes accessed | tf_op | source)
XLA Modules:
  0.0 322.0 jit_solution(12488118845461232122)
XLA Ops:
  2.5 4.1 %collective-permute-start.2 = (bf16[1,96,768]{2,1,0:T(8,128)(2,1)S(1)}, bf16[1,96,768]{2,1,0:T(8,128)(2,1)S(1)}, u32[]{:S(2)}, u32[]{:S(2)}) collective-permute-start(bf16[1,96,768]{2,1,0:T(8,128)(2,1)S(1)} %maximum_bitcast_fusion.refs_0_), channel_id=1, source_target_pairs={{0,16},{1,17},{2,18},{3,19},{4,20},{5,21},{6,22},{7,23},{8,24},{9,... | collective-permute-start | bytes 442376 | tf_op jit(solution)/shard_map/ppermute | solution.py:32
  18.1 4.5 %collective-permute-done.4.refs_3_ = bf16[1,96,768]{2,1,0:T(8,128)(2,1)S(1)} collective-permute-done((bf16[1,96,768]{2,1,0:T(8,128)(2,1)S(1)}, bf16[1,96,768]{2,1,0:T(8,128)(2,1)S(1)}, u32[]{:S(2)}, u32[]{:S(2)}) %collective-permute-start.4) | collective-permute-done | bytes 147488 | tf_op jit(solution)/shard_map/ppermute | solution.py:32
  26.2 7.5 %collective-permute-done.1 = bf16[2,1152]{1,0:T(2,128)(2,1)S(1)} collective-permute-done((bf16[2,1152]{1,0:T(2,128)(2,1)S(1)}, bf16[2,1152]{1,0:T(2,128)(2,1)S(1)}, u32[]{:S(2)}, u32[]{:S(2)}) %collective-permute-start.1) | collective-permute-done | bytes 4640 | tf_op jit(solution)/shard_map/ppermute | solution.py:37
  36.0 9.4 %collective-permute-done.6.refs_3_ = bf16[2,96,768]{2,1,0:T(8,128)(2,1)S(1)} collective-permute-done((bf16[2,96,768]{2,1,0:T(8,128)(2,1)S(1)}, bf16[2,96,768]{2,1,0:T(8,128)(2,1)S(1)}, u32[]{:S(2)}, u32[]{:S(2)}) %collective-permute-start.6) | collective-permute-done | bytes 294944 | tf_op jit(solution)/shard_map/ppermute | solution.py:32
  51.0 5.7 %collective-permute-done.9.refs_3_ = bf16[1,96,768]{2,1,0:T(8,128)(2,1)S(1)} collective-permute-done((bf16[1,96,768]{2,1,0:T(8,128)(2,1)S(1)}, bf16[1,96,768]{2,1,0:T(8,128)(2,1)S(1)}, u32[]{:S(2)}, u32[]{:S(2)}) %collective-permute-start.9) | collective-permute-done | bytes 147488 | tf_op jit(solution)/shard_map/ppermute | solution.py:32
  56.7 6.1 %collective-permute-done.8.refs_1_ = bf16[4,96,768]{2,1,0:T(8,128)(2,1)S(1)} collective-permute-done((bf16[4,96,768]{2,1,0:T(8,128)(2,1)S(1)}, bf16[4,96,768]{2,1,0:T(8,128)(2,1)S(1)}, u32[]{:S(2)}, u32[]{:S(2)}) %collective-permute-start.8) | collective-permute-done | bytes 589856 | tf_op jit(solution)/shard_map/ppermute | solution.py:32
  65.9 14.5 %collective-permute-done.14.refs_4_.refs_9_ = bf16[8,96,768]{2,1,0:T(8,128)(2,1)} collective-permute-done((bf16[8,96,768]{2,1,0:T(8,128)(2,1)S(1)}, bf16[8,96,768]{2,1,0:T(8,128)(2,1)}, u32[]{:S(2)}, u32[]{:S(2)}) %collective-permute-start.14) | collective-permute-done | bytes 1179680 | tf_op jit(solution)/shard_map/ppermute | solution.py:32
  81.4 8.8 %shard_map.249 = (bf16[2,416,576]{2,1,0:T(8,128)(2,1)}, bf16[2,416,192]{2,1,0:T(8,128)(2,1)}, bf16[416,768]{1,0:T(8,128)(2,1)}, f32[416,768]{1,0:T(8,128)}) custom-call(s32[2]{0:T(128)} %pad_add_fusion.index_ref.ids_ref, bf16[416,768]{1,0:T(8,128)(2,1)} %bitcast.38, f32[6,768]{1,0:T(8,128)} %copy-done.28, f32[6,768]{1,0:T(8,128)} %copy-done.28, ...), custom_call_target="tpu_custom_call" | custom-call | bytes 1024 | tf_op jit(solution)/shard_map/pallas_call | solution.py:304
  95.6 9.8 %shard_map.251 = (bf16[2,416,576]{2,1,0:T(8,128)(2,1)}, bf16[2,416,192]{2,1,0:T(8,128)(2,1)}, f32[416,768]{1,0:T(8,128)}, bf16[416,768]{1,0:T(8,128)(2,1)}) custom-call(s32[2]{0:T(128)} %pad_add_fusion.index_ref.ids_ref, bf16[416,768]{1,0:T(8,128)(2,1)} %bitcast.39, bf16[416,768]{1,0:T(8,128)(2,1)} %get-tuple-element.72.refs_2_.refs_1_, ...), custom_call_target="tpu_custom_call" | custom-call | bytes 1024 | tf_op jit(solution)/shard_map/pallas_call | solution.py:304
  108.6 8.5 %shard_map.253 = (bf16[2,416,768]{2,1,0:T(8,128)(2,1)}, bf16[2,416,768]{2,1,0:T(8,128)(2,1)}, bf16[16,96,768]{2,1,0:T(8,128)(2,1)}) custom-call(s32[2]{0:T(128)} %pad_add_fusion.index_ref.ids_ref, bf16[416,768]{1,0:T(8,128)(2,1)} %get-tuple-element.74.refs_2_.refs_0_, bf16[416,768]{1,0:T(8,128)(2,1)} %bitcast.44, f32[4,1,768]{2,1,0:T(1,128)} %copy-done.45, ...), custom_call_target="tpu_custom_call" | custom-call | bytes 1024 | tf_op jit(solution)/shard_map/pallas_call | solution.py:304
  117.1 8.6 %shard_map.254 = (bf16[2,416,768]{2,1,0:T(8,128)(2,1)}, bf16[2,416,768]{2,1,0:T(8,128)(2,1)}, bf16[16,96,768]{2,1,0:T(8,128)(2,1)}) custom-call(s32[2]{0:T(128)} %pad_add_fusion.index_ref.ids_ref, bf16[416,768]{1,0:T(8,128)(2,1)} %get-tuple-element.74.refs_2_.refs_0_, bf16[416,768]{1,0:T(8,128)(2,1)} %bitcast.45, f32[4,1,768]{2,1,0:T(1,128)} %copy-done.45, ...), custom_call_target="tpu_custom_call" | custom-call | bytes 1024 | tf_op jit(solution)/shard_map/pallas_call | solution.py:304
  127.1 15.2 %collective-permute-done.17.refs_11_ = bf16[8,96,768]{2,1,0:T(8,128)(2,1)} collective-permute-done((bf16[8,96,768]{2,1,0:T(8,128)(2,1)S(1)}, bf16[8,96,768]{2,1,0:T(8,128)(2,1)}, u32[]{:S(2)}, u32[]{:S(2)}) %collective-permute-start.17) | collective-permute-done | bytes 1179680 | tf_op jit(solution)/shard_map/ppermute | solution.py:32
  142.3 12.2 %shard_map.255 = (bf16[16,96,768]{2,1,0:T(8,128)(2,1)}, f32[2,1,768]{2,1,0:T(1,128)}, f32[416,768]{1,0:T(8,128)}, f32[416,768]{1,0:T(8,128)}) custom-call(s32[2]{0:T(128)} %pad_add_fusion.index_ref.ids_ref, bf16[416,768]{1,0:T(8,128)(2,1)} %get-tuple-element.74.refs_2_.refs_0_, bf16[416,768]{1,0:T(8,128)(2,1)} %bitcast.46, ...), custom_call_target="tpu_custom_call" | custom-call | bytes 1024 | tf_op jit(solution)/shard_map/pallas_call | solution.py:304
  160.9 13.1 %shard_map.257 = (bf16[16,96,768]{2,1,0:T(8,128)(2,1)}, f32[2,1,768]{2,1,0:T(1,128)}, bf16[416,768]{1,0:T(8,128)(2,1)}, f32[416,768]{1,0:T(8,128)}, f32[4,1,768]{2,1,0:T(1,128)}) custom-call(s32[2]{0:T(128)} %pad_add_fusion.index_ref.ids_ref, bf16[416,768]{1,0:T(8,128)(2,1)} %get-tuple-element.74.refs_2_.refs_0_, bf16[416,768]{1,0:T(8,128)(2,1)} %bitcast.47, ...), custom_call_target="tpu_custom_call" | custom-call | bytes 1024 | tf_op jit(solution)/shard_map/pallas_call | solution.py:304
  179.0 14.4 %shard_map.260 = (bf16[16,96,768]{2,1,0:T(8,128)(2,1)}, f32[2,1,576]{2,1,0:T(1,128)}, f32[416,768]{1,0:T(8,128)}) custom-call(s32[2]{0:T(128)} %pad_add_fusion.index_ref.ids_ref, bf16[416,768]{1,0:T(8,128)(2,1)} %bitcast.40, bf16[416,768]{1,0:T(8,128)(2,1)} %get-tuple-element.72.refs_2_.refs_1_, bf16[2,416,576]{2,1,0:T(8,128)(2,1)} %get-tuple-element.88.refs_2_, ...), custom_call_target="tpu_custom_call" | custom-call | bytes 1024 | tf_op jit(solution)/shard_map/pallas_call | solution.py:304
  194.8 8.6 %collective-permute-done.26.refs_5_.refs_14_.refs_3_ = bf16[4,96,768]{2,1,0:T(8,128)(2,1)S(1)} collective-permute-done((bf16[4,96,768]{2,1,0:T(8,128)(2,1)S(1)}, bf16[4,96,768]{2,1,0:T(8,128)(2,1)S(1)}, u32[]{:S(2)}, u32[]{:S(2)}) %collective-permute-start.26) | collective-permute-done | bytes 589856 | tf_op jit(solution)/shard_map/ppermute | solution.py:32
  209.7 14.7 %shard_map.262 = (bf16[16,96,768]{2,1,0:T(8,128)(2,1)}, f32[2,1,576]{2,1,0:T(1,128)}, f32[416,768]{1,0:T(8,128)}, f32[2,1,768]{2,1,0:T(1,128)}) custom-call(s32[2]{0:T(128)} %pad_add_fusion.index_ref.ids_ref, bf16[416,768]{1,0:T(8,128)(2,1)} %bitcast.41, bf16[416,768]{1,0:T(8,128)(2,1)} %get-tuple-element.72.refs_2_.refs_1_, ...), custom_call_target="tpu_custom_call" | custom-call | bytes 1024 | tf_op jit(solution)/shard_map/pallas_call | solution.py:304
  229.1 3.9 %shard_map.263 = (bf16[800,768]{1,0:T(8,128)(2,1)S(1)}, bf16[32,768]{1,0:T(8,128)(2,1)S(1)}, bf16[4,96,768]{2,1,0:T(8,128)(2,1)S(1)}, bf16[1,96,768]{2,1,0:T(8,128)(2,1)}) custom-call(s32[2]{0:T(128)S(1)} %copy-done.50, bf16[1536,768]{1,0:T(8,128)(2,1)} %bitcast.32, bf16[1536,768]{1,0:T(8,128)(2,1)} %copy-done.61, f32[2,1,768]{2,1,0:T(1,128)S(1)} %copy-done.57, ...), custom_call_target="tpu_custom_call" | custom-call | bytes 1024 | tf_op jit(solution)/shard_map/pallas_call | solution.py:170
  235.9 14.2 %collective-permute-done.31.refs_7_.refs_8_.refs_3_ = bf16[4,96,768]{2,1,0:T(8,128)(2,1)S(1)} collective-permute-done((bf16[4,96,768]{2,1,0:T(8,128)(2,1)S(1)}, bf16[4,96,768]{2,1,0:T(8,128)(2,1)S(1)}, u32[]{:S(2)}, u32[]{:S(2)}) %collective-permute-start.31) | collective-permute-done | bytes 589856 | tf_op jit(solution)/shard_map/ppermute | solution.py:32
  258.8 5.1 %collective-permute-done.22.refs_2_ = bf16[2,208,768]{2,1,0:T(8,128)(2,1)} collective-permute-done((bf16[2,208,768]{2,1,0:T(8,128)(2,1)}, bf16[2,208,768]{2,1,0:T(8,128)(2,1)}, u32[]{:S(2)}, u32[]{:S(2)}) %collective-permute-start.22) | collective-permute-done | bytes 639008 | tf_op jit(solution)/shard_map/ppermute | solution.py:37
  264.0 4.0 %collective-permute-start.23 = (bf16[2,208,768]{2,1,0:T(8,128)(2,1)}, bf16[2,208,768]{2,1,0:T(8,128)(2,1)}, u32[]{:S(2)}, u32[]{:S(2)}) collective-permute-start(bf16[2,208,768]{2,1,0:T(8,128)(2,1)} %collective-permute-done.22.refs_2_), channel_id=1, source_target_pairs={{0,1},{1,0},{2,3},{3,2},{4,5},{5,4},{6,7},{7,6},{8,9},{9,8},{10,11... | collective-permute-start | bytes 1916936 | tf_op jit(solution)/shard_map/ppermute | solution.py:37
  276.1 6.0 %collective-permute-done.37.refs_4_ = bf16[224,768]{1,0:T(8,128)(2,1)S(1)} collective-permute-done((bf16[224,768]{1,0:T(8,128)(2,1)S(1)}, bf16[224,768]{1,0:T(8,128)(2,1)S(1)}, u32[]{:S(2)}, u32[]{:S(2)}) %collective-permute-start.37) | collective-permute-done | bytes 344096 | tf_op jit(solution)/shard_map/ppermute | solution.py:32
  294.3 3.7 %copy.34 = bf16[8,197,768]{2,0,1:T(8,128)(2,1)} copy(bf16[8,197,768]{2,1,0:T(8,128)(2,1)} %shard_map.258) | data formatting | bytes 4841472
  298.1 8.1 %collective-permute-done.41.refs_5_ = bf16[1,96,768]{2,1,0:T(8,128)(2,1)} collective-permute-done((bf16[1,96,768]{2,1,0:T(8,128)(2,1)}, bf16[1,96,768]{2,1,0:T(8,128)(2,1)}, u32[]{:S(2)}, u32[]{:S(2)}) %collective-permute-start.41) | collective-permute-done | bytes 147488 | tf_op jit(solution)/shard_map/ppermute | solution.py:32
  (265 shorter events, 109.9 us)
Async XLA Ops:
  23.7 21.6 %collective-permute-start.5 = (bf16[4,96,768]{2,1,0:T(8,128)(2,1)S(1)}, bf16[4,96,768]{2,1,0:T(8,128)(2,1)S(1)}, u32[]{:S(2)}, u32[]{:S(2)}) collective-permute-start(bf16[4,96,768]{2,1,0:T(8,128)(2,1)S(1)} %get-tuple-element.66.refs_0_), channel_id=1, source_target_pairs={{0,2},{1,9},{2,0},{3,11},{4,6},{5,13},{6,4},{7,15},{8,10},{9,1},{1... | collective-permute-start | bytes 1769480 | tf_op jit(solution)/shard_map/ppermute | solution.py:32
  46.5 16.4 %collective-permute-start.7 = (bf16[8,96,768]{2,1,0:T(8,128)(2,1)}, bf16[8,96,768]{2,1,0:T(8,128)(2,1)S(1)}, u32[]{:S(2)}, u32[]{:S(2)}) collective-permute-start(bf16[8,96,768]{2,1,0:T(8,128)(2,1)} %get-tuple-element.68.refs_5_.refs_7_), channel_id=1, source_target_pairs={{0,4},{1,3},{2,6},{3,1},{4,0},{5,7},{6,2},{7,5},{8,12},{9,11},{10,... | collective-permute-start | bytes 3538952 | tf_op jit(solution)/shard_map/ppermute | solution.py:32
  63.9 16.4 %collective-permute-start.14 = (bf16[8,96,768]{2,1,0:T(8,128)(2,1)S(1)}, bf16[8,96,768]{2,1,0:T(8,128)(2,1)}, u32[]{:S(2)}, u32[]{:S(2)}) collective-permute-start(bf16[8,96,768]{2,1,0:T(8,128)(2,1)S(1)} %get-tuple-element.70.refs_7_.refs_3_.refs_8_), channel_id=1, source_target_pairs={{0,4},{1,3},{2,6},{3,1},{4,0},{5,7},{6,2},{7,5},{8,12},{9,11},{10,... | collective-permute-start | bytes 3538952 | tf_op jit(solution)/shard_map/ppermute | solution.py:32
  65.3 30.2 %collective-permute-start.10 = (bf16[8,96,768]{2,1,0:T(8,128)(2,1)}, bf16[8,96,768]{2,1,0:T(8,128)(2,1)}, u32[]{:S(2)}, u32[]{:S(2)}) collective-permute-start(bf16[8,96,768]{2,1,0:T(8,128)(2,1)} %get-tuple-element.68.refs_5_.refs_7_), channel_id=1, source_target_pairs={{0,1},{1,0},{2,3},{3,2},{4,5},{5,4},{6,7},{7,6},{8,9},{9,8},{10,11... | collective-permute-start | bytes 3538952 | tf_op jit(solution)/shard_map/ppermute | solution.py:37
  65.3 30.2 %collective-permute-start.11 = (bf16[8,96,768]{2,1,0:T(8,128)(2,1)S(1)}, bf16[8,96,768]{2,1,0:T(8,128)(2,1)}, u32[]{:S(2)}, u32[]{:S(2)}) collective-permute-start(bf16[8,96,768]{2,1,0:T(8,128)(2,1)S(1)} %collective-permute-done.7.refs_4_.refs_6_.refs_8_), channel_id=1, source_target_pairs={{0,1},{1,0},{2,3},{3,2},{4,5},{5,4},{6,7},{7,6},{8,9},{9,8},{10,11... | collective-permute-start | bytes 3538952 | tf_op jit(solution)/shard_map/ppermute | solution.py:37
  65.8 51.2 %collective-permute-start.13 = (bf16[8,96,768]{2,1,0:T(8,128)(2,1)S(1)}, bf16[8,96,768]{2,1,0:T(8,128)(2,1)}, u32[]{:S(2)}, u32[]{:S(2)}) collective-permute-start(bf16[8,96,768]{2,1,0:T(8,128)(2,1)S(1)} %get-tuple-element.70.refs_7_.refs_3_.refs_8_), channel_id=1, source_target_pairs={{0,1},{1,0},{2,3},{3,2},{4,5},{5,4},{6,7},{7,6},{8,9},{9,8},{10,11... | collective-permute-start | bytes 3538952 | tf_op jit(solution)/shard_map/ppermute | solution.py:37
  80.3 36.8 %collective-permute-start.15 = (bf16[8,96,768]{2,1,0:T(8,128)(2,1)}, bf16[8,96,768]{2,1,0:T(8,128)(2,1)}, u32[]{:S(2)}, u32[]{:S(2)}) collective-permute-start(bf16[8,96,768]{2,1,0:T(8,128)(2,1)} %collective-permute-done.14.refs_4_.refs_9_), channel_id=1, source_target_pairs={{0,1},{1,0},{2,3},{3,2},{4,5},{5,4},{6,7},{7,6},{8,9},{9,8},{10,11... | collective-permute-start | bytes 3538952 | tf_op jit(solution)/shard_map/ppermute | solution.py:37
  125.7 28.8 %collective-permute-start.20 = (bf16[16,96,768]{2,1,0:T(8,128)(2,1)}, bf16[16,96,768]{2,1,0:T(8,128)(2,1)S(1)}, u32[]{:S(2)}, u32[]{:S(2)}) collective-permute-start(bf16[16,96,768]{2,1,0:T(8,128)(2,1)} %get-tuple-element.81.refs_12_), channel_id=1, source_target_pairs={{0,1},{1,0},{2,3},{3,2},{4,5},{5,4},{6,7},{7,6},{8,9},{9,8},{10,11... | collective-permute-start | bytes 7077896 | tf_op jit(solution)/shard_map/ppermute | solution.py:37
  126.9 32.9 %collective-permute-start.18 = (bf16[8,96,768]{2,1,0:T(8,128)(2,1)S(1)}, bf16[8,96,768]{2,1,0:T(8,128)(2,1)S(1)}, u32[]{:S(2)}, u32[]{:S(2)}) collective-permute-start(bf16[8,96,768]{2,1,0:T(8,128)(2,1)S(1)} %copy-done.15), channel_id=1, source_target_pairs={{0,1},{1,0},{2,3},{3,2},{4,5},{5,4},{6,7},{7,6},{8,9},{9,8},{10,11... | collective-permute-start | bytes 3538952 | tf_op jit(solution)/shard_map/ppermute | solution.py:37
  142.3 17.5 %collective-permute-start.19 = (bf16[8,96,768]{2,1,0:T(8,128)(2,1)}, bf16[8,96,768]{2,1,0:T(8,128)(2,1)}, u32[]{:S(2)}, u32[]{:S(2)}) collective-permute-start(bf16[8,96,768]{2,1,0:T(8,128)(2,1)} %collective-permute-done.17.refs_11_), channel_id=1, source_target_pairs={{0,1},{1,0},{2,3},{3,2},{4,5},{5,4},{6,7},{7,6},{8,9},{9,8},{10,11... | collective-permute-start | bytes 3538952 | tf_op jit(solution)/shard_map/ppermute | solution.py:37
  174.0 29.4 %collective-permute-start.25 = (bf16[16,96,768]{2,1,0:T(8,128)(2,1)}, bf16[16,96,768]{2,1,0:T(8,128)(2,1)}, u32[]{:S(2)}, u32[]{:S(2)}) collective-permute-start(bf16[16,96,768]{2,1,0:T(8,128)(2,1)} %get-tuple-element.92), channel_id=1, source_target_pairs={{0,1},{1,0},{2,3},{3,2},{4,5},{5,4},{6,7},{7,6},{8,9},{9,8},{10,11... | collective-permute-start | bytes 7077896 | tf_op jit(solution)/shard_map/ppermute | solution.py:37
  193.3 32.8 %collective-permute-start.27 = (bf16[1536,768]{1,0:T(8,128)(2,1)}, bf16[1536,768]{1,0:T(8,128)(2,1)S(1)}, u32[]{:S(2)}, u32[]{:S(2)}) collective-permute-start(bf16[1536,768]{1,0:T(8,128)(2,1)} %bitcast.54), channel_id=1, source_target_pairs={{0,1},{1,0},{2,3},{3,2},{4,5},{5,4},{6,7},{7,6},{8,9},{9,8},{10,11... | collective-permute-start | bytes 7077896 | tf_op jit(solution)/shard_map/ppermute | solution.py:37
  207.1 19.1 %collective-permute-start.28 = (bf16[8,96,768]{2,1,0:T(8,128)(2,1)S(1)}, bf16[8,96,768]{2,1,0:T(8,128)(2,1)S(1)}, u32[]{:S(2)}, u32[]{:S(2)}) collective-permute-start(bf16[8,96,768]{2,1,0:T(8,128)(2,1)S(1)} %get-tuple-element.93.refs_9_), channel_id=1, source_target_pairs={{0,4},{1,3},{2,6},{3,1},{4,0},{5,7},{6,2},{7,5},{8,12},{9,11},{10,... | collective-permute-start | bytes 3538952 | tf_op jit(solution)/shard_map/ppermute | solution.py:32
  208.1 16.4 %collective-permute-start.29 = (bf16[2,96,768]{2,1,0:T(8,128)(2,1)S(1)}, bf16[2,96,768]{2,1,0:T(8,128)(2,1)S(1)}, u32[]{:S(2)}, u32[]{:S(2)}) collective-permute-start(bf16[2,96,768]{2,1,0:T(8,128)(2,1)S(1)} %get-tuple-element.94.refs_10_), channel_id=1, source_target_pairs={{0,8},{1,5},{2,10},{3,7},{4,12},{5,1},{6,14},{7,3},{8,0},{9,13},{1... | collective-permute-start | bytes 884744 | tf_op jit(solution)/shard_map/ppermute | solution.py:32
  233.0 17.2 %collective-permute-start.30 = (bf16[800,768]{1,0:T(8,128)(2,1)S(1)}, bf16[800,768]{1,0:T(8,128)(2,1)S(1)}, u32[]{:S(2)}, u32[]{:S(2)}) collective-permute-start(bf16[800,768]{1,0:T(8,128)(2,1)S(1)} %get-tuple-element.104), channel_id=1, source_target_pairs={{0,4},{1,3},{2,6},{3,1},{4,0},{5,7},{6,2},{7,5},{8,12},{9,11},{10,... | collective-permute-start | bytes 3686408 | tf_op jit(solution)/shard_map/ppermute | solution.py:32
  234.6 29.4 %collective-permute-start.22 = (bf16[2,208,768]{2,1,0:T(8,128)(2,1)}, bf16[2,208,768]{2,1,0:T(8,128)(2,1)}, u32[]{:S(2)}, u32[]{:S(2)}) collective-permute-start(bf16[2,208,768]{2,1,0:T(8,128)(2,1)} %bitcast.14.refs_0_), channel_id=1, source_target_pairs={{0,2},{1,3},{2,0},{3,1},{4,6},{5,7},{6,4},{7,5},{8,10},{9,11},{10,... | collective-permute-start | bytes 1916936 | tf_op jit(solution)/shard_map/ppermute | solution.py:37
  253.2 19.5 %collective-permute-start.35 = (bf16[416,768]{1,0:T(8,128)(2,1)S(1)}, bf16[416,768]{1,0:T(8,128)(2,1)S(1)}, u32[]{:S(2)}, u32[]{:S(2)}) collective-permute-start(bf16[416,768]{1,0:T(8,128)(2,1)S(1)} %get-tuple-element.108), channel_id=1, source_target_pairs={{0,2},{1,9},{2,0},{3,11},{4,6},{5,13},{6,4},{7,15},{8,10},{9,1},{1... | collective-permute-start | bytes 1916936 | tf_op jit(solution)/shard_map/ppermute | solution.py:32
  253.9 18.3 %collective-permute-start.36 = (bf16[2,96,768]{2,1,0:T(8,128)(2,1)S(1)}, bf16[2,96,768]{2,1,0:T(8,128)(2,1)S(1)}, u32[]{:S(2)}, u32[]{:S(2)}) collective-permute-start(bf16[2,96,768]{2,1,0:T(8,128)(2,1)S(1)} %get-tuple-element.109), channel_id=1, source_target_pairs={{0,8},{1,5},{2,10},{3,7},{4,12},{5,1},{6,14},{7,3},{8,0},{9,13},{1... | collective-permute-start | bytes 884744 | tf_op jit(solution)/shard_map/ppermute | solution.py:32
  255.5 32.7 %collective-permute-start.21 = (bf16[2,208,768]{2,1,0:T(8,128)(2,1)}, bf16[2,208,768]{2,1,0:T(8,128)(2,1)}, u32[]{:S(2)}, u32[]{:S(2)}) collective-permute-start(bf16[2,208,768]{2,1,0:T(8,128)(2,1)} %bitcast.14.refs_0_), channel_id=1, source_target_pairs={{0,1},{1,0},{2,3},{3,2},{4,5},{5,4},{6,7},{7,6},{8,9},{9,8},{10,11... | collective-permute-start | bytes 1916936 | tf_op jit(solution)/shard_map/ppermute | solution.py:37
  264.0 27.1 %collective-permute-start.23 = (bf16[2,208,768]{2,1,0:T(8,128)(2,1)}, bf16[2,208,768]{2,1,0:T(8,128)(2,1)}, u32[]{:S(2)}, u32[]{:S(2)}) collective-permute-start(bf16[2,208,768]{2,1,0:T(8,128)(2,1)} %collective-permute-done.22.refs_2_), channel_id=1, source_target_pairs={{0,1},{1,0},{2,3},{3,2},{4,5},{5,4},{6,7},{7,6},{8,9},{9,8},{10,11... | collective-permute-start | bytes 1916936 | tf_op jit(solution)/shard_map/ppermute | solution.py:37
  271.5 36.7 %collective-permute-start.33 = (bf16[2,208,768]{2,1,0:T(8,128)(2,1)}, bf16[2,208,768]{2,1,0:T(8,128)(2,1)}, u32[]{:S(2)}, u32[]{:S(2)}) collective-permute-start(bf16[2,208,768]{2,1,0:T(8,128)(2,1)} %bitcast.17.refs_0_), channel_id=1, source_target_pairs={{0,2},{1,3},{2,0},{3,1},{4,6},{5,7},{6,4},{7,5},{8,10},{9,11},{10,... | collective-permute-start | bytes 1916936 | tf_op jit(solution)/shard_map/ppermute | solution.py:37
  284.6 26.4 %collective-permute-start.38 = (bf16[128,768]{1,0:T(8,128)(2,1)}, bf16[128,768]{1,0:T(8,128)(2,1)}, u32[]{:S(2)}, u32[]{:S(2)}) collective-permute-start(bf16[128,768]{1,0:T(8,128)(2,1)} %get-tuple-element.112), channel_id=1, source_target_pairs={{0,16},{1,17},{2,18},{3,19},{4,20},{5,21},{6,22},{7,23},{8,24},{9,... | collective-permute-start | bytes 589832 | tf_op jit(solution)/shard_map/ppermute | solution.py:32
  288.1 18.0 %collective-permute-start.41 = (bf16[1,96,768]{2,1,0:T(8,128)(2,1)}, bf16[1,96,768]{2,1,0:T(8,128)(2,1)}, u32[]{:S(2)}, u32[]{:S(2)}) collective-permute-start(bf16[1,96,768]{2,1,0:T(8,128)(2,1)} %get-tuple-element.117), channel_id=1, source_target_pairs={{0,16},{1,17},{2,18},{3,19},{4,20},{5,21},{6,22},{7,23},{8,24},{9,... | collective-permute-start | bytes 442376 | tf_op jit(solution)/shard_map/ppermute | solution.py:32
  288.2 21.0 %collective-permute-start.40 = (bf16[1,96,768]{2,1,0:T(8,128)(2,1)}, bf16[1,96,768]{2,1,0:T(8,128)(2,1)}, u32[]{:S(2)}, u32[]{:S(2)}) collective-permute-start(bf16[1,96,768]{2,1,0:T(8,128)(2,1)} %get-tuple-element.116), channel_id=1, source_target_pairs={{0,16},{1,17},{2,18},{3,19},{4,20},{5,21},{6,22},{7,23},{8,24},{9,... | collective-permute-start | bytes 442376 | tf_op jit(solution)/shard_map/ppermute | solution.py:32
  (89 other events, 861.3 us)

commit v6 on v1

v6 whole, which is shorter than its diff:
```python
from functools import partial

import jax
import jax.numpy as jnp
from jax import lax
from jax.experimental import pallas as pl
from jax.experimental.pallas import tpu as pltpu
from jax.sharding import PartitionSpec as P

HEAD_DIM = 64
EPS = 1e-06
AXES = ("dp", "tensor")
TILE = 16
ROWS = 32
FACTOR = HEAD_DIM ** (-0.5)
bf16 = jnp.bfloat16
f32 = jnp.float32


class Cube:
    def __init__(self, n_dp, n_t, rows):
        self.n_dp, self.n_t, self.rows = n_dp, n_t, rows
        self.n = n_dp * n_t
        n_bits = self.n.bit_length() - 1
        self.fast = (1 << n_bits) == self.n and n_bits >= 4 and rows % TILE == 0
        far = list(range(n_bits - 1, 3, -1))
        self.orders = [
            ([2, 1, 3] + far, [1, 3, 2] + far),
            ([2, 3, 1] + far, [1, 3, 2] + far),
            ([3, 1, 2] + far, [2, 3, 1] + far),
        ]
        self.steps = 3 + len(far)
        self.half = self.n // 2

    def swap(self, group, value, k):
        orders = self.orders[group]
        return lax.ppermute(value, AXES, [(i, i ^ (1 << orders[i & 1][k])) for i in range(self.n)])

    def flip(self, value, bits):
        return lax.ppermute(value, AXES, [(i, i ^ bits) for i in range(self.n)])

    def at(self, group, ids_ref, core, y, block):
        relative = ((ids_ref[0] ^ block) << 2) | (y << 1)
        found = []
        for order in self.orders[group]:
            place = 0
            for k, bit in enumerate(order[::-1]):
                place = place | (((relative >> bit) & 1) << k)
            found.append(place)
        return jnp.where((ids_ref[1] & 1) == core, found[0], found[1])

    def buffers(self, cols):
        blocks = (2, self.half, self.rows, cols) if self.fast else (1, 1, 8, 128)
        shard = pltpu.VMEM((self.n_dp * self.rows, cols), bf16)
        return [pltpu.VMEM(blocks, bf16), shard, pltpu.SemaphoreType.DMA((4,))]

    def fetch(self, refs, scratch):
        if not self.fast:
            return lambda core: None
        held, _, sems = scratch
        part = self.half // 2
        copies = [
            pltpu.make_async_copy(refs[i], held.at[i // 2, pl.ds(i % 2 * part, part)], sems.at[i])
            for i in range(4)
        ]
        for copy in copies:
            copy.start()

        def wait(core):
            copies[2 * core].wait()
            copies[2 * core + 1].wait()

        return wait

    def load(self, group, ids_ref, refs, scratch, core, y):
        held, shard, sems = scratch
        if not self.fast:
            copy = pltpu.make_async_copy(refs[0].at[2 * y + core], shard, sems.at[0])
            copy.start()
            copy.wait()
            return
        for d in range(self.n_dp):
            rows = slice(d * self.rows, (d + 1) * self.rows)
            shard[rows, :] = held[core, self.at(group, ids_ref, core, y, d)]

    def grad_buffers(self, cols):
        shape = self.grad_shape(cols).shape
        return [pltpu.VMEM((2,) + shape, bf16), pltpu.SemaphoreType.DMA((2,))]

    def store(self, group, ids_ref, scratch, core, y, value):
        if not self.fast:
            scratch[0][core, y] = value
            return
        for d in range(self.n_dp):
            rows = value[d * self.rows : (d + 1) * self.rows]
            scratch[0][core, self.at(group, ids_ref, core, y, d)] = rows

    def send_out(self, scratch, core, ref):
        copy = pltpu.make_async_copy(scratch[0].at[core], ref, scratch[1].at[core])
        copy.start()
        return copy

    def grad_shape(self, cols):
        if not self.fast:
            return jax.ShapeDtypeStruct((2, self.n_dp * self.rows, cols), bf16)
        return jax.ShapeDtypeStruct((self.half, self.rows, cols), bf16)


def gather_plain(cube, piece):
    rows, cols = piece.shape
    whole = lax.all_gather(piece, AXES, axis=0, tiled=False)
    whole = whole.reshape(cube.n_dp, cube.n_t, rows, cols).transpose(1, 0, 2, 3)
    whole = whole.reshape(cube.n_t, cube.n_dp * rows, cols)
    return [jnp.take(whole, lax.axis_index("tensor") ^ jnp.arange(cube.n_t), axis=0)]


def scatter_plain(cube, own, other):
    n_t, n_dp, rows, cols = cube.n_t, cube.n_dp, cube.rows, own.shape[2]
    part = jnp.stack((own, other), axis=1).reshape(n_t, n_dp * rows, cols)
    part = jnp.take(part, lax.axis_index("tensor") ^ jnp.arange(n_t), axis=0)
    part = part.reshape(n_t, n_dp, rows, cols).transpose(1, 0, 2, 3)
    part = part.reshape(n_dp * n_t * rows, cols)
    return lax.psum_scatter(part, AXES, scatter_dimension=0, tiled=True).astype(f32)


def join(pairs, after=()):
    def kernel(*refs):
        outs = refs[2 * len(pairs) + len(after) :]
        for i, out in enumerate(outs):
            size = pairs[i][0].shape[0]
            out[:size] = refs[2 * i][...]
            out[size:] = refs[2 * i + 1][...]

    shapes = [
        jax.ShapeDtypeStruct((2 * p[0].shape[0],) + p[0].shape[1:], p[0].dtype) for p in pairs
    ]
    return plain_call(kernel, shapes, [x for p in pairs for x in p], after)


def sends(groups, after=()):
    sizes = [min(v.shape[0] for v in g) // 2 for g in groups]
    inputs = [(v, size) for g, size in zip(groups, sizes) for v in g]
    shapes = [jax.ShapeDtypeStruct((n,) + g[0].shape[1:], bf16) for g, n in zip(groups, sizes)]

    def kernel(*refs):
        outs = refs[len(inputs) + len(after) :]
        parts = pull(refs, [(size, size) for _, size in inputs], outs[len(groups) :])
        for g, out in zip(groups, outs):
            out[...] = added(parts, len(g)).astype(bf16)

    return pull_call(kernel, shapes, [v for v, _ in inputs], [n for _, n in inputs], after)


def pull(refs, spots, scratch):
    sems = scratch[len(spots)]
    copies = [
        pltpu.make_async_copy(refs[i].at[pl.ds(start, size)], scratch[i], sems.at[i])
        for i, (start, size) in enumerate(spots)
    ]
    for copy in copies:
        copy.start()

    def each():
        for i, copy in enumerate(copies):
            copy.wait()
            yield scratch[i][...]

    return each()


def added(parts, n):
    value = next(parts).astype(f32)
    for _ in range(n - 1):
        value = value + next(parts).astype(f32)
    return value


def pull_call(kernel, shapes, inputs, sizes, after, ids=None, whole=(), scratch=()):
    specs = [pl.BlockSpec(memory_space=pltpu.HBM)] * len(inputs)
    specs += [pl.BlockSpec(memory_space=pl.ANY)] * len(after)
    values = [*inputs, *after]
    pulled = [pltpu.VMEM((n,) + v.shape[1:], bf16) for v, n in zip(inputs, sizes)]
    pulled += [pltpu.SemaphoreType.DMA((len(inputs),)), *scratch]
    if ids is not None:
        specs = [
            pl.BlockSpec(memory_space=pltpu.SMEM),
            *[pl.BlockSpec(memory_space=pltpu.VMEM)] * len(whole),
            *specs,
        ]
        values = [ids, *whole, *values]
    return pl.pallas_call(
        kernel,
        out_shape=shapes,
        in_specs=specs,
        out_specs=[pl.BlockSpec(memory_space=pltpu.VMEM)] * len(shapes),
        scratch_shapes=pulled,
        compiler_params=pltpu.CompilerParams(vmem_limit_bytes=48 * 1024 * 1024),
        cost_estimate=pl.CostEstimate(flops=0, bytes_accessed=1024, transcendentals=0),
    )(*values)


def plain_call(kernel, shapes, inputs, after):
    specs = [pl.BlockSpec(x.shape, lambda i: (0, 0, 0)) for x in inputs]
    return pl.pallas_call(
        kernel,
        grid=(1,),
        out_shape=shapes,
        in_specs=specs + [pl.BlockSpec(memory_space=pl.ANY)] * len(after),
        out_specs=[pl.BlockSpec(x.shape, lambda i, n=len(x.shape): (0,) * n) for x in shapes],
        compiler_params=pltpu.CompilerParams(vmem_limit_bytes=48 * 1024 * 1024),
        cost_estimate=pl.CostEstimate(flops=0, bytes_accessed=1024, transcendentals=0),
    )(*inputs, *after)


def sends_with_small(cube, group, groups, small, ids, after=(), final=False):
    rows = cube.rows
    kept = [v.shape[0] // rows * rows for v in group]
    size = min(kept) // 2
    d = group[0].shape[1]
    first = len(small) > 1
    sizes = [min(v.shape[0] for v in g) // 2 for g in groups]
    shapes = [
        jax.ShapeDtypeStruct((size + ROWS, d), bf16),
        jax.ShapeDtypeStruct((ROWS, d), bf16),
    ]
    if final:
        shapes += [jax.ShapeDtypeStruct(g[0].shape[1:], f32) for g in groups]
    else:
        shapes += [jax.ShapeDtypeStruct((n,) + g[0].shape[1:], bf16) for g, n in zip(groups, sizes)]
    inputs = list(group) + [v for g in groups for v in g]
    spots = [(size, size)] * len(group)
    spots += [(0, 1) if final else (n, n) for g, n in zip(groups, sizes) for _ in g]
    if not first:
        inputs.append(group[-1])
        spots.append((kept[-1], ROWS))

    def kernel(ids_ref, *refs):
        extra, refs = refs[: len(small)], refs[len(small) :]
        outs = refs[len(inputs) + len(after) :]
        total_ref = outs[-1]
        parts = pull(refs, spots, outs[len(shapes) :])
        outs[0][:size, :] = added(parts, len(group)).astype(bf16)
        for g, out in zip(groups, outs[2:]):
            value = added(parts, len(g))
            out[...] = value[0] if final else value.astype(bf16)
        if first:
            gather_small(cube, ids_ref, extra, total_ref)
        else:
            total_ref[...] = extra[0][...].astype(f32) + added(parts, 1)
        low = total_ref[...].astype(bf16)
        outs[0][size:, :] = low
        outs[1][...] = low

    return pull_call(
        kernel, shapes, inputs, [n for _, n in spots], after, ids, small, [pltpu.VMEM((ROWS, d), f32)]
    )


def gather_small(cube, ids_ref, refs, out_ref):
    attn_ref, mlp_ref = refs[:2]
    out_ref[...] = jnp.zeros_like(out_ref)
    for i in range(2):
        out_ref[i : i + 1, :] = attn_ref[i]
    for i in range(4):
        out_ref[2 + i : 3 + i, :] = mlp_ref[i]
    n_t = cube.n_t
    for relative in range(n_t):
        t = relative ^ ids_ref[1]
        dbias = refs[2][relative]
        width = dbias.shape[1] // 3
        out_ref[pl.ds(6 + t, 1), :] = refs[3][relative]
        out_ref[pl.ds(6 + n_t + t, 1), :width] = dbias[:, :width]
        out_ref[pl.ds(6 + 2 * n_t + t, 1), :width] = dbias[:, 2 * width :]


def finish_with_small(cube, group, small, ids, after=()):
    rows, d = cube.rows, group[0].shape[1]
    inputs = [*group, group[-1]]
    spots = [(0, rows)] * len(group) + [(group[-1].shape[0] - ROWS, ROWS)]

    def kernel(ids_ref, small_ref, *refs):
        outs = refs[len(inputs) + len(after) :]
        parts = pull(refs, spots, outs[2:])
        outs[0][...] = added(parts, len(group))
        outs[1][...] = (small_ref[...].astype(f32) + added(parts, 1)).astype(bf16)

    shapes = [jax.ShapeDtypeStruct((rows, d), f32), jax.ShapeDtypeStruct(small.shape, bf16)]
    return pull_call(kernel, shapes, inputs, [n for _, n in spots], after, ids, [small])


def hold(values, after):
    n = len(values)

    def kernel(*refs):
        pass

    return pl.pallas_call(
        kernel,
        out_shape=[jax.ShapeDtypeStruct(v.shape, v.dtype) for v in values],
        in_specs=[pl.BlockSpec(memory_space=pl.ANY)] * (n + len(after)),
        out_specs=[pl.BlockSpec(memory_space=pl.ANY)] * n,
        input_output_aliases={i: i for i in range(n)},
        cost_estimate=pl.CostEstimate(flops=0, bytes_accessed=1024, transcendentals=0),
    )(*values, *after)


def place_images(cube, pieces, length, after=()):
    if not cube.fast:
        return lax.all_gather(pieces[0][:, :length], "tensor", axis=0, tiled=True)
    count = pieces[0].shape[0]
    index = lax.axis_index("tensor").astype(jnp.int32).reshape(1)

    def kernel(index_ref, *refs):
        for r in range(4):
            for i in range(count):
                refs[-1][(index_ref[0] ^ r) * count + i] = refs[r][i, :length, :]

    shape = (4 * count, length, pieces[0].shape[2])
    return call(kernel, [jax.ShapeDtypeStruct(shape, bf16)], index, pieces, [], [], after)[0]


def call(kernel, out_shapes, index, inputs, weights, scratch, after=(), grads=()):
    out_shapes = [*out_shapes, jax.ShapeDtypeStruct((8, 128), f32)]
    n_in, n_w, n_out = len(inputs), len(weights), len(out_shapes)
    spots = [pl.BlockSpec(memory_space=pltpu.VMEM)] * n_out
    spots += [pl.BlockSpec(memory_space=pltpu.HBM)] * len(grads)

    def body(index_ref, *refs):
        rest = refs[n_in + n_w + len(after) :]
        rest[n_out - 1][...] = jnp.zeros((8, 128), f32)
        kernel(index_ref, *refs[: n_in + n_w], *rest[: n_out - 1], *rest[n_out:])

    return pl.pallas_call(
        body,
        out_shape=[*out_shapes, *grads],
        in_specs=[pl.BlockSpec(memory_space=pltpu.SMEM)]
        + [pl.BlockSpec(memory_space=pltpu.VMEM)] * n_in
        + [pl.BlockSpec(memory_space=pltpu.HBM)] * n_w
        + [pl.BlockSpec(memory_space=pl.ANY)] * len(after),
        out_specs=spots,
        scratch_shapes=scratch,
        compiler_params=pltpu.CompilerParams(vmem_limit_bytes=56 * 1024 * 1024),
        cost_estimate=pl.CostEstimate(flops=0, bytes_accessed=1024, transcendentals=0),
    )(index, *inputs, *weights, *after)


def nn(left, right):
    return lax.dot_general(left, right, (((1,), (0,)), ((), ())), preferred_element_type=f32)


def nt(left, right):
    return lax.dot_general(left, right, (((1,), (1,)), ((), ())), preferred_element_type=f32)


def tn(left, right):
    return lax.dot_general(left, right, (((0,), (0,)), ((), ())), preferred_element_type=f32)


def normed_of(values):
    centre = values - jnp.mean(values, -1, keepdims=True)
    inverse = lax.rsqrt(jnp.mean(centre * centre, -1, keepdims=True) + EPS)
    return (centre * inverse, inverse)


def norm_back(upstream, normed, inverse, gain):
    scaled = upstream * gain
    inner = (
        scaled
        - jnp.mean(scaled, -1, keepdims=True)
        - normed * jnp.mean(scaled * normed, -1, keepdims=True)
    )
    return inverse * inner


def column_sum(values):
    return jnp.sum(values, 0, keepdims=True)


def attend_kernel(cube, count, length, width, n_w, ids_ref, *refs):
    x_ref, vec_ref, bias_ref = refs[:3]
    w_refs = refs[3 : 3 + n_w]
    n1_ref, qkv_ref, att_ref, sum_ref, n2_ref = refs[3 + n_w : 8 + n_w]
    scratch = refs[8 + n_w :]
    wait = cube.fetch(w_refs, scratch)
    x = x_ref[...].astype(f32)
    normed, _ = normed_of(x)
    n1_ref[...] = (normed * vec_ref[0:1] + vec_ref[1:2]).astype(bf16)
    sum_ref[...] = x + vec_ref[2:3]
    tokens = x_ref.shape[0] // count
    heads = width // HEAD_DIM
    keep = lax.broadcasted_iota(jnp.int32, (tokens, tokens), 1) < length
    w_ref = scratch[1]

    for core in range(2):
        wait(core)

        def step(y, carry):
            t = 2 * y + core
            cube.load(0, ids_ref, w_refs, scratch, core, y)
            qkv = nn(n1_ref[...], w_ref[:, : 3 * width]) + bias_ref[t]
            qkv_ref[t] = qkv.astype(bf16)
            for b in range(count):
                rows = slice(b * tokens, (b + 1) * tokens)
                found = []
                for h in range(heads):
                    q = qkv_ref[t, rows, h * HEAD_DIM : (h + 1) * HEAD_DIM]
                    k = qkv_ref[t, rows, width + h * HEAD_DIM : width + (h + 1) * HEAD_DIM]
                    v = qkv_ref[t, rows, 2 * width + h * HEAD_DIM : 2 * width + (h + 1) * HEAD_DIM]
                    scores = jnp.where(keep, nt(q, k) * FACTOR, -1e30)
                    weights = jnp.exp(scores - jnp.max(scores, -1, keepdims=True))
                    probs = weights * (1.0 / jnp.sum(weights, -1, keepdims=True))
                    found.append(nn(probs.astype(bf16), v).astype(bf16))
                att_ref[t, rows, :] = jnp.concatenate(found, axis=1)
            sum_ref[...] += nt(att_ref[t], w_ref[:, 3 * width :])
            return carry

        lax.fori_loop(0, cube.n_t // 2, step, 0)
    normed, _ = normed_of(sum_ref[...])
    n2_ref[...] = (normed * vec_ref[3:4] + vec_ref[4:5]).astype(bf16)


def gelu_kernel(cube, n_w, ids_ref, *refs):
    n2_ref, cot_ref, bias_ref = refs[:3]
    w_refs = refs[3 : 3 + n_w]
    act_ref, slope_ref = refs[3 + n_w : 5 + n_w]
    grad_refs = refs[5 + n_w : 7 + n_w]
    scratch, grads = refs[7 + n_w : 10 + n_w], refs[10 + n_w :]
    wait = cube.fetch(w_refs, scratch)
    copies = []
    for core in range(2):
        wait(core)

        def step(y, carry):
            t = 2 * y + core
            cube.load(1, ids_ref, w_refs, scratch, core, y)
            pre = nn(n2_ref[...], scratch[1][...]) + bias_ref[t]
            cdf = 0.5 * (1.0 + lax.erf(pre * (0.5**0.5)))
            slope = cdf + pre * (jnp.exp(-0.5 * pre * pre) * 0.3989422804014327)
            act_ref[t] = (pre * cdf).astype(bf16)
            slope_ref[t] = slope.astype(bf16)
            cube.store(2, ids_ref, grads, core, y, tn(cot_ref[...], act_ref[t]).astype(bf16))
            return carry

        lax.fori_loop(0, cube.n_t // 2, step, 0)
        copies.append(cube.send_out(grads, core, grad_refs[core]))
    for copy in copies:
        copy.wait()


def mlp_kernel(cube, n_w, ids_ref, *refs):
    n2_ref, cot_ref, act_ref, slope_ref, hidden_ref, vec_ref = refs[:6]
    one_refs, two_refs = refs[6 : 6 + n_w], refs[6 + n_w : 6 + 2 * n_w]
    outs = refs[6 + 2 * n_w :]
    sums_ref, enc_ref, dhidden_ref, small_ref = outs[:4]
    grad_refs = outs[4:6]
    one, two, grads = outs[6:9], outs[9:12], outs[12:14]
    mlp_ref, dnorm_ref = outs[14:]
    waits = [cube.fetch(one_refs, one), cube.fetch(two_refs, two)]
    mlp_ref[...] = hidden_ref[...] + vec_ref[5:6]
    dnorm_ref[...] = jnp.zeros_like(dnorm_ref)
    copies = []
    for core in range(2):
        for wait in waits:
            wait(core)

        def step(y, carry):
            t = 2 * y + core
            cube.load(1, ids_ref, one_refs, one, core, y)
            cube.load(2, ids_ref, two_refs, two, core, y)
            dact = nn(cot_ref[...], two[1][...])
            dpre = (slope_ref[t].astype(f32) * dact).astype(bf16)
            sums_ref[pl.ds(t, 1)] = column_sum(dpre.astype(f32))[None]
            cube.store(1, ids_ref, grads, core, y, tn(n2_ref[...], dpre).astype(bf16))
            dnorm_ref[...] += nt(dpre, one[1][...])
            mlp_ref[...] += nt(act_ref[t], two[1][...])
            return carry

        lax.fori_loop(0, cube.n_t // 2, step, 0)
        copies.append(cube.send_out(grads, core, grad_refs[core]))
    enc_ref[...] = mlp_ref[...].astype(bf16)
    normed, inverse = normed_of(hidden_ref[...])
    dnorm = dnorm_ref[...]
    cot = cot_ref[...].astype(f32)
    dhidden = cot + norm_back(dnorm, normed, inverse, vec_ref[3:4])
    dhidden_ref[...] = dhidden
    small_ref[0] = column_sum(dnorm * normed)
    small_ref[1] = column_sum(dnorm)
    small_ref[2] = column_sum(cot)
    small_ref[3] = column_sum(dhidden)
    for copy in copies:
        copy.wait()


def attend_back_kernel(cube, count, length, width, n_w, ids_ref, *refs):
    x_ref, n1_ref, qkv_ref, att_ref, dhidden_ref, vec_ref = refs[:6]
    w_refs = refs[6 : 6 + n_w]
    outs = refs[6 + n_w :]
    dbias_ref, dnorm_ref, small_ref = outs[:3]
    grad_refs = outs[3:5]
    scratch, grads = outs[5:8], outs[8:10]
    low_ref, dqkv_ref = outs[10:]
    wait = cube.fetch(w_refs, scratch)
    low_ref[...] = dhidden_ref[...].astype(bf16)
    dnorm_ref[...] = jnp.zeros_like(dnorm_ref)
    tokens = x_ref.shape[0] // count
    heads = width // HEAD_DIM
    keep = lax.broadcasted_iota(jnp.int32, (tokens, tokens), 0) < length
    w_ref = scratch[1]
    copies = []
    for core in (1, 0):
        wait(core)

        def step(y, carry):
            t = 2 * y + core
            cube.load(0, ids_ref, w_refs, scratch, core, y)
            datt = nn(low_ref[...], w_ref[:, 3 * width :]).astype(bf16)
            for b in range(count):
                rows = slice(b * tokens, (b + 1) * tokens)
                dqs, dks, dvs = [], [], []
                for h in range(heads):
                    q = qkv_ref[t, rows, h * HEAD_DIM : (h + 1) * HEAD_DIM]
                    k = qkv_ref[t, rows, width + h * HEAD_DIM : width + (h + 1) * HEAD_DIM]
                    v = qkv_ref[t, rows, 2 * width + h * HEAD_DIM : 2 * width + (h + 1) * HEAD_DIM]
                    do = datt[rows, h * HEAD_DIM : (h + 1) * HEAD_DIM]
                    scores = jnp.where(keep, nt(k, q) * FACTOR, -1e30)
                    weights = jnp.exp(scores - jnp.max(scores, 0, keepdims=True))
                    probs = weights * (1.0 / jnp.sum(weights, 0, keepdims=True))
                    dvs.append(nn(probs.astype(bf16), do))
                    dprobs = nt(v, do)
                    inner = jnp.sum(dprobs * probs, 0, keepdims=True)
                    dscores = (probs * (dprobs - inner)).astype(bf16)
                    dks.append(nn(dscores, q) * FACTOR)
                    dqs.append(tn(dscores, k) * FACTOR)
                dqkv_ref[rows, :] = jnp.concatenate(dqs + dks + dvs, axis=1).astype(bf16)
            dqkv = dqkv_ref[...]
            dbias_ref[pl.ds(t, 1)] = column_sum(dqkv.astype(f32))[None]
            dnorm_ref[...] += nt(dqkv, w_ref[:, : 3 * width])
            grad = jnp.concatenate((tn(n1_ref[...], dqkv), tn(low_ref[...], att_ref[t])), axis=1)
            cube.store(0, ids_ref, grads, core, y, grad.astype(bf16))
            return carry

        lax.fori_loop(0, cube.n_t // 2, step, 0)
        copies.append(cube.send_out(grads, core, grad_refs[core]))
    normed, _ = normed_of(x_ref[...].astype(f32))
    dnorm = dnorm_ref[...]
    small_ref[0] = column_sum(dnorm * normed)
    small_ref[1] = column_sum(dnorm)
    for copy in copies:
        copy.wait()


def patch_kernel(ids_ref, x_ref, dhidden_ref, dnorm_ref, vec_ref, patch_ref):
    normed, inverse = normed_of(x_ref[...].astype(f32))
    patch = dhidden_ref[...] + norm_back(dnorm_ref[...], normed, inverse, vec_ref[0:1])
    patch_ref[...] = patch.astype(bf16)


def on_device(
    n_dp,
    n_t,
    patches,
    attn_gain,
    attn_shift,
    qkv_weight,
    qv_bias,
    out_weight,
    out_bias,
    mlp_gain,
    mlp_shift,
    fc1_weight,
    fc1_bias,
    fc2_weight,
    fc2_bias,
    cotangent,
):
    t_me = lax.axis_index("tensor")
    cube = Cube(n_dp, n_t, qkv_weight.shape[1])
    order = t_me ^ jnp.arange(n_t)
    width = qkv_weight.shape[2]
    f_width = fc1_weight.shape[1]
    d = patches.shape[2]
    ids = jnp.stack((lax.axis_index("dp"), t_me)).astype(jnp.int32)
    count = patches.shape[0] // n_t
    length = patches.shape[1]
    padded = -(-length // TILE) * TILE
    tokens = count * padded

    def own_images(values):
        mine = lax.dynamic_slice_in_dim(values, t_me * count, count, 0)
        return jnp.pad(mine, ((0, 0), (0, padded - length), (0, 0))).reshape(tokens, d)

    def shape(*dims, dtype=bf16):
        return jax.ShapeDtypeStruct(dims, dtype)

    attn_piece = jnp.concatenate(
        (qkv_weight[0], qkv_weight[1], qkv_weight[2], out_weight.T), axis=1
    )
    two_piece = fc2_weight.T
    biases = jnp.concatenate((qv_bias.reshape(-1), fc1_bias))[None]
    x = own_images(patches)
    cot = own_images(cotangent)
    vecs = jnp.stack((attn_gain, attn_shift, out_bias, mlp_gain, mlp_shift, fc2_bias)).astype(f32)

    def bias_parts(biases):
        biases = biases.astype(f32)
        zeros = jnp.zeros((n_t, width), f32)
        qkv = (biases[:, :width], zeros, biases[:, width : 2 * width])
        return (jnp.concatenate(qkv, axis=1)[:, None], biases[:, None, 2 * width :])

    last = cube.steps - 1
    if cube.fast:
        held = attn_piece[None]
        one = fc1_weight[None]
        two = two_piece[None]
        for k in range(last, 0, -1):
            pairs = [(held, cube.swap(0, held, k))]
            if k < last:
                pairs.append((one, cube.swap(1, one, k + 1)))
            if k < last - 1:
                pairs.append((two, cube.swap(2, two, k + 2)))
            tokens_in = (x, cot) if k == last else (vecs, qkv_bias, f_bias) if k == 1 else ()
            found = join(pairs, tokens_in)
            held = found[0]
            one = found[1] if k < last else one
            two = found[2] if k < last - 1 else two
            if k == last:
                (biases,) = hold([biases], (held,))
                biases = [biases] + [cube.flip(biases, r) for r in range(1, n_t)]
                qkv_bias, f_bias = bias_parts(jnp.concatenate(biases))
        came = cube.swap(0, held, 0)
        pairs = [(one, cube.swap(1, one, 1)), (two, cube.swap(2, two, 2))]
        w_attn = [held, came, cube.flip(held, 1), cube.flip(came, 1)]
        one, two = join(pairs, (came,))
        slot = (one, two)
    else:
        w_attn = gather_plain(cube, attn_piece)
        w_one = gather_plain(cube, fc1_weight)
        w_two = gather_plain(cube, two_piece)
        biases = jnp.take(lax.all_gather(biases[0], "tensor", axis=0, tiled=False), order, axis=0)
        qkv_bias, f_bias = bias_parts(biases)
        slot = ()
    n_w = len(w_attn)
    buffers = cube.buffers(d)
    grad_buffers = cube.grad_buffers(d)
    grad_shapes = [cube.grad_shape(d)] * 2

    n1, qkv, att, hidden, n2, done = call(
        partial(attend_kernel, cube, count, length, width, n_w),
        [
            shape(tokens, d),
            shape(n_t, tokens, 3 * width),
            shape(n_t, tokens, width),
            shape(tokens, d, dtype=f32),
            shape(tokens, d),
        ],
        ids,
        [x, vecs, qkv_bias],
        w_attn,
        buffers,
        slot,
    )
    if cube.fast:
        (came,) = hold([cube.swap(1, one, 0)], (done,))
        w_one = [one, came, cube.flip(one, 1), cube.flip(came, 1)]
        (two,) = join([(two, cube.swap(2, two, 1))], (done,))
        slot = (two,)
    act, slope, done, *two_grads = call(
        partial(gelu_kernel, cube, n_w),
        [shape(n_t, tokens, f_width)] * 2,
        ids,
        [n2, cot, f_bias],
        w_one,
        buffers + grad_buffers,
        slot,
        grad_shapes,
    )
    if cube.fast:
        (came,) = hold([cube.swap(2, two, 0)], (done,))
        w_two = [two, came, cube.flip(two, 1), cube.flip(came, 1)]
    f_sums, enc, dhidden, mlp_small, done, *one_grads = call(
        partial(mlp_kernel, cube, n_w),
        [
            shape(n_t, 1, f_width, dtype=f32),
            shape(tokens, d),
            shape(tokens, d, dtype=f32),
            shape(4, 1, d, dtype=f32),
        ],
        ids,
        [n2, cot, act, slope, hidden, vecs],
        [*w_one, *w_two],
        buffers * 2 + grad_buffers + [pltpu.VMEM((tokens, d), f32)] * 2,
        (),
        grad_shapes,
    )
    slot = ()
    if cube.fast:
        two_terms = [two_grads[0], cube.flip(two_grads[1], 1)]
        one_terms = [one_grads[0], cube.flip(one_grads[1], 1)]
        s_two, s_one = sends([two_terms, one_terms], (done,))
        slot = (s_two, s_one)
    dbias, dnorm, attn_small, done, *attn_grads = call(
        partial(attend_back_kernel, cube, count, length, width, n_w),
        [
            shape(n_t, 1, 3 * width, dtype=f32),
            shape(tokens, d, dtype=f32),
            shape(2, 1, d, dtype=f32),
        ],
        ids,
        [x, n1, qkv, att, dhidden, vecs],
        w_attn,
        buffers
        + grad_buffers
        + [pltpu.VMEM((tokens, d), bf16), pltpu.VMEM((tokens, 3 * width), bf16)],
        slot,
        grad_shapes,
    )

    def patch_of(after):
        patch = call(
            patch_kernel, [shape(tokens, d)], ids, [x, dhidden, dnorm, vecs], [], [], after
        )[0]
        return patch.reshape(count, padded, d)

    images = enc.reshape(count, padded, d)
    sums = (attn_small, mlp_small, dbias, f_sums)
    if cube.fast:

        def spread(images, there):
            return [images, cube.flip(images, 1), there, cube.flip(there, 1)]

        two_terms.append(cube.swap(2, s_two, 0))
        one_terms.append(cube.swap(1, s_one, 0))
        there = cube.flip(images, 2)
        came = (two_terms[-1], one_terms[-1], there)
        flat = (cube.half * cube.rows, d)
        other, images = hold([attn_grads[1].reshape(flat), images], came)
        s_two, s_one = sends([two_terms, one_terms], (done,))
        attn_terms = [attn_grads[0].reshape(flat), cube.flip(other, 1)]
        small = sums
        for k in range(cube.steps):
            if k == 0:
                found = sends_with_small(cube, attn_terms, [], small, ids, (s_one,))
            elif k < last:
                found = sends_with_small(cube, attn_terms, [two_terms, one_terms], small, ids, after)
                s_two, s_one = found[2:]
            else:
                found = sends_with_small(
                    cube, attn_terms, [two_terms, one_terms], small, ids, after, True
                )
                two_grad, one_grad = found[2:]
            small, after = (found[1],), ()
            attn_terms.append(cube.swap(0, found[0], k))
            if k < last:
                two_terms.append(cube.swap(2, s_two, k + 1))
                one_terms.append(cube.swap(1, s_one, k + 1))
            if k == 0:
                images, there = hold([images, there], small)
                encoded = place_images(cube, spread(images, there), length)
                after = (encoded,)
            if k == last - 1:
                images = patch_of(small)
                there = cube.flip(images, 2)
            if k == last:
                images, there = hold([images, there], small)
                patch_grad = place_images(cube, spread(images, there), length)
        attn_grad, small = finish_with_small(cube, attn_terms, small[0], ids, (patch_grad,))
        small = small.astype(f32) + cube.flip(small, 1).astype(f32)
    else:
        two_grad = scatter_plain(cube, *two_grads)
        one_grad = scatter_plain(cube, *one_grads)
        attn_grad = scatter_plain(cube, *attn_grads)
        encoded = place_images(cube, [images], length)
        patch_grad = place_images(cube, [patch_of(())], length)

        def collect(ids_ref, *refs):
            gather_small(cube, ids_ref, refs[:4], refs[4])

        small = call(collect, [shape(ROWS, d, dtype=f32)], ids, sums, [], [])[0]
        small = lax.psum(small, AXES)

    def shard_row(at):
        return lax.dynamic_slice_in_dim(small, at + t_me, 1, 0)

    return (
        encoded,
        patch_grad,
        small[0],
        small[1],
        jnp.stack([attn_grad[:, i * width : (i + 1) * width] for i in range(3)]),
        jnp.concatenate((shard_row(6 + n_t), shard_row(6 + 2 * n_t)))[:, :width],
        attn_grad[:, 3 * width :].T,
        small[5],
        small[2],
        small[3],
        one_grad,
        shard_row(6)[0],
        two_grad.T,
        small[4],
    )


def solution(mesh):
    return jax.shard_map(
        partial(on_device, mesh.shape["dp"], mesh.shape["tensor"]),
        mesh=mesh,
        in_specs=(
            P("dp", None, None),
            P(),
            P(),
            P(None, "dp", "tensor"),
            P(None, "tensor"),
            P("tensor", "dp"),
            P(),
            P(),
            P(),
            P("dp", "tensor"),
            P("tensor"),
            P("tensor", "dp"),
            P(),
            P("dp", None, None),
        ),
        out_specs=(
            P("dp", None, None),
            P("dp", None, None),
            P(),
            P(),
            P(None, "dp", "tensor"),
            P(None, "tensor"),
            P("tensor", "dp"),
            P(),
            P(),
            P(),
            P("dp", "tensor"),
            P("tensor"),
            P("tensor", "dp"),
            P(),
        ),
        check_vma=False,
    )
```

time: 658 us -> 266 us (0.40)
  waiting for transfers between devices: 436 us -> 77.7 us
  Pallas kernels: 0 us -> 103 us
  matrix products: 69.7 us -> 0 us
  blocking collectives: 46.2 us -> 0 us
  starting transfers between devices: 0.58 us -> 45.1 us
  local copies, waits for them, and re-layouts: 59.2 us -> 30.1 us
  other arithmetic: 24.7 us -> 3.59 us
  between operations: 15.2 us -> 1.66 us
    reduce_scatter x3 -> x0, waiting for transfers between devices: 264 us -> none  [scatter_grad(): lax.psum_scatter(part, AXES, scatter_dimension=0, tiled=True).astype(f32)]
    all_gather x5 -> x0, waiting for transfers between devices: 171 us -> none  [the longest x3 171 us: gather_weight(): whole = lax.all_gather(piece, AXES, axis=0, tiled=False)]
    pallas_call x0 -> x25, Pallas kernels: none -> 103 us  [the longest x7 81.1 us: call(): pl.pallas_call(body, out_shape=[*out_shapes, *grads], in_specs=[pl.BlockS...]
    ppermute x0 -> x43, waiting for transfers between devices: none -> 77.7 us  [the longest x24 66 us: swap(): lax.ppermute(value, AXES, [(i, i ^ 1 << orders[i & 1][k]) for i in range(...]
    dot_general x18 -> x0, matrix products: 69.7 us -> none  [dot(): return jnp.einsum(spec, left, right, preferred_element_type=f32)]
    ppermute x0 -> x43, starting transfers between devices: none -> 45.1 us  [the longest x24 35 us: swap(): lax.ppermute(value, AXES, [(i, i ^ 1 << orders[i & 1][k]) for i in range(...]
    psum x1 -> x0, blocking collectives: 40 us -> none  [on_device(): small = lax.psum(small, AXES)]
    transpose x5 -> x0, local copies, waits for them, and re-layouts: 16.3 us -> none  [the longest x3 7.59 us: scatter_grad(): part.astype(bf16).reshape(n_t, n_dp, rows, part.shape[2])]
  transfers between devices with their start and end apart: 8 -> 43, of which waited for: 6 -> 20; matrix products, arithmetic and copies ran while one was open for 16% -> 5% of each run, Pallas kernels for 0% -> 33%
where the time goes in v6:
time: 266 us; the launch traced here: 261 us
  Pallas kernels  103 us (39%)
  waiting for transfers between devices  77.7 us (29%)
  starting transfers between devices  45.1 us (17%)
  local copies, waits for them, and re-layouts  30.1 us (11%)
  other arithmetic  3.59 us (1%)
    pallas_call x7, Pallas kernels, call(): pl.pallas_call(body, out_shape=[*out_shapes, *grads], in_specs=[pl.BlockS...  81.1 us
    ppermute x24, waiting for transfers between devices, swap(): lax.ppermute(value, AXES, [(i, i ^ 1 << orders[i & 1][k]) for i in range(...  66 us
    ppermute x24, starting transfers between devices, swap(): lax.ppermute(value, AXES, [(i, i ^ 1 << orders[i & 1][k]) for i in range(...  35 us
    unnamed x132, local copies, waits for them, and re-layouts  23.9 us
    pallas_call x7, Pallas kernels, pull_call(): pl.pallas_call(kernel, out_shape=shapes, in_specs=specs, out_specs=[pl.Bl...  19.2 us
    ppermute x19, waiting for transfers between devices, flip(): return lax.ppermute(value, AXES, [(i, i ^ bits) for i in range(self.n)])  11.7 us
    ppermute x19, starting transfers between devices, flip(): return lax.ppermute(value, AXES, [(i, i ^ bits) for i in range(self.n)])  10.2 us
  transfers between devices with their start and end apart: 43, of which 20 were waited for; matrix products, arithmetic and copies ran while one was open for 5% of the time, Pallas kernels for 33%

profile of v6, /device:TPU:0, one launch (start us, length us, event | category | flops | bytes accessed | tf_op | source)
XLA Modules:
  0.0 261.0 jit_solution(7252208741867224046)
XLA Ops:
  2.5 4.1 %collective-permute-start = (bf16[1,96,768]{2,1,0:T(8,128)(2,1)S(1)}, bf16[1,96,768]{2,1,0:T(8,128)(2,1)S(1)}, u32[]{:S(2)}, u32[]{:S(2)}) collective-permute-start(bf16[1,96,768]{2,1,0:T(8,128)(2,1)S(1)} %maximum_bitcast_fusion.refs_0_), channel_id=1, source_target_pairs={{0,16},{1,17},{2,18},{3,19},{4,20},{5,21},{6,22},{7,23},{8,24},{9,... | collective-permute-start | bytes 442376 | tf_op jit(solution)/shard_map/ppermute | solution.py:37
  6.6 3.7 %constant_dynamic-slice_fusion.2 = (bf16[2,197,768]{2,0,1:T(2,128)(2,1)S(1)}, bf16[2,197,768]{2,0,1:T(2,128)(2,1)S(1)}) fusion(bf16[8,197,768]{2,0,1:T(8,128)(2,1)} %param.27, s32[]{:T(128)S(6)} %select_n.13, bf16[8,197,768]{2,0,1:T(8,128)(2,1)} %param.14), kind=kLoop, calls=%fused_computation.28 | loop fusion | bytes 2420740 | tf_op jit(solution)/shard_map/dynamic_slice | solution.py:589
  14.5 3.4 %collective-permute-start.5 = (bf16[1,96,768]{2,1,0:T(8,128)(2,1)S(1)}, bf16[1,96,768]{2,1,0:T(8,128)(2,1)S(1)}, u32[]{:S(2)}, u32[]{:S(2)}) collective-permute-start(bf16[1,96,768]{2,1,0:T(8,128)(2,1)S(1)} %bitcast.46), channel_id=1, source_target_pairs={{0,16},{1,17},{2,18},{3,19},{4,20},{5,21},{6,22},{7,23},{8,24},{9,... | collective-permute-start | bytes 442376 | tf_op jit(solution)/shard_map/ppermute | solution.py:37
  17.9 4.7 %collective-permute-done.5.refs_3_ = bf16[1,96,768]{2,1,0:T(8,128)(2,1)S(1)} collective-permute-done((bf16[1,96,768]{2,1,0:T(8,128)(2,1)S(1)}, bf16[1,96,768]{2,1,0:T(8,128)(2,1)S(1)}, u32[]{:S(2)}, u32[]{:S(2)}) %collective-permute-start.5) | collective-permute-done | bytes 147488 | tf_op jit(solution)/shard_map/ppermute | solution.py:37
  37.8 3.7 %collective-permute-done.7.refs_3_ = bf16[2,96,768]{2,1,0:T(8,128)(2,1)S(1)} collective-permute-done((bf16[2,96,768]{2,1,0:T(8,128)(2,1)S(1)}, bf16[2,96,768]{2,1,0:T(8,128)(2,1)S(1)}, u32[]{:S(2)}, u32[]{:S(2)}) %collective-permute-start.7) | collective-permute-done | bytes 294944 | tf_op jit(solution)/shard_map/ppermute | solution.py:37
  45.8 12.1 %collective-permute-done.9.refs_4_.refs_7_ = bf16[8,96,768]{2,1,0:T(8,128)(2,1)S(1)} collective-permute-done((bf16[8,96,768]{2,1,0:T(8,128)(2,1)S(1)}, bf16[8,96,768]{2,1,0:T(8,128)(2,1)S(1)}, u32[]{:S(2)}, u32[]{:S(2)}) %collective-permute-start.9) | collective-permute-done | bytes 1179680 | tf_op jit(solution)/shard_map/ppermute | solution.py:37
  57.9 3.2 %collective-permute-done.13.refs_3_ = bf16[2,96,768]{2,1,0:T(8,128)(2,1)S(1)} collective-permute-done((bf16[2,96,768]{2,1,0:T(8,128)(2,1)S(1)}, bf16[2,96,768]{2,1,0:T(8,128)(2,1)S(1)}, u32[]{:S(2)}, u32[]{:S(2)}) %collective-permute-start.13) | collective-permute-done | bytes 294944 | tf_op jit(solution)/shard_map/ppermute | solution.py:37
  65.1 14.5 %shard_map.250 = (bf16[416,768]{1,0:T(8,128)(2,1)}, bf16[4,416,576]{2,1,0:T(8,128)(2,1)}, bf16[4,416,192]{2,1,0:T(8,128)(2,1)}, f32[416,768]{1,0:T(8,128)}, bf16[416,768]{1,0:T(8,128)(2,1)}, /*index=5*/f32[8,128]{1,0:T(8,128)}) custom-call(s32[2]{0:T(128)} %pad_add_fusion.index_ref.ids_ref, bf16[416,768]{1,0:T(8,128)(2,1)} %bitcast.38, f32[6,768]{1,0:T(8,128)} %copy-done.21, ...), custom_call_target="tpu_custom_call" | custom-call | bytes 1024 | tf_op jit(solution)/shard_map/pallas_call | solution.py:333
  86.5 13.6 %shard_map.253 = (bf16[4,416,768]{2,1,0:T(8,128)(2,1)}, bf16[4,416,768]{2,1,0:T(8,128)(2,1)}, f32[8,128]{1,0:T(8,128)}, bf16[16,96,768]{2,1,0:T(8,128)(2,1)}, bf16[16,96,768]{2,1,0:T(8,128)(2,1)}) custom-call(s32[2]{0:T(128)} %pad_add_fusion.index_ref.ids_ref, bf16[416,768]{1,0:T(8,128)(2,1)} %get-tuple-element.84.refs_0_, bf16[416,768]{1,0:T(8,128)(2,1)} %bitcast.42, ...), custom_call_target="tpu_custom_call" | custom-call | bytes 1024 | tf_op jit(solution)/shard_map/pallas_call | solution.py:333
  104.4 17.9 %shard_map.255 = (f32[4,1,768]{2,1,0:T(1,128)}, bf16[416,768]{1,0:T(8,128)(2,1)}, f32[416,768]{1,0:T(8,128)}, f32[4,1,768]{2,1,0:T(1,128)}, f32[8,128]{1,0:T(8,1...) custom-call(s32[2]{0:T(128)} %pad_add_fusion.index_ref.ids_ref, ...), custom_call_target="tpu_custom_call" | custom-call | bytes 1024 | tf_op jit(solution)/shard_map/pallas_call | solution.py:333
  122.8 4.4 %collective-permute-done.22.refs_3_.refs_4_.refs_9_.refs_11_.refs_13_ = bf16[16,96,768]{2,1,0:T(8,128)(2,1)S(1)} collective-permute-done((bf16[16,96,768]{2,1,0:T(8,128)(2,1)}, bf16[16,96,768]{2,1,0:T(8,128)(2,1)S(1)}, u32[]{:S(2)}, u32[]{:S(2)}) %collective-permute-start.22) | collective-permute-done | bytes 2359328 | tf_op jit(solution)/shard_map/ppermute | solution.py:40
  135.8 25.1 %shard_map.257 = (f32[4,1,576]{2,1,0:T(1,128)}, f32[416,768]{1,0:T(8,128)}, f32[2,1,768]{2,1,0:T(1,128)}, f32[8,128]{1,0:T(8,128)}, bf16[16,96,768]{2,1,0:T(8,128)(2,1)}, /*index=5*/bf16[16,96,768]{2,1,0:T(8,128)(2,1)}) custom-call(s32[2]{0:T(128)} %pad_add_fusion.index_ref.ids_ref, bf16[416,768]{1,0:T(8,128)(2,1)} %bitcast.39, ...), custom_call_target="tpu_custom_call" | custom-call | bytes 1024 | tf_op jit(solution)/shard_map/pallas_call | solution.py:333
  171.1 3.6 %shard_map.260 = (bf16[800,768]{1,0:T(8,128)(2,1)}, bf16[32,768]{1,0:T(8,128)(2,1)S(1)}) custom-call(s32[2]{0:T(128)S(1)} %copy-done.32, f32[2,1,768]{2,1,0:T(1,128)S(1)} %copy-done.38, f32[4,1,768]{2,1,0:T(1,128)S(1)} %copy-done.36, f32[4,1,576]{2,1,0:T(1,128)S(1)} %copy-done.37, f32[4,1,768]{2,1,0:T(1,128)S(1)} %copy-done.35, ...), custom_call_target="tpu_custom_call" | custom-call | bytes 1024 | tf_op jit(solution)/shard_map/pallas_call | solution.py:191
  180.9 3.2 %shard_map.262 = (bf16[8,197,768]{2,1,0:T(8,128)(2,1)}, f32[8,128]{1,0:T(8,128)}) custom-call(s32[1]{0:T(128)} %bitcast.index_ref, bf16[2,208,768]{2,1,0:T(8,128)(2,1)} %get-tuple-element.110.refs_0_, bf16[2,208,768]{2,1,0:T(8,128)(2,1)} %copy-done.54, bf16[2,208,768]{2,1,0:T(8,128)(2,1)} %get-tuple-element.111.refs_2_, ...), custom_call_target="tpu_custom_call" | custom-call | bytes 1024 | tf_op jit(solution)/shard_map/pallas_call | solution.py:333
  184.1 9.5 %collective-permute-done.30.refs_7_.refs_8_.refs_9_ = bf16[4,96,768]{2,1,0:T(8,128)(2,1)S(1)} collective-permute-done((bf16[4,96,768]{2,1,0:T(8,128)(2,1)S(1)}, bf16[4,96,768]{2,1,0:T(8,128)(2,1)S(1)}, u32[]{:S(2)}, u32[]{:S(2)}) %collective-permute-start.30) | collective-permute-done | bytes 589856 | tf_op jit(solution)/shard_map/ppermute | solution.py:37
  200.6 4.6 %collective-permute-done.33.refs_9_.refs_10_ = bf16[2,96,768]{2,1,0:T(8,128)(2,1)S(1)} collective-permute-done((bf16[2,96,768]{2,1,0:T(8,128)(2,1)S(1)}, bf16[2,96,768]{2,1,0:T(8,128)(2,1)S(1)}, u32[]{:S(2)}, u32[]{:S(2)}) %collective-permute-start.33) | collective-permute-done | bytes 294944 | tf_op jit(solution)/shard_map/ppermute | solution.py:37
  205.2 9.0 %collective-permute-done.34.refs_14_.refs_16_ = bf16[2,96,768]{2,1,0:T(8,128)(2,1)S(1)} collective-permute-done((bf16[2,96,768]{2,1,0:T(8,128)(2,1)S(1)}, bf16[2,96,768]{2,1,0:T(8,128)(2,1)S(1)}, u32[]{:S(2)}, u32[]{:S(2)}) %collective-permute-start.34) | collective-permute-done | bytes 294944 | tf_op jit(solution)/shard_map/ppermute | solution.py:37
  217.3 3.5 %shard_map.265 = (bf16[416,768]{1,0:T(8,128)(2,1)}, f32[8,128]{1,0:T(8,128)}) custom-call(s32[2]{0:T(128)} %pad_add_fusion.index_ref.ids_ref, bf16[416,768]{1,0:T(8,128)(2,1)} %bitcast.40, f32[416,768]{1,0:T(8,128)} %get-tuple-element.90.refs_4_.refs_1_, f32[416,768]{1,0:T(8,128)} %get-tuple-element.113.refs_2_, f32[6,768]{1,0:T(8,128)} %copy-done.21, ...), custom_call_target="tpu_custom_call" | custom-call | bytes 1024 | tf_op jit(solution)/shard_map/pallas_call | solution.py:333
  226.0 4.9 %collective-permute-done.37.refs_11_ = bf16[1,96,768]{2,1,0:T(8,128)(2,1)S(1)} collective-permute-done((bf16[1,96,768]{2,1,0:T(8,128)(2,1)S(1)}, bf16[1,96,768]{2,1,0:T(8,128)(2,1)S(1)}, u32[]{:S(2)}, u32[]{:S(2)}) %collective-permute-start.37) | collective-permute-done | bytes 147488 | tf_op jit(solution)/shard_map/ppermute | solution.py:37
  230.9 5.2 %collective-permute-done.38.refs_17_ = bf16[1,96,768]{2,1,0:T(8,128)(2,1)S(1)} collective-permute-done((bf16[1,96,768]{2,1,0:T(8,128)(2,1)S(1)}, bf16[1,96,768]{2,1,0:T(8,128)(2,1)S(1)}, u32[]{:S(2)}, u32[]{:S(2)}) %collective-permute-start.38) | collective-permute-done | bytes 147488 | tf_op jit(solution)/shard_map/ppermute | solution.py:37
  236.0 4.1 %shard_map.266 = (bf16[128,768]{1,0:T(8,128)(2,1)S(1)}, bf16[32,768]{1,0:T(8,128)(2,1)S(1)}, f32[96,768]{1,0:T(8,128)}, f32[96,768]{1,0:T(8,128)}) custom-call(s32[2]{0:T(128)S(1)} %copy-done.33, bf16[32,768]{1,0:T(8,128)(2,1)S(1)} %copy-done.27, bf16[1536,768]{1,0:T(8,128)(2,1)} %bitcast.34, bf16[1536,768]{1,0:T(8,128)(2,1)} %copy-done.43, ...), custom_call_target="tpu_custom_call" | custom-call | bytes 1024 | tf_op jit(solution)/shard_map/pallas_call | solution.py:191
  242.1 3.7 %copy.42 = bf16[8,197,768]{2,0,1:T(8,128)(2,1)} copy(bf16[8,197,768]{2,1,0:T(8,128)(2,1)} %get-tuple-element.134.refs_13_) | data formatting | bytes 4841472
  247.5 3.2 %shard_map.268 = (bf16[8,197,768]{2,1,0:T(8,128)(2,1)}, f32[8,128]{1,0:T(8,128)}) custom-call(s32[1]{0:T(128)} %bitcast.index_ref, bf16[2,208,768]{2,1,0:T(8,128)(2,1)} %get-tuple-element.126.refs_0_, bf16[2,208,768]{2,1,0:T(8,128)(2,1)} %copy-done.52, bf16[2,208,768]{2,1,0:T(8,128)(2,1)} %get-tuple-element.127.refs_2_, bf16[2,208,768]{2,1,0:T(8,128)(2,1)} %copy-done.53), custom_call_target="tpu_custom_call" | custom-call | bytes 1024 | tf_op jit(solution)/shard_map/pallas_call | solution.py:333
  250.7 3.3 %collective-permute-done.41.refs_5_.refs_6_ = bf16[128,768]{1,0:T(8,128)(2,1)S(1)} collective-permute-done((bf16[128,768]{1,0:T(8,128)(2,1)S(1)}, bf16[128,768]{1,0:T(8,128)(2,1)S(1)}, u32[]{:S(2)}, u32[]{:S(2)}) %collective-permute-start.41) | collective-permute-done | bytes 196640 | tf_op jit(solution)/shard_map/ppermute | solution.py:37
  (248 shorter events, 91.2 us)
Async XLA Ops:
  2.5 11.1 %collective-permute-start = (bf16[1,96,768]{2,1,0:T(8,128)(2,1)S(1)}, bf16[1,96,768]{2,1,0:T(8,128)(2,1)S(1)}, u32[]{:S(2)}, u32[]{:S(2)}) collective-permute-start(bf16[1,96,768]{2,1,0:T(8,128)(2,1)S(1)} %maximum_bitcast_fusion.refs_0_), channel_id=1, source_target_pairs={{0,16},{1,17},{2,18},{3,19},{4,20},{5,21},{6,22},{7,23},{8,24},{9,... | collective-permute-start | bytes 442376 | tf_op jit(solution)/shard_map/ppermute | solution.py:37
  23.8 17.7 %collective-permute-start.6 = (bf16[4,96,768]{2,1,0:T(8,128)(2,1)S(1)}, bf16[4,96,768]{2,1,0:T(8,128)(2,1)S(1)}, u32[]{:S(2)}, u32[]{:S(2)}) collective-permute-start(bf16[4,96,768]{2,1,0:T(8,128)(2,1)S(1)} %get-tuple-element.74.refs_0_), channel_id=1, source_target_pairs={{0,2},{1,9},{2,0},{3,11},{4,6},{5,13},{6,4},{7,15},{8,10},{9,1},{1... | collective-permute-start | bytes 1769480 | tf_op jit(solution)/shard_map/ppermute | solution.py:37
  41.6 16.3 %collective-permute-start.9 = (bf16[8,96,768]{2,1,0:T(8,128)(2,1)S(1)}, bf16[8,96,768]{2,1,0:T(8,128)(2,1)S(1)}, u32[]{:S(2)}, u32[]{:S(2)}) collective-permute-start(bf16[8,96,768]{2,1,0:T(8,128)(2,1)S(1)} %get-tuple-element.76.refs_3_.refs_6_), channel_id=1, source_target_pairs={{0,4},{1,3},{2,6},{3,1},{4,0},{5,7},{6,2},{7,5},{8,12},{9,11},{10,... | collective-permute-start | bytes 3538952 | tf_op jit(solution)/shard_map/ppermute | solution.py:37
  43.1 18.0 %collective-permute-start.12 = (bf16[4,96,768]{2,1,0:T(8,128)(2,1)S(1)}, bf16[4,96,768]{2,1,0:T(8,128)(2,1)S(1)}, u32[]{:S(2)}, u32[]{:S(2)}) collective-permute-start(bf16[4,96,768]{2,1,0:T(8,128)(2,1)S(1)} %get-tuple-element.77.refs_0_), channel_id=1, source_target_pairs={{0,8},{1,9},{2,10},{3,11},{4,12},{5,13},{6,14},{7,15},{8,0},{9,1},... | collective-permute-start | bytes 1769480 | tf_op jit(solution)/shard_map/ppermute | solution.py:37
  44.9 16.2 %collective-permute-start.13 = (bf16[2,96,768]{2,1,0:T(8,128)(2,1)S(1)}, bf16[2,96,768]{2,1,0:T(8,128)(2,1)S(1)}, u32[]{:S(2)}, u32[]{:S(2)}) collective-permute-start(bf16[2,96,768]{2,1,0:T(8,128)(2,1)S(1)} %get-tuple-element.78.refs_2_), channel_id=1, source_target_pairs={{0,4},{1,3},{2,6},{3,1},{4,0},{5,7},{6,2},{7,5},{8,12},{9,11},{10,... | collective-permute-start | bytes 884744 | tf_op jit(solution)/shard_map/ppermute | solution.py:37
  45.8 19.3 %collective-permute-start.10 = (bf16[8,96,768]{2,1,0:T(8,128)(2,1)S(1)}, bf16[8,96,768]{2,1,0:T(8,128)(2,1)}, u32[]{:S(2)}, u32[]{:S(2)}) collective-permute-start(bf16[8,96,768]{2,1,0:T(8,128)(2,1)S(1)} %get-tuple-element.76.refs_3_.refs_6_), channel_id=1, source_target_pairs={{0,1},{1,0},{2,3},{3,2},{4,5},{5,4},{6,7},{7,6},{8,9},{9,8},{10,11... | collective-permute-start | bytes 3538952 | tf_op jit(solution)/shard_map/ppermute | solution.py:40
  62.0 17.6 %collective-permute-start.14 = (bf16[8,96,768]{2,1,0:T(8,128)(2,1)S(1)}, bf16[8,96,768]{2,1,0:T(8,128)(2,1)}, u32[]{:S(2)}, u32[]{:S(2)}) collective-permute-start(bf16[8,96,768]{2,1,0:T(8,128)(2,1)S(1)} %get-tuple-element.79.refs_7_.refs_3_.refs_6_), channel_id=1, source_target_pairs={{0,4},{1,3},{2,6},{3,1},{4,0},{5,7},{6,2},{7,5},{8,12},{9,11},{10,... | collective-permute-start | bytes 3538952 | tf_op jit(solution)/shard_map/ppermute | solution.py:37
  63.5 18.5 %collective-permute-start.17 = (bf16[4,96,768]{2,1,0:T(8,128)(2,1)}, bf16[4,96,768]{2,1,0:T(8,128)(2,1)}, u32[]{:S(2)}, u32[]{:S(2)}) collective-permute-start(bf16[4,96,768]{2,1,0:T(8,128)(2,1)} %get-tuple-element.80.refs_8_.refs_0_), channel_id=1, source_target_pairs={{0,2},{1,9},{2,0},{3,11},{4,6},{5,13},{6,4},{7,15},{8,10},{9,1},{1... | collective-permute-start | bytes 1769480 | tf_op jit(solution)/shard_map/ppermute | solution.py:37
  65.1 20.3 %collective-permute-start.15 = (bf16[8,96,768]{2,1,0:T(8,128)(2,1)S(1)}, bf16[8,96,768]{2,1,0:T(8,128)(2,1)}, u32[]{:S(2)}, u32[]{:S(2)}) collective-permute-start(bf16[8,96,768]{2,1,0:T(8,128)(2,1)S(1)} %get-tuple-element.79.refs_7_.refs_3_.refs_6_), channel_id=1, source_target_pairs={{0,1},{1,0},{2,3},{3,2},{4,5},{5,4},{6,7},{7,6},{8,9},{9,8},{10,11... | collective-permute-start | bytes 3538952 | tf_op jit(solution)/shard_map/ppermute | solution.py:40
  83.3 16.8 %collective-permute-start.18 = (bf16[8,96,768]{2,1,0:T(8,128)(2,1)S(1)}, bf16[8,96,768]{2,1,0:T(8,128)(2,1)}, u32[]{:S(2)}, u32[]{:S(2)}) collective-permute-start(bf16[8,96,768]{2,1,0:T(8,128)(2,1)S(1)} %shard_map.252.refs_7_.refs_10_), channel_id=1, source_target_pairs={{0,8},{1,5},{2,10},{3,7},{4,12},{5,1},{6,14},{7,3},{8,0},{9,13},{1... | collective-permute-start | bytes 3538952 | tf_op jit(solution)/shard_map/ppermute | solution.py:37
  85.4 15.4 %collective-permute-start.19 = (bf16[8,96,768]{2,1,0:T(8,128)(2,1)S(1)}, bf16[8,96,768]{2,1,0:T(8,128)(2,1)S(1)}, u32[]{:S(2)}, u32[]{:S(2)}) collective-permute-start(bf16[8,96,768]{2,1,0:T(8,128)(2,1)S(1)} %shard_map.252.refs_7_.refs_10_), channel_id=1, source_target_pairs={{0,1},{1,0},{2,3},{3,2},{4,5},{5,4},{6,7},{7,6},{8,9},{9,8},{10,11... | collective-permute-start | bytes 3538952 | tf_op jit(solution)/shard_map/ppermute | solution.py:40
  100.7 22.1 %collective-permute-start.21 = (bf16[16,96,768]{2,1,0:T(8,128)(2,1)}, bf16[16,96,768]{2,1,0:T(8,128)(2,1)S(1)}, u32[]{:S(2)}, u32[]{:S(2)}) collective-permute-start(bf16[16,96,768]{2,1,0:T(8,128)(2,1)} %get-tuple-element.92), channel_id=1, source_target_pairs={{0,1},{1,0},{2,3},{3,2},{4,5},{5,4},{6,7},{7,6},{8,9},{9,8},{10,11... | collective-permute-start | bytes 7077896 | tf_op jit(solution)/shard_map/ppermute | solution.py:40
  131.7 29.2 %collective-permute-start.23 = (bf16[8,96,768]{2,1,0:T(8,128)(2,1)S(1)}, bf16[8,96,768]{2,1,0:T(8,128)(2,1)S(1)}, u32[]{:S(2)}, u32[]{:S(2)}) collective-permute-start(bf16[8,96,768]{2,1,0:T(8,128)(2,1)S(1)} %get-tuple-element.96.refs_10_), channel_id=1, source_target_pairs={{0,8},{1,5},{2,10},{3,7},{4,12},{5,1},{6,14},{7,3},{8,0},{9,13},{1... | collective-permute-start | bytes 3538952 | tf_op jit(solution)/shard_map/ppermute | solution.py:37
  133.2 27.8 %collective-permute-start.24 = (bf16[8,96,768]{2,1,0:T(8,128)(2,1)S(1)}, bf16[8,96,768]{2,1,0:T(8,128)(2,1)S(1)}, u32[]{:S(2)}, u32[]{:S(2)}) collective-permute-start(bf16[8,96,768]{2,1,0:T(8,128)(2,1)S(1)} %get-tuple-element.97.refs_11_), channel_id=1, source_target_pairs={{0,4},{1,3},{2,6},{3,1},{4,0},{5,7},{6,2},{7,5},{8,12},{9,11},{10,... | collective-permute-start | bytes 3538952 | tf_op jit(solution)/shard_map/ppermute | solution.py:37
  134.3 26.7 %collective-permute-start.25 = (bf16[2,208,768]{2,1,0:T(8,128)(2,1)S(1)}, bf16[2,208,768]{2,1,0:T(8,128)(2,1)}, u32[]{:S(2)}, u32[]{:S(2)}) collective-permute-start(bf16[2,208,768]{2,1,0:T(8,128)(2,1)S(1)} %bitcast.49), channel_id=1, source_target_pairs={{0,2},{1,3},{2,0},{3,1},{4,6},{5,7},{6,4},{7,5},{8,10},{9,11},{10,... | collective-permute-start | bytes 1916936 | tf_op jit(solution)/shard_map/ppermute | solution.py:40
  175.3 19.3 %collective-permute-start.29 = (bf16[800,768]{1,0:T(8,128)(2,1)}, bf16[800,768]{1,0:T(8,128)(2,1)S(1)}, u32[]{:S(2)}, u32[]{:S(2)}) collective-permute-start(bf16[800,768]{1,0:T(8,128)(2,1)} %get-tuple-element.114), channel_id=1, source_target_pairs={{0,4},{1,3},{2,6},{3,1},{4,0},{5,7},{6,2},{7,5},{8,12},{9,11},{10,... | collective-permute-start | bytes 3686408 | tf_op jit(solution)/shard_map/ppermute | solution.py:37
  177.3 16.3 %collective-permute-start.30 = (bf16[4,96,768]{2,1,0:T(8,128)(2,1)S(1)}, bf16[4,96,768]{2,1,0:T(8,128)(2,1)S(1)}, u32[]{:S(2)}, u32[]{:S(2)}) collective-permute-start(bf16[4,96,768]{2,1,0:T(8,128)(2,1)S(1)} %copy-done.42), channel_id=1, source_target_pairs={{0,2},{1,9},{2,0},{3,11},{4,6},{5,13},{6,4},{7,15},{8,10},{9,1},{1... | collective-permute-start | bytes 1769480 | tf_op jit(solution)/shard_map/ppermute | solution.py:37
  178.4 16.3 %collective-permute-start.31 = (bf16[4,96,768]{2,1,0:T(8,128)(2,1)S(1)}, bf16[4,96,768]{2,1,0:T(8,128)(2,1)S(1)}, u32[]{:S(2)}, u32[]{:S(2)}) collective-permute-start(bf16[4,96,768]{2,1,0:T(8,128)(2,1)S(1)} %get-tuple-element.108.refs_6_), channel_id=1, source_target_pairs={{0,8},{1,9},{2,10},{3,11},{4,12},{5,13},{6,14},{7,15},{8,0},{9,1},... | collective-permute-start | bytes 1769480 | tf_op jit(solution)/shard_map/ppermute | solution.py:37
  197.4 16.8 %collective-permute-start.32 = (bf16[416,768]{1,0:T(8,128)(2,1)S(1)}, bf16[416,768]{1,0:T(8,128)(2,1)S(1)}, u32[]{:S(2)}, u32[]{:S(2)}) collective-permute-start(bf16[416,768]{1,0:T(8,128)(2,1)S(1)} %get-tuple-element.117), channel_id=1, source_target_pairs={{0,2},{1,9},{2,0},{3,11},{4,6},{5,13},{6,4},{7,15},{8,10},{9,1},{1... | collective-permute-start | bytes 1916936 | tf_op jit(solution)/shard_map/ppermute | solution.py:37
  199.4 14.8 %collective-permute-start.34 = (bf16[2,96,768]{2,1,0:T(8,128)(2,1)S(1)}, bf16[2,96,768]{2,1,0:T(8,128)(2,1)S(1)}, u32[]{:S(2)}, u32[]{:S(2)}) collective-permute-start(bf16[2,96,768]{2,1,0:T(8,128)(2,1)S(1)} %get-tuple-element.119), channel_id=1, source_target_pairs={{0,2},{1,5},{2,0},{3,7},{4,6},{5,1},{6,4},{7,3},{8,10},{9,13},{10,... | collective-permute-start | bytes 884744 | tf_op jit(solution)/shard_map/ppermute | solution.py:37
  220.9 19.9 %collective-permute-start.35 = (bf16[2,208,768]{2,1,0:T(8,128)(2,1)}, bf16[2,208,768]{2,1,0:T(8,128)(2,1)S(1)}, u32[]{:S(2)}, u32[]{:S(2)}) collective-permute-start(bf16[2,208,768]{2,1,0:T(8,128)(2,1)} %bitcast.50), channel_id=1, source_target_pairs={{0,2},{1,3},{2,0},{3,1},{4,6},{5,7},{6,4},{7,5},{8,10},{9,11},{10,... | collective-permute-start | bytes 1916936 | tf_op jit(solution)/shard_map/ppermute | solution.py:40
  221.9 14.2 %collective-permute-start.36 = (bf16[224,768]{1,0:T(8,128)(2,1)S(1)}, bf16[224,768]{1,0:T(8,128)(2,1)S(1)}, u32[]{:S(2)}, u32[]{:S(2)}) collective-permute-start(bf16[224,768]{1,0:T(8,128)(2,1)S(1)} %get-tuple-element.122), channel_id=1, source_target_pairs={{0,8},{1,5},{2,10},{3,7},{4,12},{5,1},{6,14},{7,3},{8,0},{9,13},{1... | collective-permute-start | bytes 1032200 | tf_op jit(solution)/shard_map/ppermute | solution.py:37
  225.5 10.6 %collective-permute-start.38 = (bf16[1,96,768]{2,1,0:T(8,128)(2,1)S(1)}, bf16[1,96,768]{2,1,0:T(8,128)(2,1)S(1)}, u32[]{:S(2)}, u32[]{:S(2)}) collective-permute-start(bf16[1,96,768]{2,1,0:T(8,128)(2,1)S(1)} %get-tuple-element.124), channel_id=1, source_target_pairs={{0,16},{1,17},{2,18},{3,19},{4,20},{5,21},{6,22},{7,23},{8,24},{9,... | collective-permute-start | bytes 442376 | tf_op jit(solution)/shard_map/ppermute | solution.py:37
  242.1 11.9 %collective-permute-start.41 = (bf16[128,768]{1,0:T(8,128)(2,1)S(1)}, bf16[128,768]{1,0:T(8,128)(2,1)S(1)}, u32[]{:S(2)}, u32[]{:S(2)}) collective-permute-start(bf16[128,768]{1,0:T(8,128)(2,1)S(1)} %get-tuple-element.129), channel_id=1, source_target_pairs={{0,16},{1,17},{2,18},{3,19},{4,20},{5,21},{6,22},{7,23},{8,24},{9,... | collective-permute-start | bytes 589832 | tf_op jit(solution)/shard_map/ppermute | solution.py:37
  (82 other events, 605.8 us)

commit v7 on v6

--- a/solution.py
+++ b/solution.py
@@ -12,6 +12,7 @@
 AXES = ("dp", "tensor")
 TILE = 16
 ROWS = 32
+MIB = 1024 * 1024
 FACTOR = HEAD_DIM ** (-0.5)
 bf16 = jnp.bfloat16
 f32 = jnp.float32
@@ -24,25 +25,29 @@
         n_bits = self.n.bit_length() - 1
         self.fast = (1 << n_bits) == self.n and n_bits >= 4 and rows % TILE == 0
         far = list(range(n_bits - 1, 3, -1))
-        self.orders = [
+        self.gather = [
+            ([2, 3, 1] + far, [1, 2, 3] + far),
+            ([2, 3, 1] + far, [1, 3, 2] + far),
+            ([2, 3, 1] + far, [1, 3, 2] + far),
+        ]
+        self.scatter = [
             ([2, 1, 3] + far, [1, 3, 2] + far),
             ([2, 3, 1] + far, [1, 3, 2] + far),
-            ([3, 1, 2] + far, [2, 3, 1] + far),
+            ([2, 3, 1] + far, [1, 3, 2] + far),
         ]
         self.steps = 3 + len(far)
         self.half = self.n // 2
 
-    def swap(self, group, value, k):
-        orders = self.orders[group]
+    def swap(self, orders, value, k):
         return lax.ppermute(value, AXES, [(i, i ^ (1 << orders[i & 1][k])) for i in range(self.n)])
 
     def flip(self, value, bits):
         return lax.ppermute(value, AXES, [(i, i ^ bits) for i in range(self.n)])
 
-    def at(self, group, ids_ref, core, y, block):
+    def at(self, orders, ids_ref, core, y, block):
         relative = ((ids_ref[0] ^ block) << 2) | (y << 1)
         found = []
-        for order in self.orders[group]:
+        for order in orders:
             place = 0
             for k, bit in enumerate(order[::-1]):
                 place = place | (((relative >> bit) & 1) << k)
@@ -81,7 +86,7 @@
             return
         for d in range(self.n_dp):
             rows = slice(d * self.rows, (d + 1) * self.rows)
-            shard[rows, :] = held[core, self.at(group, ids_ref, core, y, d)]
+            shard[rows, :] = held[core, self.at(self.gather[group], ids_ref, core, y, d)]
 
     def grad_buffers(self, cols):
         shape = self.grad_shape(cols).shape
@@ -93,7 +98,7 @@
             return
         for d in range(self.n_dp):
             rows = value[d * self.rows : (d + 1) * self.rows]
-            scratch[0][core, self.at(group, ids_ref, core, y, d)] = rows
+            scratch[0][core, self.at(self.scatter[group], ids_ref, core, y, d)] = rows
 
     def send_out(self, scratch, core, ref):
         copy = pltpu.make_async_copy(scratch[0].at[core], ref, scratch[1].at[core])
@@ -137,64 +142,53 @@
     return plain_call(kernel, shapes, [x for p in pairs for x in p], after)
 
 
-def sends(groups, after=()):
-    sizes = [min(v.shape[0] for v in g) // 2 for g in groups]
-    inputs = [(v, size) for g, size in zip(groups, sizes) for v in g]
-    shapes = [jax.ShapeDtypeStruct((n,) + g[0].shape[1:], bf16) for g, n in zip(groups, sizes)]
+def fold(pairs, after=()):
+    shapes = []
+    for a, _ in pairs:
+        shapes += [jax.ShapeDtypeStruct((a.shape[0] // 2,) + a.shape[1:], bf16)] * 2
+    n_in = 2 * len(pairs)
 
     def kernel(*refs):
-        outs = refs[len(inputs) + len(after) :]
-        parts = pull(refs, [(size, size) for _, size in inputs], outs[len(groups) :])
-        for g, out in zip(groups, outs):
-            out[...] = added(parts, len(g)).astype(bf16)
-
-    return pull_call(kernel, shapes, [v for v, _ in inputs], [n for _, n in inputs], after)
-
-
-def pull(refs, spots, scratch):
-    sems = scratch[len(spots)]
-    copies = [
-        pltpu.make_async_copy(refs[i].at[pl.ds(start, size)], scratch[i], sems.at[i])
-        for i, (start, size) in enumerate(spots)
-    ]
-    for copy in copies:
-        copy.start()
-
-    def each():
-        for i, copy in enumerate(copies):
-            copy.wait()
-            yield scratch[i][...]
-
-    return each()
-
-
-def added(parts, n):
-    value = next(parts).astype(f32)
-    for _ in range(n - 1):
-        value = value + next(parts).astype(f32)
-    return value
-
-
-def pull_call(kernel, shapes, inputs, sizes, after, ids=None, whole=(), scratch=()):
-    specs = [pl.BlockSpec(memory_space=pltpu.HBM)] * len(inputs)
+        outs = refs[n_in + len(after) :]
+        for i in range(len(pairs)):
+            size = shapes[2 * i].shape[0]
+            for part in range(2):
+                add_rows(outs[2 * i + part], refs[2 * i : 2 * i + 2], (1 - part) * size)
+
+    found = vmem_call(kernel, shapes, [x for p in pairs for x in p], after)
+    return [found[2 * i : 2 * i + 2] for i in range(len(pairs))]
+
+
+def add_rows(out_ref, refs, start):
+    size, rows, _ = out_ref.shape
+
+    def step(i, carry):
+        for c in range(0, rows, ROWS):
+            at = (i, slice(c, c + ROWS), slice(None))
+            source = (start + i, slice(c, c + ROWS), slice(None))
+            value = refs[0][source].astype(f32)
+            for ref in refs[1:]:
+                value = value + ref[source].astype(f32)
+            out_ref[at] = value.astype(out_ref.dtype)
+        return carry
+
+    lax.fori_loop(0, size, step, 0)
+
+
+def vmem_call(kernel, shapes, inputs, after, ids=None, scratch=()):
+    specs = [pl.BlockSpec(memory_space=pltpu.VMEM)] * len(inputs)
     specs += [pl.BlockSpec(memory_space=pl.ANY)] * len(after)
     values = [*inputs, *after]
-    pulled = [pltpu.VMEM((n,) + v.shape[1:], bf16) for v, n in zip(inputs, sizes)]
-    pulled += [pltpu.SemaphoreType.DMA((len(inputs),)), *scratch]
     if ids is not None:
-        specs = [
-            pl.BlockSpec(memory_space=pltpu.SMEM),
-            *[pl.BlockSpec(memory_space=pltpu.VMEM)] * len(whole),
-            *specs,
-        ]
-        values = [ids, *whole, *values]
+        specs = [pl.BlockSpec(memory_space=pltpu.SMEM), *specs]
+        values = [ids, *values]
     return pl.pallas_call(
         kernel,
         out_shape=shapes,
         in_specs=specs,
         out_specs=[pl.BlockSpec(memory_space=pltpu.VMEM)] * len(shapes),
-        scratch_shapes=pulled,
-        compiler_params=pltpu.CompilerParams(vmem_limit_bytes=48 * 1024 * 1024),
+        scratch_shapes=list(scratch),
+        compiler_params=pltpu.CompilerParams(vmem_limit_bytes=48 * MIB),
         cost_estimate=pl.CostEstimate(flops=0, bytes_accessed=1024, transcendentals=0),
     )(*values)
 
@@ -207,52 +201,56 @@
         out_shape=shapes,
         in_specs=specs + [pl.BlockSpec(memory_space=pl.ANY)] * len(after),
         out_specs=[pl.BlockSpec(x.shape, lambda i, n=len(x.shape): (0,) * n) for x in shapes],
-        compiler_params=pltpu.CompilerParams(vmem_limit_bytes=48 * 1024 * 1024),
+        compiler_params=pltpu.CompilerParams(vmem_limit_bytes=48 * MIB),
         cost_estimate=pl.CostEstimate(flops=0, bytes_accessed=1024, transcendentals=0),
     )(*inputs, *after)
 
 
-def sends_with_small(cube, group, groups, small, ids, after=(), final=False):
-    rows = cube.rows
-    kept = [v.shape[0] // rows * rows for v in group]
-    size = min(kept) // 2
-    d = group[0].shape[1]
+def fold_with_small(cube, kept, came, small, pairs, finals, ids, after=()):
     first = len(small) > 1
-    sizes = [min(v.shape[0] for v in g) // 2 for g in groups]
+    size, d = kept.shape[0] // 2, kept.shape[1]
     shapes = [
         jax.ShapeDtypeStruct((size + ROWS, d), bf16),
+        jax.ShapeDtypeStruct((size, d), bf16),
         jax.ShapeDtypeStruct((ROWS, d), bf16),
     ]
-    if final:
-        shapes += [jax.ShapeDtypeStruct(g[0].shape[1:], f32) for g in groups]
-    else:
-        shapes += [jax.ShapeDtypeStruct((n,) + g[0].shape[1:], bf16) for g, n in zip(groups, sizes)]
-    inputs = list(group) + [v for g in groups for v in g]
-    spots = [(size, size)] * len(group)
-    spots += [(0, 1) if final else (n, n) for g, n in zip(groups, sizes) for _ in g]
-    if not first:
-        inputs.append(group[-1])
-        spots.append((kept[-1], ROWS))
-
-    def kernel(ids_ref, *refs):
+    for a, _ in pairs:
+        shapes += [jax.ShapeDtypeStruct((a.shape[0] // 2,) + a.shape[1:], bf16)] * 2
+    shapes += [jax.ShapeDtypeStruct(a.shape[1:], f32) for a, _ in finals]
+    others = [x for p in [*pairs, *finals] for x in p]
+
+    def kernel(ids_ref, kept_ref, came_ref, *refs):
         extra, refs = refs[: len(small)], refs[len(small) :]
-        outs = refs[len(inputs) + len(after) :]
+        ins, outs = refs[: len(others)], refs[len(others) + len(after) :]
+        send_ref, keep_ref, low_ref = outs[:3]
         total_ref = outs[-1]
-        parts = pull(refs, spots, outs[len(shapes) :])
-        outs[0][:size, :] = added(parts, len(group)).astype(bf16)
-        for g, out in zip(groups, outs[2:]):
-            value = added(parts, len(g))
-            out[...] = value[0] if final else value.astype(bf16)
+        for n in range(len(pairs)):
+            for part in range(2):
+                out_ref = outs[3 + 2 * n + part]
+                add_rows(out_ref, ins[2 * n : 2 * n + 2], (1 - part) * out_ref.shape[0])
+        for n in range(len(pairs), len(pairs) + len(finals)):
+            total = ins[2 * n][0].astype(f32) + ins[2 * n + 1][0].astype(f32)
+            outs[3 + len(pairs) + n][...] = total
+
+        def step(i, carry):
+            at = pl.ds(pl.multiple_of(i * ROWS, ROWS), ROWS)
+            there = pl.ds(pl.multiple_of(size + i * ROWS, ROWS), ROWS)
+            sent = kept_ref[there, :].astype(f32) + came_ref[there, :].astype(f32)
+            send_ref[at, :] = sent.astype(bf16)
+            keep_ref[at, :] = (kept_ref[at, :].astype(f32) + came_ref[at, :].astype(f32)).astype(bf16)
+            return carry
+
+        lax.fori_loop(0, size // ROWS, step, 0)
         if first:
             gather_small(cube, ids_ref, extra, total_ref)
         else:
-            total_ref[...] = extra[0][...].astype(f32) + added(parts, 1)
+            total_ref[...] = extra[0][...].astype(f32) + came_ref[2 * size :, :].astype(f32)
         low = total_ref[...].astype(bf16)
-        outs[0][size:, :] = low
-        outs[1][...] = low
-
-    return pull_call(
-        kernel, shapes, inputs, [n for _, n in spots], after, ids, small, [pltpu.VMEM((ROWS, d), f32)]
+        send_ref[size:, :] = low
+        low_ref[...] = low
+
+    return vmem_call(
+        kernel, shapes, [kept, came, *small, *others], after, ids, [pltpu.VMEM((ROWS, d), f32)]
     )
 
 
@@ -273,19 +271,16 @@
         out_ref[pl.ds(6 + 2 * n_t + t, 1), :width] = dbias[:, 2 * width :]
 
 
-def finish_with_small(cube, group, small, ids, after=()):
-    rows, d = cube.rows, group[0].shape[1]
-    inputs = [*group, group[-1]]
-    spots = [(0, rows)] * len(group) + [(group[-1].shape[0] - ROWS, ROWS)]
-
-    def kernel(ids_ref, small_ref, *refs):
-        outs = refs[len(inputs) + len(after) :]
-        parts = pull(refs, spots, outs[2:])
-        outs[0][...] = added(parts, len(group))
-        outs[1][...] = (small_ref[...].astype(f32) + added(parts, 1)).astype(bf16)
+def finish_with_small(kept, came, small, after=()):
+    rows, d = kept.shape
+
+    def kernel(kept_ref, came_ref, small_ref, *refs):
+        outs = refs[len(after) :]
+        outs[0][...] = kept_ref[...].astype(f32) + came_ref[:rows, :].astype(f32)
+        outs[1][...] = (small_ref[...].astype(f32) + came_ref[rows:, :].astype(f32)).astype(bf16)
 
     shapes = [jax.ShapeDtypeStruct((rows, d), f32), jax.ShapeDtypeStruct(small.shape, bf16)]
-    return pull_call(kernel, shapes, inputs, [n for _, n in spots], after, ids, [small])
+    return vmem_call(kernel, shapes, [kept, came, small], after)
 
 
 def hold(values, after):
@@ -311,12 +306,16 @@
     index = lax.axis_index("tensor").astype(jnp.int32).reshape(1)
 
     def kernel(index_ref, *refs):
+        out_ref, ordered = refs[4:]
         for r in range(4):
             for i in range(count):
-                refs[-1][(index_ref[0] ^ r) * count + i] = refs[r][i, :length, :]
-
-    shape = (4 * count, length, pieces[0].shape[2])
-    return call(kernel, [jax.ShapeDtypeStruct(shape, bf16)], index, pieces, [], [], after)[0]
+                ordered[(index_ref[0] ^ r) * count + i] = refs[r][i]
+        out_ref[...] = jnp.swapaxes(ordered[...], 0, 1)[:length]
+
+    shape = (length, 4 * count, pieces[0].shape[2])
+    ordered = pltpu.VMEM((4 * count,) + pieces[0].shape[1:], bf16)
+    out = call(kernel, [jax.ShapeDtypeStruct(shape, bf16)], index, pieces, [], [ordered], after)[0]
+    return out.transpose(1, 0, 2)
 
 
 def call(kernel, out_shapes, index, inputs, weights, scratch, after=(), grads=()):
@@ -339,7 +338,7 @@
         + [pl.BlockSpec(memory_space=pl.ANY)] * len(after),
         out_specs=spots,
         scratch_shapes=scratch,
-        compiler_params=pltpu.CompilerParams(vmem_limit_bytes=56 * 1024 * 1024),
+        compiler_params=pltpu.CompilerParams(vmem_limit_bytes=56 * MIB),
         cost_estimate=pl.CostEstimate(flops=0, bytes_accessed=1024, transcendentals=0),
     )(index, *inputs, *weights, *after)
 
@@ -612,23 +611,22 @@
         held = attn_piece[None]
         one = fc1_weight[None]
         two = two_piece[None]
+        (biases,) = hold([biases], (x,))
+        biases = [biases] + [cube.flip(biases, r) for r in range(1, n_t)]
+        qkv_bias, f_bias = bias_parts(jnp.concatenate(biases))
         for k in range(last, 0, -1):
-            pairs = [(held, cube.swap(0, held, k))]
+            pairs = [(held, cube.swap(cube.gather[0], held, k))]
             if k < last:
-                pairs.append((one, cube.swap(1, one, k + 1)))
+                pairs.append((one, cube.swap(cube.gather[1], one, k + 1)))
             if k < last - 1:
-                pairs.append((two, cube.swap(2, two, k + 2)))
-            tokens_in = (x, cot) if k == last else (vecs, qkv_bias, f_bias) if k == 1 else ()
+                pairs.append((two, cube.swap(cube.gather[2], two, k + 2)))
+            tokens_in = ((x, cot), (qkv_bias, f_bias), (vecs,))[min(last - k, 2)]
             found = join(pairs, tokens_in)
             held = found[0]
             one = found[1] if k < last else one
             two = found[2] if k < last - 1 else two
-            if k == last:
-                (biases,) = hold([biases], (held,))
-                biases = [biases] + [cube.flip(biases, r) for r in range(1, n_t)]
-                qkv_bias, f_bias = bias_parts(jnp.concatenate(biases))
-        came = cube.swap(0, held, 0)
-        pairs = [(one, cube.swap(1, one, 1)), (two, cube.swap(2, two, 2))]
+        came = cube.swap(cube.gather[0], held, 0)
+        pairs = [(one, cube.swap(cube.gather[1], one, 1)), (two, cube.swap(cube.gather[2], two, 2))]
         w_attn = [held, came, cube.flip(held, 1), cube.flip(came, 1)]
         one, two = join(pairs, (came,))
         slot = (one, two)
@@ -660,9 +658,11 @@
         slot,
     )
     if cube.fast:
-        (came,) = hold([cube.swap(1, one, 0)], (done,))
+        came, there = hold(
+            [cube.swap(cube.gather[1], one, 0), cube.swap(cube.gather[2], two, 1)], (done,)
+        )
         w_one = [one, came, cube.flip(one, 1), cube.flip(came, 1)]
-        (two,) = join([(two, cube.swap(2, two, 1))], (done,))
+        (two,) = join([(two, there)])
         slot = (two,)
     act, slope, done, *two_grads = call(
         partial(gelu_kernel, cube, n_w),
@@ -675,8 +675,11 @@
         grad_shapes,
     )
     if cube.fast:
-        (came,) = hold([cube.swap(2, two, 0)], (done,))
+        came, other = hold([cube.swap(cube.gather[2], two, 0), two_grads[1]], (done,))
         w_two = [two, came, cube.flip(two, 1), cube.flip(came, 1)]
+        ((s_two, k_two),) = fold([(two_grads[0], cube.flip(other, 1))])
+        c_two = cube.swap(cube.scatter[2], s_two, 0)
+        slot = (s_two,)
     f_sums, enc, dhidden, mlp_small, done, *one_grads = call(
         partial(mlp_kernel, cube, n_w),
         [
@@ -689,14 +692,16 @@
         [n2, cot, act, slope, hidden, vecs],
         [*w_one, *w_two],
         buffers * 2 + grad_buffers + [pltpu.VMEM((tokens, d), f32)] * 2,
-        (),
+        slot,
         grad_shapes,
     )
     slot = ()
     if cube.fast:
-        two_terms = [two_grads[0], cube.flip(two_grads[1], 1)]
-        one_terms = [one_grads[0], cube.flip(one_grads[1], 1)]
-        s_two, s_one = sends([two_terms, one_terms], (done,))
+        images = enc.reshape(count, padded, d)
+        c_two, other, images = hold([c_two, one_grads[1], images], (done,))
+        ((s_two, k_two),) = fold([(k_two, c_two)])
+        c_two = cube.swap(cube.scatter[2], s_two, 1)
+        ((s_one, k_one),) = fold([(one_grads[0], cube.flip(other, 1))], (s_two,))
         slot = (s_two, s_one)
     dbias, dnorm, attn_small, done, *attn_grads = call(
         partial(attend_back_kernel, cube, count, length, width, n_w),
@@ -721,55 +726,62 @@
         )[0]
         return patch.reshape(count, padded, d)
 
-    images = enc.reshape(count, padded, d)
     sums = (attn_small, mlp_small, dbias, f_sums)
     if cube.fast:
 
         def spread(images, there):
             return [images, cube.flip(images, 1), there, cube.flip(there, 1)]
 
-        two_terms.append(cube.swap(2, s_two, 0))
-        one_terms.append(cube.swap(1, s_one, 0))
+        c_one = cube.swap(cube.scatter[1], s_one, 0)
         there = cube.flip(images, 2)
-        came = (two_terms[-1], one_terms[-1], there)
         flat = (cube.half * cube.rows, d)
-        other, images = hold([attn_grads[1].reshape(flat), images], came)
-        s_two, s_one = sends([two_terms, one_terms], (done,))
-        attn_terms = [attn_grads[0].reshape(flat), cube.flip(other, 1)]
-        small = sums
+        other, images, there, c_two, c_one = hold(
+            [attn_grads[1].reshape(flat), images, there, c_two, c_one], (done,)
+        )
+        k_attn, c_attn = attn_grads[0].reshape(flat), cube.flip(other, 1)
+        waiting = {2: [2, k_two, c_two], 1: [1, k_one, c_one]}
+        grads = {}
+        found = fold([(k, c) for _, k, c in waiting.values()])
+        for (group, state), (sent, kept) in zip(waiting.items(), found):
+            state[1:] = [kept, cube.swap(cube.scatter[group], sent, state[0])]
+            state[0] += 1
+        small, after = sums, (found[0][0],)
         for k in range(cube.steps):
+            more = [g for g in waiting if k > 0 and waiting[g][0] <= last]
+            ended = [g for g in waiting if k > 0 and waiting[g][0] > last]
+            pairs = [waiting[g][1:] for g in more]
+            finals = [waiting.pop(g)[1:] for g in ended]
+            s_attn, k_attn, small, *found = fold_with_small(
+                cube, k_attn, c_attn, small, pairs, finals, ids, after
+            )
+            c_attn = cube.swap(cube.scatter[0], s_attn, k)
+            for n, g in enumerate(more):
+                came = cube.swap(cube.scatter[g], found[2 * n], waiting[g][0])
+                waiting[g] = [waiting[g][0] + 1, found[2 * n + 1], came]
+            grads.update(zip(ended, found[2 * len(more) :]))
+            after = ()
             if k == 0:
-                found = sends_with_small(cube, attn_terms, [], small, ids, (s_one,))
-            elif k < last:
-                found = sends_with_small(cube, attn_terms, [two_terms, one_terms], small, ids, after)
-                s_two, s_one = found[2:]
-            else:
-                found = sends_with_small(
-                    cube, attn_terms, [two_terms, one_terms], small, ids, after, True
-                )
-                two_grad, one_grad = found[2:]
-            small, after = (found[1],), ()
-            attn_terms.append(cube.swap(0, found[0], k))
-            if k < last:
-                two_terms.append(cube.swap(2, s_two, k + 1))
-                one_terms.append(cube.swap(1, s_one, k + 1))
-            if k == 0:
-                images, there = hold([images, there], small)
+                images, there = hold([images, there], (small,))
                 encoded = place_images(cube, spread(images, there), length)
                 after = (encoded,)
+            if k == 1:
+                images = patch_of((small,))
+                after = (images,)
             if k == last - 1:
-                images = patch_of(small)
+                (images,) = hold([images], (small,))
                 there = cube.flip(images, 2)
             if k == last:
-                images, there = hold([images, there], small)
+                images, there = hold([images, there], (small,))
                 patch_grad = place_images(cube, spread(images, there), length)
-        attn_grad, small = finish_with_small(cube, attn_terms, small[0], ids, (patch_grad,))
+            small = (small,)
+        two_grad, one_grad = grads[2], grads[1]
+        attn_grad, small = finish_with_small(k_attn, c_attn, small[0], (patch_grad,))
         small = small.astype(f32) + cube.flip(small, 1).astype(f32)
     else:
         two_grad = scatter_plain(cube, *two_grads)
         one_grad = scatter_plain(cube, *one_grads)
         attn_grad = scatter_plain(cube, *attn_grads)
-        encoded = place_images(cube, [images], length)
+        encoded = place_images(cube, [enc.reshape(count, padded, d)], length)
         patch_grad = place_images(cube, [patch_of(())], length)
 
         def collect(ids_ref, *refs):

time: 266 us -> 246 us (0.925); the launches traced: 261 us -> 245 us
  waiting for transfers between devices: 77.7 us -> 65.3 us
  local copies, waits for them, and re-layouts: 30.1 us -> 40.8 us
  starting transfers between devices: 45.1 us -> 38.1 us
  Pallas kernels: 103 us -> 96.9 us
    ppermute x24, waiting for transfers between devices: 66 us -> 52.9 us  [swap(): lax.ppermute(value, AXES, [(i, i ^ 1 << orders[i & 1][k]) for i in range(...]
    pallas_call x7 -> x9, Pallas kernels: 19.2 us -> 12.5 us  [vmem_call(): pl.pallas_call(kernel, out_shape=shapes, in_specs=specs, out_specs=[pl.Bl...]
    pallas_call x0 -> x2, local copies, waits for them, and re-layouts: none -> 5.77 us  [call(): pl.pallas_call(body, out_shape=[*out_shapes, *grads], in_specs=[pl.BlockS...]
    ppermute x24, starting transfers between devices: 35 us -> 30.7 us  [swap(): lax.ppermute(value, AXES, [(i, i ^ 1 << orders[i & 1][k]) for i in range(...]
    unnamed x132 -> x138, local copies, waits for them, and re-layouts: 23.9 us -> 27.2 us
    ppermute x19, starting transfers between devices: 10.2 us -> 7.36 us  [flip(): return lax.ppermute(value, AXES, [(i, i ^ bits) for i in range(self.n)])]
  transfers between devices with their start and end apart: 43 -> 43, of which waited for: 20 -> 22; matrix products, arithmetic and copies ran while one was open for 5% -> 6% of each run, Pallas kernels for 33% -> 36%
where the time goes in v7:
time: 246 us; the launch traced here: 245 us
  Pallas kernels  96.9 us (39%)
  waiting for transfers between devices  65.3 us (27%)
  local copies, waits for them, and re-layouts  40.8 us (17%)
  starting transfers between devices  38.1 us (15%)
    pallas_call x7, Pallas kernels, call(): pl.pallas_call(body, out_shape=[*out_shapes, *grads], in_specs=[pl.BlockS...  81.8 us
    ppermute x24, waiting for transfers between devices, swap(): lax.ppermute(value, AXES, [(i, i ^ 1 << orders[i & 1][k]) for i in range(...  52.9 us
    ppermute x24, starting transfers between devices, swap(): lax.ppermute(value, AXES, [(i, i ^ 1 << orders[i & 1][k]) for i in range(...  30.7 us
    unnamed x138, local copies, waits for them, and re-layouts  27.2 us
    pallas_call x9, Pallas kernels, vmem_call(): pl.pallas_call(kernel, out_shape=shapes, in_specs=specs, out_specs=[pl.Bl...  12.5 us
    ppermute x19, waiting for transfers between devices, flip(): return lax.ppermute(value, AXES, [(i, i ^ bits) for i in range(self.n)])  12.4 us
    ppermute x19, starting transfers between devices, flip(): return lax.ppermute(value, AXES, [(i, i ^ bits) for i in range(self.n)])  7.36 us
    pallas_call x2, local copies, waits for them, and re-layouts, call(): pl.pallas_call(body, out_shape=[*out_shapes, *grads], in_specs=[pl.BlockS...  5.77 us
  transfers between devices with their start and end apart: 43, of which 22 were waited for; matrix products, arithmetic and copies ran while one was open for 6% of the time, Pallas kernels for 36%

profile of v7, /device:TPU:0, one launch (start us, length us, event | category | flops | bytes accessed | tf_op | source)
XLA Modules:
  0.0 244.7 jit_solution(10905466673313761074)
XLA Ops:
  2.5 4.1 %collective-permute-start.3 = (bf16[1,96,768]{2,1,0:T(8,128)(2,1)S(1)}, bf16[1,96,768]{2,1,0:T(8,128)(2,1)S(1)}, u32[]{:S(2)}, u32[]{:S(2)}) collective-permute-start(bf16[1,96,768]{2,1,0:T(8,128)(2,1)S(1)} %maximum_bitcast_fusion.refs_0_), channel_id=1, source_target_pairs={{0,16},{1,17},{2,18},{3,19},{4,20},{5,21},{6,22},{7,23},{8,24},{9,... | collective-permute-start | bytes 442376 | tf_op jit(solution)/shard_map/ppermute | solution.py:42
  7.4 3.7 %constant_dynamic-slice_fusion.2 = (bf16[2,197,768]{2,0,1:T(2,128)(2,1)S(1)}, bf16[2,197,768]{2,0,1:T(2,128)(2,1)S(1)}) fusion(bf16[8,197,768]{2,0,1:T(8,128)(2,1)} %param.27, s32[]{:T(128)S(6)} %select_n.13, bf16[8,197,768]{2,0,1:T(8,128)(2,1)} %param.14), kind=kLoop, calls=%fused_computation.30 | loop fusion | bytes 2420740 | tf_op jit(solution)/shard_map/dynamic_slice | solution.py:588
  18.4 6.2 %collective-permute-done.5.refs_3_ = bf16[1,96,768]{2,1,0:T(8,128)(2,1)S(1)} collective-permute-done((bf16[1,96,768]{2,1,0:T(8,128)(2,1)S(1)}, bf16[1,96,768]{2,1,0:T(8,128)(2,1)S(1)}, u32[]{:S(2)}, u32[]{:S(2)}) %collective-permute-start.5) | collective-permute-done | bytes 147488 | tf_op jit(solution)/shard_map/ppermute | solution.py:42
  28.1 8.4 %collective-permute-done.8.refs_5_ = bf16[1,96,768]{2,1,0:T(8,128)(2,1)S(1)} collective-permute-done((bf16[1,96,768]{2,1,0:T(8,128)(2,1)S(1)}, bf16[1,96,768]{2,1,0:T(8,128)(2,1)S(1)}, u32[]{:S(2)}, u32[]{:S(2)}) %collective-permute-start.8) | collective-permute-done | bytes 147488 | tf_op jit(solution)/shard_map/ppermute | solution.py:42
  41.1 15.2 %collective-permute-done.9.refs_4_.refs_7_ = bf16[8,96,768]{2,1,0:T(8,128)(2,1)S(1)} collective-permute-done((bf16[8,96,768]{2,1,0:T(8,128)(2,1)S(1)}, bf16[8,96,768]{2,1,0:T(8,128)(2,1)S(1)}, u32[]{:S(2)}, u32[]{:S(2)}) %collective-permute-start.9) | collective-permute-done | bytes 1179680 | tf_op jit(solution)/shard_map/ppermute | solution.py:42
  60.8 14.0 %shard_map.250 = (bf16[416,768]{1,0:T(8,128)(2,1)}, bf16[4,416,576]{2,1,0:T(8,128)(2,1)}, bf16[4,416,192]{2,1,0:T(8,128)(2,1)}, f32[416,768]{1,0:T(8,128)}, bf16[416,768]{1,0:T(8,128)(2,1)}, /*index=5*/f32[8,128]{1,0:T(8,128)}) custom-call(s32[2]{0:T(128)} %pad_add_fusion.index_ref.ids_ref, bf16[416,768]{1,0:T(8,128)(2,1)} %bitcast.41, f32[6,768]{1,0:T(8,128)} %copy-done.22, ...), custom_call_target="tpu_custom_call" | custom-call | bytes 1024 | tf_op jit(solution)/shard_map/pallas_call | solution.py:332
  79.1 13.6 %shard_map.253 = (bf16[4,416,768]{2,1,0:T(8,128)(2,1)}, bf16[4,416,768]{2,1,0:T(8,128)(2,1)}, f32[8,128]{1,0:T(8,128)}, bf16[16,96,768]{2,1,0:T(8,128)(2,1)}, bf16[16,96,768]{2,1,0:T(8,128)(2,1)}) custom-call(s32[2]{0:T(128)} %pad_add_fusion.index_ref.ids_ref, bf16[416,768]{1,0:T(8,128)(2,1)} %get-tuple-element.106.refs_0_, bf16[416,768]{1,0:T(8,128)(2,1)} %bitcast.48, ...), custom_call_target="tpu_custom_call" | custom-call | bytes 1024 | tf_op jit(solution)/shard_map/pallas_call | solution.py:332
  95.8 3.0 %collective-permute-done.21.refs_1_ = bf16[16,96,768]{2,1,0:T(8,128)(2,1)S(1)} collective-permute-done((bf16[16,96,768]{2,1,0:T(8,128)(2,1)}, bf16[16,96,768]{2,1,0:T(8,128)(2,1)S(1)}, u32[]{:S(2)}, u32[]{:S(2)}) %collective-permute-start.21) | collective-permute-done | bytes 2359328 | tf_op jit(solution)/shard_map/ppermute | solution.py:45
  105.5 17.9 %shard_map.256 = (f32[4,1,768]{2,1,0:T(1,128)}, bf16[416,768]{1,0:T(8,128)(2,1)}, f32[416,768]{1,0:T(8,128)}, f32[4,1,768]{2,1,0:T(1,128)}, f32[8,128]{1,0:T(8,1...) custom-call(s32[2]{0:T(128)} %pad_add_fusion.index_ref.ids_ref, ...), custom_call_target="tpu_custom_call" | custom-call | bytes 1024 | tf_op jit(solution)/shard_map/pallas_call | solution.py:332
  132.5 2.3 shard_map.259
  138.4 25.2 %shard_map.260 = (f32[4,1,576]{2,1,0:T(1,128)}, f32[416,768]{1,0:T(8,128)}, f32[2,1,768]{2,1,0:T(1,128)}, f32[8,128]{1,0:T(8,128)}, bf16[16,96,768]{2,1,0:T(8,128)(2,1)}, /*index=5*/bf16[16,96,768]{2,1,0:T(8,128)(2,1)}) custom-call(s32[2]{0:T(128)} %pad_add_fusion.index_ref.ids_ref, bf16[416,768]{1,0:T(8,128)(2,1)} %bitcast.42, ...), custom_call_target="tpu_custom_call" | custom-call | bytes 1024 | tf_op jit(solution)/shard_map/pallas_call | solution.py:332
  171.0 2.4 shard_map.263
  179.4 3.8 %shard_map.265 = (bf16[197,8,768]{2,1,0:T(8,128)(2,1)}, f32[8,128]{1,0:T(8,128)}) custom-call(s32[1]{0:T(128)} %bitcast.index_ref, bf16[2,208,768]{2,1,0:T(8,128)(2,1)} %get-tuple-element.146.refs_0_, bf16[2,208,768]{2,1,0:T(8,128)(2,1)} %copy-done.57, bf16[2,208,768]{2,1,0:T(8,128)(2,1)} %get-tuple-element.147.refs_2_, bf16[2,208,768]{2,1,0:T(8,128)(2,1)} %copy-done.58), custom_call_target="tpu_custom_call" | custom-call | bytes 1024 | tf_op jit(solution)/shard_map/pallas_call | solution.py:332
  183.2 3.6 %copy.63 = bf16[197,8,768]{2,0,1:T(8,128)(2,1)} copy(bf16[197,8,768]{2,1,0:T(8,128)(2,1)} %get-tuple-element.148) | data formatting | bytes 4841472 | tf_op jit(solution)/shard_map/pallas_call | solution.py:332
  186.9 4.0 %collective-permute-done.32.refs_4_ = bf16[4,96,768]{2,1,0:T(8,128)(2,1)S(1)} collective-permute-done((bf16[4,96,768]{2,1,0:T(8,128)(2,1)}, bf16[4,96,768]{2,1,0:T(8,128)(2,1)S(1)}, u32[]{:S(2)}, u32[]{:S(2)}) %collective-permute-start.32) | collective-permute-done | bytes 589856 | tf_op jit(solution)/shard_map/ppermute | solution.py:42
  190.9 3.1 %collective-permute-done.30.came_ref = bf16[800,768]{1,0:T(8,128)(2,1)} collective-permute-done((bf16[800,768]{1,0:T(8,128)(2,1)S(1)}, bf16[800,768]{1,0:T(8,128)(2,1)}, u32[]{:S(2)}, u32[]{:S(2)}) %collective-permute-start.30) | collective-permute-done | bytes 1228832 | tf_op jit(solution)/shard_map/ppermute | solution.py:42
  198.5 2.4 collective-permute-start.35
  200.9 3.5 %shard_map.267 = (bf16[416,768]{1,0:T(8,128)(2,1)}, f32[8,128]{1,0:T(8,128)}) custom-call(s32[2]{0:T(128)} %pad_add_fusion.index_ref.ids_ref, bf16[416,768]{1,0:T(8,128)(2,1)} %bitcast.43, f32[416,768]{1,0:T(8,128)} %get-tuple-element.119.refs_4_.refs_1_, f32[416,768]{1,0:T(8,128)} %get-tuple-element.149.refs_2_, f32[6,768]{1,0:T(8,128)} %copy-done.22, ...), custom_call_target="tpu_custom_call" | custom-call | bytes 1024 | tf_op jit(solution)/shard_map/pallas_call | solution.py:332
  205.6 4.5 %collective-permute-done.34.refs_2_ = bf16[2,96,768]{2,1,0:T(8,128)(2,1)S(1)} collective-permute-done((bf16[2,96,768]{2,1,0:T(8,128)(2,1)S(1)}, bf16[2,96,768]{2,1,0:T(8,128)(2,1)S(1)}, u32[]{:S(2)}, u32[]{:S(2)}) %collective-permute-start.34) | collective-permute-done | bytes 294944 | tf_op jit(solution)/shard_map/ppermute | solution.py:42
  215.1 2.7 %collective-permute-start.38 = (bf16[1,96,768]{2,1,0:T(8,128)(2,1)S(1)}, bf16[1,96,768]{2,1,0:T(8,128)(2,1)S(1)}, u32[]{:S(2)}, u32[]{:S(2)}) collective-permute-start(bf16[1,96,768]{2,1,0:T(8,128)(2,1)S(1)} %get-tuple-element.167), channel_id=1, source_target_pairs={{0,16},{1,17},{2,18},{3,19},{4,20},{5,21},{6,22},{7,23},{8,24},{9,... | collective-permute-start | bytes 442376 | tf_op jit(solution)/shard_map/ppermute | solution.py:42
  217.8 4.4 %collective-permute-done.38.refs_2_ = bf16[1,96,768]{2,1,0:T(8,128)(2,1)S(1)} collective-permute-done((bf16[1,96,768]{2,1,0:T(8,128)(2,1)S(1)}, bf16[1,96,768]{2,1,0:T(8,128)(2,1)S(1)}, u32[]{:S(2)}, u32[]{:S(2)}) %collective-permute-start.38) | collective-permute-done | bytes 147488 | tf_op jit(solution)/shard_map/ppermute | solution.py:42
  226.0 2.4 collective-permute-done.36.refs_1_
  233.3 3.8 %shard_map.272 = (bf16[197,8,768]{2,1,0:T(8,128)(2,1)}, f32[8,128]{1,0:T(8,128)}) custom-call(s32[1]{0:T(128)} %bitcast.index_ref, bf16[2,208,768]{2,1,0:T(8,128)(2,1)} %get-tuple-element.169.refs_0_, bf16[2,208,768]{2,1,0:T(8,128)(2,1)} %copy-done.55, bf16[2,208,768]{2,1,0:T(8,128)(2,1)} %get-tuple-element.170.refs_2_, bf16[2,208,768]{2,1,0:T(8,128)(2,1)} %copy-done.56), custom_call_target="tpu_custom_call" | custom-call | bytes 1024 | tf_op jit(solution)/shard_map/pallas_call | solution.py:332
  239.3 2.4 collective-permute-done.41.came_ref
  (260 shorter events, 86.7 us)
Async XLA Ops:
  2.5 14.8 %collective-permute-start.3 = (bf16[1,96,768]{2,1,0:T(8,128)(2,1)S(1)}, bf16[1,96,768]{2,1,0:T(8,128)(2,1)S(1)}, u32[]{:S(2)}, u32[]{:S(2)}) collective-permute-start(bf16[1,96,768]{2,1,0:T(8,128)(2,1)S(1)} %maximum_bitcast_fusion.refs_0_), channel_id=1, source_target_pairs={{0,16},{1,17},{2,18},{3,19},{4,20},{5,21},{6,22},{7,23},{8,24},{9,... | collective-permute-start | bytes 442376 | tf_op jit(solution)/shard_map/ppermute | solution.py:42
  14.5 10.2 %collective-permute-start.5 = (bf16[1,96,768]{2,1,0:T(8,128)(2,1)S(1)}, bf16[1,96,768]{2,1,0:T(8,128)(2,1)S(1)}, u32[]{:S(2)}, u32[]{:S(2)}) collective-permute-start(bf16[1,96,768]{2,1,0:T(8,128)(2,1)S(1)} %bitcast.54), channel_id=1, source_target_pairs={{0,16},{1,17},{2,18},{3,19},{4,20},{5,21},{6,22},{7,23},{8,24},{9,... | collective-permute-start | bytes 442376 | tf_op jit(solution)/shard_map/ppermute | solution.py:42
  24.8 13.1 %collective-permute-start.6 = (bf16[4,96,768]{2,1,0:T(8,128)(2,1)S(1)}, bf16[4,96,768]{2,1,0:T(8,128)(2,1)S(1)}, u32[]{:S(2)}, u32[]{:S(2)}) collective-permute-start(bf16[4,96,768]{2,1,0:T(8,128)(2,1)S(1)} %get-tuple-element.96.refs_0_), channel_id=1, source_target_pairs={{0,8},{1,5},{2,10},{3,7},{4,12},{5,1},{6,14},{7,3},{8,0},{9,13},{1... | collective-permute-start | bytes 1769480 | tf_op jit(solution)/shard_map/ppermute | solution.py:42
  25.9 10.6 %collective-permute-start.7 = (bf16[2,96,768]{2,1,0:T(8,128)(2,1)S(1)}, bf16[2,96,768]{2,1,0:T(8,128)(2,1)S(1)}, u32[]{:S(2)}, u32[]{:S(2)}) collective-permute-start(bf16[2,96,768]{2,1,0:T(8,128)(2,1)S(1)} %get-tuple-element.97.refs_2_), channel_id=1, source_target_pairs={{0,2},{1,5},{2,0},{3,7},{4,6},{5,1},{6,4},{7,3},{8,10},{9,13},{10,... | collective-permute-start | bytes 884744 | tf_op jit(solution)/shard_map/ppermute | solution.py:42
  38.0 18.3 %collective-permute-start.9 = (bf16[8,96,768]{2,1,0:T(8,128)(2,1)S(1)}, bf16[8,96,768]{2,1,0:T(8,128)(2,1)S(1)}, u32[]{:S(2)}, u32[]{:S(2)}) collective-permute-start(bf16[8,96,768]{2,1,0:T(8,128)(2,1)S(1)} %get-tuple-element.98.refs_3_.refs_6_), channel_id=1, source_target_pairs={{0,4},{1,3},{2,6},{3,1},{4,0},{5,7},{6,2},{7,5},{8,12},{9,11},{10,... | collective-permute-start | bytes 3538952 | tf_op jit(solution)/shard_map/ppermute | solution.py:42
  39.6 16.7 %collective-permute-start.12 = (bf16[4,96,768]{2,1,0:T(8,128)(2,1)S(1)}, bf16[4,96,768]{2,1,0:T(8,128)(2,1)S(1)}, u32[]{:S(2)}, u32[]{:S(2)}) collective-permute-start(bf16[4,96,768]{2,1,0:T(8,128)(2,1)S(1)} %get-tuple-element.99.refs_0_), channel_id=1, source_target_pairs={{0,8},{1,9},{2,10},{3,11},{4,12},{5,13},{6,14},{7,15},{8,0},{9,1},... | collective-permute-start | bytes 1769480 | tf_op jit(solution)/shard_map/ppermute | solution.py:42
  39.6 16.7 %collective-permute-start.13 = (bf16[2,96,768]{2,1,0:T(8,128)(2,1)S(1)}, bf16[2,96,768]{2,1,0:T(8,128)(2,1)S(1)}, u32[]{:S(2)}, u32[]{:S(2)}) collective-permute-start(bf16[2,96,768]{2,1,0:T(8,128)(2,1)S(1)} %get-tuple-element.100.refs_2_), channel_id=1, source_target_pairs={{0,2},{1,5},{2,0},{3,7},{4,6},{5,1},{6,4},{7,3},{8,10},{9,13},{10,... | collective-permute-start | bytes 884744 | tf_op jit(solution)/shard_map/ppermute | solution.py:42
  41.1 19.7 %collective-permute-start.10 = (bf16[8,96,768]{2,1,0:T(8,128)(2,1)S(1)}, bf16[8,96,768]{2,1,0:T(8,128)(2,1)}, u32[]{:S(2)}, u32[]{:S(2)}) collective-permute-start(bf16[8,96,768]{2,1,0:T(8,128)(2,1)S(1)} %get-tuple-element.98.refs_3_.refs_6_), channel_id=1, source_target_pairs={{0,1},{1,0},{2,3},{3,2},{4,5},{5,4},{6,7},{7,6},{8,9},{9,8},{10,11... | collective-permute-start | bytes 3538952 | tf_op jit(solution)/shard_map/ppermute | solution.py:45
  57.6 17.2 %collective-permute-start.14 = (bf16[8,96,768]{2,1,0:T(8,128)(2,1)S(1)}, bf16[8,96,768]{2,1,0:T(8,128)(2,1)}, u32[]{:S(2)}, u32[]{:S(2)}) collective-permute-start(bf16[8,96,768]{2,1,0:T(8,128)(2,1)S(1)} %get-tuple-element.101.refs_7_.refs_3_.refs_6_), channel_id=1, source_target_pairs={{0,4},{1,3},{2,6},{3,1},{4,0},{5,7},{6,2},{7,5},{8,12},{9,11},{10,... | collective-permute-start | bytes 3538952 | tf_op jit(solution)/shard_map/ppermute | solution.py:42
  59.1 15.7 %collective-permute-start.15 = (bf16[4,96,768]{2,1,0:T(8,128)(2,1)}, bf16[4,96,768]{2,1,0:T(8,128)(2,1)}, u32[]{:S(2)}, u32[]{:S(2)}) collective-permute-start(bf16[4,96,768]{2,1,0:T(8,128)(2,1)} %get-tuple-element.102.refs_8_.refs_0_), channel_id=1, source_target_pairs={{0,8},{1,9},{2,10},{3,11},{4,12},{5,13},{6,14},{7,15},{8,0},{9,1},... | collective-permute-start | bytes 1769480 | tf_op jit(solution)/shard_map/ppermute | solution.py:42
  60.8 16.8 %collective-permute-start.16 = (bf16[8,96,768]{2,1,0:T(8,128)(2,1)S(1)}, bf16[8,96,768]{2,1,0:T(8,128)(2,1)}, u32[]{:S(2)}, u32[]{:S(2)}) collective-permute-start(bf16[8,96,768]{2,1,0:T(8,128)(2,1)S(1)} %get-tuple-element.101.refs_7_.refs_3_.refs_6_), channel_id=1, source_target_pairs={{0,1},{1,0},{2,3},{3,2},{4,5},{5,4},{6,7},{7,6},{8,9},{9,8},{10,11... | collective-permute-start | bytes 3538952 | tf_op jit(solution)/shard_map/ppermute | solution.py:45
  76.7 16.3 %collective-permute-start.18 = (bf16[8,96,768]{2,1,0:T(8,128)(2,1)S(1)}, bf16[8,96,768]{2,1,0:T(8,128)(2,1)S(1)}, u32[]{:S(2)}, u32[]{:S(2)}) collective-permute-start(bf16[8,96,768]{2,1,0:T(8,128)(2,1)S(1)} %shard_map.252.refs_7_.refs_10_), channel_id=1, source_target_pairs={{0,4},{1,3},{2,6},{3,1},{4,0},{5,7},{6,2},{7,5},{8,12},{9,11},{10,... | collective-permute-start | bytes 3538952 | tf_op jit(solution)/shard_map/ppermute | solution.py:42
  102.5 21.0 %collective-permute-start.22 = (bf16[8,96,768]{2,1,0:T(8,128)(2,1)S(1)}, bf16[8,96,768]{2,1,0:T(8,128)(2,1)S(1)}, u32[]{:S(2)}, u32[]{:S(2)}) collective-permute-start(bf16[8,96,768]{2,1,0:T(8,128)(2,1)S(1)} %get-tuple-element.118.refs_14_), channel_id=1, source_target_pairs={{0,4},{1,3},{2,6},{3,1},{4,0},{5,7},{6,2},{7,5},{8,12},{9,11},{10,... | collective-permute-start | bytes 3538952 | tf_op jit(solution)/shard_map/ppermute | solution.py:42
  134.8 28.8 %collective-permute-start.26 = (bf16[8,96,768]{2,1,0:T(8,128)(2,1)S(1)}, bf16[8,96,768]{2,1,0:T(8,128)(2,1)S(1)}, u32[]{:S(2)}, u32[]{:S(2)}) collective-permute-start(bf16[8,96,768]{2,1,0:T(8,128)(2,1)S(1)} %get-tuple-element.128.refs_11_), channel_id=1, source_target_pairs={{0,4},{1,3},{2,6},{3,1},{4,0},{5,7},{6,2},{7,5},{8,12},{9,11},{10,... | collective-permute-start | bytes 3538952 | tf_op jit(solution)/shard_map/ppermute | solution.py:42
  135.9 27.7 %collective-permute-start.24 = (bf16[2,208,768]{2,1,0:T(8,128)(2,1)S(1)}, bf16[2,208,768]{2,1,0:T(8,128)(2,1)}, u32[]{:S(2)}, u32[]{:S(2)}) collective-permute-start(bf16[2,208,768]{2,1,0:T(8,128)(2,1)S(1)} %copy-done.46), channel_id=1, source_target_pairs={{0,2},{1,3},{2,0},{3,1},{4,6},{5,7},{6,4},{7,5},{8,10},{9,11},{10,... | collective-permute-start | bytes 1916936 | tf_op jit(solution)/shard_map/ppermute | solution.py:45
  137.4 26.1 %collective-permute-start.25 = (bf16[4,96,768]{2,1,0:T(8,128)(2,1)S(1)}, bf16[4,96,768]{2,1,0:T(8,128)(2,1)S(1)}, u32[]{:S(2)}, u32[]{:S(2)}) collective-permute-start(bf16[4,96,768]{2,1,0:T(8,128)(2,1)S(1)} %get-tuple-element.125.refs_2_.refs_10_), channel_id=1, source_target_pairs={{0,8},{1,9},{2,10},{3,11},{4,12},{5,13},{6,14},{7,15},{8,0},{9,1},... | collective-permute-start | bytes 1769480 | tf_op jit(solution)/shard_map/ppermute | solution.py:42
  174.0 20.0 %collective-permute-start.30 = (bf16[800,768]{1,0:T(8,128)(2,1)S(1)}, bf16[800,768]{1,0:T(8,128)(2,1)}, u32[]{:S(2)}, u32[]{:S(2)}) collective-permute-start(bf16[800,768]{1,0:T(8,128)(2,1)S(1)} %get-tuple-element.151), channel_id=1, source_target_pairs={{0,4},{1,3},{2,6},{3,1},{4,0},{5,7},{6,2},{7,5},{8,12},{9,11},{10,... | collective-permute-start | bytes 3686408 | tf_op jit(solution)/shard_map/ppermute | solution.py:42
  175.3 15.6 %collective-permute-start.32 = (bf16[4,96,768]{2,1,0:T(8,128)(2,1)}, bf16[4,96,768]{2,1,0:T(8,128)(2,1)S(1)}, u32[]{:S(2)}, u32[]{:S(2)}) collective-permute-start(bf16[4,96,768]{2,1,0:T(8,128)(2,1)} %copy-done.45), channel_id=1, source_target_pairs={{0,8},{1,9},{2,10},{3,11},{4,12},{5,13},{6,14},{7,15},{8,0},{9,1},... | collective-permute-start | bytes 1769480 | tf_op jit(solution)/shard_map/ppermute | solution.py:42
  176.2 10.7 %collective-permute-start.31 = (bf16[2,96,768]{2,1,0:T(8,128)(2,1)S(1)}, bf16[2,96,768]{2,1,0:T(8,128)(2,1)S(1)}, u32[]{:S(2)}, u32[]{:S(2)}) collective-permute-start(bf16[2,96,768]{2,1,0:T(8,128)(2,1)S(1)} %copy-done.26), channel_id=1, source_target_pairs={{0,2},{1,5},{2,0},{3,7},{4,6},{5,1},{6,4},{7,3},{8,10},{9,13},{10,... | collective-permute-start | bytes 884744 | tf_op jit(solution)/shard_map/ppermute | solution.py:42
  196.5 13.6 %collective-permute-start.33 = (bf16[416,768]{1,0:T(8,128)(2,1)S(1)}, bf16[416,768]{1,0:T(8,128)(2,1)S(1)}, u32[]{:S(2)}, u32[]{:S(2)}) collective-permute-start(bf16[416,768]{1,0:T(8,128)(2,1)S(1)} %get-tuple-element.158), channel_id=1, source_target_pairs={{0,2},{1,9},{2,0},{3,11},{4,6},{5,13},{6,4},{7,15},{8,10},{9,1},{1... | collective-permute-start | bytes 1916936 | tf_op jit(solution)/shard_map/ppermute | solution.py:42
  197.3 12.7 %collective-permute-start.34 = (bf16[2,96,768]{2,1,0:T(8,128)(2,1)S(1)}, bf16[2,96,768]{2,1,0:T(8,128)(2,1)S(1)}, u32[]{:S(2)}, u32[]{:S(2)}) collective-permute-start(bf16[2,96,768]{2,1,0:T(8,128)(2,1)S(1)} %get-tuple-element.160), channel_id=1, source_target_pairs={{0,2},{1,5},{2,0},{3,7},{4,6},{5,1},{6,4},{7,3},{8,10},{9,13},{10,... | collective-permute-start | bytes 884744 | tf_op jit(solution)/shard_map/ppermute | solution.py:42
  213.3 15.1 %collective-permute-start.36 = (bf16[2,208,768]{2,1,0:T(8,128)(2,1)}, bf16[2,208,768]{2,1,0:T(8,128)(2,1)S(1)}, u32[]{:S(2)}, u32[]{:S(2)}) collective-permute-start(bf16[2,208,768]{2,1,0:T(8,128)(2,1)} %shard_map.269.refs_0_), channel_id=1, source_target_pairs={{0,2},{1,3},{2,0},{3,1},{4,6},{5,7},{6,4},{7,5},{8,10},{9,11},{10,... | collective-permute-start | bytes 1916936 | tf_op jit(solution)/shard_map/ppermute | solution.py:45
  214.1 9.8 %collective-permute-start.37 = (bf16[224,768]{1,0:T(8,128)(2,1)S(1)}, bf16[224,768]{1,0:T(8,128)(2,1)S(1)}, u32[]{:S(2)}, u32[]{:S(2)}) collective-permute-start(bf16[224,768]{1,0:T(8,128)(2,1)S(1)} %get-tuple-element.165), channel_id=1, source_target_pairs={{0,8},{1,5},{2,10},{3,7},{4,12},{5,1},{6,14},{7,3},{8,0},{9,13},{1... | collective-permute-start | bytes 1032200 | tf_op jit(solution)/shard_map/ppermute | solution.py:42
  229.7 11.9 %collective-permute-start.41 = (bf16[128,768]{1,0:T(8,128)(2,1)S(1)}, bf16[128,768]{1,0:T(8,128)(2,1)S(1)}, u32[]{:S(2)}, u32[]{:S(2)}) collective-permute-start(bf16[128,768]{1,0:T(8,128)(2,1)S(1)} %get-tuple-element.173), channel_id=1, source_target_pairs={{0,16},{1,17},{2,18},{3,19},{4,20},{5,21},{6,22},{7,23},{8,24},{9,... | collective-permute-start | bytes 589832 | tf_op jit(solution)/shard_map/ppermute | solution.py:42
  (86 other events, 443.5 us)

commit v8 on v7

--- a/solution.py
+++ b/solution.py
@@ -188,7 +188,7 @@
         in_specs=specs,
         out_specs=[pl.BlockSpec(memory_space=pltpu.VMEM)] * len(shapes),
         scratch_shapes=list(scratch),
-        compiler_params=pltpu.CompilerParams(vmem_limit_bytes=48 * MIB),
+        compiler_params=pltpu.CompilerParams(vmem_limit_bytes=24 * MIB),
         cost_estimate=pl.CostEstimate(flops=0, bytes_accessed=1024, transcendentals=0),
     )(*values)
 

time: 246 us -> 237 us (0.963)
  local copies, waits for them, and re-layouts: 40.8 us -> 32.5 us
  waiting for transfers between devices: 65.3 us -> 70.1 us
  Pallas kernels: 96.9 us -> 92.7 us
    unnamed x138 -> x136, local copies, waits for them, and re-layouts: 27.2 us -> 20.4 us
    pallas_call x9, Pallas kernels: 12.5 us -> 8.25 us  [vmem_call(): pl.pallas_call(kernel, out_shape=shapes, in_specs=specs, out_specs=[pl.Bl...]
    ppermute x19, waiting for transfers between devices: 12.4 us -> 15.7 us  [flip(): return lax.ppermute(value, AXES, [(i, i ^ bits) for i in range(self.n)])]
  transfers between devices with their start and end apart: 43 -> 43, of which waited for: 22 -> 25; matrix products, arithmetic and copies ran while one was open for 6% -> 5% of each run, Pallas kernels for 36% -> 37%
where the time goes in v8:
time: 237 us; the launch traced here: 236 us
  Pallas kernels  92.7 us (39%)
  waiting for transfers between devices  70.1 us (30%)
  starting transfers between devices  37.1 us (16%)
  local copies, waits for them, and re-layouts  32.5 us (14%)
    pallas_call x7, Pallas kernels, call(): pl.pallas_call(body, out_shape=[*out_shapes, *grads], in_specs=[pl.BlockS...  81.9 us
    ppermute x24, waiting for transfers between devices, swap(): lax.ppermute(value, AXES, [(i, i ^ 1 << orders[i & 1][k]) for i in range(...  54.4 us
    ppermute x24, starting transfers between devices, swap(): lax.ppermute(value, AXES, [(i, i ^ 1 << orders[i & 1][k]) for i in range(...  29.5 us
    unnamed x136, local copies, waits for them, and re-layouts  20.4 us
    ppermute x19, waiting for transfers between devices, flip(): return lax.ppermute(value, AXES, [(i, i ^ bits) for i in range(self.n)])  15.7 us
    pallas_call x9, Pallas kernels, vmem_call(): pl.pallas_call(kernel, out_shape=shapes, in_specs=specs, out_specs=[pl.Bl...  8.25 us
    ppermute x19, starting transfers between devices, flip(): return lax.ppermute(value, AXES, [(i, i ^ bits) for i in range(self.n)])  7.6 us
  transfers between devices with their start and end apart: 43, of which 25 were waited for; matrix products, arithmetic and copies ran while one was open for 5% of the time, Pallas kernels for 37%

profile of v8, /device:TPU:0, one launch (start us, length us, event | category | flops | bytes accessed | tf_op | source)
XLA Modules:
  0.0 236.0 jit_solution(12278168162215230714)
XLA Ops:
  2.5 4.1 %collective-permute-start.3 = (bf16[1,96,768]{2,1,0:T(8,128)(2,1)S(1)}, bf16[1,96,768]{2,1,0:T(8,128)(2,1)S(1)}, u32[]{:S(2)}, u32[]{:S(2)}) collective-permute-start(bf16[1,96,768]{2,1,0:T(8,128)(2,1)S(1)} %maximum_bitcast_fusion.refs_0_), channel_id=1, source_target_pairs={{0,16},{1,17},{2,18},{3,19},{4,20},{5,21},{6,22},{7,23},{8,24},{9,... | collective-permute-start | bytes 442376 | tf_op jit(solution)/shard_map/ppermute | solution.py:42
  7.4 3.7 %constant_dynamic-slice_fusion.2 = (bf16[2,197,768]{2,0,1:T(2,128)(2,1)S(1)}, bf16[2,197,768]{2,0,1:T(2,128)(2,1)S(1)}) fusion(bf16[8,197,768]{2,0,1:T(8,128)(2,1)} %param.27, s32[]{:T(128)S(6)} %select_n.13, bf16[8,197,768]{2,0,1:T(8,128)(2,1)} %param.14), kind=kLoop, calls=%fused_computation.30 | loop fusion | bytes 2420740 | tf_op jit(solution)/shard_map/dynamic_slice | solution.py:588
  18.5 6.2 %collective-permute-done.5.refs_3_ = bf16[1,96,768]{2,1,0:T(8,128)(2,1)S(1)} collective-permute-done((bf16[1,96,768]{2,1,0:T(8,128)(2,1)S(1)}, bf16[1,96,768]{2,1,0:T(8,128)(2,1)S(1)}, u32[]{:S(2)}, u32[]{:S(2)}) %collective-permute-start.5) | collective-permute-done | bytes 147488 | tf_op jit(solution)/shard_map/ppermute | solution.py:42
  28.1 8.4 %collective-permute-done.8.refs_5_ = bf16[1,96,768]{2,1,0:T(8,128)(2,1)S(1)} collective-permute-done((bf16[1,96,768]{2,1,0:T(8,128)(2,1)S(1)}, bf16[1,96,768]{2,1,0:T(8,128)(2,1)S(1)}, u32[]{:S(2)}, u32[]{:S(2)}) %collective-permute-start.8) | collective-permute-done | bytes 147488 | tf_op jit(solution)/shard_map/ppermute | solution.py:42
  41.1 15.2 %collective-permute-done.9.refs_4_.refs_7_ = bf16[8,96,768]{2,1,0:T(8,128)(2,1)S(1)} collective-permute-done((bf16[8,96,768]{2,1,0:T(8,128)(2,1)S(1)}, bf16[8,96,768]{2,1,0:T(8,128)(2,1)S(1)}, u32[]{:S(2)}, u32[]{:S(2)}) %collective-permute-start.9) | collective-permute-done | bytes 1179680 | tf_op jit(solution)/shard_map/ppermute | solution.py:42
  60.8 14.0 %shard_map.250 = (bf16[416,768]{1,0:T(8,128)(2,1)}, bf16[4,416,576]{2,1,0:T(8,128)(2,1)}, bf16[4,416,192]{2,1,0:T(8,128)(2,1)}, f32[416,768]{1,0:T(8,128)}, bf16[416,768]{1,0:T(8,128)(2,1)}, /*index=5*/f32[8,128]{1,0:T(8,128)}) custom-call(s32[2]{0:T(128)} %pad_add_fusion.index_ref.ids_ref, bf16[416,768]{1,0:T(8,128)(2,1)} %bitcast.41, f32[6,768]{1,0:T(8,128)} %copy-done.22, ...), custom_call_target="tpu_custom_call" | custom-call | bytes 1024 | tf_op jit(solution)/shard_map/pallas_call | solution.py:332
  79.1 13.6 %shard_map.253 = (bf16[4,416,768]{2,1,0:T(8,128)(2,1)}, bf16[4,416,768]{2,1,0:T(8,128)(2,1)}, f32[8,128]{1,0:T(8,128)}, bf16[16,96,768]{2,1,0:T(8,128)(2,1)}, bf16[16,96,768]{2,1,0:T(8,128)(2,1)}) custom-call(s32[2]{0:T(128)} %pad_add_fusion.index_ref.ids_ref, bf16[416,768]{1,0:T(8,128)(2,1)} %get-tuple-element.106.refs_0_, bf16[416,768]{1,0:T(8,128)(2,1)} %bitcast.48, ...), custom_call_target="tpu_custom_call" | custom-call | bytes 1024 | tf_op jit(solution)/shard_map/pallas_call | solution.py:332
  94.9 3.0 %collective-permute-done.21.refs_1_ = bf16[16,96,768]{2,1,0:T(8,128)(2,1)S(1)} collective-permute-done((bf16[16,96,768]{2,1,0:T(8,128)(2,1)}, bf16[16,96,768]{2,1,0:T(8,128)(2,1)S(1)}, u32[]{:S(2)}, u32[]{:S(2)}) %collective-permute-start.21) | collective-permute-done | bytes 2359328 | tf_op jit(solution)/shard_map/ppermute | solution.py:45
  102.5 17.9 %shard_map.256 = (f32[4,1,768]{2,1,0:T(1,128)}, bf16[416,768]{1,0:T(8,128)(2,1)}, f32[416,768]{1,0:T(8,128)}, f32[4,1,768]{2,1,0:T(1,128)}, f32[8,128]{1,0:T(8,1...) custom-call(s32[2]{0:T(128)} %pad_add_fusion.index_ref.ids_ref, ...), custom_call_target="tpu_custom_call" | custom-call | bytes 1024 | tf_op jit(solution)/shard_map/pallas_call | solution.py:332
  131.6 25.2 %shard_map.260 = (f32[4,1,576]{2,1,0:T(1,128)}, f32[416,768]{1,0:T(8,128)}, f32[2,1,768]{2,1,0:T(1,128)}, f32[8,128]{1,0:T(8,128)}, bf16[16,96,768]{2,1,0:T(8,128)(2,1)}, /*index=5*/bf16[16,96,768]{2,1,0:T(8,128)(2,1)}) custom-call(s32[2]{0:T(128)} %pad_add_fusion.index_ref.ids_ref, bf16[416,768]{1,0:T(8,128)(2,1)} %bitcast.42, ...), custom_call_target="tpu_custom_call" | custom-call | bytes 1024 | tf_op jit(solution)/shard_map/pallas_call | solution.py:332
  163.1 2.3 shard_map.263
  171.3 3.8 %shard_map.265 = (bf16[197,8,768]{2,1,0:T(8,128)(2,1)}, f32[8,128]{1,0:T(8,128)}) custom-call(s32[1]{0:T(128)} %bitcast.index_ref, bf16[2,208,768]{2,1,0:T(8,128)(2,1)} %get-tuple-element.146.refs_0_, bf16[2,208,768]{2,1,0:T(8,128)(2,1)} %copy-done.56, bf16[2,208,768]{2,1,0:T(8,128)(2,1)} %get-tuple-element.147.refs_2_, bf16[2,208,768]{2,1,0:T(8,128)(2,1)} %copy-done.57), custom_call_target="tpu_custom_call" | custom-call | bytes 1024 | tf_op jit(solution)/shard_map/pallas_call | solution.py:332
  175.1 2.2 copy.63
  178.7 4.6 %collective-permute-done.32.refs_4_ = bf16[4,96,768]{2,1,0:T(8,128)(2,1)S(1)} collective-permute-done((bf16[4,96,768]{2,1,0:T(8,128)(2,1)S(1)}, bf16[4,96,768]{2,1,0:T(8,128)(2,1)S(1)}, u32[]{:S(2)}, u32[]{:S(2)}) %collective-permute-start.32) | collective-permute-done | bytes 589856 | tf_op jit(solution)/shard_map/ppermute | solution.py:42
  183.4 2.8 %collective-permute-done.30.came_ref = bf16[800,768]{1,0:T(8,128)(2,1)S(1)} collective-permute-done((bf16[800,768]{1,0:T(8,128)(2,1)}, bf16[800,768]{1,0:T(8,128)(2,1)S(1)}, u32[]{:S(2)}, u32[]{:S(2)}) %collective-permute-start.30) | collective-permute-done | bytes 1228832 | tf_op jit(solution)/shard_map/ppermute | solution.py:42
  189.9 2.0 collective-permute-start.35
  191.9 3.5 %shard_map.267 = (bf16[416,768]{1,0:T(8,128)(2,1)}, f32[8,128]{1,0:T(8,128)}) custom-call(s32[2]{0:T(128)} %pad_add_fusion.index_ref.ids_ref, bf16[416,768]{1,0:T(8,128)(2,1)} %bitcast.43, f32[416,768]{1,0:T(8,128)} %get-tuple-element.119.refs_4_.refs_1_, f32[416,768]{1,0:T(8,128)} %get-tuple-element.149.refs_2_, f32[6,768]{1,0:T(8,128)} %copy-done.22, ...), custom_call_target="tpu_custom_call" | custom-call | bytes 1024 | tf_op jit(solution)/shard_map/pallas_call | solution.py:332
  196.9 4.5 %collective-permute-done.34.refs_2_ = bf16[2,96,768]{2,1,0:T(8,128)(2,1)S(1)} collective-permute-done((bf16[2,96,768]{2,1,0:T(8,128)(2,1)S(1)}, bf16[2,96,768]{2,1,0:T(8,128)(2,1)S(1)}, u32[]{:S(2)}, u32[]{:S(2)}) %collective-permute-start.34) | collective-permute-done | bytes 294944 | tf_op jit(solution)/shard_map/ppermute | solution.py:42
  207.1 2.4 %collective-permute-start.38 = (bf16[1,96,768]{2,1,0:T(8,128)(2,1)S(1)}, bf16[1,96,768]{2,1,0:T(8,128)(2,1)S(1)}, u32[]{:S(2)}, u32[]{:S(2)}) collective-permute-start(bf16[1,96,768]{2,1,0:T(8,128)(2,1)S(1)} %get-tuple-element.167), channel_id=1, source_target_pairs={{0,16},{1,17},{2,18},{3,19},{4,20},{5,21},{6,22},{7,23},{8,24},{9,... | collective-permute-start | bytes 442376 | tf_op jit(solution)/shard_map/ppermute | solution.py:42
  209.5 4.1 %collective-permute-done.38.refs_2_ = bf16[1,96,768]{2,1,0:T(8,128)(2,1)S(1)} collective-permute-done((bf16[1,96,768]{2,1,0:T(8,128)(2,1)S(1)}, bf16[1,96,768]{2,1,0:T(8,128)(2,1)S(1)}, u32[]{:S(2)}, u32[]{:S(2)}) %collective-permute-start.38) | collective-permute-done | bytes 147488 | tf_op jit(solution)/shard_map/ppermute | solution.py:42
  217.1 2.7 %collective-permute-done.36.refs_1_ = bf16[2,208,768]{2,1,0:T(8,128)(2,1)S(1)} collective-permute-done((bf16[2,208,768]{2,1,0:T(8,128)(2,1)}, bf16[2,208,768]{2,1,0:T(8,128)(2,1)S(1)}, u32[]{:S(2)}, u32[]{:S(2)}) %collective-permute-start.36) | collective-permute-done | bytes 639008 | tf_op jit(solution)/shard_map/ppermute | solution.py:45
  224.6 3.8 %shard_map.272 = (bf16[197,8,768]{2,1,0:T(8,128)(2,1)}, f32[8,128]{1,0:T(8,128)}) custom-call(s32[1]{0:T(128)} %bitcast.index_ref, bf16[2,208,768]{2,1,0:T(8,128)(2,1)} %get-tuple-element.169.refs_0_, bf16[2,208,768]{2,1,0:T(8,128)(2,1)} %copy-done.54, bf16[2,208,768]{2,1,0:T(8,128)(2,1)} %get-tuple-element.170.refs_2_, bf16[2,208,768]{2,1,0:T(8,128)(2,1)} %copy-done.55), custom_call_target="tpu_custom_call" | custom-call | bytes 1024 | tf_op jit(solution)/shard_map/pallas_call | solution.py:332
  228.5 2.2 copy.62
  230.6 2.4 %collective-permute-done.41.came_ref = bf16[128,768]{1,0:T(8,128)(2,1)S(1)} collective-permute-done((bf16[128,768]{1,0:T(8,128)(2,1)S(1)}, bf16[128,768]{1,0:T(8,128)(2,1)S(1)}, u32[]{:S(2)}, u32[]{:S(2)}) %collective-permute-start.41) | collective-permute-done | bytes 196640 | tf_op jit(solution)/shard_map/ppermute | solution.py:42
  (258 shorter events, 80.1 us)
Async XLA Ops:
  2.5 14.8 %collective-permute-start.3 = (bf16[1,96,768]{2,1,0:T(8,128)(2,1)S(1)}, bf16[1,96,768]{2,1,0:T(8,128)(2,1)S(1)}, u32[]{:S(2)}, u32[]{:S(2)}) collective-permute-start(bf16[1,96,768]{2,1,0:T(8,128)(2,1)S(1)} %maximum_bitcast_fusion.refs_0_), channel_id=1, source_target_pairs={{0,16},{1,17},{2,18},{3,19},{4,20},{5,21},{6,22},{7,23},{8,24},{9,... | collective-permute-start | bytes 442376 | tf_op jit(solution)/shard_map/ppermute | solution.py:42
  14.5 10.2 %collective-permute-start.5 = (bf16[1,96,768]{2,1,0:T(8,128)(2,1)S(1)}, bf16[1,96,768]{2,1,0:T(8,128)(2,1)S(1)}, u32[]{:S(2)}, u32[]{:S(2)}) collective-permute-start(bf16[1,96,768]{2,1,0:T(8,128)(2,1)S(1)} %bitcast.55), channel_id=1, source_target_pairs={{0,16},{1,17},{2,18},{3,19},{4,20},{5,21},{6,22},{7,23},{8,24},{9,... | collective-permute-start | bytes 442376 | tf_op jit(solution)/shard_map/ppermute | solution.py:42
  24.8 13.1 %collective-permute-start.6 = (bf16[4,96,768]{2,1,0:T(8,128)(2,1)S(1)}, bf16[4,96,768]{2,1,0:T(8,128)(2,1)S(1)}, u32[]{:S(2)}, u32[]{:S(2)}) collective-permute-start(bf16[4,96,768]{2,1,0:T(8,128)(2,1)S(1)} %get-tuple-element.96.refs_0_), channel_id=1, source_target_pairs={{0,8},{1,5},{2,10},{3,7},{4,12},{5,1},{6,14},{7,3},{8,0},{9,13},{1... | collective-permute-start | bytes 1769480 | tf_op jit(solution)/shard_map/ppermute | solution.py:42
  25.9 10.6 %collective-permute-start.7 = (bf16[2,96,768]{2,1,0:T(8,128)(2,1)S(1)}, bf16[2,96,768]{2,1,0:T(8,128)(2,1)S(1)}, u32[]{:S(2)}, u32[]{:S(2)}) collective-permute-start(bf16[2,96,768]{2,1,0:T(8,128)(2,1)S(1)} %get-tuple-element.97.refs_2_), channel_id=1, source_target_pairs={{0,2},{1,5},{2,0},{3,7},{4,6},{5,1},{6,4},{7,3},{8,10},{9,13},{10,... | collective-permute-start | bytes 884744 | tf_op jit(solution)/shard_map/ppermute | solution.py:42
  26.8 9.7 %collective-permute-start.8 = (bf16[1,96,768]{2,1,0:T(8,128)(2,1)S(1)}, bf16[1,96,768]{2,1,0:T(8,128)(2,1)S(1)}, u32[]{:S(2)}, u32[]{:S(2)}) collective-permute-start(bf16[1,96,768]{2,1,0:T(8,128)(2,1)S(1)} %bitcast.53), channel_id=1, source_target_pairs={{0,16},{1,17},{2,18},{3,19},{4,20},{5,21},{6,22},{7,23},{8,24},{9,... | collective-permute-start | bytes 442376 | tf_op jit(solution)/shard_map/ppermute | solution.py:42
  38.0 18.3 %collective-permute-start.9 = (bf16[8,96,768]{2,1,0:T(8,128)(2,1)S(1)}, bf16[8,96,768]{2,1,0:T(8,128)(2,1)S(1)}, u32[]{:S(2)}, u32[]{:S(2)}) collective-permute-start(bf16[8,96,768]{2,1,0:T(8,128)(2,1)S(1)} %get-tuple-element.98.refs_3_.refs_6_), channel_id=1, source_target_pairs={{0,4},{1,3},{2,6},{3,1},{4,0},{5,7},{6,2},{7,5},{8,12},{9,11},{10,... | collective-permute-start | bytes 3538952 | tf_op jit(solution)/shard_map/ppermute | solution.py:42
  39.6 16.7 %collective-permute-start.12 = (bf16[4,96,768]{2,1,0:T(8,128)(2,1)S(1)}, bf16[4,96,768]{2,1,0:T(8,128)(2,1)S(1)}, u32[]{:S(2)}, u32[]{:S(2)}) collective-permute-start(bf16[4,96,768]{2,1,0:T(8,128)(2,1)S(1)} %get-tuple-element.99.refs_0_), channel_id=1, source_target_pairs={{0,8},{1,9},{2,10},{3,11},{4,12},{5,13},{6,14},{7,15},{8,0},{9,1},... | collective-permute-start | bytes 1769480 | tf_op jit(solution)/shard_map/ppermute | solution.py:42
  39.6 16.7 %collective-permute-start.13 = (bf16[2,96,768]{2,1,0:T(8,128)(2,1)S(1)}, bf16[2,96,768]{2,1,0:T(8,128)(2,1)S(1)}, u32[]{:S(2)}, u32[]{:S(2)}) collective-permute-start(bf16[2,96,768]{2,1,0:T(8,128)(2,1)S(1)} %get-tuple-element.100.refs_2_), channel_id=1, source_target_pairs={{0,2},{1,5},{2,0},{3,7},{4,6},{5,1},{6,4},{7,3},{8,10},{9,13},{10,... | collective-permute-start | bytes 884744 | tf_op jit(solution)/shard_map/ppermute | solution.py:42
  41.1 19.7 %collective-permute-start.10 = (bf16[8,96,768]{2,1,0:T(8,128)(2,1)S(1)}, bf16[8,96,768]{2,1,0:T(8,128)(2,1)}, u32[]{:S(2)}, u32[]{:S(2)}) collective-permute-start(bf16[8,96,768]{2,1,0:T(8,128)(2,1)S(1)} %get-tuple-element.98.refs_3_.refs_6_), channel_id=1, source_target_pairs={{0,1},{1,0},{2,3},{3,2},{4,5},{5,4},{6,7},{7,6},{8,9},{9,8},{10,11... | collective-permute-start | bytes 3538952 | tf_op jit(solution)/shard_map/ppermute | solution.py:45
  57.6 17.2 %collective-permute-start.14 = (bf16[8,96,768]{2,1,0:T(8,128)(2,1)S(1)}, bf16[8,96,768]{2,1,0:T(8,128)(2,1)}, u32[]{:S(2)}, u32[]{:S(2)}) collective-permute-start(bf16[8,96,768]{2,1,0:T(8,128)(2,1)S(1)} %get-tuple-element.101.refs_7_.refs_3_.refs_6_), channel_id=1, source_target_pairs={{0,4},{1,3},{2,6},{3,1},{4,0},{5,7},{6,2},{7,5},{8,12},{9,11},{10,... | collective-permute-start | bytes 3538952 | tf_op jit(solution)/shard_map/ppermute | solution.py:42
  59.1 15.7 %collective-permute-start.15 = (bf16[4,96,768]{2,1,0:T(8,128)(2,1)}, bf16[4,96,768]{2,1,0:T(8,128)(2,1)}, u32[]{:S(2)}, u32[]{:S(2)}) collective-permute-start(bf16[4,96,768]{2,1,0:T(8,128)(2,1)} %get-tuple-element.102.refs_8_.refs_0_), channel_id=1, source_target_pairs={{0,8},{1,9},{2,10},{3,11},{4,12},{5,13},{6,14},{7,15},{8,0},{9,1},... | collective-permute-start | bytes 1769480 | tf_op jit(solution)/shard_map/ppermute | solution.py:42
  60.8 16.8 %collective-permute-start.16 = (bf16[8,96,768]{2,1,0:T(8,128)(2,1)S(1)}, bf16[8,96,768]{2,1,0:T(8,128)(2,1)}, u32[]{:S(2)}, u32[]{:S(2)}) collective-permute-start(bf16[8,96,768]{2,1,0:T(8,128)(2,1)S(1)} %get-tuple-element.101.refs_7_.refs_3_.refs_6_), channel_id=1, source_target_pairs={{0,1},{1,0},{2,3},{3,2},{4,5},{5,4},{6,7},{7,6},{8,9},{9,8},{10,11... | collective-permute-start | bytes 3538952 | tf_op jit(solution)/shard_map/ppermute | solution.py:45
  76.7 16.4 %collective-permute-start.18 = (bf16[8,96,768]{2,1,0:T(8,128)(2,1)S(1)}, bf16[8,96,768]{2,1,0:T(8,128)(2,1)}, u32[]{:S(2)}, u32[]{:S(2)}) collective-permute-start(bf16[8,96,768]{2,1,0:T(8,128)(2,1)S(1)} %shard_map.252.refs_7_.refs_10_), channel_id=1, source_target_pairs={{0,4},{1,3},{2,6},{3,1},{4,0},{5,7},{6,2},{7,5},{8,12},{9,11},{10,... | collective-permute-start | bytes 3538952 | tf_op jit(solution)/shard_map/ppermute | solution.py:42
  98.5 22.0 %collective-permute-start.22 = (bf16[8,96,768]{2,1,0:T(8,128)(2,1)S(1)}, bf16[8,96,768]{2,1,0:T(8,128)(2,1)S(1)}, u32[]{:S(2)}, u32[]{:S(2)}) collective-permute-start(bf16[8,96,768]{2,1,0:T(8,128)(2,1)S(1)} %get-tuple-element.118.refs_14_), channel_id=1, source_target_pairs={{0,4},{1,3},{2,6},{3,1},{4,0},{5,7},{6,2},{7,5},{8,12},{9,11},{10,... | collective-permute-start | bytes 3538952 | tf_op jit(solution)/shard_map/ppermute | solution.py:42
  128.5 28.3 %collective-permute-start.26 = (bf16[8,96,768]{2,1,0:T(8,128)(2,1)S(1)}, bf16[8,96,768]{2,1,0:T(8,128)(2,1)S(1)}, u32[]{:S(2)}, u32[]{:S(2)}) collective-permute-start(bf16[8,96,768]{2,1,0:T(8,128)(2,1)S(1)} %get-tuple-element.128.refs_11_), channel_id=1, source_target_pairs={{0,4},{1,3},{2,6},{3,1},{4,0},{5,7},{6,2},{7,5},{8,12},{9,11},{10,... | collective-permute-start | bytes 3538952 | tf_op jit(solution)/shard_map/ppermute | solution.py:42
  129.4 27.4 %collective-permute-start.24 = (bf16[2,208,768]{2,1,0:T(8,128)(2,1)S(1)}, bf16[2,208,768]{2,1,0:T(8,128)(2,1)}, u32[]{:S(2)}, u32[]{:S(2)}) collective-permute-start(bf16[2,208,768]{2,1,0:T(8,128)(2,1)S(1)} %copy-done.49), channel_id=1, source_target_pairs={{0,2},{1,3},{2,0},{3,1},{4,6},{5,7},{6,4},{7,5},{8,10},{9,11},{10,... | collective-permute-start | bytes 1916936 | tf_op jit(solution)/shard_map/ppermute | solution.py:45
  130.6 26.1 %collective-permute-start.25 = (bf16[4,96,768]{2,1,0:T(8,128)(2,1)S(1)}, bf16[4,96,768]{2,1,0:T(8,128)(2,1)S(1)}, u32[]{:S(2)}, u32[]{:S(2)}) collective-permute-start(bf16[4,96,768]{2,1,0:T(8,128)(2,1)S(1)} %get-tuple-element.125.refs_2_.refs_10_), channel_id=1, source_target_pairs={{0,8},{1,9},{2,10},{3,11},{4,12},{5,13},{6,14},{7,15},{8,0},{9,1},... | collective-permute-start | bytes 1769480 | tf_op jit(solution)/shard_map/ppermute | solution.py:42
  166.0 20.1 %collective-permute-start.30 = (bf16[800,768]{1,0:T(8,128)(2,1)}, bf16[800,768]{1,0:T(8,128)(2,1)S(1)}, u32[]{:S(2)}, u32[]{:S(2)}) collective-permute-start(bf16[800,768]{1,0:T(8,128)(2,1)} %get-tuple-element.151), channel_id=1, source_target_pairs={{0,4},{1,3},{2,6},{3,1},{4,0},{5,7},{6,2},{7,5},{8,12},{9,11},{10,... | collective-permute-start | bytes 3686408 | tf_op jit(solution)/shard_map/ppermute | solution.py:42
  167.7 15.7 %collective-permute-start.32 = (bf16[4,96,768]{2,1,0:T(8,128)(2,1)S(1)}, bf16[4,96,768]{2,1,0:T(8,128)(2,1)S(1)}, u32[]{:S(2)}, u32[]{:S(2)}) collective-permute-start(bf16[4,96,768]{2,1,0:T(8,128)(2,1)S(1)} %copy-done.48), channel_id=1, source_target_pairs={{0,8},{1,9},{2,10},{3,11},{4,12},{5,13},{6,14},{7,15},{8,0},{9,1},... | collective-permute-start | bytes 1769480 | tf_op jit(solution)/shard_map/ppermute | solution.py:42
  168.8 9.9 %collective-permute-start.31 = (bf16[2,96,768]{2,1,0:T(8,128)(2,1)S(1)}, bf16[2,96,768]{2,1,0:T(8,128)(2,1)S(1)}, u32[]{:S(2)}, u32[]{:S(2)}) collective-permute-start(bf16[2,96,768]{2,1,0:T(8,128)(2,1)S(1)} %copy-done.28), channel_id=1, source_target_pairs={{0,2},{1,5},{2,0},{3,7},{4,6},{5,1},{6,4},{7,3},{8,10},{9,13},{10,... | collective-permute-start | bytes 884744 | tf_op jit(solution)/shard_map/ppermute | solution.py:42
  187.9 13.6 %collective-permute-start.33 = (bf16[416,768]{1,0:T(8,128)(2,1)S(1)}, bf16[416,768]{1,0:T(8,128)(2,1)S(1)}, u32[]{:S(2)}, u32[]{:S(2)}) collective-permute-start(bf16[416,768]{1,0:T(8,128)(2,1)S(1)} %get-tuple-element.158), channel_id=1, source_target_pairs={{0,2},{1,9},{2,0},{3,11},{4,6},{5,13},{6,4},{7,15},{8,10},{9,1},{1... | collective-permute-start | bytes 1916936 | tf_op jit(solution)/shard_map/ppermute | solution.py:42
  189.4 12.0 %collective-permute-start.34 = (bf16[2,96,768]{2,1,0:T(8,128)(2,1)S(1)}, bf16[2,96,768]{2,1,0:T(8,128)(2,1)S(1)}, u32[]{:S(2)}, u32[]{:S(2)}) collective-permute-start(bf16[2,96,768]{2,1,0:T(8,128)(2,1)S(1)} %get-tuple-element.160), channel_id=1, source_target_pairs={{0,2},{1,5},{2,0},{3,7},{4,6},{5,1},{6,4},{7,3},{8,10},{9,13},{10,... | collective-permute-start | bytes 884744 | tf_op jit(solution)/shard_map/ppermute | solution.py:42
  204.7 15.1 %collective-permute-start.36 = (bf16[2,208,768]{2,1,0:T(8,128)(2,1)}, bf16[2,208,768]{2,1,0:T(8,128)(2,1)S(1)}, u32[]{:S(2)}, u32[]{:S(2)}) collective-permute-start(bf16[2,208,768]{2,1,0:T(8,128)(2,1)} %shard_map.269.refs_0_), channel_id=1, source_target_pairs={{0,2},{1,3},{2,0},{3,1},{4,6},{5,7},{6,4},{7,5},{8,10},{9,11},{10,... | collective-permute-start | bytes 1916936 | tf_op jit(solution)/shard_map/ppermute | solution.py:45
  221.1 11.9 %collective-permute-start.41 = (bf16[128,768]{1,0:T(8,128)(2,1)S(1)}, bf16[128,768]{1,0:T(8,128)(2,1)S(1)}, u32[]{:S(2)}, u32[]{:S(2)}) collective-permute-start(bf16[128,768]{1,0:T(8,128)(2,1)S(1)} %get-tuple-element.173), channel_id=1, source_target_pairs={{0,16},{1,17},{2,18},{3,19},{4,20},{5,21},{6,22},{7,23},{8,24},{9,... | collective-permute-start | bytes 589832 | tf_op jit(solution)/shard_map/ppermute | solution.py:42
  (85 other events, 436.3 us)

commit v9 on v8

--- a/solution.py
+++ b/solution.py
@@ -271,15 +271,22 @@
         out_ref[pl.ds(6 + 2 * n_t + t, 1), :width] = dbias[:, 2 * width :]
 
 
-def finish_with_small(kept, came, small, after=()):
+def finish_with_small(kept, came, small, width, after=()):
     rows, d = kept.shape
 
     def kernel(kept_ref, came_ref, small_ref, *refs):
-        outs = refs[len(after) :]
-        outs[0][...] = kept_ref[...].astype(f32) + came_ref[:rows, :].astype(f32)
-        outs[1][...] = (small_ref[...].astype(f32) + came_ref[rows:, :].astype(f32)).astype(bf16)
-
-    shapes = [jax.ShapeDtypeStruct((rows, d), f32), jax.ShapeDtypeStruct(small.shape, bf16)]
+        qkv_ref, out_ref, low_ref = refs[len(after) :]
+        value = kept_ref[...].astype(f32) + came_ref[:rows, :].astype(f32)
+        for i in range(3):
+            qkv_ref[i] = value[:, i * width : (i + 1) * width]
+        out_ref[...] = value[:, 3 * width :].T
+        low_ref[...] = (small_ref[...].astype(f32) + came_ref[rows:, :].astype(f32)).astype(bf16)
+
+    shapes = [
+        jax.ShapeDtypeStruct((3, rows, width), f32),
+        jax.ShapeDtypeStruct((width, rows), f32),
+        jax.ShapeDtypeStruct(small.shape, bf16),
+    ]
     return vmem_call(kernel, shapes, [kept, came, small], after)
 
 
@@ -775,12 +782,16 @@
                 patch_grad = place_images(cube, spread(images, there), length)
             small = (small,)
         two_grad, one_grad = grads[2], grads[1]
-        attn_grad, small = finish_with_small(k_attn, c_attn, small[0], (patch_grad,))
+        qkv_grad, out_grad, small = finish_with_small(
+            k_attn, c_attn, small[0], width
+        )
         small = small.astype(f32) + cube.flip(small, 1).astype(f32)
     else:
         two_grad = scatter_plain(cube, *two_grads)
         one_grad = scatter_plain(cube, *one_grads)
         attn_grad = scatter_plain(cube, *attn_grads)
+        qkv_grad = jnp.stack([attn_grad[:, i * width : (i + 1) * width] for i in range(3)])
+        out_grad = attn_grad[:, 3 * width :].T
         encoded = place_images(cube, [enc.reshape(count, padded, d)], length)
         patch_grad = place_images(cube, [patch_of(())], length)
 
@@ -798,9 +809,9 @@
         patch_grad,
         small[0],
         small[1],
-        jnp.stack([attn_grad[:, i * width : (i + 1) * width] for i in range(3)]),
+        qkv_grad,
         jnp.concatenate((shard_row(6 + n_t), shard_row(6 + 2 * n_t)))[:, :width],
-        attn_grad[:, 3 * width :].T,
+        out_grad,
         small[5],
         small[2],
         small[3],

time: 237 us -> 235 us (level)
    unnamed x136 -> x135, local copies, waits for them, and re-layouts: 20.4 us -> 20.5 us
  transfers between devices with their start and end apart: 43 -> 43, of which waited for: 25 -> 24; matrix products, arithmetic and copies ran while one was open for 5% -> 4% of each run, Pallas kernels for 37% -> 36%
where the time goes in v9:
time: 235 us
  Pallas kernels  93.5 us (40%)
  waiting for transfers between devices  70.3 us (30%)
  starting transfers between devices  37.6 us (16%)
  local copies, waits for them, and re-layouts  30.4 us (13%)
    pallas_call x7, Pallas kernels, call(): pl.pallas_call(body, out_shape=[*out_shapes, *grads], in_specs=[pl.BlockS...  81.8 us
    ppermute x24, waiting for transfers between devices, swap(): lax.ppermute(value, AXES, [(i, i ^ 1 << orders[i & 1][k]) for i in range(...  56.6 us
    ppermute x24, starting transfers between devices, swap(): lax.ppermute(value, AXES, [(i, i ^ 1 << orders[i & 1][k]) for i in range(...  30.1 us
    unnamed x135, local copies, waits for them, and re-layouts  20.5 us
    ppermute x19, waiting for transfers between devices, flip(): return lax.ppermute(value, AXES, [(i, i ^ bits) for i in range(self.n)])  13.7 us
    pallas_call x9, Pallas kernels, vmem_call(): pl.pallas_call(kernel, out_shape=shapes, in_specs=specs, out_specs=[pl.Bl...  9.07 us
    ppermute x19, starting transfers between devices, flip(): return lax.ppermute(value, AXES, [(i, i ^ bits) for i in range(self.n)])  7.54 us
  transfers between devices with their start and end apart: 43, of which 24 were waited for; matrix products, arithmetic and copies ran while one was open for 4% of the time, Pallas kernels for 36%

profile of v9, /device:TPU:0, one launch (start us, length us, event | category | flops | bytes accessed | tf_op | source)
XLA Modules:
  0.0 234.6 jit_solution(10901807968133787583)
XLA Ops:
  2.5 4.1 %collective-permute-start.3 = (bf16[1,96,768]{2,1,0:T(8,128)(2,1)S(1)}, bf16[1,96,768]{2,1,0:T(8,128)(2,1)S(1)}, u32[]{:S(2)}, u32[]{:S(2)}) collective-permute-start(bf16[1,96,768]{2,1,0:T(8,128)(2,1)S(1)} %maximum_bitcast_fusion.refs_0_), channel_id=1, source_target_pairs={{0,16},{1,17},{2,18},{3,19},{4,20},{5,21},{6,22},{7,23},{8,24},{9,... | collective-permute-start | bytes 442376 | tf_op jit(solution)/shard_map/ppermute | solution.py:42
  7.4 3.7 %constant_dynamic-slice_fusion.2 = (bf16[2,197,768]{2,0,1:T(2,128)(2,1)S(1)}, bf16[2,197,768]{2,0,1:T(2,128)(2,1)S(1)}) fusion(bf16[8,197,768]{2,0,1:T(8,128)(2,1)} %param.27, s32[]{:T(128)S(6)} %select_n.13, bf16[8,197,768]{2,0,1:T(8,128)(2,1)} %param.14), kind=kLoop, calls=%fused_computation.24 | loop fusion | bytes 2420740 | tf_op jit(solution)/shard_map/dynamic_slice | solution.py:595
  18.5 6.2 %collective-permute-done.5.refs_3_ = bf16[1,96,768]{2,1,0:T(8,128)(2,1)S(1)} collective-permute-done((bf16[1,96,768]{2,1,0:T(8,128)(2,1)S(1)}, bf16[1,96,768]{2,1,0:T(8,128)(2,1)S(1)}, u32[]{:S(2)}, u32[]{:S(2)}) %collective-permute-start.5) | collective-permute-done | bytes 147488 | tf_op jit(solution)/shard_map/ppermute | solution.py:42
  28.1 8.4 %collective-permute-done.8.refs_5_ = bf16[1,96,768]{2,1,0:T(8,128)(2,1)S(1)} collective-permute-done((bf16[1,96,768]{2,1,0:T(8,128)(2,1)S(1)}, bf16[1,96,768]{2,1,0:T(8,128)(2,1)S(1)}, u32[]{:S(2)}, u32[]{:S(2)}) %collective-permute-start.8) | collective-permute-done | bytes 147488 | tf_op jit(solution)/shard_map/ppermute | solution.py:42
  41.1 15.2 %collective-permute-done.9.refs_4_.refs_7_ = bf16[8,96,768]{2,1,0:T(8,128)(2,1)S(1)} collective-permute-done((bf16[8,96,768]{2,1,0:T(8,128)(2,1)S(1)}, bf16[8,96,768]{2,1,0:T(8,128)(2,1)S(1)}, u32[]{:S(2)}, u32[]{:S(2)}) %collective-permute-start.9) | collective-permute-done | bytes 1179680 | tf_op jit(solution)/shard_map/ppermute | solution.py:42
  60.8 14.0 %shard_map.250 = (bf16[416,768]{1,0:T(8,128)(2,1)}, bf16[4,416,576]{2,1,0:T(8,128)(2,1)}, bf16[4,416,192]{2,1,0:T(8,128)(2,1)}, f32[416,768]{1,0:T(8,128)}, bf16[416,768]{1,0:T(8,128)(2,1)}, /*index=5*/f32[8,128]{1,0:T(8,128)}) custom-call(s32[2]{0:T(128)} %pad_add_fusion.index_ref.ids_ref, bf16[416,768]{1,0:T(8,128)(2,1)} %bitcast.30, f32[6,768]{1,0:T(8,128)} %copy-done.22, ...), custom_call_target="tpu_custom_call" | custom-call | bytes 1024 | tf_op jit(solution)/shard_map/pallas_call | solution.py:339
  79.1 13.6 %shard_map.253 = (bf16[4,416,768]{2,1,0:T(8,128)(2,1)}, bf16[4,416,768]{2,1,0:T(8,128)(2,1)}, f32[8,128]{1,0:T(8,128)}, bf16[16,96,768]{2,1,0:T(8,128)(2,1)}, bf16[16,96,768]{2,1,0:T(8,128)(2,1)}) custom-call(s32[2]{0:T(128)} %pad_add_fusion.index_ref.ids_ref, bf16[416,768]{1,0:T(8,128)(2,1)} %get-tuple-element.107.refs_0_, bf16[416,768]{1,0:T(8,128)(2,1)} %bitcast.37, ...), custom_call_target="tpu_custom_call" | custom-call | bytes 1024 | tf_op jit(solution)/shard_map/pallas_call | solution.py:339
  94.9 3.0 %collective-permute-done.21.refs_1_ = bf16[16,96,768]{2,1,0:T(8,128)(2,1)S(1)} collective-permute-done((bf16[16,96,768]{2,1,0:T(8,128)(2,1)}, bf16[16,96,768]{2,1,0:T(8,128)(2,1)S(1)}, u32[]{:S(2)}, u32[]{:S(2)}) %collective-permute-start.21) | collective-permute-done | bytes 2359328 | tf_op jit(solution)/shard_map/ppermute | solution.py:45
  102.5 17.9 %shard_map.256 = (f32[4,1,768]{2,1,0:T(1,128)}, bf16[416,768]{1,0:T(8,128)(2,1)}, f32[416,768]{1,0:T(8,128)}, f32[4,1,768]{2,1,0:T(1,128)}, f32[8,128]{1,0:T(8,1...) custom-call(s32[2]{0:T(128)} %pad_add_fusion.index_ref.ids_ref, ...), custom_call_target="tpu_custom_call" | custom-call | bytes 1024 | tf_op jit(solution)/shard_map/pallas_call | solution.py:339
  124.4 1.9 collective-permute-done.23.refs_1_
  131.6 25.2 %shard_map.260 = (f32[4,1,576]{2,1,0:T(1,128)}, f32[416,768]{1,0:T(8,128)}, f32[2,1,768]{2,1,0:T(1,128)}, f32[8,128]{1,0:T(8,128)}, bf16[16,96,768]{2,1,0:T(8,128)(2,1)}, /*index=5*/bf16[16,96,768]{2,1,0:T(8,128)(2,1)}) custom-call(s32[2]{0:T(128)} %pad_add_fusion.index_ref.ids_ref, bf16[416,768]{1,0:T(8,128)(2,1)} %bitcast.31, ...), custom_call_target="tpu_custom_call" | custom-call | bytes 1024 | tf_op jit(solution)/shard_map/pallas_call | solution.py:339
  163.1 2.3 shard_map.263
  171.3 3.8 %shard_map.265 = (bf16[197,8,768]{2,1,0:T(8,128)(2,1)}, f32[8,128]{1,0:T(8,128)}) custom-call(s32[1]{0:T(128)} %bitcast.index_ref, bf16[2,208,768]{2,1,0:T(8,128)(2,1)} %get-tuple-element.147.refs_0_, bf16[2,208,768]{2,1,0:T(8,128)(2,1)} %copy-done.56, bf16[2,208,768]{2,1,0:T(8,128)(2,1)} %get-tuple-element.148.refs_2_, bf16[2,208,768]{2,1,0:T(8,128)(2,1)} %copy-done.57), custom_call_target="tpu_custom_call" | custom-call | bytes 1024 | tf_op jit(solution)/shard_map/pallas_call | solution.py:339
  175.1 2.2 copy.57
  178.7 4.6 %collective-permute-done.32.refs_4_ = bf16[4,96,768]{2,1,0:T(8,128)(2,1)S(1)} collective-permute-done((bf16[4,96,768]{2,1,0:T(8,128)(2,1)S(1)}, bf16[4,96,768]{2,1,0:T(8,128)(2,1)S(1)}, u32[]{:S(2)}, u32[]{:S(2)}) %collective-permute-start.32) | collective-permute-done | bytes 589856 | tf_op jit(solution)/shard_map/ppermute | solution.py:42
  183.3 2.8 %collective-permute-done.30.came_ref = bf16[800,768]{1,0:T(8,128)(2,1)S(1)} collective-permute-done((bf16[800,768]{1,0:T(8,128)(2,1)}, bf16[800,768]{1,0:T(8,128)(2,1)S(1)}, u32[]{:S(2)}, u32[]{:S(2)}) %collective-permute-start.30) | collective-permute-done | bytes 1228832 | tf_op jit(solution)/shard_map/ppermute | solution.py:42
  189.9 2.0 collective-permute-start.35
  192.0 3.5 %shard_map.267 = (bf16[416,768]{1,0:T(8,128)(2,1)}, f32[8,128]{1,0:T(8,128)}) custom-call(s32[2]{0:T(128)} %pad_add_fusion.index_ref.ids_ref, bf16[416,768]{1,0:T(8,128)(2,1)} %bitcast.32, f32[416,768]{1,0:T(8,128)} %get-tuple-element.120.refs_4_.refs_1_, f32[416,768]{1,0:T(8,128)} %get-tuple-element.150.refs_2_, f32[6,768]{1,0:T(8,128)} %copy-done.22, ...), custom_call_target="tpu_custom_call" | custom-call | bytes 1024 | tf_op jit(solution)/shard_map/pallas_call | solution.py:339
  196.9 4.5 %collective-permute-done.34.refs_2_ = bf16[2,96,768]{2,1,0:T(8,128)(2,1)S(1)} collective-permute-done((bf16[2,96,768]{2,1,0:T(8,128)(2,1)S(1)}, bf16[2,96,768]{2,1,0:T(8,128)(2,1)S(1)}, u32[]{:S(2)}, u32[]{:S(2)}) %collective-permute-start.34) | collective-permute-done | bytes 294944 | tf_op jit(solution)/shard_map/ppermute | solution.py:42
  207.2 2.4 %collective-permute-start.38 = (bf16[1,96,768]{2,1,0:T(8,128)(2,1)S(1)}, bf16[1,96,768]{2,1,0:T(8,128)(2,1)S(1)}, u32[]{:S(2)}, u32[]{:S(2)}) collective-permute-start(bf16[1,96,768]{2,1,0:T(8,128)(2,1)S(1)} %get-tuple-element.168), channel_id=1, source_target_pairs={{0,16},{1,17},{2,18},{3,19},{4,20},{5,21},{6,22},{7,23},{8,24},{9,... | collective-permute-start | bytes 442376 | tf_op jit(solution)/shard_map/ppermute | solution.py:42
  209.5 4.1 %collective-permute-done.38.refs_2_ = bf16[1,96,768]{2,1,0:T(8,128)(2,1)S(1)} collective-permute-done((bf16[1,96,768]{2,1,0:T(8,128)(2,1)S(1)}, bf16[1,96,768]{2,1,0:T(8,128)(2,1)S(1)}, u32[]{:S(2)}, u32[]{:S(2)}) %collective-permute-start.38) | collective-permute-done | bytes 147488 | tf_op jit(solution)/shard_map/ppermute | solution.py:42
  217.1 2.1 collective-permute-start.41
  221.1 4.6 %collective-permute-done.41.came_ref = bf16[128,768]{1,0:T(8,128)(2,1)S(1)} collective-permute-done((bf16[128,768]{1,0:T(8,128)(2,1)S(1)}, bf16[128,768]{1,0:T(8,128)(2,1)S(1)}, u32[]{:S(2)}, u32[]{:S(2)}) %collective-permute-start.41) | collective-permute-done | bytes 196640 | tf_op jit(solution)/shard_map/ppermute | solution.py:42
  230.8 3.8 %shard_map.272 = (bf16[197,8,768]{2,1,0:T(8,128)(2,1)}, f32[8,128]{1,0:T(8,128)}) custom-call(s32[1]{0:T(128)} %bitcast.index_ref, bf16[2,208,768]{2,1,0:T(8,128)(2,1)} %get-tuple-element.170.refs_0_, bf16[2,208,768]{2,1,0:T(8,128)(2,1)} %copy-done.54, bf16[2,208,768]{2,1,0:T(8,128)(2,1)} %get-tuple-element.171.refs_2_, bf16[2,208,768]{2,1,0:T(8,128)(2,1)} %copy-done.55), custom_call_target="tpu_custom_call" | custom-call | bytes 1024 | tf_op jit(solution)/shard_map/pallas_call | solution.py:339
  (254 shorter events, 77.3 us)
Async XLA Ops:
  2.5 14.8 %collective-permute-start.3 = (bf16[1,96,768]{2,1,0:T(8,128)(2,1)S(1)}, bf16[1,96,768]{2,1,0:T(8,128)(2,1)S(1)}, u32[]{:S(2)}, u32[]{:S(2)}) collective-permute-start(bf16[1,96,768]{2,1,0:T(8,128)(2,1)S(1)} %maximum_bitcast_fusion.refs_0_), channel_id=1, source_target_pairs={{0,16},{1,17},{2,18},{3,19},{4,20},{5,21},{6,22},{7,23},{8,24},{9,... | collective-permute-start | bytes 442376 | tf_op jit(solution)/shard_map/ppermute | solution.py:42
  14.5 10.2 %collective-permute-start.5 = (bf16[1,96,768]{2,1,0:T(8,128)(2,1)S(1)}, bf16[1,96,768]{2,1,0:T(8,128)(2,1)S(1)}, u32[]{:S(2)}, u32[]{:S(2)}) collective-permute-start(bf16[1,96,768]{2,1,0:T(8,128)(2,1)S(1)} %bitcast.43), channel_id=1, source_target_pairs={{0,16},{1,17},{2,18},{3,19},{4,20},{5,21},{6,22},{7,23},{8,24},{9,... | collective-permute-start | bytes 442376 | tf_op jit(solution)/shard_map/ppermute | solution.py:42
  24.8 13.1 %collective-permute-start.6 = (bf16[4,96,768]{2,1,0:T(8,128)(2,1)S(1)}, bf16[4,96,768]{2,1,0:T(8,128)(2,1)S(1)}, u32[]{:S(2)}, u32[]{:S(2)}) collective-permute-start(bf16[4,96,768]{2,1,0:T(8,128)(2,1)S(1)} %get-tuple-element.97.refs_0_), channel_id=1, source_target_pairs={{0,8},{1,5},{2,10},{3,7},{4,12},{5,1},{6,14},{7,3},{8,0},{9,13},{1... | collective-permute-start | bytes 1769480 | tf_op jit(solution)/shard_map/ppermute | solution.py:42
  25.9 10.6 %collective-permute-start.7 = (bf16[2,96,768]{2,1,0:T(8,128)(2,1)S(1)}, bf16[2,96,768]{2,1,0:T(8,128)(2,1)S(1)}, u32[]{:S(2)}, u32[]{:S(2)}) collective-permute-start(bf16[2,96,768]{2,1,0:T(8,128)(2,1)S(1)} %get-tuple-element.98.refs_2_), channel_id=1, source_target_pairs={{0,2},{1,5},{2,0},{3,7},{4,6},{5,1},{6,4},{7,3},{8,10},{9,13},{10,... | collective-permute-start | bytes 884744 | tf_op jit(solution)/shard_map/ppermute | solution.py:42
  26.8 9.7 %collective-permute-start.8 = (bf16[1,96,768]{2,1,0:T(8,128)(2,1)S(1)}, bf16[1,96,768]{2,1,0:T(8,128)(2,1)S(1)}, u32[]{:S(2)}, u32[]{:S(2)}) collective-permute-start(bf16[1,96,768]{2,1,0:T(8,128)(2,1)S(1)} %bitcast.41), channel_id=1, source_target_pairs={{0,16},{1,17},{2,18},{3,19},{4,20},{5,21},{6,22},{7,23},{8,24},{9,... | collective-permute-start | bytes 442376 | tf_op jit(solution)/shard_map/ppermute | solution.py:42
  38.0 18.3 %collective-permute-start.9 = (bf16[8,96,768]{2,1,0:T(8,128)(2,1)S(1)}, bf16[8,96,768]{2,1,0:T(8,128)(2,1)S(1)}, u32[]{:S(2)}, u32[]{:S(2)}) collective-permute-start(bf16[8,96,768]{2,1,0:T(8,128)(2,1)S(1)} %get-tuple-element.99.refs_3_.refs_6_), channel_id=1, source_target_pairs={{0,4},{1,3},{2,6},{3,1},{4,0},{5,7},{6,2},{7,5},{8,12},{9,11},{10,... | collective-permute-start | bytes 3538952 | tf_op jit(solution)/shard_map/ppermute | solution.py:42
  39.6 16.7 %collective-permute-start.12 = (bf16[4,96,768]{2,1,0:T(8,128)(2,1)S(1)}, bf16[4,96,768]{2,1,0:T(8,128)(2,1)S(1)}, u32[]{:S(2)}, u32[]{:S(2)}) collective-permute-start(bf16[4,96,768]{2,1,0:T(8,128)(2,1)S(1)} %get-tuple-element.100.refs_0_), channel_id=1, source_target_pairs={{0,8},{1,9},{2,10},{3,11},{4,12},{5,13},{6,14},{7,15},{8,0},{9,1},... | collective-permute-start | bytes 1769480 | tf_op jit(solution)/shard_map/ppermute | solution.py:42
  39.6 16.7 %collective-permute-start.13 = (bf16[2,96,768]{2,1,0:T(8,128)(2,1)S(1)}, bf16[2,96,768]{2,1,0:T(8,128)(2,1)S(1)}, u32[]{:S(2)}, u32[]{:S(2)}) collective-permute-start(bf16[2,96,768]{2,1,0:T(8,128)(2,1)S(1)} %get-tuple-element.101.refs_2_), channel_id=1, source_target_pairs={{0,2},{1,5},{2,0},{3,7},{4,6},{5,1},{6,4},{7,3},{8,10},{9,13},{10,... | collective-permute-start | bytes 884744 | tf_op jit(solution)/shard_map/ppermute | solution.py:42
  41.1 19.7 %collective-permute-start.10 = (bf16[8,96,768]{2,1,0:T(8,128)(2,1)S(1)}, bf16[8,96,768]{2,1,0:T(8,128)(2,1)}, u32[]{:S(2)}, u32[]{:S(2)}) collective-permute-start(bf16[8,96,768]{2,1,0:T(8,128)(2,1)S(1)} %get-tuple-element.99.refs_3_.refs_6_), channel_id=1, source_target_pairs={{0,1},{1,0},{2,3},{3,2},{4,5},{5,4},{6,7},{7,6},{8,9},{9,8},{10,11... | collective-permute-start | bytes 3538952 | tf_op jit(solution)/shard_map/ppermute | solution.py:45
  57.6 17.2 %collective-permute-start.14 = (bf16[8,96,768]{2,1,0:T(8,128)(2,1)S(1)}, bf16[8,96,768]{2,1,0:T(8,128)(2,1)}, u32[]{:S(2)}, u32[]{:S(2)}) collective-permute-start(bf16[8,96,768]{2,1,0:T(8,128)(2,1)S(1)} %get-tuple-element.102.refs_7_.refs_3_.refs_6_), channel_id=1, source_target_pairs={{0,4},{1,3},{2,6},{3,1},{4,0},{5,7},{6,2},{7,5},{8,12},{9,11},{10,... | collective-permute-start | bytes 3538952 | tf_op jit(solution)/shard_map/ppermute | solution.py:42
  59.1 15.7 %collective-permute-start.15 = (bf16[4,96,768]{2,1,0:T(8,128)(2,1)}, bf16[4,96,768]{2,1,0:T(8,128)(2,1)}, u32[]{:S(2)}, u32[]{:S(2)}) collective-permute-start(bf16[4,96,768]{2,1,0:T(8,128)(2,1)} %get-tuple-element.103.refs_8_.refs_0_), channel_id=1, source_target_pairs={{0,8},{1,9},{2,10},{3,11},{4,12},{5,13},{6,14},{7,15},{8,0},{9,1},... | collective-permute-start | bytes 1769480 | tf_op jit(solution)/shard_map/ppermute | solution.py:42
  60.8 16.8 %collective-permute-start.16 = (bf16[8,96,768]{2,1,0:T(8,128)(2,1)S(1)}, bf16[8,96,768]{2,1,0:T(8,128)(2,1)}, u32[]{:S(2)}, u32[]{:S(2)}) collective-permute-start(bf16[8,96,768]{2,1,0:T(8,128)(2,1)S(1)} %get-tuple-element.102.refs_7_.refs_3_.refs_6_), channel_id=1, source_target_pairs={{0,1},{1,0},{2,3},{3,2},{4,5},{5,4},{6,7},{7,6},{8,9},{9,8},{10,11... | collective-permute-start | bytes 3538952 | tf_op jit(solution)/shard_map/ppermute | solution.py:45
  76.8 16.4 %collective-permute-start.18 = (bf16[8,96,768]{2,1,0:T(8,128)(2,1)S(1)}, bf16[8,96,768]{2,1,0:T(8,128)(2,1)}, u32[]{:S(2)}, u32[]{:S(2)}) collective-permute-start(bf16[8,96,768]{2,1,0:T(8,128)(2,1)S(1)} %shard_map.252.refs_7_.refs_10_), channel_id=1, source_target_pairs={{0,4},{1,3},{2,6},{3,1},{4,0},{5,7},{6,2},{7,5},{8,12},{9,11},{10,... | collective-permute-start | bytes 3538952 | tf_op jit(solution)/shard_map/ppermute | solution.py:42
  98.5 22.0 %collective-permute-start.22 = (bf16[8,96,768]{2,1,0:T(8,128)(2,1)S(1)}, bf16[8,96,768]{2,1,0:T(8,128)(2,1)S(1)}, u32[]{:S(2)}, u32[]{:S(2)}) collective-permute-start(bf16[8,96,768]{2,1,0:T(8,128)(2,1)S(1)} %get-tuple-element.119.refs_14_), channel_id=1, source_target_pairs={{0,4},{1,3},{2,6},{3,1},{4,0},{5,7},{6,2},{7,5},{8,12},{9,11},{10,... | collective-permute-start | bytes 3538952 | tf_op jit(solution)/shard_map/ppermute | solution.py:42
  128.5 28.3 %collective-permute-start.26 = (bf16[8,96,768]{2,1,0:T(8,128)(2,1)S(1)}, bf16[8,96,768]{2,1,0:T(8,128)(2,1)S(1)}, u32[]{:S(2)}, u32[]{:S(2)}) collective-permute-start(bf16[8,96,768]{2,1,0:T(8,128)(2,1)S(1)} %get-tuple-element.129.refs_11_), channel_id=1, source_target_pairs={{0,4},{1,3},{2,6},{3,1},{4,0},{5,7},{6,2},{7,5},{8,12},{9,11},{10,... | collective-permute-start | bytes 3538952 | tf_op jit(solution)/shard_map/ppermute | solution.py:42
  129.4 27.4 %collective-permute-start.24 = (bf16[2,208,768]{2,1,0:T(8,128)(2,1)S(1)}, bf16[2,208,768]{2,1,0:T(8,128)(2,1)}, u32[]{:S(2)}, u32[]{:S(2)}) collective-permute-start(bf16[2,208,768]{2,1,0:T(8,128)(2,1)S(1)} %copy-done.49), channel_id=1, source_target_pairs={{0,2},{1,3},{2,0},{3,1},{4,6},{5,7},{6,4},{7,5},{8,10},{9,11},{10,... | collective-permute-start | bytes 1916936 | tf_op jit(solution)/shard_map/ppermute | solution.py:45
  130.7 26.1 %collective-permute-start.25 = (bf16[4,96,768]{2,1,0:T(8,128)(2,1)S(1)}, bf16[4,96,768]{2,1,0:T(8,128)(2,1)S(1)}, u32[]{:S(2)}, u32[]{:S(2)}) collective-permute-start(bf16[4,96,768]{2,1,0:T(8,128)(2,1)S(1)} %get-tuple-element.126.refs_2_.refs_10_), channel_id=1, source_target_pairs={{0,8},{1,9},{2,10},{3,11},{4,12},{5,13},{6,14},{7,15},{8,0},{9,1},... | collective-permute-start | bytes 1769480 | tf_op jit(solution)/shard_map/ppermute | solution.py:42
  166.1 20.1 %collective-permute-start.30 = (bf16[800,768]{1,0:T(8,128)(2,1)}, bf16[800,768]{1,0:T(8,128)(2,1)S(1)}, u32[]{:S(2)}, u32[]{:S(2)}) collective-permute-start(bf16[800,768]{1,0:T(8,128)(2,1)} %get-tuple-element.152), channel_id=1, source_target_pairs={{0,4},{1,3},{2,6},{3,1},{4,0},{5,7},{6,2},{7,5},{8,12},{9,11},{10,... | collective-permute-start | bytes 3686408 | tf_op jit(solution)/shard_map/ppermute | solution.py:42
  167.7 15.6 %collective-permute-start.32 = (bf16[4,96,768]{2,1,0:T(8,128)(2,1)S(1)}, bf16[4,96,768]{2,1,0:T(8,128)(2,1)S(1)}, u32[]{:S(2)}, u32[]{:S(2)}) collective-permute-start(bf16[4,96,768]{2,1,0:T(8,128)(2,1)S(1)} %copy-done.48), channel_id=1, source_target_pairs={{0,8},{1,9},{2,10},{3,11},{4,12},{5,13},{6,14},{7,15},{8,0},{9,1},... | collective-permute-start | bytes 1769480 | tf_op jit(solution)/shard_map/ppermute | solution.py:42
  168.8 9.9 %collective-permute-start.31 = (bf16[2,96,768]{2,1,0:T(8,128)(2,1)S(1)}, bf16[2,96,768]{2,1,0:T(8,128)(2,1)S(1)}, u32[]{:S(2)}, u32[]{:S(2)}) collective-permute-start(bf16[2,96,768]{2,1,0:T(8,128)(2,1)S(1)} %copy-done.28), channel_id=1, source_target_pairs={{0,2},{1,5},{2,0},{3,7},{4,6},{5,1},{6,4},{7,3},{8,10},{9,13},{10,... | collective-permute-start | bytes 884744 | tf_op jit(solution)/shard_map/ppermute | solution.py:42
  187.9 13.6 %collective-permute-start.33 = (bf16[416,768]{1,0:T(8,128)(2,1)S(1)}, bf16[416,768]{1,0:T(8,128)(2,1)S(1)}, u32[]{:S(2)}, u32[]{:S(2)}) collective-permute-start(bf16[416,768]{1,0:T(8,128)(2,1)S(1)} %get-tuple-element.159), channel_id=1, source_target_pairs={{0,2},{1,9},{2,0},{3,11},{4,6},{5,13},{6,4},{7,15},{8,10},{9,1},{1... | collective-permute-start | bytes 1916936 | tf_op jit(solution)/shard_map/ppermute | solution.py:42
  189.4 12.1 %collective-permute-start.34 = (bf16[2,96,768]{2,1,0:T(8,128)(2,1)S(1)}, bf16[2,96,768]{2,1,0:T(8,128)(2,1)S(1)}, u32[]{:S(2)}, u32[]{:S(2)}) collective-permute-start(bf16[2,96,768]{2,1,0:T(8,128)(2,1)S(1)} %get-tuple-element.161), channel_id=1, source_target_pairs={{0,2},{1,5},{2,0},{3,7},{4,6},{5,1},{6,4},{7,3},{8,10},{9,13},{10,... | collective-permute-start | bytes 884744 | tf_op jit(solution)/shard_map/ppermute | solution.py:42
  204.7 15.1 %collective-permute-start.36 = (bf16[2,208,768]{2,1,0:T(8,128)(2,1)}, bf16[2,208,768]{2,1,0:T(8,128)(2,1)S(1)}, u32[]{:S(2)}, u32[]{:S(2)}) collective-permute-start(bf16[2,208,768]{2,1,0:T(8,128)(2,1)} %shard_map.269.refs_0_), channel_id=1, source_target_pairs={{0,2},{1,3},{2,0},{3,1},{4,6},{5,7},{6,4},{7,5},{8,10},{9,11},{10,... | collective-permute-start | bytes 1916936 | tf_op jit(solution)/shard_map/ppermute | solution.py:45
  206.2 8.9 %collective-permute-start.37 = (bf16[224,768]{1,0:T(8,128)(2,1)S(1)}, bf16[224,768]{1,0:T(8,128)(2,1)S(1)}, u32[]{:S(2)}, u32[]{:S(2)}) collective-permute-start(bf16[224,768]{1,0:T(8,128)(2,1)S(1)} %get-tuple-element.166), channel_id=1, source_target_pairs={{0,8},{1,5},{2,10},{3,7},{4,12},{5,1},{6,14},{7,3},{8,0},{9,13},{1... | collective-permute-start | bytes 1032200 | tf_op jit(solution)/shard_map/ppermute | solution.py:42
  (85 other events, 451.2 us)
